TPU v7x, 32 devices: a whole 2x2x4 slice. The times are simulated.
32 devices in a mesh: row: 2 (over core), col: 16 (over z, y, x).
Axes of the slice: x: 2, y: 2, z: 4, core: 2. Of those that a mesh axis runs over, the one named last changes fastest.
Arguments:
- image_emb: bfloat16 [2560, 1152], P(('row', 'col')), may hold values from -6 to 6
- text_emb: bfloat16 [2560, 1152], P('col', 'row'), may hold values from -6 to 6
- image_valid: int32 [2560], P(('row', 'col')), may hold values from 0 to 4
- text_valid: int32 [2560], P('col'), may hold values from 0 to 4
- sample_count: int32 [1], replicated, may hold values from 2560 to 5119
- logit_scale: float32 [1], replicated, may hold values from 0.029462783 to 0.088388346
- logit_bias: float32 [1], replicated, may hold values from -4 to -1
- loss_grad: float32 [1], replicated, may hold values from 256 to 1024
Outputs:
- image_grad: bfloat16 [2560, 1152], P(('row', 'col'))
- text_grad: bfloat16 [2560, 1152], P('col', 'row')
All inputs are finite; a program needn't handle non-finite values.
Results may differ from a plain program's by a relative error of at most 0.0042.
Values may be sent and summed in bfloat16 or wider, within the bound.
No kernel may reach another device: no remote copies, remote signals or barrier semaphores. Data moves between devices by JAX's collectives and lax.ppermute only.
A program may use at most 64 MiB of HBM per device.

v0:
```python
import jax
import jax.numpy as jnp
from jax import lax
from jax.sharding import PartitionSpec as P


def partner(block, axis, distance):
    count = lax.axis_size(axis)
    route = []
    for low in range(count):
        high = low | 1 << distance
        if high != low and high < count:
            route += [(low, high), (high, low)]
    return lax.ppermute(block, axis, route)


def coefficients(
    image_rows, valid_rows, row_ids, texts, weight_text, text_ids, factor, logit_scale, logit_bias
):
    logits = lax.dot_general(
        image_rows, texts, (((1,), (1,)), ((), ())), preferred_element_type=jnp.float32
    )
    logits = logits * logit_scale[0] + logit_bias[0]
    label_sign = jnp.where(row_ids[:, None] == text_ids[None, :], 1.0, -1.0).astype(jnp.float32)
    weights = valid_rows.astype(jnp.float32)[:, None] * weight_text[None, :]
    return (-factor * label_sign * jax.nn.sigmoid(-label_sign * logits) * weights).astype(
        jnp.bfloat16
    )


def text_part(coefficient, image_rows):
    return lax.dot_general(
        coefficient, image_rows, (((0,), (0,)), ((), ())), preferred_element_type=jnp.float32
    )


def body(
    image_emb, text_emb, image_valid, text_valid, sample_count, logit_scale, logit_bias, loss_grad
):
    text_block = lax.all_gather(text_emb, "row", axis=1, tiled=True)
    per_device = image_emb.shape[0]
    col_count = lax.axis_size("col")
    col_index = lax.axis_index("col")
    row_index = lax.axis_index("row")
    text_count = text_block.shape[0]
    factor = loss_grad[0] * logit_scale[0] / sample_count[0].astype(jnp.float32)
    valid_wire = image_valid.astype(jnp.bfloat16)
    parity = col_index % 2
    bit_count = col_count.bit_length() - 1
    text_wire = text_valid.astype(jnp.bfloat16)
    other_texts, other_valid = partner((text_block, text_wire), "col", 0)
    own_first = parity == 0
    texts = jnp.where(
        own_first,
        jnp.concatenate([text_block, other_texts], 0),
        jnp.concatenate([other_texts, text_block], 0),
    )
    text_weights = jnp.where(
        own_first,
        jnp.concatenate([text_wire, other_valid], 0),
        jnp.concatenate([other_valid, text_wire], 0),
    ).astype(jnp.float32)
    text_ids = (col_index - parity) * text_count + jnp.arange(2 * text_count, dtype=jnp.int32)
    image_rows, valid_rows = (image_emb, valid_wire)
    for bit in range(1, bit_count):
        other_rows, other_counts = partner((image_rows, valid_rows), "col", bit)
        lower = col_index >> bit & 1 == 0
        image_rows = jnp.where(
            lower,
            jnp.concatenate([image_rows, other_rows], 0),
            jnp.concatenate([other_rows, image_rows], 0),
        )
        valid_rows = jnp.where(
            lower,
            jnp.concatenate([valid_rows, other_counts], 0),
            jnp.concatenate([other_counts, valid_rows], 0),
        )
    positions = jnp.arange(image_rows.shape[0], dtype=jnp.int32)
    row_ids = (
        row_index * col_count + 2 * (positions // per_device) + parity
    ) * per_device + positions % per_device
    coefficient = coefficients(
        image_rows,
        valid_rows,
        row_ids,
        texts,
        text_weights,
        text_ids,
        factor,
        logit_scale,
        logit_bias,
    )
    partial_image = jnp.dot(coefficient, texts, preferred_element_type=jnp.float32)
    for bit in range(bit_count - 1, 0, -1):
        half = partial_image.shape[0] // 2
        upper = col_index >> bit & 1 == 1
        send = jnp.where(upper, partial_image[:half], partial_image[half:])
        keep = jnp.where(upper, partial_image[half:], partial_image[:half])
        partial_image = keep + partner(send, "col", bit)
    partial_text = text_part(coefficient, image_rows)
    odd = parity == 1
    send_text = jnp.where(odd, partial_text[:text_count], partial_text[text_count:])
    keep_text = jnp.where(odd, partial_text[text_count:], partial_text[:text_count])
    text_partial = keep_text + partner(send_text, "col", 0)
    text_grad = lax.psum_scatter(text_partial, "row", scatter_dimension=1, tiled=True)
    return (partial_image.astype(jnp.bfloat16), text_grad.astype(jnp.bfloat16))


def solution(mesh):
    in_specs = (
        P(("row", "col"), None),
        P("col", "row"),
        P(("row", "col")),
        P("col"),
        P(),
        P(),
        P(),
        P(),
    )
    out_specs = (P(("row", "col"), None), P("col", "row"))
    return jax.shard_map(body, mesh=mesh, in_specs=in_specs, out_specs=out_specs, check_vma=False)
```

profile of v0, /device:TPU:0, one launch (start us, length us, event | category | flops | bytes accessed | tf_op | source)
XLA Modules:
  0.0 164.8 jit_solution(11183775856939679000)
XLA Ops:
  7.2 0.0 reduce-scatter.4.cloned.1.call-start
  7.2 3.0 %collective-permute-start = (bf16[80,1152]{1,0:T(8,128)(2,1)}, bf16[80,1152]{1,0:T(8,128)(2,1)S(1)}, u32[]{:S(2)}, u32[]{:S(2)}) collective-permute-start(bf16[80,1152]{1,0:T(8,128)(2,1)} %param.8), channel_id=1, source_target_pairs={{0,2},{2,0},{1,3},{3,1},{4,6},{6,4},{5,7},{7,5},{8,10},{10,8},{9,1... | collective-permute-start | bytes 552968 | tf_op jit(solution)/shard_map/ppermute | solution.py:14
  10.3 4.8 %collective-permute-done = bf16[80,1152]{1,0:T(8,128)(2,1)S(1)} collective-permute-done((bf16[80,1152]{1,0:T(8,128)(2,1)}, bf16[80,1152]{1,0:T(8,128)(2,1)S(1)}, u32[]{:S(2)}, u32[]{:S(2)}) %collective-permute-start) | collective-permute-done | bytes 184352 | tf_op jit(solution)/shard_map/ppermute | solution.py:14
  15.1 1.1 maximum_select_fusion.3
  16.2 1.9 %collective-permute-start.1 = (bf16[160,1152]{1,0:T(8,128)(2,1)S(1)}, bf16[160,1152]{1,0:T(8,128)(2,1)S(1)}, u32[]{:S(2)}, u32[]{:S(2)}) collective-permute-start(bf16[160,1152]{1,0:T(8,128)(2,1)S(1)} %maximum_select_fusion.3), channel_id=1, source_target_pairs={{0,4},{4,0},{1,5},{5,1},{2,6},{6,2},{3,7},{7,3},{8,12},{12,8},{9,1... | collective-permute-start | bytes 1105928 | tf_op jit(solution)/shard_map/ppermute | solution.py:14
  18.1 0.7 convert_element_type.39
  18.7 1.5 collective-permute-start.7
  20.2 0.7 convert_element_type.37
  20.9 1.5 collective-permute-start.4
  22.4 3.6 %collective-permute-done.1 = bf16[160,1152]{1,0:T(8,128)(2,1)S(1)} collective-permute-done((bf16[160,1152]{1,0:T(8,128)(2,1)S(1)}, bf16[160,1152]{1,0:T(8,128)(2,1)S(1)}, u32[]{:S(2)}, u32[]{:S(2)}) %collective-permute-start.1) | collective-permute-done | bytes 368672 | tf_op jit(solution)/shard_map/ppermute | solution.py:14
  26.0 0.2 maximum_select_fusion.1
  26.2 2.6 %collective-permute-start.2 = (bf16[320,1152]{1,0:T(8,128)(2,1)S(1)}, bf16[320,1152]{1,0:T(8,128)(2,1)S(1)}, u32[]{:S(2)}, u32[]{:S(2)}) collective-permute-start(bf16[320,1152]{1,0:T(8,128)(2,1)S(1)} %maximum_select_fusion.1), channel_id=1, source_target_pairs={{0,8},{8,0},{1,9},{9,1},{2,10},{10,2},{3,11},{11,3},{4,12},{12,4},... | collective-permute-start | bytes 2211848 | tf_op jit(solution)/shard_map/ppermute | solution.py:14
  28.8 2.1 %all-gather = bf16[2,576,160]{1,2,0:T(8,128)(2,1)S(1)} all-gather(bf16[1,576,160]{1,2,0:T(8,128)(2,1)S(1)} %bitcast.23), channel_id=1, replica_groups=mesh['row'=2,'col'=16] {'row'}, dimensions={0}, use_global_device_ids=true | all-gather | bytes 552960 | tf_op jit(solution)/shard_map/all_gather | solution.py:40
  30.9 0.3 copy.11
  31.2 0.3 reshape.108
  31.5 1.6 collective-permute-start.3
  35.7 0.0 collective-permute-done.4
  35.7 0.1 broadcast_select_fusion
  35.8 1.6 collective-permute-start.5
  37.4 5.4 %collective-permute-done.5 = bf16[160]{0:T(256)(128)(2,1)S(1)} collective-permute-done((bf16[160]{0:T(256)(128)(2,1)S(1)}, bf16[160]{0:T(256)(128)(2,1)S(1)}, u32[]{:S(2)}, u32[]{:S(2)}) %collective-permute-start.5) | collective-permute-done | bytes 352 | tf_op jit(solution)/shard_map/ppermute | solution.py:14
  42.9 0.1 maximum_select_fusion.9
  42.9 2.3 %collective-permute-start.6 = (bf16[320]{0:T(512)(128)(2,1)S(1)}, bf16[320]{0:T(512)(128)(2,1)S(1)}, u32[]{:S(2)}, u32[]{:S(2)}) collective-permute-start(bf16[320]{0:T(512)(128)(2,1)S(1)} %maximum_select_fusion.9), channel_id=1, source_target_pairs={{0,8},{8,0},{1,9},{9,1},{2,10},{10,2},{3,11},{11,3},{4,12},{12,4},... | collective-permute-start | bytes 1928 | tf_op jit(solution)/shard_map/ppermute | solution.py:14
  45.2 0.0 collective-permute-done.7
  45.2 0.1 fusion.24
  45.3 14.5 %collective-permute-done.6 = bf16[320]{0:T(512)(128)(2,1)S(1)} collective-permute-done((bf16[320]{0:T(512)(128)(2,1)S(1)}, bf16[320]{0:T(512)(128)(2,1)S(1)}, u32[]{:S(2)}, u32[]{:S(2)}) %collective-permute-start.6) | collective-permute-done | bytes 672 | tf_op jit(solution)/shard_map/ppermute | solution.py:14
  59.8 0.1 fusion.23
  59.9 0.0 collective-permute-done.3
  59.9 1.1 fusion.8
  61.0 1.0 fusion.10
  62.1 0.2 slice_select_fusion
  62.2 1.4 copy-done
  63.7 2.8 %fusion.9 = f32[320,1152]{1,0:T(8,128)S(1)} fusion(bf16[640,320]{0,1:T(8,128)(2,1)S(1)} %fusion.8, bf16[320,1152]{1,0:T(8,128)(2,1)} %copy-done.4, bf16[320,1152]{1,0:T(8,128)(2,1)} %copy-done.2, pred[]{:T(512)S(6)} %eq.47), kind=kOutput, calls=%fused_computation.24 | convolution fusion | flops 478494720 | bytes 3358721 | tf_op jit(solution)/shard_map/dot_general | solution.py:32
  66.4 0.1 slice_select_fusion.1
  66.5 1.1 collective-permute-start.11
  67.7 62.0 %collective-permute-done.8 = f32[320,1152]{1,0:T(8,128)S(1)} collective-permute-done((f32[320,1152]{1,0:T(8,128)S(1)}, f32[320,1152]{1,0:T(8,128)S(1)}, u32[]{:S(2)}, u32[]{:S(2)}) %collective-permute-start.8) | collective-permute-done | bytes 1474592 | tf_op jit(solution)/shard_map/ppermute | solution.py:14
  129.7 0.2 select_add_fusion
  129.9 0.1 slice_select_fusion.2
  130.0 0.1 collective-permute-start.9
  130.1 0.1 select_add_fusion.1
  130.2 1.4 copy.12
  131.6 0.0 reduce-scatter.4.cloned.1.call-update
  131.7 15.8 %collective-permute-done.9 = f32[160,1152]{1,0:T(8,128)} collective-permute-done((f32[160,1152]{1,0:T(8,128)S(1)}, f32[160,1152]{1,0:T(8,128)}, u32[]{:S(2)}, u32[]{:S(2)}) %collective-permute-start.9) | collective-permute-done | bytes 737312 | tf_op jit(solution)/shard_map/ppermute | solution.py:14
  147.4 1.2 select_add_fusion.2
  148.7 0.1 collective-permute-start.10
  148.8 0.0 reduce-scatter.4.cloned.1.call-done
  148.8 1.9 %copy.13 = bf16[160,576]{1,0:T(8,128)(2,1)} copy(f32[160,576]{0,1:T(8,128)} %bitcast.19) | data formatting | bytes 552960
  150.7 6.5 %collective-permute-done.10 = f32[80,1152]{1,0:T(8,128)S(1)} collective-permute-done((f32[80,1152]{1,0:T(8,128)S(1)}, f32[80,1152]{1,0:T(8,128)S(1)}, u32[]{:S(2)}, u32[]{:S(2)}) %collective-permute-start.10) | collective-permute-done | bytes 368672 | tf_op jit(solution)/shard_map/ppermute | solution.py:14
  157.2 0.7 add_convert_fusion
  (15 shorter events, 0.1 us)
Async XLA Ops:
  7.2 21.6 %copy-start.3 = (bf16[160,576]{1,0:T(8,128)(2,1)S(1)}, bf16[160,576]{1,0:T(8,128)(2,1)}, u32[]{:S(2)}) copy-start(bf16[160,576]{1,0:T(8,128)(2,1)} %param.9) | copy-start | bytes 552964
  7.2 141.6 %reduce-scatter.4.cloned.1.call-start = ((), (), s32[]{:S(2)}) async-start(), calls=%async_computation.1 | async-start | bytes 1769472
  7.2 7.9 %collective-permute-start = (bf16[80,1152]{1,0:T(8,128)(2,1)}, bf16[80,1152]{1,0:T(8,128)(2,1)S(1)}, u32[]{:S(2)}, u32[]{:S(2)}) collective-permute-start(bf16[80,1152]{1,0:T(8,128)(2,1)} %param.8), channel_id=1, source_target_pairs={{0,2},{2,0},{1,3},{3,1},{4,6},{6,4},{5,7},{7,5},{8,10},{10,8},{9,1... | collective-permute-start | bytes 552968 | tf_op jit(solution)/shard_map/ppermute | solution.py:14
  16.2 9.8 %collective-permute-start.1 = (bf16[160,1152]{1,0:T(8,128)(2,1)S(1)}, bf16[160,1152]{1,0:T(8,128)(2,1)S(1)}, u32[]{:S(2)}, u32[]{:S(2)}) collective-permute-start(bf16[160,1152]{1,0:T(8,128)(2,1)S(1)} %maximum_select_fusion.3), channel_id=1, source_target_pairs={{0,4},{4,0},{1,5},{5,1},{2,6},{6,2},{3,7},{7,3},{8,12},{12,8},{9,1... | collective-permute-start | bytes 1105928 | tf_op jit(solution)/shard_map/ppermute | solution.py:14
  18.7 26.5 %collective-permute-start.7 = (bf16[160]{0:T(256)(128)(2,1)S(1)}, bf16[160]{0:T(256)(128)(2,1)S(1)}, u32[]{:S(2)}, u32[]{:S(2)}) collective-permute-start(bf16[160]{0:T(256)(128)(2,1)S(1)} %convert_element_type.39), channel_id=1, source_target_pairs={{0,1},{1,0},{2,3},{3,2},{4,5},{5,4},{6,7},{7,6},{8,9},{9,8},{10,11... | collective-permute-start | bytes 968 | tf_op jit(solution)/shard_map/ppermute | solution.py:14
  20.9 14.8 %collective-permute-start.4 = (bf16[80]{0:T(256)(128)(2,1)S(1)}, bf16[80]{0:T(256)(128)(2,1)S(1)}, u32[]{:S(2)}, u32[]{:S(2)}) collective-permute-start(bf16[80]{0:T(256)(128)(2,1)S(1)} %convert_element_type.37), channel_id=1, source_target_pairs={{0,2},{2,0},{1,3},{3,1},{4,6},{6,4},{5,7},{7,5},{8,10},{10,8},{9,1... | collective-permute-start | bytes 488 | tf_op jit(solution)/shard_map/ppermute | solution.py:14
  26.2 34.8 %copy-start.2 = (bf16[320,1152]{1,0:T(8,128)(2,1)}, bf16[320,1152]{1,0:T(8,128)(2,1)S(1)}, u32[]{:S(2)}) copy-start(bf16[320,1152]{1,0:T(8,128)(2,1)S(1)} %maximum_select_fusion.1) | copy-start | bytes 2211844
  26.2 33.7 %collective-permute-start.2 = (bf16[320,1152]{1,0:T(8,128)(2,1)S(1)}, bf16[320,1152]{1,0:T(8,128)(2,1)S(1)}, u32[]{:S(2)}, u32[]{:S(2)}) collective-permute-start(bf16[320,1152]{1,0:T(8,128)(2,1)S(1)} %maximum_select_fusion.1), channel_id=1, source_target_pairs={{0,8},{8,0},{1,9},{9,1},{2,10},{10,2},{3,11},{11,3},{4,12},{12,4},... | collective-permute-start | bytes 2211848 | tf_op jit(solution)/shard_map/ppermute | solution.py:14
  31.5 28.4 %collective-permute-start.3 = (bf16[160,1152]{1,0:T(8,128)(2,1)S(1)}, bf16[160,1152]{1,0:T(8,128)(2,1)S(1)}, u32[]{:S(2)}, u32[]{:S(2)}) collective-permute-start(bf16[160,1152]{1,0:T(8,128)(2,1)S(1)} %bitcast.20), channel_id=1, source_target_pairs={{0,1},{1,0},{2,3},{3,2},{4,5},{5,4},{6,7},{7,6},{8,9},{9,8},{10,11... | collective-permute-start | bytes 1105928 | tf_op jit(solution)/shard_map/ppermute | solution.py:14
  35.8 7.1 %collective-permute-start.5 = (bf16[160]{0:T(256)(128)(2,1)S(1)}, bf16[160]{0:T(256)(128)(2,1)S(1)}, u32[]{:S(2)}, u32[]{:S(2)}) collective-permute-start(bf16[160]{0:T(256)(128)(2,1)S(1)} %broadcast_select_fusion), channel_id=1, source_target_pairs={{0,4},{4,0},{1,5},{5,1},{2,6},{6,2},{3,7},{7,3},{8,12},{12,8},{9,1... | collective-permute-start | bytes 968 | tf_op jit(solution)/shard_map/ppermute | solution.py:14
  42.9 16.9 %collective-permute-start.6 = (bf16[320]{0:T(512)(128)(2,1)S(1)}, bf16[320]{0:T(512)(128)(2,1)S(1)}, u32[]{:S(2)}, u32[]{:S(2)}) collective-permute-start(bf16[320]{0:T(512)(128)(2,1)S(1)} %maximum_select_fusion.9), channel_id=1, source_target_pairs={{0,8},{8,0},{1,9},{9,1},{2,10},{10,2},{3,11},{11,3},{4,12},{12,4},... | collective-permute-start | bytes 1928 | tf_op jit(solution)/shard_map/ppermute | solution.py:14
  59.9 1.1 copy-start.4
  62.1 1.6 copy-start
  63.7 66.0 %collective-permute-start.8 = (f32[320,1152]{1,0:T(8,128)S(1)}, f32[320,1152]{1,0:T(8,128)S(1)}, u32[]{:S(2)}, u32[]{:S(2)}) collective-permute-start(f32[320,1152]{1,0:T(8,128)S(1)} %slice_select_fusion), channel_id=1, source_target_pairs={{0,8},{8,0},{1,9},{9,1},{2,10},{10,2},{3,11},{11,3},{4,12},{12,4},... | collective-permute-start | bytes 4423688 | tf_op jit(solution)/shard_map/ppermute | solution.py:14
  63.7 66.0 %copy-start.1 = (f32[640,1152]{1,0:T(8,128)S(1)}, f32[640,1152]{1,0:T(8,128)}, u32[]{:S(2)}) copy-start(f32[640,1152]{1,0:T(8,128)} %copy-done) | copy-start | bytes 8847364
  66.5 63.6 %collective-permute-start.11 = (f32[160,1152]{1,0:T(8,128)S(1)}, f32[160,1152]{1,0:T(8,128)S(1)}, u32[]{:S(2)}, u32[]{:S(2)}) collective-permute-start(f32[160,1152]{1,0:T(8,128)S(1)} %slice_select_fusion.1), channel_id=1, source_target_pairs={{0,1},{1,0},{2,3},{3,2},{4,5},{5,4},{6,7},{7,6},{8,9},{9,8},{10,11... | collective-permute-start | bytes 2211848 | tf_op jit(solution)/shard_map/ppermute | solution.py:14
  130.0 17.4 %collective-permute-start.9 = (f32[160,1152]{1,0:T(8,128)S(1)}, f32[160,1152]{1,0:T(8,128)}, u32[]{:S(2)}, u32[]{:S(2)}) collective-permute-start(f32[160,1152]{1,0:T(8,128)S(1)} %slice_select_fusion.2), channel_id=1, source_target_pairs={{0,4},{4,0},{1,5},{5,1},{2,6},{6,2},{3,7},{7,3},{8,12},{12,8},{9,1... | collective-permute-start | bytes 2211848 | tf_op jit(solution)/shard_map/ppermute | solution.py:14
  148.7 8.5 %collective-permute-start.10 = (f32[80,1152]{1,0:T(8,128)S(1)}, f32[80,1152]{1,0:T(8,128)S(1)}, u32[]{:S(2)}, u32[]{:S(2)}) collective-permute-start(f32[80,1152]{1,0:T(8,128)S(1)} %slice_select_fusion.3), channel_id=1, source_target_pairs={{0,2},{2,0},{1,3},{3,1},{4,6},{6,4},{5,7},{7,5},{8,10},{10,8},{9,1... | collective-permute-start | bytes 1105928 | tf_op jit(solution)/shard_map/ppermute | solution.py:14
Sparse Core Ops, SparseCore 0:
  131.8 7.4 reduce-scatter.3
where the time goes:
time: 165 us
  waiting for transfers between devices  113 us (68%)
  starting transfers between devices  17.2 us (10%)
  between operations  16.9 us (10%)
  other arithmetic  5.61 us (3%)
  local copies, waits for them, and re-layouts  5.35 us (3%)
  matrix products  4.87 us (3%)
  blocking collectives  2.09 us (1%)
    ppermute x12, waiting for transfers between devices, partner(): return lax.ppermute(block, axis, route)  113 us
    ppermute x12, starting transfers between devices, partner(): return lax.ppermute(block, axis, route)  17.2 us
    unnamed x13, local copies, waits for them, and re-layouts  5.03 us
  transfers between devices with their start and end apart: 13, of which 7 were waited for; matrix products, arithmetic and copies ran while one was open for 6% of the time, Pallas kernels for 0%

commit v1 on v0

--- a/solution.py
+++ b/solution.py
@@ -1,7 +1,148 @@
+import functools
+
 import jax
 import jax.numpy as jnp
 from jax import lax
+from jax.experimental import pallas as pl
+from jax.experimental.pallas import tpu as pltpu
 from jax.sharding import PartitionSpec as P
+
+SPARE = 8
+
+
+def hop(block, image_bit, text_bit):
+    count = lax.axis_size("col")
+    route = [(c, c ^ image_bit) for c in range(count)]
+    route += [(count + c, count + (c ^ text_bit)) for c in range(count)]
+    return lax.ppermute(block, ("row", "col"), route)
+
+
+def swap(block):
+    return lax.ppermute(block, "row", [(0, 1), (1, 0)])
+
+
+def pack_kernel(row_ref, image_ref, text_ref, other_image_ref, other_text_ref, image_valid_ref,
+                other_valid_ref, text_valid_ref, out_ref):
+    half, width = image_ref.shape
+    count, part = text_ref.shape
+    lanes = 256 if count <= 256 else width
+
+    def put_valid(pieces):
+        used = sum(piece.shape[1] for piece in pieces)
+        pieces = pieces + [jnp.zeros((1, lanes - used), jnp.float32)]
+        line = jnp.concatenate(pieces, axis=1)
+        out_ref[count:, :lanes] = jnp.broadcast_to(line, (SPARE, lanes)).astype(out_ref.dtype)
+
+    @pl.when(row_ref[0] == 0)
+    def _():
+        out_ref[:half] = image_ref[...]
+        out_ref[half:count] = other_image_ref[...]
+        put_valid([image_valid_ref[...].astype(jnp.float32), other_valid_ref[...].astype(jnp.float32)])
+
+    @pl.when(row_ref[0] != 0)
+    def _():
+        out_ref[:count, :part] = other_text_ref[...]
+        out_ref[:count, part:] = text_ref[...]
+        put_valid([text_valid_ref[...].astype(jnp.float32)])
+
+
+def partial_kernel(kinds, place_ref, scalar_ref, sample_ref, mine_ref, *refs):
+    others, out_ref = refs[:-1], refs[-1]
+    count = others[0].shape[0] - SPARE
+    scale, bias = scalar_ref[0], scalar_ref[1]
+    factor = scalar_ref[2] * scale / sample_ref[0].astype(jnp.float32)
+    mine = mine_ref[...]
+    line = mine[count:, :256].astype(jnp.float32)[:1, :count]
+    at = lax.broadcasted_iota(jnp.int32, (count, count), 0)
+    to = lax.broadcasted_iota(jnp.int32, (count, count), 1)
+    weight = jnp.sum(jnp.where(at == to, line, 0.0), axis=1, keepdims=True)
+    my_id = lax.broadcasted_iota(jnp.int32, (count, 1), 0)
+    my_id = my_id + place_ref[0] + jnp.where(my_id >= count // 2, place_ref[1], 0)
+    parts = []
+    for n, ref in enumerate(others):
+        other = ref[...]
+        logits = lax.dot_general(mine[:count], other[:count], (((1,), (1,)), ((), ())),
+                                 preferred_element_type=jnp.float32)
+        logits = logits * scale + bias
+        other_id = lax.broadcasted_iota(jnp.int32, (1, count), 1)
+        other_id = other_id + place_ref[3 + n] + jnp.where(other_id >= count // 2, place_ref[2], 0)
+        match = my_id == other_id
+        rate = 1.0 / (1.0 + jnp.exp(jnp.where(match, logits, -logits)))
+        signed = jnp.where(match, -factor, factor) * rate
+        other_weight = other[count:, :256].astype(jnp.float32)[:1, :count]
+        parts.append((signed * weight * other_weight).astype(jnp.bfloat16))
+    coefficient = jnp.concatenate(parts, axis=1)
+    block = jnp.concatenate([ref[:count] for ref in others], axis=0)
+    total = jnp.dot(coefficient, block, preferred_element_type=jnp.float32)
+    out_ref[...] = total.astype(out_ref.dtype)
+
+
+def call(kernel, out_shape, smem, *arrays):
+    return pl.pallas_call(
+        kernel,
+        out_shape=out_shape,
+        in_specs=[pl.BlockSpec(memory_space=pltpu.SMEM)] * smem
+        + [pl.BlockSpec(memory_space=pltpu.VMEM)] * (len(arrays) - smem),
+        out_specs=pl.BlockSpec(memory_space=pltpu.VMEM),
+        compiler_params=pltpu.CompilerParams(vmem_limit_bytes=24 * 1024 * 1024),
+    )(*arrays)
+
+
+def pair_body(
+    image_emb, text_emb, image_valid, text_valid, sample_count, logit_scale, logit_bias, loss_grad
+):
+    half, width = image_emb.shape
+    count, part = text_emb.shape
+    col_count = lax.axis_size("col")
+    col = lax.axis_index("col")
+    row = lax.axis_index("row")
+    top = col_count // 2
+    near = (1, 2)
+    far = (top, top // 2)
+    near_mask = jnp.where(row == 0, *near)
+    far_mask = jnp.where(row == 0, *far)
+    near_other = jnp.where(row == 0, *near[::-1])
+    far_other = jnp.where(row == 0, *far[::-1])
+
+    other_image = lax.ppermute(image_emb, "row", [(1, 0)])
+    other_text = lax.ppermute(text_emb, "row", [(0, 1)])
+    other_valid = lax.ppermute(image_valid, "row", [(1, 0)])
+    block_shape = jax.ShapeDtypeStruct((count + SPARE, width), jnp.bfloat16)
+    own = call(pack_kernel, block_shape, 1, row[None], image_emb, text_emb, other_image, other_text,
+               image_valid[None], other_valid[None], text_valid[None])
+    far_block = hop(own, *far)
+    near_block = hop(own, *near)
+    both_block = hop(far_block, *near)
+    own_b, near_b, far_b, both_b = swap(own), swap(near_block), swap(far_block), swap(both_block)
+    others = (own_b, near_b, far_b, both_b)
+
+    other_cols = jnp.stack([col, col ^ near_other, col ^ far_other, col ^ near_other ^ far_other])
+    other_first = other_cols * jnp.where(row == 0, count, half)
+    jump = (col_count - 1) * half
+    my_jump, other_jump = jnp.where(row == 0, jump, 0), jnp.where(row == 0, 0, jump)
+    scalars = jnp.concatenate([logit_scale, logit_bias, loss_grad])
+
+    def partial(mine, mask, dtype):
+        first = (col ^ mask) * jnp.where(row == 0, half, count)
+        place = jnp.concatenate([jnp.stack([first, my_jump, other_jump]), other_first])
+        return call(functools.partial(partial_kernel, None), jax.ShapeDtypeStruct((count, width), dtype), 3,
+                    place, scalars, sample_count, mine, *others)
+
+    both_sum = partial(both_block, near_mask ^ far_mask, jnp.bfloat16)
+    both_in = hop(both_sum, *near)
+    near_sum = partial(near_block, near_mask, jnp.bfloat16)
+    far_sum = partial(far_block, far_mask, jnp.float32)
+    far_out = (far_sum + both_in.astype(jnp.float32)).astype(jnp.bfloat16)
+    far_in = hop(far_out, *far)
+    near_in = hop(near_sum, *near)
+    own_sum = partial(own, 0, jnp.float32)
+    total = own_sum + near_in.astype(jnp.float32) + far_in.astype(jnp.float32)
+    total = total.astype(jnp.bfloat16)
+    image_back = lax.ppermute(total[half:], "row", [(0, 1)])
+    text_back = lax.ppermute(total[:, :part], "row", [(1, 0)])
+    image_grad = jnp.where(row == 0, total[:half], image_back)
+    text_grad = jnp.where(row == 0, text_back, total[:, part:])
+    return image_grad, text_grad
 
 
 def partner(block, axis, distance):
@@ -118,4 +259,6 @@
         P(),
     )
     out_specs = (P(("row", "col"), None), P("col", "row"))
-    return jax.shard_map(body, mesh=mesh, in_specs=in_specs, out_specs=out_specs, check_vma=False)
+    paired = mesh.shape["row"] == 2 and mesh.shape["col"] == 16
+    run = pair_body if paired else body
+    return jax.shard_map(run, mesh=mesh, in_specs=in_specs, out_specs=out_specs, check_vma=False)

time: 165 us -> 61.4 us (0.37)
  waiting for transfers between devices: 113 us -> 23.6 us
  between operations: 16.9 us -> 3.39 us
  Pallas kernels: 0 us -> 7.03 us
  matrix products: 4.87 us -> 0 us
  starting transfers between devices: 17.2 us -> 21.9 us
  other arithmetic: 5.61 us -> 2.02 us
  local copies, waits for them, and re-layouts: 5.35 us -> 2.56 us
  blocking collectives: 2.09 us -> 0 us
    ppermute x12 -> x15, waiting for transfers between devices: 113 us -> 23.6 us  [the longest x6 20.4 us: hop(): return lax.ppermute(block, ('row', 'col'), route)]
    pallas_call x0 -> x5, Pallas kernels: none -> 7.03 us  [call(): pl.pallas_call(kernel, out_shape=out_shape, in_specs=[pl.BlockSpec(memory...]
    dot_general x3 -> x0, matrix products: 4.87 us -> none  [the longest x1 2.76 us: text_part(): lax.dot_general(coefficient, image_rows, (((0,), (0,)), ((), ())), prefer...]
    ppermute x12 -> x15, starting transfers between devices: 17.2 us -> 21.9 us  [the longest x6 12.3 us: hop(): return lax.ppermute(block, ('row', 'col'), route)]
    unnamed x13 -> x8, local copies, waits for them, and re-layouts: 5.03 us -> 2.52 us
    all_gather x1 -> x0, blocking collectives: 2.09 us -> none  [body(): text_block = lax.all_gather(text_emb, 'row', axis=1, tiled=True)]
    convert_element_type x5 -> x2, other arithmetic: 2.22 us -> 0.21 us  [the longest x1 0.15 us: pair_body(): total = total.astype(jnp.bfloat16)]
  transfers between devices with their start and end apart: 13 -> 15, of which waited for: 7 -> 6; matrix products, arithmetic and copies ran while one was open for 6% -> 2% of each run, Pallas kernels for 0% -> 9%
where the time goes in v1:
time: 61.4 us; the launch traced here: 60.5 us
  waiting for transfers between devices  23.6 us (38%)
  starting transfers between devices  21.9 us (36%)
  Pallas kernels  7.03 us (11%)
  between operations  3.39 us (6%)
  local copies, waits for them, and re-layouts  2.56 us (4%)
  other arithmetic  2.02 us (3%)
    ppermute x6, waiting for transfers between devices, hop(): return lax.ppermute(block, ('row', 'col'), route)  20.4 us
    ppermute x6, starting transfers between devices, hop(): return lax.ppermute(block, ('row', 'col'), route)  12.3 us
    pallas_call x5, Pallas kernels, call(): pl.pallas_call(kernel, out_shape=out_shape, in_specs=[pl.BlockSpec(memory...  7.03 us
    ppermute x1, starting transfers between devices, pair_body(): other_text = lax.ppermute(text_emb, 'row', [(0, 1)])  3.05 us
    unnamed x8, local copies, waits for them, and re-layouts  2.52 us
    ppermute x1, starting transfers between devices, pair_body(): image_back = lax.ppermute(total[half:], 'row', [(0, 1)])  2.17 us
    ppermute x1, waiting for transfers between devices, pair_body(): other_valid = lax.ppermute(image_valid, 'row', [(1, 0)])  1.84 us
    ppermute x1, waiting for transfers between devices, pair_body(): text_back = lax.ppermute(total[:, :part], 'row', [(1, 0)])  1.34 us
  transfers between devices with their start and end apart: 15, of which 6 were waited for; matrix products, arithmetic and copies ran while one was open for 2% of the time, Pallas kernels for 9%

profile of v1, /device:TPU:0, one launch (start us, length us, event | category | flops | bytes accessed | tf_op | source)
XLA Modules:
  0.0 60.5 jit_solution(4544710335374101508)
XLA Ops:
  0.6 1.3 %collective-permute-start = (bf16[80,1152]{1,0:T(8,128)(2,1)}, bf16[80,1152]{1,0:T(8,128)(2,1)S(1)}, u32[]{:S(2)}, u32[]{:S(2)}) collective-permute-start(bf16[80,1152]{1,0:T(8,128)(2,1)} %image_ref.1), channel_id=1, source_target_pairs={{16,0},{17,1},{18,2},{19,3},{20,4},{21,5},{22,6},{23,7},{24,8},{25... | collective-permute-start | bytes 552968 | tf_op jit(solution)/shard_map/ppermute | solution.py:107
  1.9 3.0 %collective-permute-start.1 = (bf16[160,576]{1,0:T(8,128)(2,1)}, bf16[160,576]{1,0:T(8,128)(2,1)S(1)}, u32[]{:S(2)}, u32[]{:S(2)}) collective-permute-start(bf16[160,576]{1,0:T(8,128)(2,1)} %text_ref.1), channel_id=1, source_target_pairs={{0,16},{1,17},{2,18},{3,19},{4,20},{5,21},{6,22},{7,23},{8,24},{9,... | collective-permute-start | bytes 552968 | tf_op jit(solution)/shard_map/ppermute | solution.py:108
  5.0 1.3 %collective-permute-start.2 = (s32[80]{0:T(128)}, s32[80]{0:T(128)S(1)}, u32[]{:S(2)}, u32[]{:S(2)}) collective-permute-start(s32[80]{0:T(128)} %param.10), channel_id=1, source_target_pairs={{16,0},{17,1},{18,2},{19,3},{20,4},{21,5},{22,6},{23,7},{24,8},{25... | collective-permute-start | bytes 968 | tf_op jit(solution)/shard_map/ppermute | solution.py:109
  6.3 1.8 %collective-permute-done.2 = s32[80]{0:T(128)S(1)} collective-permute-done((s32[80]{0:T(128)}, s32[80]{0:T(128)S(1)}, u32[]{:S(2)}, u32[]{:S(2)}) %collective-permute-start.2) | collective-permute-done | bytes 352 | tf_op jit(solution)/shard_map/ppermute | solution.py:109
  8.1 0.0 collective-permute-done.other_image_ref
  8.1 0.0 collective-permute-done.1.other_text_ref
  8.1 0.0 copy-start.3
  8.2 0.7 %copy-done.2 = s32[160]{0:T(256)S(1)} copy-done((s32[160]{0:T(256)S(1)}, s32[160]{0:T(256)}, u32[]{:S(2)}) %copy-start.2) | copy-done | bytes 664
  8.8 0.0 copy-done.3
  8.8 0.9 %copy-done = bf16[160,576]{1,0:T(8,128)(2,1)S(1)} copy-done((bf16[160,576]{1,0:T(8,128)(2,1)S(1)}, bf16[160,576]{1,0:T(8,128)(2,1)}, u32[]{:S(2)}) %copy-start) | copy-done | bytes 184344
  9.8 0.9 %copy-done.1 = bf16[80,1152]{1,0:T(8,128)(2,1)S(1)} copy-done((bf16[80,1152]{1,0:T(8,128)(2,1)S(1)}, bf16[80,1152]{1,0:T(8,128)(2,1)}, u32[]{:S(2)}) %copy-start.1) | copy-done | bytes 184344
  10.7 0.1 shard_map.95.mine_ref
  10.8 4.0 %collective-permute-start.6 = (bf16[168,1152]{1,0:T(8,128)(2,1)S(1)}, bf16[168,1152]{1,0:T(8,128)(2,1)S(1)}, u32[]{:S(2)}, u32[]{:S(2)}) collective-permute-start(bf16[168,1152]{1,0:T(8,128)(2,1)S(1)} %shard_map.95.mine_ref), channel_id=1, source_target_pairs={{0,8},{1,9},{2,10},{3,11},{4,12},{5,13},{6,14},{7,15},{8,0},{9,1},... | collective-permute-start | bytes 1161224 | tf_op jit(solution)/shard_map/ppermute | solution.py:17
  14.8 1.5 %collective-permute-start.4 = (bf16[168,1152]{1,0:T(8,128)(2,1)S(1)}, bf16[168,1152]{1,0:T(8,128)(2,1)S(1)}, u32[]{:S(2)}, u32[]{:S(2)}) collective-permute-start(bf16[168,1152]{1,0:T(8,128)(2,1)S(1)} %shard_map.95.mine_ref), channel_id=1, source_target_pairs={{0,1},{1,0},{2,3},{3,2},{4,5},{5,4},{6,7},{7,6},{8,9},{9,8},{10,11... | collective-permute-start | bytes 1161224 | tf_op jit(solution)/shard_map/ppermute | solution.py:17
  16.3 7.2 %collective-permute-done.6.mine_ref = bf16[168,1152]{1,0:T(8,128)(2,1)S(1)} collective-permute-done((bf16[168,1152]{1,0:T(8,128)(2,1)S(1)}, bf16[168,1152]{1,0:T(8,128)(2,1)S(1)}, u32[]{:S(2)}, u32[]{:S(2)}) %collective-permute-start.6) | collective-permute-done | bytes 387104 | tf_op jit(solution)/shard_map/ppermute | solution.py:17
  23.5 2.1 %collective-permute-start.8 = (bf16[168,1152]{1,0:T(8,128)(2,1)S(1)}, bf16[168,1152]{1,0:T(8,128)(2,1)S(1)}, u32[]{:S(2)}, u32[]{:S(2)}) collective-permute-start(bf16[168,1152]{1,0:T(8,128)(2,1)S(1)} %collective-permute-done.6.mine_ref), channel_id=1, source_target_pairs={{0,1},{1,0},{2,3},{3,2},{4,5},{5,4},{6,7},{7,6},{8,9},{9,8},{10,11... | collective-permute-start | bytes 1161224 | tf_op jit(solution)/shard_map/ppermute | solution.py:17
  25.6 0.0 collective-permute-start.3
  25.6 0.5 collective-permute-start.7
  26.1 0.0 collective-permute-done.4.mine_ref
  26.1 0.0 collective-permute-start.5
  26.1 5.2 %collective-permute-done.8.mine_ref = bf16[168,1152]{1,0:T(8,128)(2,1)S(1)} collective-permute-done((bf16[168,1152]{1,0:T(8,128)(2,1)S(1)}, bf16[168,1152]{1,0:T(8,128)(2,1)S(1)}, u32[]{:S(2)}, u32[]{:S(2)}) %collective-permute-start.8) | collective-permute-done | bytes 387104 | tf_op jit(solution)/shard_map/ppermute | solution.py:17
  31.3 0.0 collective-permute-start.9
  33.9 0.1 pad_maximum_fusion.scalar_ref
  34.0 0.1 add_multiply_fusion
  34.1 0.1 add_add_fusion
  34.1 0.0 collective-permute-done.3.refs_0_
  34.1 0.0 collective-permute-done.5.refs_1_
  34.2 0.0 collective-permute-done.7.refs_2_
  34.2 0.0 collective-permute-done.9.refs_3_
  34.2 1.7 %shard_map.99 = bf16[160,1152]{1,0:T(8,128)(2,1)S(1)} custom-call(s32[7]{0:T(128)S(1)} %get-tuple-element.5.place_ref, f32[3]{0:T(128)S(1)} %pad_maximum_fusion.scalar_ref, s32[1]{0:T(128)S(6)} %copy.10.sample_ref, bf16[168,1152]{1,0:T(8,128)(2,1)S(1)} %collective-permute-done.8.mine_ref, bf16[168,1152]{1,0:T(8,128)(2,1)S(1)} %collective-permute-done.3.refs_0_, ...), custom_call_target="tpu_custom_call" | custom-call | tf_op jit(solution)/shard_map/pallas_call | solution.py:81
  35.9 2.1 %collective-permute-start.11 = (bf16[160,1152]{1,0:T(8,128)(2,1)S(1)}, bf16[160,1152]{1,0:T(8,128)(2,1)S(1)}, u32[]{:S(2)}, u32[]{:S(2)}) collective-permute-start(bf16[160,1152]{1,0:T(8,128)(2,1)S(1)} %shard_map.99), channel_id=1, source_target_pairs={{0,1},{1,0},{2,3},{3,2},{4,5},{5,4},{6,7},{7,6},{8,9},{9,8},{10,11... | collective-permute-start | bytes 1105928 | tf_op jit(solution)/shard_map/ppermute | solution.py:17
  38.0 0.1 add_add_fusion.1
  38.1 1.7 %shard_map.97 = bf16[160,1152]{1,0:T(8,128)(2,1)S(1)} custom-call(s32[7]{0:T(128)S(1)} %get-tuple-element.2.place_ref, f32[3]{0:T(128)S(1)} %pad_maximum_fusion.scalar_ref, s32[1]{0:T(128)S(6)} %copy.10.sample_ref, bf16[168,1152]{1,0:T(8,128)(2,1)S(1)} %collective-permute-done.4.mine_ref, bf16[168,1152]{1,0:T(8,128)(2,1)S(1)} %collective-permute-done.3.refs_0_, ...), custom_call_target="tpu_custom_call" | custom-call | tf_op jit(solution)/shard_map/pallas_call | solution.py:81
  39.8 0.1 collective-permute-start.10
  39.9 1.7 %shard_map.98 = f32[160,1152]{1,0:T(8,128)S(1)} custom-call(s32[7]{0:T(128)S(1)} %get-tuple-element.3.place_ref, f32[3]{0:T(128)S(1)} %pad_maximum_fusion.scalar_ref, s32[1]{0:T(128)S(6)} %copy.10.sample_ref, bf16[168,1152]{1,0:T(8,128)(2,1)S(1)} %collective-permute-done.6.mine_ref, bf16[168,1152]{1,0:T(8,128)(2,1)S(1)} %collective-permute-done.3.refs_0_, ...), custom_call_target="tpu_custom_call" | custom-call | tf_op jit(solution)/shard_map/pallas_call | solution.py:81
  41.7 1.8 %collective-permute-done.11 = bf16[160,1152]{1,0:T(8,128)(2,1)S(1)} collective-permute-done((bf16[160,1152]{1,0:T(8,128)(2,1)S(1)}, bf16[160,1152]{1,0:T(8,128)(2,1)S(1)}, u32[]{:S(2)}, u32[]{:S(2)}) %collective-permute-start.11) | collective-permute-done | bytes 368672 | tf_op jit(solution)/shard_map/ppermute | solution.py:17
  43.5 0.1 add_convert_fusion.1
  43.6 2.5 %collective-permute-start.12 = (bf16[160,1152]{1,0:T(8,128)(2,1)S(1)}, bf16[160,1152]{1,0:T(8,128)(2,1)S(1)}, u32[]{:S(2)}, u32[]{:S(2)}) collective-permute-start(bf16[160,1152]{1,0:T(8,128)(2,1)S(1)} %add_convert_fusion.1), channel_id=1, source_target_pairs={{0,8},{1,9},{2,10},{3,11},{4,12},{5,13},{6,14},{7,15},{8,0},{9,1},... | collective-permute-start | bytes 1105928 | tf_op jit(solution)/shard_map/ppermute | solution.py:17
  46.0 1.7 %shard_map.96 = f32[160,1152]{1,0:T(8,128)S(1)} custom-call(s32[7]{0:T(128)S(1)} %get-tuple-element.4.place_ref, f32[3]{0:T(128)S(1)} %pad_maximum_fusion.scalar_ref, s32[1]{0:T(128)S(6)} %copy.10.sample_ref, bf16[168,1152]{1,0:T(8,128)(2,1)S(1)} %shard_map.95.mine_ref, bf16[168,1152]{1,0:T(8,128)(2,1)S(1)} %collective-permute-done.3.refs_0_, ...), custom_call_target="tpu_custom_call" | custom-call | tf_op jit(solution)/shard_map/pallas_call | solution.py:81
  47.8 0.0 collective-permute-done.10
  47.8 6.2 %collective-permute-done.12 = bf16[160,1152]{1,0:T(8,128)(2,1)S(1)} collective-permute-done((bf16[160,1152]{1,0:T(8,128)(2,1)S(1)}, bf16[160,1152]{1,0:T(8,128)(2,1)S(1)}, u32[]{:S(2)}, u32[]{:S(2)}) %collective-permute-start.12) | collective-permute-done | bytes 368672 | tf_op jit(solution)/shard_map/ppermute | solution.py:17
  54.0 0.1 add_convert_fusion
  54.2 2.2 %collective-permute-start.13 = (bf16[80,1152]{1,0:T(8,128)(2,1)S(1)}, bf16[80,1152]{1,0:T(8,128)(2,1)S(1)}, u32[]{:S(2)}, u32[]{:S(2)}) collective-permute-start(bf16[80,1152]{1,0:T(8,128)(2,1)S(1)} %slice.17), channel_id=1, source_target_pairs={{0,16},{1,17},{2,18},{3,19},{4,20},{5,21},{6,22},{7,23},{8,24},{9,... | collective-permute-start | bytes 552968 | tf_op jit(solution)/shard_map/ppermute | solution.py:141
  56.4 1.3 %collective-permute-start.14 = (bf16[160,576]{1,0:T(8,128)(2,1)S(1)}, bf16[160,576]{1,0:T(8,128)(2,1)S(1)}, u32[]{:S(2)}, u32[]{:S(2)}) collective-permute-start(bf16[160,576]{1,0:T(8,128)(2,1)S(1)} %slice.18), channel_id=1, source_target_pairs={{16,0},{17,1},{18,2},{19,3},{20,4},{21,5},{22,6},{23,7},{24,8},{25... | collective-permute-start | bytes 552968 | tf_op jit(solution)/shard_map/ppermute | solution.py:142
  57.7 0.0 collective-permute-done.13
  57.7 0.7 %slice_select_fusion.1 = bf16[80,1152]{1,0:T(8,128)(2,1)} fusion(bf16[80,1152]{1,0:T(8,128)(2,1)S(1)} %collective-permute-done.13, bf16[160,1152]{1,0:T(8,128)(2,1)S(1)} %add_convert_fusion, pred[]{:T(512)S(6)} %eq.2), kind=kLoop, calls=%fused_computation.3 | loop fusion | flops 92160 | bytes 552961 | tf_op jit(solution)/shard_map/jit(_where)/select_n | solution.py:143
  58.4 1.3 %collective-permute-done.14 = bf16[160,576]{1,0:T(8,128)(2,1)S(1)} collective-permute-done((bf16[160,576]{1,0:T(8,128)(2,1)S(1)}, bf16[160,576]{1,0:T(8,128)(2,1)S(1)}, u32[]{:S(2)}, u32[]{:S(2)}) %collective-permute-start.14) | collective-permute-done | bytes 184352 | tf_op jit(solution)/shard_map/ppermute | solution.py:142
  59.7 0.8 %slice_select_fusion = bf16[160,576]{1,0:T(8,128)(2,1)} fusion(bf16[160,576]{1,0:T(8,128)(2,1)S(1)} %collective-permute-done.14, bf16[160,1152]{1,0:T(8,128)(2,1)S(1)} %add_convert_fusion, pred[]{:T(512)S(6)} %eq.2), kind=kLoop, calls=%fused_computation.2 | loop fusion | flops 92160 | bytes 552961 | tf_op jit(solution)/shard_map/jit(_where)/select_n | solution.py:144
  (5 shorter events, 0.0 us)
Async XLA Ops:
  0.6 7.5 %collective-permute-start = (bf16[80,1152]{1,0:T(8,128)(2,1)}, bf16[80,1152]{1,0:T(8,128)(2,1)S(1)}, u32[]{:S(2)}, u32[]{:S(2)}) collective-permute-start(bf16[80,1152]{1,0:T(8,128)(2,1)} %image_ref.1), channel_id=1, source_target_pairs={{16,0},{17,1},{18,2},{19,3},{20,4},{21,5},{22,6},{23,7},{24,8},{25... | collective-permute-start | bytes 552968 | tf_op jit(solution)/shard_map/ppermute | solution.py:107
  1.9 6.2 %collective-permute-start.1 = (bf16[160,576]{1,0:T(8,128)(2,1)}, bf16[160,576]{1,0:T(8,128)(2,1)S(1)}, u32[]{:S(2)}, u32[]{:S(2)}) collective-permute-start(bf16[160,576]{1,0:T(8,128)(2,1)} %text_ref.1), channel_id=1, source_target_pairs={{0,16},{1,17},{2,18},{3,19},{4,20},{5,21},{6,22},{7,23},{8,24},{9,... | collective-permute-start | bytes 552968 | tf_op jit(solution)/shard_map/ppermute | solution.py:108
  5.0 3.1 %collective-permute-start.2 = (s32[80]{0:T(128)}, s32[80]{0:T(128)S(1)}, u32[]{:S(2)}, u32[]{:S(2)}) collective-permute-start(s32[80]{0:T(128)} %param.10), channel_id=1, source_target_pairs={{16,0},{17,1},{18,2},{19,3},{20,4},{21,5},{22,6},{23,7},{24,8},{25... | collective-permute-start | bytes 968 | tf_op jit(solution)/shard_map/ppermute | solution.py:109
  8.1 0.7 %copy-start.2 = (s32[160]{0:T(256)S(1)}, s32[160]{0:T(256)}, u32[]{:S(2)}) copy-start(s32[160]{0:T(256)} %param.11) | copy-start | bytes 1924
  8.1 0.7 %copy-start.3 = (s32[80]{0:T(128)S(1)}, s32[80]{0:T(128)}, u32[]{:S(2)}) copy-start(s32[80]{0:T(128)} %param.10) | copy-start | bytes 964
  8.8 0.9 %copy-start = (bf16[160,576]{1,0:T(8,128)(2,1)S(1)}, bf16[160,576]{1,0:T(8,128)(2,1)}, u32[]{:S(2)}) copy-start(bf16[160,576]{1,0:T(8,128)(2,1)} %text_ref.1) | copy-start | bytes 552964
  9.8 0.9 %copy-start.1 = (bf16[80,1152]{1,0:T(8,128)(2,1)S(1)}, bf16[80,1152]{1,0:T(8,128)(2,1)}, u32[]{:S(2)}) copy-start(bf16[80,1152]{1,0:T(8,128)(2,1)} %image_ref.1) | copy-start | bytes 552964
  10.8 12.7 %collective-permute-start.6 = (bf16[168,1152]{1,0:T(8,128)(2,1)S(1)}, bf16[168,1152]{1,0:T(8,128)(2,1)S(1)}, u32[]{:S(2)}, u32[]{:S(2)}) collective-permute-start(bf16[168,1152]{1,0:T(8,128)(2,1)S(1)} %shard_map.95.mine_ref), channel_id=1, source_target_pairs={{0,8},{1,9},{2,10},{3,11},{4,12},{5,13},{6,14},{7,15},{8,0},{9,1},... | collective-permute-start | bytes 1161224 | tf_op jit(solution)/shard_map/ppermute | solution.py:17
  14.8 11.3 %collective-permute-start.4 = (bf16[168,1152]{1,0:T(8,128)(2,1)S(1)}, bf16[168,1152]{1,0:T(8,128)(2,1)S(1)}, u32[]{:S(2)}, u32[]{:S(2)}) collective-permute-start(bf16[168,1152]{1,0:T(8,128)(2,1)S(1)} %shard_map.95.mine_ref), channel_id=1, source_target_pairs={{0,1},{1,0},{2,3},{3,2},{4,5},{5,4},{6,7},{7,6},{8,9},{9,8},{10,11... | collective-permute-start | bytes 1161224 | tf_op jit(solution)/shard_map/ppermute | solution.py:17
  23.5 7.8 %collective-permute-start.8 = (bf16[168,1152]{1,0:T(8,128)(2,1)S(1)}, bf16[168,1152]{1,0:T(8,128)(2,1)S(1)}, u32[]{:S(2)}, u32[]{:S(2)}) collective-permute-start(bf16[168,1152]{1,0:T(8,128)(2,1)S(1)} %collective-permute-done.6.mine_ref), channel_id=1, source_target_pairs={{0,1},{1,0},{2,3},{3,2},{4,5},{5,4},{6,7},{7,6},{8,9},{9,8},{10,11... | collective-permute-start | bytes 1161224 | tf_op jit(solution)/shard_map/ppermute | solution.py:17
  25.6 8.5 %collective-permute-start.3 = (bf16[168,1152]{1,0:T(8,128)(2,1)S(1)}, bf16[168,1152]{1,0:T(8,128)(2,1)S(1)}, u32[]{:S(2)}, u32[]{:S(2)}) collective-permute-start(bf16[168,1152]{1,0:T(8,128)(2,1)S(1)} %shard_map.95.mine_ref), channel_id=1, source_target_pairs={{0,16},{16,0},{1,17},{17,1},{2,18},{18,2},{3,19},{19,3},{4,20},{20... | collective-permute-start | bytes 1161224 | tf_op jit(solution)/shard_map/ppermute | solution.py:21
  25.6 8.5 %collective-permute-start.7 = (bf16[168,1152]{1,0:T(8,128)(2,1)S(1)}, bf16[168,1152]{1,0:T(8,128)(2,1)S(1)}, u32[]{:S(2)}, u32[]{:S(2)}) collective-permute-start(bf16[168,1152]{1,0:T(8,128)(2,1)S(1)} %collective-permute-done.6.mine_ref), channel_id=1, source_target_pairs={{0,16},{16,0},{1,17},{17,1},{2,18},{18,2},{3,19},{19,3},{4,20},{20... | collective-permute-start | bytes 1161224 | tf_op jit(solution)/shard_map/ppermute | solution.py:21
  26.1 8.0 %collective-permute-start.5 = (bf16[168,1152]{1,0:T(8,128)(2,1)S(1)}, bf16[168,1152]{1,0:T(8,128)(2,1)S(1)}, u32[]{:S(2)}, u32[]{:S(2)}) collective-permute-start(bf16[168,1152]{1,0:T(8,128)(2,1)S(1)} %collective-permute-done.4.mine_ref), channel_id=1, source_target_pairs={{0,16},{16,0},{1,17},{17,1},{2,18},{18,2},{3,19},{19,3},{4,20},{20... | collective-permute-start | bytes 1161224 | tf_op jit(solution)/shard_map/ppermute | solution.py:21
  31.3 2.9 %collective-permute-start.9 = (bf16[168,1152]{1,0:T(8,128)(2,1)S(1)}, bf16[168,1152]{1,0:T(8,128)(2,1)S(1)}, u32[]{:S(2)}, u32[]{:S(2)}) collective-permute-start(bf16[168,1152]{1,0:T(8,128)(2,1)S(1)} %collective-permute-done.8.mine_ref), channel_id=1, source_target_pairs={{0,16},{16,0},{1,17},{17,1},{2,18},{18,2},{3,19},{19,3},{4,20},{20... | collective-permute-start | bytes 1161224 | tf_op jit(solution)/shard_map/ppermute | solution.py:21
  35.9 7.6 %collective-permute-start.11 = (bf16[160,1152]{1,0:T(8,128)(2,1)S(1)}, bf16[160,1152]{1,0:T(8,128)(2,1)S(1)}, u32[]{:S(2)}, u32[]{:S(2)}) collective-permute-start(bf16[160,1152]{1,0:T(8,128)(2,1)S(1)} %shard_map.99), channel_id=1, source_target_pairs={{0,1},{1,0},{2,3},{3,2},{4,5},{5,4},{6,7},{7,6},{8,9},{9,8},{10,11... | collective-permute-start | bytes 1105928 | tf_op jit(solution)/shard_map/ppermute | solution.py:17
  39.8 7.9 %collective-permute-start.10 = (bf16[160,1152]{1,0:T(8,128)(2,1)S(1)}, bf16[160,1152]{1,0:T(8,128)(2,1)S(1)}, u32[]{:S(2)}, u32[]{:S(2)}) collective-permute-start(bf16[160,1152]{1,0:T(8,128)(2,1)S(1)} %shard_map.97), channel_id=1, source_target_pairs={{0,1},{1,0},{2,3},{3,2},{4,5},{5,4},{6,7},{7,6},{8,9},{9,8},{10,11... | collective-permute-start | bytes 1105928 | tf_op jit(solution)/shard_map/ppermute | solution.py:17
  43.6 10.5 %collective-permute-start.12 = (bf16[160,1152]{1,0:T(8,128)(2,1)S(1)}, bf16[160,1152]{1,0:T(8,128)(2,1)S(1)}, u32[]{:S(2)}, u32[]{:S(2)}) collective-permute-start(bf16[160,1152]{1,0:T(8,128)(2,1)S(1)} %add_convert_fusion.1), channel_id=1, source_target_pairs={{0,8},{1,9},{2,10},{3,11},{4,12},{5,13},{6,14},{7,15},{8,0},{9,1},... | collective-permute-start | bytes 1105928 | tf_op jit(solution)/shard_map/ppermute | solution.py:17
  54.2 3.5 %collective-permute-start.13 = (bf16[80,1152]{1,0:T(8,128)(2,1)S(1)}, bf16[80,1152]{1,0:T(8,128)(2,1)S(1)}, u32[]{:S(2)}, u32[]{:S(2)}) collective-permute-start(bf16[80,1152]{1,0:T(8,128)(2,1)S(1)} %slice.17), channel_id=1, source_target_pairs={{0,16},{1,17},{2,18},{3,19},{4,20},{5,21},{6,22},{7,23},{8,24},{9,... | collective-permute-start | bytes 552968 | tf_op jit(solution)/shard_map/ppermute | solution.py:141
  56.4 3.3 %collective-permute-start.14 = (bf16[160,576]{1,0:T(8,128)(2,1)S(1)}, bf16[160,576]{1,0:T(8,128)(2,1)S(1)}, u32[]{:S(2)}, u32[]{:S(2)}) collective-permute-start(bf16[160,576]{1,0:T(8,128)(2,1)S(1)} %slice.18), channel_id=1, source_target_pairs={{16,0},{17,1},{18,2},{19,3},{20,4},{21,5},{22,6},{23,7},{24,8},{25... | collective-permute-start | bytes 552968 | tf_op jit(solution)/shard_map/ppermute | solution.py:142

commit v2 on v0

--- a/solution.py
+++ b/solution.py
@@ -1,7 +1,289 @@
+import functools
+
 import jax
 import jax.numpy as jnp
 from jax import lax
+from jax.experimental import pallas as pl
+from jax.experimental.pallas import tpu as pltpu
 from jax.sharding import PartitionSpec as P
+
+SPARE = 8
+LINE = 256
+
+
+def hop(block, image_bit, text_bit, across=False):
+    count = lax.axis_size("col")
+    turn = count if across else 0
+    route = [(c, turn + (c ^ image_bit)) for c in range(count)]
+    route += [(count + c, count - turn + (c ^ text_bit)) for c in range(count)]
+    return lax.ppermute(block, ("row", "col"), route)
+
+
+def swap(block):
+    return lax.ppermute(block, "row", [(0, 1), (1, 0)])
+
+
+def masks(count, row):
+    top = count // 2
+    near, far = (1, 2), (top, top // 2)
+    if row is None:
+        return near, far
+    return tuple(jnp.where(row == 0, *pair) for pair in (near, far, near[::-1], far[::-1]))
+
+
+def put_line(ref, *pieces):
+    pieces = [piece.astype(jnp.float32) for piece in pieces]
+    pieces += [jnp.zeros((1, LINE - sum(piece.shape[1] for piece in pieces)), jnp.float32)]
+    line = jnp.broadcast_to(jnp.concatenate(pieces, axis=1), (SPARE, LINE))
+    ref[ref.shape[0] - SPARE :, :LINE] = line.astype(ref.dtype)
+
+
+def put_texts(ref, text_ref):
+    half, part = text_ref.shape[0] // 2, text_ref.shape[1]
+    ref[:half, :part] = text_ref[:half]
+    ref[:half, part:] = text_ref[half:]
+
+
+def first_kernel(spot_ref, image_ref, text_ref, image_valid_ref, text_valid_ref, mine_ref, give_ref):
+    half = image_ref.shape[0]
+
+    def fill(image_to, text_to):
+        image_to[:half] = image_ref[...]
+        put_line(image_to, image_valid_ref[...])
+        put_texts(text_to, text_ref)
+        put_line(text_to, text_valid_ref[...])
+
+    @pl.when(spot_ref[0] == 0)
+    def _():
+        fill(mine_ref, give_ref)
+
+    @pl.when(spot_ref[0] != 0)
+    def _():
+        fill(give_ref, mine_ref)
+
+
+def unpack(pair, texts, out_ref, start):
+    one, two = pair
+    half, part = one.shape[0] - SPARE, one.shape[1] // 2
+
+    @pl.when(texts)
+    def _():
+        out_ref[start : start + half, :part] = two[:half, :part]
+        out_ref[start : start + half, part:] = one[:half, :part]
+        out_ref[start + half : start + 2 * half, :part] = two[:half, part:]
+        out_ref[start + half : start + 2 * half, part:] = one[:half, part:]
+
+    @pl.when(jnp.logical_not(texts))
+    def _():
+        out_ref[start : start + half] = one[:half]
+        out_ref[start + half : start + 2 * half] = two[:half]
+
+
+def counts(pair, texts):
+    one, two = pair
+    half = one.shape[0] - SPARE
+    line_one = one[half:, :LINE].astype(jnp.float32)[:1]
+    line_two = two[half:, :LINE].astype(jnp.float32)[:1]
+    images = jnp.concatenate([line_one[:, :half], line_two[:, :half]], axis=1)
+    return jnp.where(texts, line_one[:, : 2 * half], images)
+
+
+def upright(line):
+    size = line.shape[1]
+    at = lax.broadcasted_iota(jnp.int32, (size, size), 0)
+    to = lax.broadcasted_iota(jnp.int32, (size, size), 1)
+    return jnp.sum(jnp.where(at == to, line, 0.0), axis=1, keepdims=True)
+
+
+def sample_ids(col, texts, half, cols, axis):
+    shape = (2 * half, 1) if axis == 0 else (1, 2 * half)
+    at = lax.broadcasted_iota(jnp.int32, shape, axis)
+    jump = jnp.where(texts, 0, (cols - 1) * half)
+    first = col * jnp.where(texts, 2 * half, half)
+    return at + first + jnp.where(at >= half, jump, 0)
+
+
+def coefficients_of(cols, spot_ref, scale_ref, bias_ref, grad_ref, sample_ref, mine, others, my_sets, other_sets):
+    row, col = spot_ref[0], spot_ref[1]
+    my_texts, other_texts = row != 0, row == 0
+    near, far, other_near, other_far = masks(cols, row)
+    my_masks = {"own": 0, "near": near, "far": far, "both": near ^ far}
+    other_masks = {"own": 0, "near": other_near, "far": other_far, "both": other_near ^ other_far}
+    half = my_sets[0][1][0].shape[0] - SPARE
+    scale, bias = scale_ref[0], bias_ref[0]
+    factor = grad_ref[0] * scale / sample_ref[0].astype(jnp.float32)
+    my_ids = jnp.concatenate([sample_ids(col ^ my_masks[k], my_texts, half, cols, 0) for k, _ in my_sets], axis=0)
+    other_ids = jnp.concatenate(
+        [sample_ids(col ^ other_masks[k], other_texts, half, cols, 1) for k, _ in other_sets], axis=1)
+    my_weights = jnp.concatenate([upright(counts(pair, my_texts)) for _, pair in my_sets], axis=0)
+    other_weights = factor * jnp.concatenate([counts(pair, other_texts) for _, pair in other_sets], axis=1)
+    logits = lax.dot_general(mine, others, (((1,), (1,)), ((), ())), preferred_element_type=jnp.float32)
+    logits = logits * scale + bias
+    match = my_ids == other_ids
+    rate = 1.0 / (1.0 + jnp.exp(jnp.where(match, logits, -logits)))
+    return (jnp.where(match, -rate, rate) * my_weights * other_weights).astype(jnp.bfloat16)
+
+
+def pairs(refs):
+    return [refs[n : n + 2] for n in range(0, len(refs), 2)]
+
+
+THREE = ("own", "near", "far")
+
+
+def early_kernel(cols, spot_ref, scale_ref, bias_ref, grad_ref, sample_ref, *refs):
+    mine_pairs, other_pairs = pairs(refs[:6]), pairs(refs[6:12])
+    mine_ref, others_ref, total_ref = refs[12:]
+    texts = spot_ref[0] != 0
+    size = 2 * (refs[0].shape[0] - SPARE)
+    for n in range(3):
+        unpack(mine_pairs[n], texts, mine_ref, n * size)
+        unpack(other_pairs[n], jnp.logical_not(texts), others_ref, n * size)
+    others = others_ref[...]
+    coefficient = coefficients_of(cols, spot_ref, scale_ref, bias_ref, grad_ref, sample_ref, mine_ref[...], others,
+                                  list(zip(THREE, mine_pairs)), list(zip(THREE, other_pairs)))
+    total_ref[...] = jnp.dot(coefficient, others, preferred_element_type=jnp.float32)
+
+
+def both_kernel(cols, spot_ref, scale_ref, bias_ref, grad_ref, sample_ref, *refs):
+    mine_pair, other_pairs = refs[:2], pairs(refs[2:8])
+    others_ref, mine_ref, total_ref = refs[8:]
+    unpack(mine_pair, spot_ref[0] != 0, mine_ref, 0)
+    others = others_ref[...]
+    coefficient = coefficients_of(cols, spot_ref, scale_ref, bias_ref, grad_ref, sample_ref, mine_ref[...], others,
+                                  [("both", mine_pair)], list(zip(THREE, other_pairs)))
+    total_ref[...] = jnp.dot(coefficient, others, preferred_element_type=jnp.float32)
+
+
+def pack_sum(total, texts, stay_ref, cross_ref, start=0):
+    half, part = total.shape[0] // 2, total.shape[1] // 2
+    rows = slice(start, start + half)
+
+    @pl.when(texts)
+    def _():
+        stay_ref[rows, :part] = total[:half, part:].astype(stay_ref.dtype)
+        stay_ref[rows, part:] = total[half:, part:].astype(stay_ref.dtype)
+        cross_ref[:half, :part] = total[:half, :part].astype(cross_ref.dtype)
+        cross_ref[:half, part:] = total[half:, :part].astype(cross_ref.dtype)
+
+    @pl.when(jnp.logical_not(texts))
+    def _():
+        stay_ref[rows] = total[:half].astype(stay_ref.dtype)
+        cross_ref[:half] = total[half:].astype(cross_ref.dtype)
+
+
+def late_kernel(cols, spot_ref, scale_ref, bias_ref, grad_ref, sample_ref, *refs):
+    mine_pair, other_pair = refs[:2], refs[2:4]
+    mine_ref, total_ref = refs[4:6]
+    others_ref, stay_ref, cross_ref = refs[6:]
+    texts = spot_ref[0] != 0
+    unpack(other_pair, jnp.logical_not(texts), others_ref, 0)
+    others = others_ref[...]
+    coefficient = coefficients_of(cols, spot_ref, scale_ref, bias_ref, grad_ref, sample_ref, mine_ref[...], others,
+                                  [("both", mine_pair)], [("both", other_pair)])
+    total = total_ref[...] + jnp.dot(coefficient, others, preferred_element_type=jnp.float32)
+    pack_sum(total, texts, stay_ref, cross_ref)
+
+
+def rest_kernel(cols, spot_ref, scale_ref, bias_ref, grad_ref, sample_ref, *refs):
+    mine_pairs, other_pair = pairs(refs[:6]), refs[6:8]
+    mine_ref, others_ref, total_ref = refs[8:11]
+    own_stay, own_cross, near_ref, far_stay, far_cross = refs[11:]
+    texts = spot_ref[0] != 0
+    others = others_ref[...]
+    coefficient = coefficients_of(cols, spot_ref, scale_ref, bias_ref, grad_ref, sample_ref, mine_ref[...], others,
+                                  list(zip(THREE, mine_pairs)), [("both", other_pair)])
+    total = total_ref[...] + jnp.dot(coefficient, others, preferred_element_type=jnp.float32)
+    size = total.shape[0] // 3
+    pack_sum(total[2 * size :], texts, far_stay, far_cross)
+    pack_sum(total[size : 2 * size], texts, near_ref, near_ref, size // 2)
+    pack_sum(total[:size], texts, own_stay, own_cross)
+
+
+def last_kernel(spot_ref, stay_ref, crossed_ref, stay_in_ref, cross_in_ref, image_ref, text_ref):
+    half, part = text_ref.shape[0] // 2, text_ref.shape[1]
+    stay = (stay_ref[...] + stay_in_ref[...].astype(jnp.float32)).astype(image_ref.dtype)
+    crossed = (crossed_ref[...] + cross_in_ref[...].astype(jnp.float32)).astype(image_ref.dtype)
+
+    def put(images, texts):
+        image_ref[...] = images
+        text_ref[:half] = texts[:, :part]
+        text_ref[half:] = texts[:, part:]
+
+    @pl.when(spot_ref[0] == 0)
+    def _():
+        put(stay, crossed)
+
+    @pl.when(spot_ref[0] != 0)
+    def _():
+        put(crossed, stay)
+
+
+def call(kernel, out_shape, smem, *arrays, flops=0):
+    size = sum(a.size * a.dtype.itemsize for a in (*arrays, *jax.tree.leaves(out_shape)))
+    return pl.pallas_call(
+        kernel,
+        out_shape=out_shape,
+        in_specs=[pl.BlockSpec(memory_space=pltpu.SMEM)] * smem
+        + [pl.BlockSpec(memory_space=pltpu.VMEM)] * (len(arrays) - smem),
+        out_specs=jax.tree.map(lambda _: pl.BlockSpec(memory_space=pltpu.VMEM), out_shape),
+        compiler_params=pltpu.CompilerParams(vmem_limit_bytes=24 * 1024 * 1024),
+        cost_estimate=pl.CostEstimate(flops=flops, bytes_accessed=size, transcendentals=0),
+    )(*arrays)
+
+
+def pair_body(
+    image_emb, text_emb, image_valid, text_valid, sample_count, logit_scale, logit_bias, loss_grad
+):
+    half, width = image_emb.shape
+    size = 2 * half
+    cols = lax.axis_size("col")
+    spot = jnp.stack([lax.axis_index("row"), lax.axis_index("col")]).astype(jnp.int32)
+    near, far = masks(cols, None)
+    scalars = (spot, logit_scale, logit_bias, loss_grad, sample_count)
+
+    def shape(rows, dtype):
+        return jax.ShapeDtypeStruct((rows, width), dtype)
+
+    bf16, f32 = jnp.bfloat16, jnp.float32
+    sent = shape(half + SPARE, bf16)
+    own_a, give = call(first_kernel, (sent, sent), 1, spot, image_emb, text_emb, image_valid[None],
+                       text_valid[None])
+    far_a = hop(own_a, *far)
+    own_b = swap(give)
+    far_b = hop(own_b, *far)
+    near_a = hop(own_a, *near)
+    near_b = hop(own_b, *near)
+    both_a = hop(far_a, *near)
+    both_b = hop(far_b, *near)
+    mine = (own_a, own_b, near_a, near_b, far_a, far_b)
+    others = (swap(own_a), give, swap(near_a), swap(near_b), swap(far_a), swap(far_b))
+    both = (both_a, both_b)
+    other_both = (swap(both_a), swap(both_b))
+
+    pair_flops = 4 * size * size * width
+    mine_rows, other_rows, early = call(
+        functools.partial(early_kernel, cols), (shape(3 * size, bf16), shape(3 * size, bf16), shape(3 * size, f32)),
+        5, *scalars, *mine, *others, flops=9 * pair_flops)
+    both_rows, both_early = call(
+        functools.partial(both_kernel, cols), (shape(size, bf16), shape(size, f32)), 5, *scalars, *both, *others,
+        other_rows, flops=3 * pair_flops)
+    other_late, late_stay, late_cross = call(
+        functools.partial(late_kernel, cols), (shape(size, bf16), shape(half, bf16), shape(half, bf16)), 5, *scalars,
+        *both, *other_both, both_rows, both_early, flops=pair_flops)
+    in_cross = hop(late_cross, *near)
+    in_stay = hop(late_stay, *near)
+    own_stay, own_cross, near_out, far_stay, far_cross = call(
+        functools.partial(rest_kernel, cols),
+        (shape(half, f32), shape(half, f32), shape(size, bf16), shape(half, f32), shape(half, f32)), 5, *scalars,
+        *mine, *other_both, mine_rows, other_late, early, flops=3 * pair_flops)
+    far_cross = hop((far_cross + in_cross.astype(f32)).astype(bf16), *far, across=True)
+    near_in = hop(near_out, *near)
+    far_stay = hop((far_stay + in_stay.astype(f32)).astype(bf16), *far)
+    crossed = swap(own_cross + near_in[:half].astype(f32))
+    stay = own_stay + near_in[half:].astype(f32)
+    return call(last_kernel, (shape(half, bf16), jax.ShapeDtypeStruct(text_emb.shape, bf16)), 1, spot, stay, crossed,
+                far_stay, far_cross)
 
 
 def partner(block, axis, distance):
@@ -118,4 +400,6 @@
         P(),
     )
     out_specs = (P(("row", "col"), None), P("col", "row"))
-    return jax.shard_map(body, mesh=mesh, in_specs=in_specs, out_specs=out_specs, check_vma=False)
+    paired = mesh.shape["row"] == 2 and mesh.shape["col"] == 16
+    run = pair_body if paired else body
+    return jax.shard_map(run, mesh=mesh, in_specs=in_specs, out_specs=out_specs, check_vma=False)

time: 165 us -> 54.5 us (0.33)
  waiting for transfers between devices: 113 us -> 20.9 us
  between operations: 16.9 us -> 3.35 us
  Pallas kernels: 0 us -> 10 us
  other arithmetic: 5.61 us -> 0.24 us
  matrix products: 4.87 us -> 0 us
  local copies, waits for them, and re-layouts: 5.35 us -> 3.19 us
  blocking collectives: 2.09 us -> 0 us
    ppermute x12 -> x20, waiting for transfers between devices: 113 us -> 20.9 us  [the longest x11 20.9 us: hop(): return lax.ppermute(block, ('row', 'col'), route)]
    pallas_call x0 -> x6, Pallas kernels: none -> 10 us  [call(): pl.pallas_call(kernel, out_shape=out_shape, in_specs=[pl.BlockSpec(memory...]
    dot_general x3 -> x0, matrix products: 4.87 us -> none  [the longest x1 2.76 us: text_part(): lax.dot_general(coefficient, image_rows, (((0,), (0,)), ((), ())), prefer...]
    convert_element_type x5 -> x2, other arithmetic: 2.22 us -> 0.08 us  [the longest x1 0.05 us: pair_body(): (far_cross + in_cross.astype(f32)).astype(bf16)]
    all_gather x1 -> x0, blocking collectives: 2.09 us -> none  [body(): text_block = lax.all_gather(text_emb, 'row', axis=1, tiled=True)]
    unnamed x13 -> x8, local copies, waits for them, and re-layouts: 5.03 us -> 3.19 us
    select_n x8 -> x0, other arithmetic: 1.79 us -> none  [the longest x2 1.28 us: body(): jnp.where(lower, jnp.concatenate([image_rows, other_rows], 0), jnp.concat...]
    ppermute x12 -> x20, starting transfers between devices: 17.2 us -> 16.6 us  [the longest x11 15 us: hop(): return lax.ppermute(block, ('row', 'col'), route)]
  transfers between devices with their start and end apart: 13 -> 20, of which waited for: 7 -> 7; matrix products, arithmetic and copies ran while one was open for 6% -> 0% of each run, Pallas kernels for 0% -> 12%
where the time goes in v2:
time: 54.5 us; the launch traced here: 54.3 us
  waiting for transfers between devices  20.9 us (38%)
  starting transfers between devices  16.6 us (30%)
  Pallas kernels  10 us (18%)
  between operations  3.35 us (6%)
  local copies, waits for them, and re-layouts  3.19 us (6%)
    ppermute x11, waiting for transfers between devices, hop(): return lax.ppermute(block, ('row', 'col'), route)  20.9 us
    ppermute x11, starting transfers between devices, hop(): return lax.ppermute(block, ('row', 'col'), route)  15 us
    pallas_call x6, Pallas kernels, call(): pl.pallas_call(kernel, out_shape=out_shape, in_specs=[pl.BlockSpec(memory...  10 us
    unnamed x8, local copies, waits for them, and re-layouts  3.19 us
    ppermute x9, starting transfers between devices, swap(): return lax.ppermute(block, 'row', [(0, 1), (1, 0)])  1.62 us
  transfers between devices with their start and end apart: 20, of which 7 were waited for; matrix products, arithmetic and copies ran while one was open for 0% of the time, Pallas kernels for 12%

profile of v2, /device:TPU:0, one launch (start us, length us, event | category | flops | bytes accessed | tf_op | source)
XLA Modules:
  0.0 54.3 jit_solution(12160301681494211960)
XLA Ops:
  0.6 0.1 pad_add_fusion.spot_ref
  0.7 0.9 %copy-done = bf16[160,576]{1,0:T(8,128)(2,1)S(1)} copy-done((bf16[160,576]{1,0:T(8,128)(2,1)S(1)}, bf16[160,576]{1,0:T(8,128)(2,1)}, u32[]{:S(2)}) %copy-start) | copy-done | bytes 184344
  1.6 0.9 %copy-done.1 = bf16[80,1152]{1,0:T(8,128)(2,1)S(1)} copy-done((bf16[80,1152]{1,0:T(8,128)(2,1)S(1)}, bf16[80,1152]{1,0:T(8,128)(2,1)}, u32[]{:S(2)}) %copy-start.1) | copy-done | bytes 184344
  2.6 0.7 %copy-done.2 = s32[160]{0:T(256)S(1)} copy-done((s32[160]{0:T(256)S(1)}, s32[160]{0:T(256)}, u32[]{:S(2)}) %copy-start.2) | copy-done | bytes 664
  3.2 0.7 %copy-done.3 = s32[80]{0:T(128)S(1)} copy-done((s32[80]{0:T(128)S(1)}, s32[80]{0:T(128)}, u32[]{:S(2)}) %copy-start.3) | copy-done | bytes 344
  3.9 0.6 %shard_map.95 = (bf16[88,1152]{1,0:T(8,128)(2,1)S(1)}, bf16[88,1152]{1,0:T(8,128)(2,1)S(1)}) custom-call(s32[2]{0:T(128)S(1)} %pad_add_fusion.spot_ref, bf16[80,1152]{1,0:T(8,128)(2,1)S(1)} %copy-done.1, bf16[160,576]{1,0:T(8,128)(2,1)S(1)} %copy-done, s32[1,80]{1,0:T(1,128)S(1)} %bitcast.5, s32[1,160]{1,0:T(1,128)S(1)} %bitcast.4), custom_call_target="tpu_custom_call" | custom-call | bytes 775112 | tf_op jit(solution)/shard_map/pallas_call | solution.py:224
  4.5 0.5 collective-permute-start
  5.1 3.7 %collective-permute-start.3 = (bf16[88,1152]{1,0:T(8,128)(2,1)S(1)}, bf16[88,1152]{1,0:T(8,128)(2,1)S(1)}, u32[]{:S(2)}, u32[]{:S(2)}) collective-permute-start(bf16[88,1152]{1,0:T(8,128)(2,1)S(1)} %get-tuple-element.17.refs_0_), channel_id=1, source_target_pairs={{0,8},{1,9},{2,10},{3,11},{4,12},{5,13},{6,14},{7,15},{8,0},{9,1},... | collective-permute-start | bytes 608264 | tf_op jit(solution)/shard_map/ppermute | solution.py:19
  8.7 1.5 %collective-permute-start.1 = (bf16[88,1152]{1,0:T(8,128)(2,1)S(1)}, bf16[88,1152]{1,0:T(8,128)(2,1)S(1)}, u32[]{:S(2)}, u32[]{:S(2)}) collective-permute-start(bf16[88,1152]{1,0:T(8,128)(2,1)S(1)} %get-tuple-element.17.refs_0_), channel_id=1, source_target_pairs={{0,1},{1,0},{2,3},{3,2},{4,5},{5,4},{6,7},{7,6},{8,9},{9,8},{10,11... | collective-permute-start | bytes 608264 | tf_op jit(solution)/shard_map/ppermute | solution.py:19
  10.2 0.0 collective-permute-done.refs_1_
  10.2 0.3 collective-permute-start.4
  10.6 0.0 collective-permute-start.9
  10.6 1.0 %collective-permute-start.2 = (bf16[88,1152]{1,0:T(8,128)(2,1)S(1)}, bf16[88,1152]{1,0:T(8,128)(2,1)S(1)}, u32[]{:S(2)}, u32[]{:S(2)}) collective-permute-start(bf16[88,1152]{1,0:T(8,128)(2,1)S(1)} %collective-permute-done.refs_1_), channel_id=1, source_target_pairs={{0,1},{1,0},{2,3},{3,2},{4,5},{5,4},{6,7},{7,6},{8,9},{9,8},{10,11... | collective-permute-start | bytes 608264 | tf_op jit(solution)/shard_map/ppermute | solution.py:19
  11.6 2.6 %collective-permute-done.3.refs_4_ = bf16[88,1152]{1,0:T(8,128)(2,1)S(1)} collective-permute-done((bf16[88,1152]{1,0:T(8,128)(2,1)S(1)}, bf16[88,1152]{1,0:T(8,128)(2,1)S(1)}, u32[]{:S(2)}, u32[]{:S(2)}) %collective-permute-start.3) | collective-permute-done | bytes 202784 | tf_op jit(solution)/shard_map/ppermute | solution.py:19
  14.2 0.0 collective-permute-start.12
  14.2 0.2 collective-permute-done.1.refs_2_
  14.5 1.5 %collective-permute-start.5 = (bf16[88,1152]{1,0:T(8,128)(2,1)S(1)}, bf16[88,1152]{1,0:T(8,128)(2,1)S(1)}, u32[]{:S(2)}, u32[]{:S(2)}) collective-permute-start(bf16[88,1152]{1,0:T(8,128)(2,1)S(1)} %collective-permute-done.3.refs_4_), channel_id=1, source_target_pairs={{0,1},{1,0},{2,3},{3,2},{4,5},{5,4},{6,7},{7,6},{8,9},{9,8},{10,11... | collective-permute-start | bytes 608264 | tf_op jit(solution)/shard_map/ppermute | solution.py:19
  16.0 3.1 %collective-permute-done.4.refs_5_ = bf16[88,1152]{1,0:T(8,128)(2,1)S(1)} collective-permute-done((bf16[88,1152]{1,0:T(8,128)(2,1)S(1)}, bf16[88,1152]{1,0:T(8,128)(2,1)S(1)}, u32[]{:S(2)}, u32[]{:S(2)}) %collective-permute-start.4) | collective-permute-done | bytes 202784 | tf_op jit(solution)/shard_map/ppermute | solution.py:19
  19.0 0.9 %collective-permute-start.7 = (bf16[88,1152]{1,0:T(8,128)(2,1)S(1)}, bf16[88,1152]{1,0:T(8,128)(2,1)S(1)}, u32[]{:S(2)}, u32[]{:S(2)}) collective-permute-start(bf16[88,1152]{1,0:T(8,128)(2,1)S(1)} %collective-permute-done.4.refs_5_), channel_id=1, source_target_pairs={{0,1},{1,0},{2,3},{3,2},{4,5},{5,4},{6,7},{7,6},{8,9},{9,8},{10,11... | collective-permute-start | bytes 608264 | tf_op jit(solution)/shard_map/ppermute | solution.py:19
  19.9 0.0 collective-permute-done.9.refs_6_.refs_2_
  19.9 0.0 collective-permute-start.10
  20.0 0.0 collective-permute-done.2.refs_3_
  20.0 0.5 collective-permute-start.13
  20.5 0.0 collective-permute-done.12.refs_10_.refs_6_
  20.5 0.1 collective-permute-start.11
  20.5 0.0 collective-permute-done.5.refs_0_
  20.5 0.4 collective-permute-start.6
  21.0 3.8 %collective-permute-done.7.refs_1_ = bf16[88,1152]{1,0:T(8,128)(2,1)S(1)} collective-permute-done((bf16[88,1152]{1,0:T(8,128)(2,1)S(1)}, bf16[88,1152]{1,0:T(8,128)(2,1)S(1)}, u32[]{:S(2)}, u32[]{:S(2)}) %collective-permute-start.7) | collective-permute-done | bytes 202784 | tf_op jit(solution)/shard_map/ppermute | solution.py:19
  24.8 0.0 collective-permute-start.8
  27.4 0.0 collective-permute-done.11.refs_9_.refs_5_
  27.4 2.7 %shard_map.96 = (bf16[480,1152]{1,0:T(8,128)(2,1)S(1)}, bf16[480,1152]{1,0:T(8,128)(2,1)S(1)}, f32[480,1152]{1,0:T(8,128)S(1)}) custom-call(s32[2]{0:T(128)S(1)} %pad_add_fusion.spot_ref, f32[1]{0:T(128)S(6)} %copy.11.scale_ref, f32[1]{0:T(128)S(6)} %copy.12.bias_ref, f32[1]{0:T(128)S(6)} %copy.13.grad_ref, s32[1]{0:T(128)S(6)} %copy.10.sample_ref, ...), custom_call_target="tpu_custom_call" | custom-call | flops 1061683200 | bytes 6856728 | tf_op jit(solution)/shard_map/pallas_call | solution.py:224
  30.1 1.5 %shard_map.97 = (bf16[160,1152]{1,0:T(8,128)(2,1)S(1)}, f32[160,1152]{1,0:T(8,128)S(1)}) custom-call(s32[2]{0:T(128)S(1)} %pad_add_fusion.spot_ref, f32[1]{0:T(128)S(6)} %copy.11.scale_ref, f32[1]{0:T(128)S(6)} %copy.12.bias_ref, f32[1]{0:T(128)S(6)} %copy.13.grad_ref, s32[1]{0:T(128)S(6)} %copy.10.sample_ref, ...), custom_call_target="tpu_custom_call" | custom-call | flops 353894400 | bytes 3833880 | tf_op jit(solution)/shard_map/pallas_call | solution.py:224
  31.6 0.0 collective-permute-done.6.refs_2_.refs_6_
  31.6 0.0 collective-permute-done.8.refs_3_.refs_7_
  31.7 1.4 %shard_map.98 = (bf16[160,1152]{1,0:T(8,128)(2,1)S(1)}, bf16[80,1152]{1,0:T(8,128)(2,1)S(1)}, bf16[80,1152]{1,0:T(8,128)(2,1)S(1)}) custom-call(s32[2]{0:T(128)S(1)} %pad_add_fusion.spot_ref, f32[1]{0:T(128)S(6)} %copy.11.scale_ref, f32[1]{0:T(128)S(6)} %copy.12.bias_ref, f32[1]{0:T(128)S(6)} %copy.13.grad_ref, s32[1]{0:T(128)S(6)} %copy.10.sample_ref, ...), custom_call_target="tpu_custom_call" | custom-call | flops 117964800 | bytes 2654232 | tf_op jit(solution)/shard_map/pallas_call | solution.py:224
  33.1 1.0 %collective-permute-start.18 = (bf16[80,1152]{1,0:T(8,128)(2,1)S(1)}, bf16[80,1152]{1,0:T(8,128)(2,1)S(1)}, u32[]{:S(2)}, u32[]{:S(2)}) collective-permute-start(bf16[80,1152]{1,0:T(8,128)(2,1)S(1)} %get-tuple-element.31), channel_id=1, source_target_pairs={{0,1},{1,0},{2,3},{3,2},{4,5},{5,4},{6,7},{7,6},{8,9},{9,8},{10,11... | collective-permute-start | bytes 552968 | tf_op jit(solution)/shard_map/ppermute | solution.py:19
  34.1 1.1 %collective-permute-start.16 = (bf16[80,1152]{1,0:T(8,128)(2,1)S(1)}, bf16[80,1152]{1,0:T(8,128)(2,1)S(1)}, u32[]{:S(2)}, u32[]{:S(2)}) collective-permute-start(bf16[80,1152]{1,0:T(8,128)(2,1)S(1)} %get-tuple-element.29), channel_id=1, source_target_pairs={{0,1},{1,0},{2,3},{3,2},{4,5},{5,4},{6,7},{7,6},{8,9},{9,8},{10,11... | collective-permute-start | bytes 552968 | tf_op jit(solution)/shard_map/ppermute | solution.py:19
  35.2 2.3 %shard_map.99 = (f32[80,1152]{1,0:T(8,128)S(1)}, f32[80,1152]{1,0:T(8,128)S(1)}, bf16[160,1152]{1,0:T(8,128)(2,1)S(1)}, f32[80,1152]{1,0:T(8,128)S(1)}, f32[80,1152]{1,0:T(8,128)S(1)}) custom-call(s32[2]{0:T(128)S(1)} %pad_add_fusion.spot_ref, f32[1]{0:T(128)S(6)} %copy.11.scale_ref, f32[1]{0:T(128)S(6)} %copy.12.bias_ref, f32[1]{0:T(128)S(6)} %copy.13.grad_ref, ...), custom_call_target="tpu_custom_call" | custom-call | flops 353894400 | bytes 7151640 | tf_op jit(solution)/shard_map/pallas_call | solution.py:224
  37.4 1.0 %collective-permute-start.14 = (bf16[160,1152]{1,0:T(8,128)(2,1)S(1)}, bf16[160,1152]{1,0:T(8,128)(2,1)S(1)}, u32[]{:S(2)}, u32[]{:S(2)}) collective-permute-start(bf16[160,1152]{1,0:T(8,128)(2,1)S(1)} %get-tuple-element.26), channel_id=1, source_target_pairs={{0,1},{1,0},{2,3},{3,2},{4,5},{5,4},{6,7},{7,6},{8,9},{9,8},{10,11... | collective-permute-start | bytes 1105928 | tf_op jit(solution)/shard_map/ppermute | solution.py:19
  38.4 0.3 collective-permute-done.18
  38.7 1.5 %collective-permute-start.19 = (bf16[80,1152]{1,0:T(8,128)(2,1)S(1)}, bf16[80,1152]{1,0:T(8,128)(2,1)S(1)}, u32[]{:S(2)}, u32[]{:S(2)}) collective-permute-start(bf16[80,1152]{1,0:T(8,128)(2,1)S(1)} %add_convert_fusion), channel_id=1, source_target_pairs={{0,24},{1,25},{2,26},{3,27},{4,28},{5,29},{6,30},{7,31},{8,16},{9,... | collective-permute-start | bytes 552968 | tf_op jit(solution)/shard_map/ppermute | solution.py:19
  40.3 4.7 %collective-permute-done.14 = bf16[160,1152]{1,0:T(8,128)(2,1)S(1)} collective-permute-done((bf16[160,1152]{1,0:T(8,128)(2,1)S(1)}, bf16[160,1152]{1,0:T(8,128)(2,1)S(1)}, u32[]{:S(2)}, u32[]{:S(2)}) %collective-permute-start.14) | collective-permute-done | bytes 368672 | tf_op jit(solution)/shard_map/ppermute | solution.py:19
  45.0 0.1 convert_add_fusion
  45.1 0.1 collective-permute-start.15
  45.2 1.5 %collective-permute-start.17 = (bf16[80,1152]{1,0:T(8,128)(2,1)S(1)}, bf16[80,1152]{1,0:T(8,128)(2,1)S(1)}, u32[]{:S(2)}, u32[]{:S(2)}) collective-permute-start(bf16[80,1152]{1,0:T(8,128)(2,1)S(1)} %add_convert_fusion.1), channel_id=1, source_target_pairs={{0,8},{1,9},{2,10},{3,11},{4,12},{5,13},{6,14},{7,15},{8,0},{9,1},... | collective-permute-start | bytes 552968 | tf_op jit(solution)/shard_map/ppermute | solution.py:19
  46.7 0.0 collective-permute-done.19.cross_in_ref
  46.7 6.1 %collective-permute-done.17.stay_in_ref = bf16[80,1152]{1,0:T(8,128)(2,1)S(1)} collective-permute-done((bf16[80,1152]{1,0:T(8,128)(2,1)S(1)}, bf16[80,1152]{1,0:T(8,128)(2,1)S(1)}, u32[]{:S(2)}, u32[]{:S(2)}) %collective-permute-start.17) | collective-permute-done | bytes 184352 | tf_op jit(solution)/shard_map/ppermute | solution.py:19
  52.8 1.5 %shard_map.100 = (bf16[80,1152]{1,0:T(8,128)(2,1)}, bf16[160,576]{1,0:T(8,128)(2,1)}) custom-call(s32[2]{0:T(128)S(1)} %pad_add_fusion.spot_ref, f32[80,1152]{1,0:T(8,128)S(1)} %get-tuple-element.33.stay_ref, f32[80,1152]{1,0:T(8,128)S(1)} %collective-permute-done.15.crossed_ref, bf16[80,1152]{1,0:T(8,128)(2,1)S(1)} %collective-permute-done.17.stay_in_ref, ...), custom_call_target="tpu_custom_call" | custom-call | bytes 1474568 | tf_op jit(solution)/shard_map/pallas_call | solution.py:224
  (10 shorter events, 0.1 us)
Async XLA Ops:
  0.7 0.9 %copy-start = (bf16[160,576]{1,0:T(8,128)(2,1)S(1)}, bf16[160,576]{1,0:T(8,128)(2,1)}, u32[]{:S(2)}) copy-start(bf16[160,576]{1,0:T(8,128)(2,1)} %text_ref.1) | copy-start | bytes 552964
  1.6 0.9 %copy-start.1 = (bf16[80,1152]{1,0:T(8,128)(2,1)S(1)}, bf16[80,1152]{1,0:T(8,128)(2,1)}, u32[]{:S(2)}) copy-start(bf16[80,1152]{1,0:T(8,128)(2,1)} %image_ref.1) | copy-start | bytes 552964
  2.6 0.7 %copy-start.2 = (s32[160]{0:T(256)S(1)}, s32[160]{0:T(256)}, u32[]{:S(2)}) copy-start(s32[160]{0:T(256)} %param.11) | copy-start | bytes 1924
  3.2 0.7 %copy-start.3 = (s32[80]{0:T(128)S(1)}, s32[80]{0:T(128)}, u32[]{:S(2)}) copy-start(s32[80]{0:T(128)} %param.10) | copy-start | bytes 964
  4.5 5.7 %collective-permute-start = (bf16[88,1152]{1,0:T(8,128)(2,1)S(1)}, bf16[88,1152]{1,0:T(8,128)(2,1)S(1)}, u32[]{:S(2)}, u32[]{:S(2)}) collective-permute-start(bf16[88,1152]{1,0:T(8,128)(2,1)S(1)} %get-tuple-element.18.refs_7_.refs_3_), channel_id=1, source_target_pairs={{0,16},{16,0},{1,17},{17,1},{2,18},{18,2},{3,19},{19,3},{4,20},{20... | collective-permute-start | bytes 608264 | tf_op jit(solution)/shard_map/ppermute | solution.py:23
  5.1 9.2 %collective-permute-start.3 = (bf16[88,1152]{1,0:T(8,128)(2,1)S(1)}, bf16[88,1152]{1,0:T(8,128)(2,1)S(1)}, u32[]{:S(2)}, u32[]{:S(2)}) collective-permute-start(bf16[88,1152]{1,0:T(8,128)(2,1)S(1)} %get-tuple-element.17.refs_0_), channel_id=1, source_target_pairs={{0,8},{1,9},{2,10},{3,11},{4,12},{5,13},{6,14},{7,15},{8,0},{9,1},... | collective-permute-start | bytes 608264 | tf_op jit(solution)/shard_map/ppermute | solution.py:19
  8.7 5.7 %collective-permute-start.1 = (bf16[88,1152]{1,0:T(8,128)(2,1)S(1)}, bf16[88,1152]{1,0:T(8,128)(2,1)S(1)}, u32[]{:S(2)}, u32[]{:S(2)}) collective-permute-start(bf16[88,1152]{1,0:T(8,128)(2,1)S(1)} %get-tuple-element.17.refs_0_), channel_id=1, source_target_pairs={{0,1},{1,0},{2,3},{3,2},{4,5},{5,4},{6,7},{7,6},{8,9},{9,8},{10,11... | collective-permute-start | bytes 608264 | tf_op jit(solution)/shard_map/ppermute | solution.py:19
  10.2 8.8 %collective-permute-start.4 = (bf16[88,1152]{1,0:T(8,128)(2,1)S(1)}, bf16[88,1152]{1,0:T(8,128)(2,1)S(1)}, u32[]{:S(2)}, u32[]{:S(2)}) collective-permute-start(bf16[88,1152]{1,0:T(8,128)(2,1)S(1)} %collective-permute-done.refs_1_), channel_id=1, source_target_pairs={{0,8},{1,9},{2,10},{3,11},{4,12},{5,13},{6,14},{7,15},{8,0},{9,1},... | collective-permute-start | bytes 608264 | tf_op jit(solution)/shard_map/ppermute | solution.py:19
  10.6 9.4 %collective-permute-start.9 = (bf16[88,1152]{1,0:T(8,128)(2,1)S(1)}, bf16[88,1152]{1,0:T(8,128)(2,1)S(1)}, u32[]{:S(2)}, u32[]{:S(2)}) collective-permute-start(bf16[88,1152]{1,0:T(8,128)(2,1)S(1)} %get-tuple-element.17.refs_0_), channel_id=1, source_target_pairs={{0,16},{16,0},{1,17},{17,1},{2,18},{18,2},{3,19},{19,3},{4,20},{20... | collective-permute-start | bytes 608264 | tf_op jit(solution)/shard_map/ppermute | solution.py:23
  10.6 9.4 %collective-permute-start.2 = (bf16[88,1152]{1,0:T(8,128)(2,1)S(1)}, bf16[88,1152]{1,0:T(8,128)(2,1)S(1)}, u32[]{:S(2)}, u32[]{:S(2)}) collective-permute-start(bf16[88,1152]{1,0:T(8,128)(2,1)S(1)} %collective-permute-done.refs_1_), channel_id=1, source_target_pairs={{0,1},{1,0},{2,3},{3,2},{4,5},{5,4},{6,7},{7,6},{8,9},{9,8},{10,11... | collective-permute-start | bytes 608264 | tf_op jit(solution)/shard_map/ppermute | solution.py:19
  14.2 6.2 %collective-permute-start.12 = (bf16[88,1152]{1,0:T(8,128)(2,1)S(1)}, bf16[88,1152]{1,0:T(8,128)(2,1)S(1)}, u32[]{:S(2)}, u32[]{:S(2)}) collective-permute-start(bf16[88,1152]{1,0:T(8,128)(2,1)S(1)} %collective-permute-done.3.refs_4_), channel_id=1, source_target_pairs={{0,16},{16,0},{1,17},{17,1},{2,18},{18,2},{3,19},{19,3},{4,20},{20... | collective-permute-start | bytes 608264 | tf_op jit(solution)/shard_map/ppermute | solution.py:23
  14.5 6.1 %collective-permute-start.5 = (bf16[88,1152]{1,0:T(8,128)(2,1)S(1)}, bf16[88,1152]{1,0:T(8,128)(2,1)S(1)}, u32[]{:S(2)}, u32[]{:S(2)}) collective-permute-start(bf16[88,1152]{1,0:T(8,128)(2,1)S(1)} %collective-permute-done.3.refs_4_), channel_id=1, source_target_pairs={{0,1},{1,0},{2,3},{3,2},{4,5},{5,4},{6,7},{7,6},{8,9},{9,8},{10,11... | collective-permute-start | bytes 608264 | tf_op jit(solution)/shard_map/ppermute | solution.py:19
  19.0 5.7 %collective-permute-start.7 = (bf16[88,1152]{1,0:T(8,128)(2,1)S(1)}, bf16[88,1152]{1,0:T(8,128)(2,1)S(1)}, u32[]{:S(2)}, u32[]{:S(2)}) collective-permute-start(bf16[88,1152]{1,0:T(8,128)(2,1)S(1)} %collective-permute-done.4.refs_5_), channel_id=1, source_target_pairs={{0,1},{1,0},{2,3},{3,2},{4,5},{5,4},{6,7},{7,6},{8,9},{9,8},{10,11... | collective-permute-start | bytes 608264 | tf_op jit(solution)/shard_map/ppermute | solution.py:19
  19.9 7.4 %collective-permute-start.10 = (bf16[88,1152]{1,0:T(8,128)(2,1)S(1)}, bf16[88,1152]{1,0:T(8,128)(2,1)S(1)}, u32[]{:S(2)}, u32[]{:S(2)}) collective-permute-start(bf16[88,1152]{1,0:T(8,128)(2,1)S(1)} %collective-permute-done.1.refs_2_), channel_id=1, source_target_pairs={{0,16},{16,0},{1,17},{17,1},{2,18},{18,2},{3,19},{19,3},{4,20},{20... | collective-permute-start | bytes 608264 | tf_op jit(solution)/shard_map/ppermute | solution.py:23
  20.0 7.4 %collective-permute-start.13 = (bf16[88,1152]{1,0:T(8,128)(2,1)S(1)}, bf16[88,1152]{1,0:T(8,128)(2,1)S(1)}, u32[]{:S(2)}, u32[]{:S(2)}) collective-permute-start(bf16[88,1152]{1,0:T(8,128)(2,1)S(1)} %collective-permute-done.4.refs_5_), channel_id=1, source_target_pairs={{0,16},{16,0},{1,17},{17,1},{2,18},{18,2},{3,19},{19,3},{4,20},{20... | collective-permute-start | bytes 608264 | tf_op jit(solution)/shard_map/ppermute | solution.py:23
  20.5 6.9 %collective-permute-start.11 = (bf16[88,1152]{1,0:T(8,128)(2,1)S(1)}, bf16[88,1152]{1,0:T(8,128)(2,1)S(1)}, u32[]{:S(2)}, u32[]{:S(2)}) collective-permute-start(bf16[88,1152]{1,0:T(8,128)(2,1)S(1)} %collective-permute-done.2.refs_3_), channel_id=1, source_target_pairs={{0,16},{16,0},{1,17},{17,1},{2,18},{18,2},{3,19},{19,3},{4,20},{20... | collective-permute-start | bytes 608264 | tf_op jit(solution)/shard_map/ppermute | solution.py:23
  20.5 11.1 %collective-permute-start.6 = (bf16[88,1152]{1,0:T(8,128)(2,1)S(1)}, bf16[88,1152]{1,0:T(8,128)(2,1)S(1)}, u32[]{:S(2)}, u32[]{:S(2)}) collective-permute-start(bf16[88,1152]{1,0:T(8,128)(2,1)S(1)} %collective-permute-done.5.refs_0_), channel_id=1, source_target_pairs={{0,16},{16,0},{1,17},{17,1},{2,18},{18,2},{3,19},{19,3},{4,20},{20... | collective-permute-start | bytes 608264 | tf_op jit(solution)/shard_map/ppermute | solution.py:23
  24.8 6.9 %collective-permute-start.8 = (bf16[88,1152]{1,0:T(8,128)(2,1)S(1)}, bf16[88,1152]{1,0:T(8,128)(2,1)S(1)}, u32[]{:S(2)}, u32[]{:S(2)}) collective-permute-start(bf16[88,1152]{1,0:T(8,128)(2,1)S(1)} %collective-permute-done.7.refs_1_), channel_id=1, source_target_pairs={{0,16},{16,0},{1,17},{17,1},{2,18},{18,2},{3,19},{19,3},{4,20},{20... | collective-permute-start | bytes 608264 | tf_op jit(solution)/shard_map/ppermute | solution.py:23
  33.1 5.6 %collective-permute-start.18 = (bf16[80,1152]{1,0:T(8,128)(2,1)S(1)}, bf16[80,1152]{1,0:T(8,128)(2,1)S(1)}, u32[]{:S(2)}, u32[]{:S(2)}) collective-permute-start(bf16[80,1152]{1,0:T(8,128)(2,1)S(1)} %get-tuple-element.31), channel_id=1, source_target_pairs={{0,1},{1,0},{2,3},{3,2},{4,5},{5,4},{6,7},{7,6},{8,9},{9,8},{10,11... | collective-permute-start | bytes 552968 | tf_op jit(solution)/shard_map/ppermute | solution.py:19
  34.1 11.1 %collective-permute-start.16 = (bf16[80,1152]{1,0:T(8,128)(2,1)S(1)}, bf16[80,1152]{1,0:T(8,128)(2,1)S(1)}, u32[]{:S(2)}, u32[]{:S(2)}) collective-permute-start(bf16[80,1152]{1,0:T(8,128)(2,1)S(1)} %get-tuple-element.29), channel_id=1, source_target_pairs={{0,1},{1,0},{2,3},{3,2},{4,5},{5,4},{6,7},{7,6},{8,9},{9,8},{10,11... | collective-permute-start | bytes 552968 | tf_op jit(solution)/shard_map/ppermute | solution.py:19
  37.4 7.6 %collective-permute-start.14 = (bf16[160,1152]{1,0:T(8,128)(2,1)S(1)}, bf16[160,1152]{1,0:T(8,128)(2,1)S(1)}, u32[]{:S(2)}, u32[]{:S(2)}) collective-permute-start(bf16[160,1152]{1,0:T(8,128)(2,1)S(1)} %get-tuple-element.26), channel_id=1, source_target_pairs={{0,1},{1,0},{2,3},{3,2},{4,5},{5,4},{6,7},{7,6},{8,9},{9,8},{10,11... | collective-permute-start | bytes 1105928 | tf_op jit(solution)/shard_map/ppermute | solution.py:19
  38.7 8.0 %collective-permute-start.19 = (bf16[80,1152]{1,0:T(8,128)(2,1)S(1)}, bf16[80,1152]{1,0:T(8,128)(2,1)S(1)}, u32[]{:S(2)}, u32[]{:S(2)}) collective-permute-start(bf16[80,1152]{1,0:T(8,128)(2,1)S(1)} %add_convert_fusion), channel_id=1, source_target_pairs={{0,24},{1,25},{2,26},{3,27},{4,28},{5,29},{6,30},{7,31},{8,16},{9,... | collective-permute-start | bytes 552968 | tf_op jit(solution)/shard_map/ppermute | solution.py:19
  45.1 7.7 %collective-permute-start.15 = (f32[80,1152]{1,0:T(8,128)S(1)}, f32[80,1152]{1,0:T(8,128)S(1)}, u32[]{:S(2)}, u32[]{:S(2)}) collective-permute-start(f32[80,1152]{1,0:T(8,128)S(1)} %get-tuple-element.32), channel_id=1, source_target_pairs={{0,16},{16,0},{1,17},{17,1},{2,18},{18,2},{3,19},{19,3},{4,20},{20... | collective-permute-start | bytes 1105928 | tf_op jit(solution)/shard_map/ppermute | solution.py:23
  45.2 7.6 %collective-permute-start.17 = (bf16[80,1152]{1,0:T(8,128)(2,1)S(1)}, bf16[80,1152]{1,0:T(8,128)(2,1)S(1)}, u32[]{:S(2)}, u32[]{:S(2)}) collective-permute-start(bf16[80,1152]{1,0:T(8,128)(2,1)S(1)} %add_convert_fusion.1), channel_id=1, source_target_pairs={{0,8},{1,9},{2,10},{3,11},{4,12},{5,13},{6,14},{7,15},{8,0},{9,1},... | collective-permute-start | bytes 552968 | tf_op jit(solution)/shard_map/ppermute | solution.py:19

commit v3 on v2

--- a/solution.py
+++ b/solution.py
@@ -44,14 +44,25 @@
     ref[:half, part:] = text_ref[half:]
 
 
-def first_kernel(spot_ref, image_ref, text_ref, image_valid_ref, text_valid_ref, mine_ref, give_ref):
+def first_kernel(spot_ref, image_ref, text_ref, image_valid_ref, text_valid_ref, mine_ref, give_ref, texts, image_line,
+                 text_line, sems):
     half = image_ref.shape[0]
 
     def fill(image_to, text_to):
-        image_to[:half] = image_ref[...]
-        put_line(image_to, image_valid_ref[...])
-        put_texts(text_to, text_ref)
-        put_line(text_to, text_valid_ref[...])
+        copies = [
+            pltpu.make_async_copy(source, target, sems.at[n])
+            for n, (source, target) in enumerate((
+                (text_ref, texts), (image_ref, image_to.at[pl.ds(0, half)]), (image_valid_ref, image_line),
+                (text_valid_ref, text_line)))
+        ]
+        for copy in copies:
+            copy.start()
+        copies[0].wait()
+        put_texts(text_to, texts)
+        for copy in copies[1:]:
+            copy.wait()
+        put_line(image_to, image_line[...])
+        put_line(text_to, text_line[...])
 
     @pl.when(spot_ref[0] == 0)
     def _():
@@ -155,21 +166,20 @@
     total_ref[...] = jnp.dot(coefficient, others, preferred_element_type=jnp.float32)
 
 
-def pack_sum(total, texts, stay_ref, cross_ref, start=0):
+def pack_sum(total, texts, stay_ref, cross_ref):
     half, part = total.shape[0] // 2, total.shape[1] // 2
-    rows = slice(start, start + half)
 
     @pl.when(texts)
     def _():
-        stay_ref[rows, :part] = total[:half, part:].astype(stay_ref.dtype)
-        stay_ref[rows, part:] = total[half:, part:].astype(stay_ref.dtype)
-        cross_ref[:half, :part] = total[:half, :part].astype(cross_ref.dtype)
-        cross_ref[:half, part:] = total[half:, :part].astype(cross_ref.dtype)
+        stay_ref[:, :part] = total[:half, part:].astype(stay_ref.dtype)
+        stay_ref[:, part:] = total[half:, part:].astype(stay_ref.dtype)
+        cross_ref[:, :part] = total[:half, :part].astype(cross_ref.dtype)
+        cross_ref[:, part:] = total[half:, :part].astype(cross_ref.dtype)
 
     @pl.when(jnp.logical_not(texts))
     def _():
-        stay_ref[rows] = total[:half].astype(stay_ref.dtype)
-        cross_ref[:half] = total[half:].astype(cross_ref.dtype)
+        stay_ref[...] = total[:half].astype(stay_ref.dtype)
+        cross_ref[...] = total[half:].astype(cross_ref.dtype)
 
 
 def late_kernel(cols, spot_ref, scale_ref, bias_ref, grad_ref, sample_ref, *refs):
@@ -188,7 +198,7 @@
 def rest_kernel(cols, spot_ref, scale_ref, bias_ref, grad_ref, sample_ref, *refs):
     mine_pairs, other_pair = pairs(refs[:6]), refs[6:8]
     mine_ref, others_ref, total_ref = refs[8:11]
-    own_stay, own_cross, near_ref, far_stay, far_cross = refs[11:]
+    own_stay, own_cross, near_stay, near_cross, far_stay, far_cross = refs[11:]
     texts = spot_ref[0] != 0
     others = others_ref[...]
     coefficient = coefficients_of(cols, spot_ref, scale_ref, bias_ref, grad_ref, sample_ref, mine_ref[...], others,
@@ -196,14 +206,19 @@
     total = total_ref[...] + jnp.dot(coefficient, others, preferred_element_type=jnp.float32)
     size = total.shape[0] // 3
     pack_sum(total[2 * size :], texts, far_stay, far_cross)
-    pack_sum(total[size : 2 * size], texts, near_ref, near_ref, size // 2)
+    pack_sum(total[size : 2 * size], texts, near_stay, near_cross)
     pack_sum(total[:size], texts, own_stay, own_cross)
 
 
-def last_kernel(spot_ref, stay_ref, crossed_ref, stay_in_ref, cross_in_ref, image_ref, text_ref):
+def last_kernel(spot_ref, stay_ref, crossed_ref, near_stay_ref, near_cross_ref, far_stay_ref, far_cross_ref,
+                image_ref, text_ref):
     half, part = text_ref.shape[0] // 2, text_ref.shape[1]
-    stay = (stay_ref[...] + stay_in_ref[...].astype(jnp.float32)).astype(image_ref.dtype)
-    crossed = (crossed_ref[...] + cross_in_ref[...].astype(jnp.float32)).astype(image_ref.dtype)
+
+    def add(own, near, far):
+        return (own[...] + near[...].astype(jnp.float32) + far[...].astype(jnp.float32)).astype(image_ref.dtype)
+
+    stay = add(stay_ref, near_stay_ref, far_stay_ref)
+    crossed = add(crossed_ref, near_cross_ref, far_cross_ref)
 
     def put(images, texts):
         image_ref[...] = images
@@ -247,8 +262,15 @@
 
     bf16, f32 = jnp.bfloat16, jnp.float32
     sent = shape(half + SPARE, bf16)
-    own_a, give = call(first_kernel, (sent, sent), 1, spot, image_emb, text_emb, image_valid[None],
-                       text_valid[None])
+    first = (image_emb, text_emb, image_valid[None], text_valid[None])
+    own_a, give = pl.pallas_call(
+        first_kernel,
+        out_shape=(sent, sent),
+        in_specs=[pl.BlockSpec(memory_space=pltpu.SMEM)] + [pl.BlockSpec(memory_space=pltpu.HBM)] * 4,
+        out_specs=(pl.BlockSpec(memory_space=pltpu.VMEM),) * 2,
+        scratch_shapes=[pltpu.VMEM(a.shape, a.dtype) for a in first[1:]] + [pltpu.SemaphoreType.DMA((4,))],
+        compiler_params=pltpu.CompilerParams(vmem_limit_bytes=60 * 1024 * 1024),
+    )(spot, *first)
     far_a = hop(own_a, *far)
     own_b = swap(give)
     far_b = hop(own_b, *far)
@@ -259,12 +281,13 @@
     mine = (own_a, own_b, near_a, near_b, far_a, far_b)
     others = (swap(own_a), give, swap(near_a), swap(near_b), swap(far_a), swap(far_b))
     both = (both_a, both_b)
-    other_both = (swap(both_a), swap(both_b))
 
     pair_flops = 4 * size * size * width
     mine_rows, other_rows, early = call(
         functools.partial(early_kernel, cols), (shape(3 * size, bf16), shape(3 * size, bf16), shape(3 * size, f32)),
         5, *scalars, *mine, *others, flops=9 * pair_flops)
+    both, early = lax.optimization_barrier((both, early))
+    other_both = (swap(both[0]), swap(both[1]))
     both_rows, both_early = call(
         functools.partial(both_kernel, cols), (shape(size, bf16), shape(size, f32)), 5, *scalars, *both, *others,
         other_rows, flops=3 * pair_flops)
@@ -273,17 +296,19 @@
         *both, *other_both, both_rows, both_early, flops=pair_flops)
     in_cross = hop(late_cross, *near)
     in_stay = hop(late_stay, *near)
-    own_stay, own_cross, near_out, far_stay, far_cross = call(
+    own_stay, own_cross, near_stay, near_cross, far_stay, far_cross = call(
         functools.partial(rest_kernel, cols),
-        (shape(half, f32), shape(half, f32), shape(size, bf16), shape(half, f32), shape(half, f32)), 5, *scalars,
-        *mine, *other_both, mine_rows, other_late, early, flops=3 * pair_flops)
-    far_cross = hop((far_cross + in_cross.astype(f32)).astype(bf16), *far, across=True)
-    near_in = hop(near_out, *near)
+        (shape(half, f32), shape(half, f32), shape(half, bf16), shape(half, bf16), shape(half, f32), shape(half, f32)),
+        5, *scalars, *mine, *other_both, mine_rows, other_late, early, flops=3 * pair_flops)
+    crossed = swap(own_cross)
+    far_cross = (far_cross + in_cross.astype(f32)).astype(bf16)
     far_stay = hop((far_stay + in_stay.astype(f32)).astype(bf16), *far)
-    crossed = swap(own_cross + near_in[:half].astype(f32))
-    stay = own_stay + near_in[half:].astype(f32)
-    return call(last_kernel, (shape(half, bf16), jax.ShapeDtypeStruct(text_emb.shape, bf16)), 1, spot, stay, crossed,
-                far_stay, far_cross)
+    near_stay, near_cross, _ = lax.optimization_barrier((near_stay, near_cross, far_cross))
+    far_cross = hop(far_cross, *far, across=True)
+    near_cross = hop(near_cross, *near, across=True)
+    near_stay = hop(near_stay, *near)
+    return call(last_kernel, (shape(half, bf16), jax.ShapeDtypeStruct(text_emb.shape, bf16)), 1, spot, own_stay, crossed,
+                near_stay, near_cross, far_stay, far_cross)
 
 
 def partner(block, axis, distance):

time: 54.5 us -> 52.4 us (0.961)
  waiting for transfers between devices: 20.9 us -> 13.5 us
  starting transfers between devices: 16.6 us -> 20.1 us
  Pallas kernels: 10 us -> 11.9 us
  local copies, waits for them, and re-layouts: 3.19 us -> 2.5 us
    ppermute x11 -> x12, waiting for transfers between devices: 20.9 us -> 13.5 us  [hop(): return lax.ppermute(block, ('row', 'col'), route)]
    ppermute x11 -> x12, starting transfers between devices: 15 us -> 18 us  [hop(): return lax.ppermute(block, ('row', 'col'), route)]
    pallas_call x0 -> x1, Pallas kernels: none -> 2.5 us  [pair_body(): pl.pallas_call(first_kernel, out_shape=(sent, sent), in_specs=[pl.BlockSp...]
    unnamed x8 -> x10, local copies, waits for them, and re-layouts: 3.19 us -> 2.5 us
    pallas_call x6 -> x5, Pallas kernels: 10 us -> 9.42 us  [call(): pl.pallas_call(kernel, out_shape=out_shape, in_specs=[pl.BlockSpec(memory...]
  transfers between devices with their start and end apart: 20 -> 21, of which waited for: 7 -> 6; matrix products, arithmetic and copies ran while one was open for 0% -> 0% of each run, Pallas kernels for 12% -> 12%
where the time goes in v3:
time: 52.4 us; the launch traced here: 52.1 us
  starting transfers between devices  20.1 us (38%)
  waiting for transfers between devices  13.5 us (26%)
  Pallas kernels  11.9 us (23%)
  between operations  3.37 us (6%)
  local copies, waits for them, and re-layouts  2.5 us (5%)
  other arithmetic  0.7 us (1%)
    ppermute x12, starting transfers between devices, hop(): return lax.ppermute(block, ('row', 'col'), route)  18 us
    ppermute x12, waiting for transfers between devices, hop(): return lax.ppermute(block, ('row', 'col'), route)  13.5 us
    pallas_call x5, Pallas kernels, call(): pl.pallas_call(kernel, out_shape=out_shape, in_specs=[pl.BlockSpec(memory...  9.42 us
    unnamed x10, local copies, waits for them, and re-layouts  2.5 us
    pallas_call x1, Pallas kernels, pair_body(): pl.pallas_call(first_kernel, out_shape=(sent, sent), in_specs=[pl.BlockSp...  2.5 us
    ppermute x9, starting transfers between devices, swap(): return lax.ppermute(block, 'row', [(0, 1), (1, 0)])  2.05 us
  transfers between devices with their start and end apart: 21, of which 6 were waited for; matrix products, arithmetic and copies ran while one was open for 0% of the time, Pallas kernels for 12%

profile of v3, /device:TPU:0, one launch (start us, length us, event | category | flops | bytes accessed | tf_op | source)
XLA Modules:
  0.0 52.1 jit_solution(14293205561626172548)
XLA Ops:
  0.6 0.6 %pad_add_fusion.spot_ref = s32[2]{0:T(128)} fusion(s32[1]{0:T(128)} %bitcast.1, s32[1]{0:T(128)} %bitcast), kind=kLoop, calls=%fused_computation.2 | loop fusion | flops 2 | bytes 16 | tf_op jit(solution)/shard_map/stack | solution.py:256
  1.3 2.5 %shard_map.95 = (bf16[88,1152]{1,0:T(8,128)(2,1)}, bf16[88,1152]{1,0:T(8,128)(2,1)}) custom-call(s32[2]{0:T(128)} %pad_add_fusion.spot_ref, bf16[80,1152]{1,0:T(8,128)(2,1)} %image_ref.1, bf16[160,576]{1,0:T(8,128)(2,1)} %text_ref.1, s32[1,80]{1,0:T(1,128)} %bitcast.5, s32[1,160]{1,0:T(1,128)} %bitcast.4), custom_call_target="tpu_custom_call" | custom-call | tf_op jit(solution)/shard_map/pallas_call | solution.py:266
  3.8 0.5 %collective-permute-start = (bf16[88,1152]{1,0:T(8,128)(2,1)}, bf16[88,1152]{1,0:T(8,128)(2,1)S(1)}, u32[]{:S(2)}, u32[]{:S(2)}) collective-permute-start(bf16[88,1152]{1,0:T(8,128)(2,1)} %get-tuple-element.24.refs_7_.refs_3_), channel_id=1, source_target_pairs={{0,16},{16,0},{1,17},{17,1},{2,18},{18,2},{3,19},{19,3},{4,20},{20... | collective-permute-start | bytes 608264 | tf_op jit(solution)/shard_map/ppermute | solution.py:23
  4.3 3.7 %collective-permute-start.3 = (bf16[88,1152]{1,0:T(8,128)(2,1)}, bf16[88,1152]{1,0:T(8,128)(2,1)S(1)}, u32[]{:S(2)}, u32[]{:S(2)}) collective-permute-start(bf16[88,1152]{1,0:T(8,128)(2,1)} %get-tuple-element.23.refs_0_), channel_id=1, source_target_pairs={{0,8},{1,9},{2,10},{3,11},{4,12},{5,13},{6,14},{7,15},{8,0},{9,1},... | collective-permute-start | bytes 608264 | tf_op jit(solution)/shard_map/ppermute | solution.py:19
  7.9 1.5 %collective-permute-start.1 = (bf16[88,1152]{1,0:T(8,128)(2,1)}, bf16[88,1152]{1,0:T(8,128)(2,1)S(1)}, u32[]{:S(2)}, u32[]{:S(2)}) collective-permute-start(bf16[88,1152]{1,0:T(8,128)(2,1)} %get-tuple-element.23.refs_0_), channel_id=1, source_target_pairs={{0,1},{1,0},{2,3},{3,2},{4,5},{5,4},{6,7},{7,6},{8,9},{9,8},{10,11... | collective-permute-start | bytes 608264 | tf_op jit(solution)/shard_map/ppermute | solution.py:19
  9.4 0.0 collective-permute-done.refs_1_
  9.4 0.3 collective-permute-start.4
  9.8 1.2 %collective-permute-start.2 = (bf16[88,1152]{1,0:T(8,128)(2,1)S(1)}, bf16[88,1152]{1,0:T(8,128)(2,1)S(1)}, u32[]{:S(2)}, u32[]{:S(2)}) collective-permute-start(bf16[88,1152]{1,0:T(8,128)(2,1)S(1)} %collective-permute-done.refs_1_), channel_id=1, source_target_pairs={{0,1},{1,0},{2,3},{3,2},{4,5},{5,4},{6,7},{7,6},{8,9},{9,8},{10,11... | collective-permute-start | bytes 608264 | tf_op jit(solution)/shard_map/ppermute | solution.py:19
  11.0 0.0 collective-permute-start.7
  11.0 2.7 %collective-permute-done.3.refs_4_ = bf16[88,1152]{1,0:T(8,128)(2,1)S(1)} collective-permute-done((bf16[88,1152]{1,0:T(8,128)(2,1)}, bf16[88,1152]{1,0:T(8,128)(2,1)S(1)}, u32[]{:S(2)}, u32[]{:S(2)}) %collective-permute-start.3) | collective-permute-done | bytes 202784 | tf_op jit(solution)/shard_map/ppermute | solution.py:19
  13.7 0.0 collective-permute-start.10
  13.7 0.1 collective-permute-done.1.refs_2_
  13.9 0.4 collective-permute-start.8
  14.3 4.0 %collective-permute-done.4.refs_5_ = bf16[88,1152]{1,0:T(8,128)(2,1)S(1)} collective-permute-done((bf16[88,1152]{1,0:T(8,128)(2,1)S(1)}, bf16[88,1152]{1,0:T(8,128)(2,1)S(1)}, u32[]{:S(2)}, u32[]{:S(2)}) %collective-permute-start.4) | collective-permute-done | bytes 202784 | tf_op jit(solution)/shard_map/ppermute | solution.py:19
  18.2 0.0 collective-permute-start.11
  18.2 0.0 collective-permute-done.2.refs_3_
  18.2 0.5 collective-permute-start.9
  18.8 0.0 collective-permute-done.7.refs_6_.refs_2_
  18.8 1.1 %collective-permute-start.5 = (bf16[88,1152]{1,0:T(8,128)(2,1)S(1)}, bf16[88,1152]{1,0:T(8,128)(2,1)S(1)}, u32[]{:S(2)}, u32[]{:S(2)}) collective-permute-start(bf16[88,1152]{1,0:T(8,128)(2,1)S(1)} %collective-permute-done.3.refs_4_), channel_id=1, source_target_pairs={{0,1},{1,0},{2,3},{3,2},{4,5},{5,4},{6,7},{7,6},{8,9},{9,8},{10,11... | collective-permute-start | bytes 608264 | tf_op jit(solution)/shard_map/ppermute | solution.py:19
  19.9 0.0 collective-permute-done.10.refs_10_.refs_6_
  19.9 0.9 %collective-permute-start.6 = (bf16[88,1152]{1,0:T(8,128)(2,1)S(1)}, bf16[88,1152]{1,0:T(8,128)(2,1)S(1)}, u32[]{:S(2)}, u32[]{:S(2)}) collective-permute-start(bf16[88,1152]{1,0:T(8,128)(2,1)S(1)} %collective-permute-done.4.refs_5_), channel_id=1, source_target_pairs={{0,1},{1,0},{2,3},{3,2},{4,5},{5,4},{6,7},{7,6},{8,9},{9,8},{10,11... | collective-permute-start | bytes 608264 | tf_op jit(solution)/shard_map/ppermute | solution.py:19
  23.4 0.0 collective-permute-done.8.refs_8_.refs_4_
  23.4 0.0 copy-start
  23.4 0.9 %copy-done = bf16[88,1152]{1,0:T(8,128)(2,1)S(1)} copy-done((bf16[88,1152]{1,0:T(8,128)(2,1)S(1)}, bf16[88,1152]{1,0:T(8,128)(2,1)}, u32[]{:S(2)}) %copy-start) | copy-done | bytes 202776
  24.3 0.9 %copy-done.2 = bf16[88,1152]{1,0:T(8,128)(2,1)S(1)} copy-done((bf16[88,1152]{1,0:T(8,128)(2,1)S(1)}, bf16[88,1152]{1,0:T(8,128)(2,1)}, u32[]{:S(2)}) %copy-start.2) | copy-done | bytes 202776
  25.3 0.6 %copy-done.4 = s32[2]{0:T(128)S(1)} copy-done((s32[2]{0:T(128)S(1)}, s32[2]{0:T(128)}, u32[]{:S(2)}) %copy-start.4) | copy-done | bytes 32
  25.9 2.7 %shard_map.96 = (bf16[480,1152]{1,0:T(8,128)(2,1)S(1)}, bf16[480,1152]{1,0:T(8,128)(2,1)S(1)}, f32[480,1152]{1,0:T(8,128)S(1)}) custom-call(s32[2]{0:T(128)S(1)} %copy-done.4, f32[1]{0:T(128)S(6)} %copy.11.scale_ref, f32[1]{0:T(128)S(6)} %copy.12.bias_ref, f32[1]{0:T(128)S(6)} %copy.13.grad_ref, s32[1]{0:T(128)S(6)} %copy.10.sample_ref, ...), custom_call_target="tpu_custom_call" | custom-call | flops 1061683200 | bytes 6856728 | tf_op jit(solution)/shard_map/pallas_call | solution.py:239
  28.6 0.0 collective-permute-done.5.refs_0_
  28.6 0.1 collective-permute-start.12
  28.7 0.5 collective-permute-start.13
  29.2 1.5 %shard_map.97 = (bf16[160,1152]{1,0:T(8,128)(2,1)S(1)}, f32[160,1152]{1,0:T(8,128)S(1)}) custom-call(s32[2]{0:T(128)S(1)} %copy-done.4, f32[1]{0:T(128)S(6)} %copy.11.scale_ref, f32[1]{0:T(128)S(6)} %copy.12.bias_ref, f32[1]{0:T(128)S(6)} %copy.13.grad_ref, s32[1]{0:T(128)S(6)} %copy.10.sample_ref, bf16[88,1152]{1,0:T(8,128)(2,1)S(1)} %collective-permute-done.5.refs_0_, ...), custom_call_target="tpu_custom_call" | custom-call | flops 353894400 | bytes 3833880 | tf_op jit(solution)/shard_map/pallas_call | solution.py:239
  30.7 0.0 copy-start.1
  30.7 0.0 collective-permute-done.12.refs_2_.refs_6_
  30.8 1.4 %shard_map.98 = (bf16[160,1152]{1,0:T(8,128)(2,1)S(1)}, bf16[80,1152]{1,0:T(8,128)(2,1)S(1)}, bf16[80,1152]{1,0:T(8,128)(2,1)S(1)}) custom-call(s32[2]{0:T(128)S(1)} %copy-done.4, f32[1]{0:T(128)S(6)} %copy.11.scale_ref, f32[1]{0:T(128)S(6)} %copy.12.bias_ref, f32[1]{0:T(128)S(6)} %copy.13.grad_ref, s32[1]{0:T(128)S(6)} %copy.10.sample_ref, ...), custom_call_target="tpu_custom_call" | custom-call | flops 117964800 | bytes 2654232 | tf_op jit(solution)/shard_map/pallas_call | solution.py:239
  32.2 1.2 %collective-permute-start.15 = (bf16[80,1152]{1,0:T(8,128)(2,1)S(1)}, bf16[80,1152]{1,0:T(8,128)(2,1)S(1)}, u32[]{:S(2)}, u32[]{:S(2)}) collective-permute-start(bf16[80,1152]{1,0:T(8,128)(2,1)S(1)} %get-tuple-element.39), channel_id=1, source_target_pairs={{0,1},{1,0},{2,3},{3,2},{4,5},{5,4},{6,7},{7,6},{8,9},{9,8},{10,11... | collective-permute-start | bytes 552968 | tf_op jit(solution)/shard_map/ppermute | solution.py:19
  33.4 0.9 %collective-permute-start.18 = (bf16[80,1152]{1,0:T(8,128)(2,1)S(1)}, bf16[80,1152]{1,0:T(8,128)(2,1)S(1)}, u32[]{:S(2)}, u32[]{:S(2)}) collective-permute-start(bf16[80,1152]{1,0:T(8,128)(2,1)S(1)} %get-tuple-element.43), channel_id=1, source_target_pairs={{0,1},{1,0},{2,3},{3,2},{4,5},{5,4},{6,7},{7,6},{8,9},{9,8},{10,11... | collective-permute-start | bytes 552968 | tf_op jit(solution)/shard_map/ppermute | solution.py:19
  34.3 2.2 %shard_map.99 = (f32[80,1152]{1,0:T(8,128)S(1)}, f32[80,1152]{1,0:T(8,128)S(1)}, bf16[80,1152]{1,0:T(8,128)(2,1)S(1)}, bf16[80,1152]{1,0:T(8,128)(2,1)S(1)}, f32...) custom-call(s32[2]{0:T(128)S(1)} %copy-done.4, f32[1]{0:T(128)S(6)} %copy.11.scale_ref, f32[1]{0:T(128)S(6)} %copy.12.bias_ref, ...), custom_call_target="tpu_custom_call" | custom-call | flops 353894400 | bytes 7151640 | tf_op jit(solution)/shard_map/pallas_call | solution.py:239
  36.5 0.1 collective-permute-start.14
  36.6 1.2 %collective-permute-done.15 = bf16[80,1152]{1,0:T(8,128)(2,1)S(1)} collective-permute-done((bf16[80,1152]{1,0:T(8,128)(2,1)S(1)}, bf16[80,1152]{1,0:T(8,128)(2,1)S(1)}, u32[]{:S(2)}, u32[]{:S(2)}) %collective-permute-start.15) | collective-permute-done | bytes 184352 | tf_op jit(solution)/shard_map/ppermute | solution.py:19
  37.8 0.6 %collective-permute-start.20 = (bf16[80,1152]{1,0:T(8,128)(2,1)S(1)}, bf16[80,1152]{1,0:T(8,128)(2,1)S(1)}, u32[]{:S(2)}, u32[]{:S(2)}) collective-permute-start(bf16[80,1152]{1,0:T(8,128)(2,1)S(1)} %add_convert_fusion.1), channel_id=1, source_target_pairs={{0,24},{1,25},{2,26},{3,27},{4,28},{5,29},{6,30},{7,31},{8,16},{9,... | collective-permute-start | bytes 552968 | tf_op jit(solution)/shard_map/ppermute | solution.py:19
  38.4 1.5 %collective-permute-start.16 = (bf16[80,1152]{1,0:T(8,128)(2,1)S(1)}, bf16[80,1152]{1,0:T(8,128)(2,1)S(1)}, u32[]{:S(2)}, u32[]{:S(2)}) collective-permute-start(bf16[80,1152]{1,0:T(8,128)(2,1)S(1)} %get-tuple-element.40), channel_id=1, source_target_pairs={{0,1},{1,0},{2,3},{3,2},{4,5},{5,4},{6,7},{7,6},{8,9},{9,8},{10,11... | collective-permute-start | bytes 552968 | tf_op jit(solution)/shard_map/ppermute | solution.py:19
  39.9 2.0 %collective-permute-start.17 = (bf16[80,1152]{1,0:T(8,128)(2,1)S(1)}, bf16[80,1152]{1,0:T(8,128)(2,1)S(1)}, u32[]{:S(2)}, u32[]{:S(2)}) collective-permute-start(bf16[80,1152]{1,0:T(8,128)(2,1)S(1)} %get-tuple-element.41), channel_id=1, source_target_pairs={{0,17},{1,16},{2,19},{3,18},{4,21},{5,20},{6,23},{7,22},{8,25},{9,... | collective-permute-start | bytes 552968 | tf_op jit(solution)/shard_map/ppermute | solution.py:19
  42.0 0.0 collective-permute-done.18
  42.0 3.1 %collective-permute-start.19 = (bf16[80,1152]{1,0:T(8,128)(2,1)S(1)}, bf16[80,1152]{1,0:T(8,128)(2,1)S(1)}, u32[]{:S(2)}, u32[]{:S(2)}) collective-permute-start(bf16[80,1152]{1,0:T(8,128)(2,1)S(1)} %add_convert_fusion), channel_id=1, source_target_pairs={{0,8},{1,9},{2,10},{3,11},{4,12},{5,13},{6,14},{7,15},{8,0},{9,1},... | collective-permute-start | bytes 552968 | tf_op jit(solution)/shard_map/ppermute | solution.py:19
  45.1 1.1 %collective-permute-done.17.near_cross_ref = bf16[80,1152]{1,0:T(8,128)(2,1)S(1)} collective-permute-done((bf16[80,1152]{1,0:T(8,128)(2,1)S(1)}, bf16[80,1152]{1,0:T(8,128)(2,1)S(1)}, u32[]{:S(2)}, u32[]{:S(2)}) %collective-permute-start.17) | collective-permute-done | bytes 184352 | tf_op jit(solution)/shard_map/ppermute | solution.py:19
  46.2 0.0 collective-permute-done.20.far_cross_ref
  46.2 4.4 %collective-permute-done.19.far_stay_ref = bf16[80,1152]{1,0:T(8,128)(2,1)S(1)} collective-permute-done((bf16[80,1152]{1,0:T(8,128)(2,1)S(1)}, bf16[80,1152]{1,0:T(8,128)(2,1)S(1)}, u32[]{:S(2)}, u32[]{:S(2)}) %collective-permute-start.19) | collective-permute-done | bytes 184352 | tf_op jit(solution)/shard_map/ppermute | solution.py:19
  50.6 1.5 %shard_map.100 = (bf16[80,1152]{1,0:T(8,128)(2,1)}, bf16[160,576]{1,0:T(8,128)(2,1)}) custom-call(s32[2]{0:T(128)S(1)} %copy-done.4, f32[80,1152]{1,0:T(8,128)S(1)} %get-tuple-element.34.stay_ref, f32[80,1152]{1,0:T(8,128)S(1)} %collective-permute-done.14.crossed_ref, bf16[80,1152]{1,0:T(8,128)(2,1)S(1)} %collective-permute-done.16.near_stay_ref, ...), custom_call_target="tpu_custom_call" | custom-call | bytes 1843208 | tf_op jit(solution)/shard_map/pallas_call | solution.py:239
  (13 shorter events, 0.1 us)
Async XLA Ops:
  3.8 5.7 %collective-permute-start = (bf16[88,1152]{1,0:T(8,128)(2,1)}, bf16[88,1152]{1,0:T(8,128)(2,1)S(1)}, u32[]{:S(2)}, u32[]{:S(2)}) collective-permute-start(bf16[88,1152]{1,0:T(8,128)(2,1)} %get-tuple-element.24.refs_7_.refs_3_), channel_id=1, source_target_pairs={{0,16},{16,0},{1,17},{17,1},{2,18},{18,2},{3,19},{19,3},{4,20},{20... | collective-permute-start | bytes 608264 | tf_op jit(solution)/shard_map/ppermute | solution.py:23
  4.3 9.5 %collective-permute-start.3 = (bf16[88,1152]{1,0:T(8,128)(2,1)}, bf16[88,1152]{1,0:T(8,128)(2,1)S(1)}, u32[]{:S(2)}, u32[]{:S(2)}) collective-permute-start(bf16[88,1152]{1,0:T(8,128)(2,1)} %get-tuple-element.23.refs_0_), channel_id=1, source_target_pairs={{0,8},{1,9},{2,10},{3,11},{4,12},{5,13},{6,14},{7,15},{8,0},{9,1},... | collective-permute-start | bytes 608264 | tf_op jit(solution)/shard_map/ppermute | solution.py:19
  7.9 5.9 %collective-permute-start.1 = (bf16[88,1152]{1,0:T(8,128)(2,1)}, bf16[88,1152]{1,0:T(8,128)(2,1)S(1)}, u32[]{:S(2)}, u32[]{:S(2)}) collective-permute-start(bf16[88,1152]{1,0:T(8,128)(2,1)} %get-tuple-element.23.refs_0_), channel_id=1, source_target_pairs={{0,1},{1,0},{2,3},{3,2},{4,5},{5,4},{6,7},{7,6},{8,9},{9,8},{10,11... | collective-permute-start | bytes 608264 | tf_op jit(solution)/shard_map/ppermute | solution.py:19
  9.4 8.8 %collective-permute-start.4 = (bf16[88,1152]{1,0:T(8,128)(2,1)S(1)}, bf16[88,1152]{1,0:T(8,128)(2,1)S(1)}, u32[]{:S(2)}, u32[]{:S(2)}) collective-permute-start(bf16[88,1152]{1,0:T(8,128)(2,1)S(1)} %collective-permute-done.refs_1_), channel_id=1, source_target_pairs={{0,8},{1,9},{2,10},{3,11},{4,12},{5,13},{6,14},{7,15},{8,0},{9,1},... | collective-permute-start | bytes 608264 | tf_op jit(solution)/shard_map/ppermute | solution.py:19
  9.8 8.5 %collective-permute-start.2 = (bf16[88,1152]{1,0:T(8,128)(2,1)S(1)}, bf16[88,1152]{1,0:T(8,128)(2,1)S(1)}, u32[]{:S(2)}, u32[]{:S(2)}) collective-permute-start(bf16[88,1152]{1,0:T(8,128)(2,1)S(1)} %collective-permute-done.refs_1_), channel_id=1, source_target_pairs={{0,1},{1,0},{2,3},{3,2},{4,5},{5,4},{6,7},{7,6},{8,9},{9,8},{10,11... | collective-permute-start | bytes 608264 | tf_op jit(solution)/shard_map/ppermute | solution.py:19
  11.0 7.7 %collective-permute-start.7 = (bf16[88,1152]{1,0:T(8,128)(2,1)}, bf16[88,1152]{1,0:T(8,128)(2,1)S(1)}, u32[]{:S(2)}, u32[]{:S(2)}) collective-permute-start(bf16[88,1152]{1,0:T(8,128)(2,1)} %get-tuple-element.23.refs_0_), channel_id=1, source_target_pairs={{0,16},{16,0},{1,17},{17,1},{2,18},{18,2},{3,19},{19,3},{4,20},{20... | collective-permute-start | bytes 608264 | tf_op jit(solution)/shard_map/ppermute | solution.py:23
  13.7 6.1 %collective-permute-start.10 = (bf16[88,1152]{1,0:T(8,128)(2,1)S(1)}, bf16[88,1152]{1,0:T(8,128)(2,1)S(1)}, u32[]{:S(2)}, u32[]{:S(2)}) collective-permute-start(bf16[88,1152]{1,0:T(8,128)(2,1)S(1)} %collective-permute-done.3.refs_4_), channel_id=1, source_target_pairs={{0,16},{16,0},{1,17},{17,1},{2,18},{18,2},{3,19},{19,3},{4,20},{20... | collective-permute-start | bytes 608264 | tf_op jit(solution)/shard_map/ppermute | solution.py:23
  13.9 9.5 %collective-permute-start.8 = (bf16[88,1152]{1,0:T(8,128)(2,1)S(1)}, bf16[88,1152]{1,0:T(8,128)(2,1)S(1)}, u32[]{:S(2)}, u32[]{:S(2)}) collective-permute-start(bf16[88,1152]{1,0:T(8,128)(2,1)S(1)} %collective-permute-done.1.refs_2_), channel_id=1, source_target_pairs={{0,16},{16,0},{1,17},{17,1},{2,18},{18,2},{3,19},{19,3},{4,20},{20... | collective-permute-start | bytes 608264 | tf_op jit(solution)/shard_map/ppermute | solution.py:23
  18.2 5.2 %collective-permute-start.11 = (bf16[88,1152]{1,0:T(8,128)(2,1)S(1)}, bf16[88,1152]{1,0:T(8,128)(2,1)S(1)}, u32[]{:S(2)}, u32[]{:S(2)}) collective-permute-start(bf16[88,1152]{1,0:T(8,128)(2,1)S(1)} %collective-permute-done.4.refs_5_), channel_id=1, source_target_pairs={{0,16},{16,0},{1,17},{17,1},{2,18},{18,2},{3,19},{19,3},{4,20},{20... | collective-permute-start | bytes 608264 | tf_op jit(solution)/shard_map/ppermute | solution.py:23
  18.2 5.2 %collective-permute-start.9 = (bf16[88,1152]{1,0:T(8,128)(2,1)S(1)}, bf16[88,1152]{1,0:T(8,128)(2,1)S(1)}, u32[]{:S(2)}, u32[]{:S(2)}) collective-permute-start(bf16[88,1152]{1,0:T(8,128)(2,1)S(1)} %collective-permute-done.2.refs_3_), channel_id=1, source_target_pairs={{0,16},{16,0},{1,17},{17,1},{2,18},{18,2},{3,19},{19,3},{4,20},{20... | collective-permute-start | bytes 608264 | tf_op jit(solution)/shard_map/ppermute | solution.py:23
  18.8 9.9 %collective-permute-start.5 = (bf16[88,1152]{1,0:T(8,128)(2,1)S(1)}, bf16[88,1152]{1,0:T(8,128)(2,1)S(1)}, u32[]{:S(2)}, u32[]{:S(2)}) collective-permute-start(bf16[88,1152]{1,0:T(8,128)(2,1)S(1)} %collective-permute-done.3.refs_4_), channel_id=1, source_target_pairs={{0,1},{1,0},{2,3},{3,2},{4,5},{5,4},{6,7},{7,6},{8,9},{9,8},{10,11... | collective-permute-start | bytes 608264 | tf_op jit(solution)/shard_map/ppermute | solution.py:19
  19.9 8.8 %collective-permute-start.6 = (bf16[88,1152]{1,0:T(8,128)(2,1)S(1)}, bf16[88,1152]{1,0:T(8,128)(2,1)S(1)}, u32[]{:S(2)}, u32[]{:S(2)}) collective-permute-start(bf16[88,1152]{1,0:T(8,128)(2,1)S(1)} %collective-permute-done.4.refs_5_), channel_id=1, source_target_pairs={{0,1},{1,0},{2,3},{3,2},{4,5},{5,4},{6,7},{7,6},{8,9},{9,8},{10,11... | collective-permute-start | bytes 608264 | tf_op jit(solution)/shard_map/ppermute | solution.py:19
  23.4 0.9 %copy-start = (bf16[88,1152]{1,0:T(8,128)(2,1)S(1)}, bf16[88,1152]{1,0:T(8,128)(2,1)}, u32[]{:S(2)}) copy-start(bf16[88,1152]{1,0:T(8,128)(2,1)} %get-tuple-element.23.refs_0_) | copy-start | bytes 608260
  24.3 0.9 %copy-start.2 = (bf16[88,1152]{1,0:T(8,128)(2,1)S(1)}, bf16[88,1152]{1,0:T(8,128)(2,1)}, u32[]{:S(2)}) copy-start(bf16[88,1152]{1,0:T(8,128)(2,1)} %get-tuple-element.24.refs_7_.refs_3_) | copy-start | bytes 608260
  25.3 0.6 %copy-start.4 = (s32[2]{0:T(128)S(1)}, s32[2]{0:T(128)}, u32[]{:S(2)}) copy-start(s32[2]{0:T(128)} %pad_add_fusion.spot_ref) | copy-start | bytes 28
  25.9 3.3 %copy-start.3 = (bf16[88,1152]{1,0:T(8,128)(2,1)S(1)}, bf16[88,1152]{1,0:T(8,128)(2,1)}, u32[]{:S(2)}) copy-start(bf16[88,1152]{1,0:T(8,128)(2,1)} %get-tuple-element.24.refs_7_.refs_3_) | copy-start | bytes 608260
  28.6 2.1 %collective-permute-start.12 = (bf16[88,1152]{1,0:T(8,128)(2,1)S(1)}, bf16[88,1152]{1,0:T(8,128)(2,1)S(1)}, u32[]{:S(2)}, u32[]{:S(2)}) collective-permute-start(bf16[88,1152]{1,0:T(8,128)(2,1)S(1)} %collective-permute-done.5.refs_0_), channel_id=1, source_target_pairs={{0,16},{16,0},{1,17},{17,1},{2,18},{18,2},{3,19},{19,3},{4,20},{20... | collective-permute-start | bytes 608264 | tf_op jit(solution)/shard_map/ppermute | solution.py:23
  28.7 2.0 %collective-permute-start.13 = (bf16[88,1152]{1,0:T(8,128)(2,1)S(1)}, bf16[88,1152]{1,0:T(8,128)(2,1)S(1)}, u32[]{:S(2)}, u32[]{:S(2)}) collective-permute-start(bf16[88,1152]{1,0:T(8,128)(2,1)S(1)} %collective-permute-done.6.refs_1_), channel_id=1, source_target_pairs={{0,16},{16,0},{1,17},{17,1},{2,18},{18,2},{3,19},{19,3},{4,20},{20... | collective-permute-start | bytes 608264 | tf_op jit(solution)/shard_map/ppermute | solution.py:23
  30.7 3.6 %copy-start.1 = (bf16[88,1152]{1,0:T(8,128)(2,1)S(1)}, bf16[88,1152]{1,0:T(8,128)(2,1)}, u32[]{:S(2)}) copy-start(bf16[88,1152]{1,0:T(8,128)(2,1)} %get-tuple-element.23.refs_0_) | copy-start | bytes 608260
  32.2 5.6 %collective-permute-start.15 = (bf16[80,1152]{1,0:T(8,128)(2,1)S(1)}, bf16[80,1152]{1,0:T(8,128)(2,1)S(1)}, u32[]{:S(2)}, u32[]{:S(2)}) collective-permute-start(bf16[80,1152]{1,0:T(8,128)(2,1)S(1)} %get-tuple-element.39), channel_id=1, source_target_pairs={{0,1},{1,0},{2,3},{3,2},{4,5},{5,4},{6,7},{7,6},{8,9},{9,8},{10,11... | collective-permute-start | bytes 552968 | tf_op jit(solution)/shard_map/ppermute | solution.py:19
  33.4 8.6 %collective-permute-start.18 = (bf16[80,1152]{1,0:T(8,128)(2,1)S(1)}, bf16[80,1152]{1,0:T(8,128)(2,1)S(1)}, u32[]{:S(2)}, u32[]{:S(2)}) collective-permute-start(bf16[80,1152]{1,0:T(8,128)(2,1)S(1)} %get-tuple-element.43), channel_id=1, source_target_pairs={{0,1},{1,0},{2,3},{3,2},{4,5},{5,4},{6,7},{7,6},{8,9},{9,8},{10,11... | collective-permute-start | bytes 552968 | tf_op jit(solution)/shard_map/ppermute | solution.py:19
  36.5 8.5 %collective-permute-start.14 = (f32[80,1152]{1,0:T(8,128)S(1)}, f32[80,1152]{1,0:T(8,128)S(1)}, u32[]{:S(2)}, u32[]{:S(2)}) collective-permute-start(f32[80,1152]{1,0:T(8,128)S(1)} %get-tuple-element.35), channel_id=1, source_target_pairs={{0,16},{16,0},{1,17},{17,1},{2,18},{18,2},{3,19},{19,3},{4,20},{20... | collective-permute-start | bytes 1105928 | tf_op jit(solution)/shard_map/ppermute | solution.py:23
  37.8 8.3 %collective-permute-start.20 = (bf16[80,1152]{1,0:T(8,128)(2,1)S(1)}, bf16[80,1152]{1,0:T(8,128)(2,1)S(1)}, u32[]{:S(2)}, u32[]{:S(2)}) collective-permute-start(bf16[80,1152]{1,0:T(8,128)(2,1)S(1)} %add_convert_fusion.1), channel_id=1, source_target_pairs={{0,24},{1,25},{2,26},{3,27},{4,28},{5,29},{6,30},{7,31},{8,16},{9,... | collective-permute-start | bytes 552968 | tf_op jit(solution)/shard_map/ppermute | solution.py:19
  38.4 6.6 %collective-permute-start.16 = (bf16[80,1152]{1,0:T(8,128)(2,1)S(1)}, bf16[80,1152]{1,0:T(8,128)(2,1)S(1)}, u32[]{:S(2)}, u32[]{:S(2)}) collective-permute-start(bf16[80,1152]{1,0:T(8,128)(2,1)S(1)} %get-tuple-element.40), channel_id=1, source_target_pairs={{0,1},{1,0},{2,3},{3,2},{4,5},{5,4},{6,7},{7,6},{8,9},{9,8},{10,11... | collective-permute-start | bytes 552968 | tf_op jit(solution)/shard_map/ppermute | solution.py:19
  39.9 6.3 %collective-permute-start.17 = (bf16[80,1152]{1,0:T(8,128)(2,1)S(1)}, bf16[80,1152]{1,0:T(8,128)(2,1)S(1)}, u32[]{:S(2)}, u32[]{:S(2)}) collective-permute-start(bf16[80,1152]{1,0:T(8,128)(2,1)S(1)} %get-tuple-element.41), channel_id=1, source_target_pairs={{0,17},{1,16},{2,19},{3,18},{4,21},{5,20},{6,23},{7,22},{8,25},{9,... | collective-permute-start | bytes 552968 | tf_op jit(solution)/shard_map/ppermute | solution.py:19
  42.0 8.5 %collective-permute-start.19 = (bf16[80,1152]{1,0:T(8,128)(2,1)S(1)}, bf16[80,1152]{1,0:T(8,128)(2,1)S(1)}, u32[]{:S(2)}, u32[]{:S(2)}) collective-permute-start(bf16[80,1152]{1,0:T(8,128)(2,1)S(1)} %add_convert_fusion), channel_id=1, source_target_pairs={{0,8},{1,9},{2,10},{3,11},{4,12},{5,13},{6,14},{7,15},{8,0},{9,1},... | collective-permute-start | bytes 552968 | tf_op jit(solution)/shard_map/ppermute | solution.py:19

commit v4 on v3

--- a/solution.py
+++ b/solution.py
@@ -114,8 +114,8 @@
     return at + first + jnp.where(at >= half, jump, 0)
 
 
-def coefficients_of(cols, spot_ref, scale_ref, bias_ref, grad_ref, sample_ref, mine, others, my_sets, other_sets):
-    row, col = spot_ref[0], spot_ref[1]
+def coefficients_of(cols, row_ref, col_ref, scale_ref, bias_ref, grad_ref, sample_ref, mine, others, my_sets, other_sets):
+    row, col = row_ref[0], col_ref[0]
     my_texts, other_texts = row != 0, row == 0
     near, far, other_near, other_far = masks(cols, row)
     my_masks = {"own": 0, "near": near, "far": far, "both": near ^ far}
@@ -142,26 +142,26 @@
 THREE = ("own", "near", "far")
 
 
-def early_kernel(cols, spot_ref, scale_ref, bias_ref, grad_ref, sample_ref, *refs):
+def early_kernel(cols, row_ref, col_ref, scale_ref, bias_ref, grad_ref, sample_ref, *refs):
     mine_pairs, other_pairs = pairs(refs[:6]), pairs(refs[6:12])
     mine_ref, others_ref, total_ref = refs[12:]
-    texts = spot_ref[0] != 0
+    texts = row_ref[0] != 0
     size = 2 * (refs[0].shape[0] - SPARE)
     for n in range(3):
         unpack(mine_pairs[n], texts, mine_ref, n * size)
         unpack(other_pairs[n], jnp.logical_not(texts), others_ref, n * size)
     others = others_ref[...]
-    coefficient = coefficients_of(cols, spot_ref, scale_ref, bias_ref, grad_ref, sample_ref, mine_ref[...], others,
+    coefficient = coefficients_of(cols, row_ref, col_ref, scale_ref, bias_ref, grad_ref, sample_ref, mine_ref[...], others,
                                   list(zip(THREE, mine_pairs)), list(zip(THREE, other_pairs)))
     total_ref[...] = jnp.dot(coefficient, others, preferred_element_type=jnp.float32)
 
 
-def both_kernel(cols, spot_ref, scale_ref, bias_ref, grad_ref, sample_ref, *refs):
+def both_kernel(cols, row_ref, col_ref, scale_ref, bias_ref, grad_ref, sample_ref, *refs):
     mine_pair, other_pairs = refs[:2], pairs(refs[2:8])
     others_ref, mine_ref, total_ref = refs[8:]
-    unpack(mine_pair, spot_ref[0] != 0, mine_ref, 0)
+    unpack(mine_pair, row_ref[0] != 0, mine_ref, 0)
     others = others_ref[...]
-    coefficient = coefficients_of(cols, spot_ref, scale_ref, bias_ref, grad_ref, sample_ref, mine_ref[...], others,
+    coefficient = coefficients_of(cols, row_ref, col_ref, scale_ref, bias_ref, grad_ref, sample_ref, mine_ref[...], others,
                                   [("both", mine_pair)], list(zip(THREE, other_pairs)))
     total_ref[...] = jnp.dot(coefficient, others, preferred_element_type=jnp.float32)
 
@@ -182,26 +182,26 @@
         cross_ref[...] = total[half:].astype(cross_ref.dtype)
 
 
-def late_kernel(cols, spot_ref, scale_ref, bias_ref, grad_ref, sample_ref, *refs):
+def late_kernel(cols, row_ref, col_ref, scale_ref, bias_ref, grad_ref, sample_ref, *refs):
     mine_pair, other_pair = refs[:2], refs[2:4]
     mine_ref, total_ref = refs[4:6]
     others_ref, stay_ref, cross_ref = refs[6:]
-    texts = spot_ref[0] != 0
+    texts = row_ref[0] != 0
     unpack(other_pair, jnp.logical_not(texts), others_ref, 0)
     others = others_ref[...]
-    coefficient = coefficients_of(cols, spot_ref, scale_ref, bias_ref, grad_ref, sample_ref, mine_ref[...], others,
+    coefficient = coefficients_of(cols, row_ref, col_ref, scale_ref, bias_ref, grad_ref, sample_ref, mine_ref[...], others,
                                   [("both", mine_pair)], [("both", other_pair)])
     total = total_ref[...] + jnp.dot(coefficient, others, preferred_element_type=jnp.float32)
     pack_sum(total, texts, stay_ref, cross_ref)
 
 
-def rest_kernel(cols, spot_ref, scale_ref, bias_ref, grad_ref, sample_ref, *refs):
+def rest_kernel(cols, row_ref, col_ref, scale_ref, bias_ref, grad_ref, sample_ref, *refs):
     mine_pairs, other_pair = pairs(refs[:6]), refs[6:8]
     mine_ref, others_ref, total_ref = refs[8:11]
     own_stay, own_cross, near_stay, near_cross, far_stay, far_cross = refs[11:]
-    texts = spot_ref[0] != 0
+    texts = row_ref[0] != 0
     others = others_ref[...]
-    coefficient = coefficients_of(cols, spot_ref, scale_ref, bias_ref, grad_ref, sample_ref, mine_ref[...], others,
+    coefficient = coefficients_of(cols, row_ref, col_ref, scale_ref, bias_ref, grad_ref, sample_ref, mine_ref[...], others,
                                   list(zip(THREE, mine_pairs)), [("both", other_pair)])
     total = total_ref[...] + jnp.dot(coefficient, others, preferred_element_type=jnp.float32)
     size = total.shape[0] // 3
@@ -253,9 +253,9 @@
     half, width = image_emb.shape
     size = 2 * half
     cols = lax.axis_size("col")
-    spot = jnp.stack([lax.axis_index("row"), lax.axis_index("col")]).astype(jnp.int32)
+    row, col = lax.axis_index("row")[None], lax.axis_index("col")[None]
     near, far = masks(cols, None)
-    scalars = (spot, logit_scale, logit_bias, loss_grad, sample_count)
+    scalars = (row, col, logit_scale, logit_bias, loss_grad, sample_count)
 
     def shape(rows, dtype):
         return jax.ShapeDtypeStruct((rows, width), dtype)
@@ -270,7 +270,7 @@
         out_specs=(pl.BlockSpec(memory_space=pltpu.VMEM),) * 2,
         scratch_shapes=[pltpu.VMEM(a.shape, a.dtype) for a in first[1:]] + [pltpu.SemaphoreType.DMA((4,))],
         compiler_params=pltpu.CompilerParams(vmem_limit_bytes=60 * 1024 * 1024),
-    )(spot, *first)
+    )(row, *first)
     far_a = hop(own_a, *far)
     own_b = swap(give)
     far_b = hop(own_b, *far)
@@ -280,34 +280,37 @@
     both_b = hop(far_b, *near)
     mine = (own_a, own_b, near_a, near_b, far_a, far_b)
     others = (swap(own_a), give, swap(near_a), swap(near_b), swap(far_a), swap(far_b))
-    both = (both_a, both_b)
+    others, other_both_a = lax.optimization_barrier((others, swap(both_a)))
 
     pair_flops = 4 * size * size * width
     mine_rows, other_rows, early = call(
         functools.partial(early_kernel, cols), (shape(3 * size, bf16), shape(3 * size, bf16), shape(3 * size, f32)),
-        5, *scalars, *mine, *others, flops=9 * pair_flops)
-    both, early = lax.optimization_barrier((both, early))
-    other_both = (swap(both[0]), swap(both[1]))
+        6, *scalars, *mine, *others, flops=9 * pair_flops)
+    both_b, early = lax.optimization_barrier((both_b, early))
+    both = (both_a, both_b)
+    other_both = (other_both_a, swap(both_b))
     both_rows, both_early = call(
-        functools.partial(both_kernel, cols), (shape(size, bf16), shape(size, f32)), 5, *scalars, *both, *others,
+        functools.partial(both_kernel, cols), (shape(size, bf16), shape(size, f32)), 6, *scalars, *both, *others,
         other_rows, flops=3 * pair_flops)
     other_late, late_stay, late_cross = call(
-        functools.partial(late_kernel, cols), (shape(size, bf16), shape(half, bf16), shape(half, bf16)), 5, *scalars,
+        functools.partial(late_kernel, cols), (shape(size, bf16), shape(half, bf16), shape(half, bf16)), 6, *scalars,
         *both, *other_both, both_rows, both_early, flops=pair_flops)
     in_cross = hop(late_cross, *near)
     in_stay = hop(late_stay, *near)
     own_stay, own_cross, near_stay, near_cross, far_stay, far_cross = call(
         functools.partial(rest_kernel, cols),
         (shape(half, f32), shape(half, f32), shape(half, bf16), shape(half, bf16), shape(half, f32), shape(half, f32)),
-        5, *scalars, *mine, *other_both, mine_rows, other_late, early, flops=3 * pair_flops)
+        6, *scalars, *mine, *other_both, mine_rows, other_late, early, flops=3 * pair_flops)
     crossed = swap(own_cross)
     far_cross = (far_cross + in_cross.astype(f32)).astype(bf16)
-    far_stay = hop((far_stay + in_stay.astype(f32)).astype(bf16), *far)
-    near_stay, near_cross, _ = lax.optimization_barrier((near_stay, near_cross, far_cross))
+    far_stay = (far_stay + in_stay.astype(f32)).astype(bf16)
+    near_stay, _ = lax.optimization_barrier((near_stay, far_cross))
+    near_stay = hop(near_stay, *near)
+    near_cross, _, _ = lax.optimization_barrier((near_cross, far_cross, far_stay))
     far_cross = hop(far_cross, *far, across=True)
+    far_stay = hop(far_stay, *far)
     near_cross = hop(near_cross, *near, across=True)
-    near_stay = hop(near_stay, *near)
-    return call(last_kernel, (shape(half, bf16), jax.ShapeDtypeStruct(text_emb.shape, bf16)), 1, spot, own_stay, crossed,
+    return call(last_kernel, (shape(half, bf16), jax.ShapeDtypeStruct(text_emb.shape, bf16)), 1, row, own_stay, crossed,
                 near_stay, near_cross, far_stay, far_cross)
 
 

time: 52.4 us -> 48.6 us (0.927)
  Pallas kernels: 11.9 us -> 8.52 us
  starting transfers between devices: 20.1 us -> 23 us
  waiting for transfers between devices: 13.5 us -> 11.6 us
  local copies, waits for them, and re-layouts: 2.5 us -> 1.86 us
  other arithmetic: 0.7 us -> 0.08 us
    pallas_call x5, Pallas kernels: 9.42 us -> 6.68 us  [call(): pl.pallas_call(kernel, out_shape=out_shape, in_specs=[pl.BlockSpec(memory...]
    ppermute x12, starting transfers between devices: 18 us -> 20.6 us  [hop(): return lax.ppermute(block, ('row', 'col'), route)]
    ppermute x12, waiting for transfers between devices: 13.5 us -> 11.5 us  [hop(): return lax.ppermute(block, ('row', 'col'), route)]
    pallas_call x1, Pallas kernels: 2.5 us -> 1.84 us  [pair_body(): pl.pallas_call(first_kernel, out_shape=(sent, sent), in_specs=[pl.BlockSp...]
    unnamed x10 -> x8, local copies, waits for them, and re-layouts: 2.5 us -> 1.86 us
    another operation x1 -> x0, other arithmetic: 0.62 us -> none  [pair_body(): jnp.stack([lax.axis_index('row'), lax.axis_index('col')]).astype(jnp.int32)]
  transfers between devices with their start and end apart: 21 -> 21, of which waited for: 6 -> 8; matrix products, arithmetic and copies ran while one was open for 0% -> 0% of each run, Pallas kernels for 12% -> 10%
where the time goes in v4:
time: 48.6 us; the launch traced here: 48.4 us
  starting transfers between devices  23 us (47%)
  waiting for transfers between devices  11.6 us (24%)
  Pallas kernels  8.52 us (18%)
  between operations  3.36 us (7%)
  local copies, waits for them, and re-layouts  1.86 us (4%)
    ppermute x12, starting transfers between devices, hop(): return lax.ppermute(block, ('row', 'col'), route)  20.6 us
    ppermute x12, waiting for transfers between devices, hop(): return lax.ppermute(block, ('row', 'col'), route)  11.5 us
    pallas_call x5, Pallas kernels, call(): pl.pallas_call(kernel, out_shape=out_shape, in_specs=[pl.BlockSpec(memory...  6.68 us
    ppermute x9, starting transfers between devices, swap(): return lax.ppermute(block, 'row', [(0, 1), (1, 0)])  2.35 us
    unnamed x8, local copies, waits for them, and re-layouts  1.86 us
    pallas_call x1, Pallas kernels, pair_body(): pl.pallas_call(first_kernel, out_shape=(sent, sent), in_specs=[pl.BlockSp...  1.84 us
  transfers between devices with their start and end apart: 21, of which 8 were waited for; matrix products, arithmetic and copies ran while one was open for 0% of the time, Pallas kernels for 10%

profile of v4, /device:TPU:0, one launch (start us, length us, event | category | flops | bytes accessed | tf_op | source)
XLA Modules:
  0.0 48.4 jit_solution(9485906385785353858)
XLA Ops:
  0.6 1.8 %shard_map.95 = (bf16[88,1152]{1,0:T(8,128)(2,1)}, bf16[88,1152]{1,0:T(8,128)(2,1)}) custom-call(s32[1]{0:T(128)} %bitcast.spot_ref.row_ref, bf16[80,1152]{1,0:T(8,128)(2,1)} %image_ref.1, bf16[160,576]{1,0:T(8,128)(2,1)} %text_ref.1, s32[1,80]{1,0:T(1,128)} %bitcast.5, s32[1,160]{1,0:T(1,128)} %bitcast.4), custom_call_target="tpu_custom_call" | custom-call | tf_op jit(solution)/shard_map/pallas_call | solution.py:266
  2.5 0.5 %collective-permute-start = (bf16[88,1152]{1,0:T(8,128)(2,1)}, bf16[88,1152]{1,0:T(8,128)(2,1)S(1)}, u32[]{:S(2)}, u32[]{:S(2)}) collective-permute-start(bf16[88,1152]{1,0:T(8,128)(2,1)} %get-tuple-element.33.refs_7_.refs_3_), channel_id=1, source_target_pairs={{0,16},{16,0},{1,17},{17,1},{2,18},{18,2},{3,19},{19,3},{4,20},{20... | collective-permute-start | bytes 608264 | tf_op jit(solution)/shard_map/ppermute | solution.py:23
  3.0 3.7 %collective-permute-start.3 = (bf16[88,1152]{1,0:T(8,128)(2,1)}, bf16[88,1152]{1,0:T(8,128)(2,1)S(1)}, u32[]{:S(2)}, u32[]{:S(2)}) collective-permute-start(bf16[88,1152]{1,0:T(8,128)(2,1)} %get-tuple-element.29.refs_0_), channel_id=1, source_target_pairs={{0,8},{1,9},{2,10},{3,11},{4,12},{5,13},{6,14},{7,15},{8,0},{9,1},... | collective-permute-start | bytes 608264 | tf_op jit(solution)/shard_map/ppermute | solution.py:19
  6.7 0.0 collective-permute-start.5
  6.7 1.5 %collective-permute-start.1 = (bf16[88,1152]{1,0:T(8,128)(2,1)}, bf16[88,1152]{1,0:T(8,128)(2,1)S(1)}, u32[]{:S(2)}, u32[]{:S(2)}) collective-permute-start(bf16[88,1152]{1,0:T(8,128)(2,1)} %get-tuple-element.29.refs_0_), channel_id=1, source_target_pairs={{0,1},{1,0},{2,3},{3,2},{4,5},{5,4},{6,7},{7,6},{8,9},{9,8},{10,11... | collective-permute-start | bytes 608264 | tf_op jit(solution)/shard_map/ppermute | solution.py:19
  8.2 0.0 collective-permute-done.refs_1_
  8.2 1.7 %collective-permute-start.4 = (bf16[88,1152]{1,0:T(8,128)(2,1)S(1)}, bf16[88,1152]{1,0:T(8,128)(2,1)S(1)}, u32[]{:S(2)}, u32[]{:S(2)}) collective-permute-start(bf16[88,1152]{1,0:T(8,128)(2,1)S(1)} %collective-permute-done.refs_1_), channel_id=1, source_target_pairs={{0,8},{1,9},{2,10},{3,11},{4,12},{5,13},{6,14},{7,15},{8,0},{9,1},... | collective-permute-start | bytes 608264 | tf_op jit(solution)/shard_map/ppermute | solution.py:19
  9.9 0.5 %collective-permute-start.2 = (bf16[88,1152]{1,0:T(8,128)(2,1)S(1)}, bf16[88,1152]{1,0:T(8,128)(2,1)S(1)}, u32[]{:S(2)}, u32[]{:S(2)}) collective-permute-start(bf16[88,1152]{1,0:T(8,128)(2,1)S(1)} %collective-permute-done.refs_1_), channel_id=1, source_target_pairs={{0,1},{1,0},{2,3},{3,2},{4,5},{5,4},{6,7},{7,6},{8,9},{9,8},{10,11... | collective-permute-start | bytes 608264 | tf_op jit(solution)/shard_map/ppermute | solution.py:19
  10.4 1.2 %collective-permute-done.3.refs_4_ = bf16[88,1152]{1,0:T(8,128)(2,1)S(1)} collective-permute-done((bf16[88,1152]{1,0:T(8,128)(2,1)}, bf16[88,1152]{1,0:T(8,128)(2,1)S(1)}, u32[]{:S(2)}, u32[]{:S(2)}) %collective-permute-start.3) | collective-permute-done | bytes 202784 | tf_op jit(solution)/shard_map/ppermute | solution.py:19
  11.6 2.1 %collective-permute-start.10 = (bf16[88,1152]{1,0:T(8,128)(2,1)S(1)}, bf16[88,1152]{1,0:T(8,128)(2,1)S(1)}, u32[]{:S(2)}, u32[]{:S(2)}) collective-permute-start(bf16[88,1152]{1,0:T(8,128)(2,1)S(1)} %collective-permute-done.3.refs_4_), channel_id=1, source_target_pairs={{0,1},{1,0},{2,3},{3,2},{4,5},{5,4},{6,7},{7,6},{8,9},{9,8},{10,11... | collective-permute-start | bytes 608264 | tf_op jit(solution)/shard_map/ppermute | solution.py:19
  13.7 0.0 collective-permute-done.5.refs_6_.refs_2_
  13.7 0.0 collective-permute-start.8
  13.7 0.0 collective-permute-done.1.refs_2_
  13.7 0.5 %collective-permute-start.6 = (bf16[88,1152]{1,0:T(8,128)(2,1)S(1)}, bf16[88,1152]{1,0:T(8,128)(2,1)S(1)}, u32[]{:S(2)}, u32[]{:S(2)}) collective-permute-start(bf16[88,1152]{1,0:T(8,128)(2,1)S(1)} %collective-permute-done.1.refs_2_), channel_id=1, source_target_pairs={{0,16},{16,0},{1,17},{17,1},{2,18},{18,2},{3,19},{19,3},{4,20},{20... | collective-permute-start | bytes 608264 | tf_op jit(solution)/shard_map/ppermute | solution.py:23
  14.2 2.7 %collective-permute-done.4.refs_5_ = bf16[88,1152]{1,0:T(8,128)(2,1)S(1)} collective-permute-done((bf16[88,1152]{1,0:T(8,128)(2,1)S(1)}, bf16[88,1152]{1,0:T(8,128)(2,1)S(1)}, u32[]{:S(2)}, u32[]{:S(2)}) %collective-permute-start.4) | collective-permute-done | bytes 202784 | tf_op jit(solution)/shard_map/ppermute | solution.py:19
  17.0 0.0 collective-permute-start.9
  17.0 0.0 collective-permute-done.2.refs_3_
  17.0 0.5 %collective-permute-start.7 = (bf16[88,1152]{1,0:T(8,128)(2,1)S(1)}, bf16[88,1152]{1,0:T(8,128)(2,1)S(1)}, u32[]{:S(2)}, u32[]{:S(2)}) collective-permute-start(bf16[88,1152]{1,0:T(8,128)(2,1)S(1)} %collective-permute-done.2.refs_3_), channel_id=1, source_target_pairs={{0,16},{16,0},{1,17},{17,1},{2,18},{18,2},{3,19},{19,3},{4,20},{20... | collective-permute-start | bytes 608264 | tf_op jit(solution)/shard_map/ppermute | solution.py:23
  17.5 0.3 collective-permute-done.10.refs_0_
  17.8 0.0 collective-permute-start.11
  17.8 0.0 collective-permute-done.8.refs_10_.refs_6_
  17.8 1.7 %collective-permute-start.12 = (bf16[88,1152]{1,0:T(8,128)(2,1)S(1)}, bf16[88,1152]{1,0:T(8,128)(2,1)S(1)}, u32[]{:S(2)}, u32[]{:S(2)}) collective-permute-start(bf16[88,1152]{1,0:T(8,128)(2,1)S(1)} %collective-permute-done.4.refs_5_), channel_id=1, source_target_pairs={{0,1},{1,0},{2,3},{3,2},{4,5},{5,4},{6,7},{7,6},{8,9},{9,8},{10,11... | collective-permute-start | bytes 608264 | tf_op jit(solution)/shard_map/ppermute | solution.py:19
  22.1 0.0 collective-permute-done.9.refs_11_.refs_7_
  22.1 0.0 collective-permute-done.7.refs_9_.refs_5_
  22.1 0.0 copy-start
  22.1 0.9 %copy-done = bf16[88,1152]{1,0:T(8,128)(2,1)S(1)} copy-done((bf16[88,1152]{1,0:T(8,128)(2,1)S(1)}, bf16[88,1152]{1,0:T(8,128)(2,1)}, u32[]{:S(2)}) %copy-start) | copy-done | bytes 202776
  23.0 0.9 %copy-done.2 = bf16[88,1152]{1,0:T(8,128)(2,1)S(1)} copy-done((bf16[88,1152]{1,0:T(8,128)(2,1)S(1)}, bf16[88,1152]{1,0:T(8,128)(2,1)}, u32[]{:S(2)}) %copy-start.2) | copy-done | bytes 202776
  24.0 2.2 %shard_map.96 = (bf16[480,1152]{1,0:T(8,128)(2,1)S(1)}, bf16[480,1152]{1,0:T(8,128)(2,1)S(1)}, f32[480,1152]{1,0:T(8,128)S(1)}) custom-call(s32[1]{0:T(128)} %bitcast.spot_ref.row_ref, s32[1]{0:T(128)} %bitcast.1.col_ref, f32[1]{0:T(128)S(6)} %copy.11.scale_ref, f32[1]{0:T(128)S(6)} %copy.12.bias_ref, f32[1]{0:T(128)S(6)} %copy.13.grad_ref, ...), custom_call_target="tpu_custom_call" | custom-call | flops 1061683200 | bytes 6856728 | tf_op jit(solution)/shard_map/pallas_call | solution.py:239
  26.1 0.6 %collective-permute-start.13 = (bf16[88,1152]{1,0:T(8,128)(2,1)S(1)}, bf16[88,1152]{1,0:T(8,128)(2,1)S(1)}, u32[]{:S(2)}, u32[]{:S(2)}) collective-permute-start(bf16[88,1152]{1,0:T(8,128)(2,1)S(1)} %collective-permute-done.12.refs_1_), channel_id=1, source_target_pairs={{0,16},{16,0},{1,17},{17,1},{2,18},{18,2},{3,19},{19,3},{4,20},{20... | collective-permute-start | bytes 608264 | tf_op jit(solution)/shard_map/ppermute | solution.py:23
  26.7 0.9 %shard_map.97 = (bf16[160,1152]{1,0:T(8,128)(2,1)S(1)}, f32[160,1152]{1,0:T(8,128)S(1)}) custom-call(s32[1]{0:T(128)} %bitcast.spot_ref.row_ref, s32[1]{0:T(128)} %bitcast.1.col_ref, f32[1]{0:T(128)S(6)} %copy.11.scale_ref, f32[1]{0:T(128)S(6)} %copy.12.bias_ref, f32[1]{0:T(128)S(6)} %copy.13.grad_ref, s32[1]{0:T(128)S(6)} %copy.10.sample_ref, ...), custom_call_target="tpu_custom_call" | custom-call | flops 353894400 | bytes 3833880 | tf_op jit(solution)/shard_map/pallas_call | solution.py:239
  27.7 0.0 copy-start.1
  27.7 0.1 collective-permute-done.13.refs_3_.refs_7_
  27.8 0.9 %shard_map.98 = (bf16[160,1152]{1,0:T(8,128)(2,1)S(1)}, bf16[80,1152]{1,0:T(8,128)(2,1)S(1)}, bf16[80,1152]{1,0:T(8,128)(2,1)S(1)}) custom-call(s32[1]{0:T(128)} %bitcast.spot_ref.row_ref, s32[1]{0:T(128)} %bitcast.1.col_ref, f32[1]{0:T(128)S(6)} %copy.11.scale_ref, f32[1]{0:T(128)S(6)} %copy.12.bias_ref, f32[1]{0:T(128)S(6)} %copy.13.grad_ref, ...), custom_call_target="tpu_custom_call" | custom-call | flops 117964800 | bytes 2654232 | tf_op jit(solution)/shard_map/pallas_call | solution.py:239
  28.7 1.6 %collective-permute-start.15 = (bf16[80,1152]{1,0:T(8,128)(2,1)S(1)}, bf16[80,1152]{1,0:T(8,128)(2,1)S(1)}, u32[]{:S(2)}, u32[]{:S(2)}) collective-permute-start(bf16[80,1152]{1,0:T(8,128)(2,1)S(1)} %get-tuple-element.50), channel_id=1, source_target_pairs={{0,1},{1,0},{2,3},{3,2},{4,5},{5,4},{6,7},{7,6},{8,9},{9,8},{10,11... | collective-permute-start | bytes 552968 | tf_op jit(solution)/shard_map/ppermute | solution.py:19
  30.2 0.5 %collective-permute-start.17 = (bf16[80,1152]{1,0:T(8,128)(2,1)S(1)}, bf16[80,1152]{1,0:T(8,128)(2,1)S(1)}, u32[]{:S(2)}, u32[]{:S(2)}) collective-permute-start(bf16[80,1152]{1,0:T(8,128)(2,1)S(1)} %get-tuple-element.54), channel_id=1, source_target_pairs={{0,1},{1,0},{2,3},{3,2},{4,5},{5,4},{6,7},{7,6},{8,9},{9,8},{10,11... | collective-permute-start | bytes 552968 | tf_op jit(solution)/shard_map/ppermute | solution.py:19
  30.8 1.7 %shard_map.99 = (f32[80,1152]{1,0:T(8,128)S(1)}, f32[80,1152]{1,0:T(8,128)S(1)}, bf16[80,1152]{1,0:T(8,128)(2,1)S(1)}, bf16[80,1152]{1,0:T(8,128)(2,1)S(1)}, f32...) custom-call(s32[1]{0:T(128)} %bitcast.spot_ref.row_ref, s32[1]{0:T(128)} %bitcast.1.col_ref, f32[1]{0:T(128)S(6)} %copy.11.scale_ref, ...), custom_call_target="tpu_custom_call" | custom-call | flops 353894400 | bytes 7151640 | tf_op jit(solution)/shard_map/pallas_call | solution.py:239
  32.5 0.2 collective-permute-start.14
  32.7 1.6 %collective-permute-done.15 = bf16[80,1152]{1,0:T(8,128)(2,1)S(1)} collective-permute-done((bf16[80,1152]{1,0:T(8,128)(2,1)S(1)}, bf16[80,1152]{1,0:T(8,128)(2,1)S(1)}, u32[]{:S(2)}, u32[]{:S(2)}) %collective-permute-start.15) | collective-permute-done | bytes 184352 | tf_op jit(solution)/shard_map/ppermute | solution.py:19
  34.3 2.4 %collective-permute-start.20 = (bf16[80,1152]{1,0:T(8,128)(2,1)S(1)}, bf16[80,1152]{1,0:T(8,128)(2,1)S(1)}, u32[]{:S(2)}, u32[]{:S(2)}) collective-permute-start(bf16[80,1152]{1,0:T(8,128)(2,1)S(1)} %add_convert_fusion.1), channel_id=1, source_target_pairs={{0,24},{1,25},{2,26},{3,27},{4,28},{5,29},{6,30},{7,31},{8,16},{9,... | collective-permute-start | bytes 552968 | tf_op jit(solution)/shard_map/ppermute | solution.py:19
  36.8 1.5 %collective-permute-start.16 = (bf16[80,1152]{1,0:T(8,128)(2,1)S(1)}, bf16[80,1152]{1,0:T(8,128)(2,1)S(1)}, u32[]{:S(2)}, u32[]{:S(2)}) collective-permute-start(bf16[80,1152]{1,0:T(8,128)(2,1)S(1)} %get-tuple-element.51), channel_id=1, source_target_pairs={{0,1},{1,0},{2,3},{3,2},{4,5},{5,4},{6,7},{7,6},{8,9},{9,8},{10,11... | collective-permute-start | bytes 552968 | tf_op jit(solution)/shard_map/ppermute | solution.py:19
  38.3 0.1 collective-permute-start.18
  38.4 3.3 %collective-permute-start.19 = (bf16[80,1152]{1,0:T(8,128)(2,1)S(1)}, bf16[80,1152]{1,0:T(8,128)(2,1)S(1)}, u32[]{:S(2)}, u32[]{:S(2)}) collective-permute-start(bf16[80,1152]{1,0:T(8,128)(2,1)S(1)} %add_convert_fusion), channel_id=1, source_target_pairs={{0,8},{1,9},{2,10},{3,11},{4,12},{5,13},{6,14},{7,15},{8,0},{9,1},... | collective-permute-start | bytes 552968 | tf_op jit(solution)/shard_map/ppermute | solution.py:19
  41.7 0.0 collective-permute-done.14.crossed_ref
  41.7 0.6 %collective-permute-done.16.near_stay_ref = bf16[80,1152]{1,0:T(8,128)(2,1)S(1)} collective-permute-done((bf16[80,1152]{1,0:T(8,128)(2,1)S(1)}, bf16[80,1152]{1,0:T(8,128)(2,1)S(1)}, u32[]{:S(2)}, u32[]{:S(2)}) %collective-permute-start.16) | collective-permute-done | bytes 184352 | tf_op jit(solution)/shard_map/ppermute | solution.py:19
  42.3 0.0 collective-permute-done.20.far_cross_ref
  42.3 1.2 %collective-permute-done.18.near_cross_ref = bf16[80,1152]{1,0:T(8,128)(2,1)S(1)} collective-permute-done((bf16[80,1152]{1,0:T(8,128)(2,1)S(1)}, bf16[80,1152]{1,0:T(8,128)(2,1)S(1)}, u32[]{:S(2)}, u32[]{:S(2)}) %collective-permute-start.18) | collective-permute-done | bytes 184352 | tf_op jit(solution)/shard_map/ppermute | solution.py:19
  43.5 3.9 %collective-permute-done.19.far_stay_ref = bf16[80,1152]{1,0:T(8,128)(2,1)S(1)} collective-permute-done((bf16[80,1152]{1,0:T(8,128)(2,1)S(1)}, bf16[80,1152]{1,0:T(8,128)(2,1)S(1)}, u32[]{:S(2)}, u32[]{:S(2)}) %collective-permute-start.19) | collective-permute-done | bytes 184352 | tf_op jit(solution)/shard_map/ppermute | solution.py:19
  47.4 1.0 %shard_map.100 = (bf16[80,1152]{1,0:T(8,128)(2,1)}, bf16[160,576]{1,0:T(8,128)(2,1)}) custom-call(s32[1]{0:T(128)} %bitcast.spot_ref.row_ref, f32[80,1152]{1,0:T(8,128)S(1)} %get-tuple-element.46.stay_ref, f32[80,1152]{1,0:T(8,128)S(1)} %collective-permute-done.14.crossed_ref, bf16[80,1152]{1,0:T(8,128)(2,1)S(1)} %collective-permute-done.16.near_stay_ref, ...), custom_call_target="tpu_custom_call" | custom-call | bytes 1843204 | tf_op jit(solution)/shard_map/pallas_call | solution.py:239
  (10 shorter events, 0.1 us)
Async XLA Ops:
  2.5 5.7 %collective-permute-start = (bf16[88,1152]{1,0:T(8,128)(2,1)}, bf16[88,1152]{1,0:T(8,128)(2,1)S(1)}, u32[]{:S(2)}, u32[]{:S(2)}) collective-permute-start(bf16[88,1152]{1,0:T(8,128)(2,1)} %get-tuple-element.33.refs_7_.refs_3_), channel_id=1, source_target_pairs={{0,16},{16,0},{1,17},{17,1},{2,18},{18,2},{3,19},{19,3},{4,20},{20... | collective-permute-start | bytes 608264 | tf_op jit(solution)/shard_map/ppermute | solution.py:23
  3.0 8.6 %collective-permute-start.3 = (bf16[88,1152]{1,0:T(8,128)(2,1)}, bf16[88,1152]{1,0:T(8,128)(2,1)S(1)}, u32[]{:S(2)}, u32[]{:S(2)}) collective-permute-start(bf16[88,1152]{1,0:T(8,128)(2,1)} %get-tuple-element.29.refs_0_), channel_id=1, source_target_pairs={{0,8},{1,9},{2,10},{3,11},{4,12},{5,13},{6,14},{7,15},{8,0},{9,1},... | collective-permute-start | bytes 608264 | tf_op jit(solution)/shard_map/ppermute | solution.py:19
  6.7 7.1 %collective-permute-start.5 = (bf16[88,1152]{1,0:T(8,128)(2,1)}, bf16[88,1152]{1,0:T(8,128)(2,1)S(1)}, u32[]{:S(2)}, u32[]{:S(2)}) collective-permute-start(bf16[88,1152]{1,0:T(8,128)(2,1)} %get-tuple-element.29.refs_0_), channel_id=1, source_target_pairs={{0,16},{16,0},{1,17},{17,1},{2,18},{18,2},{3,19},{19,3},{4,20},{20... | collective-permute-start | bytes 608264 | tf_op jit(solution)/shard_map/ppermute | solution.py:23
  6.7 7.1 %collective-permute-start.1 = (bf16[88,1152]{1,0:T(8,128)(2,1)}, bf16[88,1152]{1,0:T(8,128)(2,1)S(1)}, u32[]{:S(2)}, u32[]{:S(2)}) collective-permute-start(bf16[88,1152]{1,0:T(8,128)(2,1)} %get-tuple-element.29.refs_0_), channel_id=1, source_target_pairs={{0,1},{1,0},{2,3},{3,2},{4,5},{5,4},{6,7},{7,6},{8,9},{9,8},{10,11... | collective-permute-start | bytes 608264 | tf_op jit(solution)/shard_map/ppermute | solution.py:19
  8.2 8.8 %collective-permute-start.4 = (bf16[88,1152]{1,0:T(8,128)(2,1)S(1)}, bf16[88,1152]{1,0:T(8,128)(2,1)S(1)}, u32[]{:S(2)}, u32[]{:S(2)}) collective-permute-start(bf16[88,1152]{1,0:T(8,128)(2,1)S(1)} %collective-permute-done.refs_1_), channel_id=1, source_target_pairs={{0,8},{1,9},{2,10},{3,11},{4,12},{5,13},{6,14},{7,15},{8,0},{9,1},... | collective-permute-start | bytes 608264 | tf_op jit(solution)/shard_map/ppermute | solution.py:19
  9.9 7.1 %collective-permute-start.2 = (bf16[88,1152]{1,0:T(8,128)(2,1)S(1)}, bf16[88,1152]{1,0:T(8,128)(2,1)S(1)}, u32[]{:S(2)}, u32[]{:S(2)}) collective-permute-start(bf16[88,1152]{1,0:T(8,128)(2,1)S(1)} %collective-permute-done.refs_1_), channel_id=1, source_target_pairs={{0,1},{1,0},{2,3},{3,2},{4,5},{5,4},{6,7},{7,6},{8,9},{9,8},{10,11... | collective-permute-start | bytes 608264 | tf_op jit(solution)/shard_map/ppermute | solution.py:19
  11.6 6.2 %collective-permute-start.10 = (bf16[88,1152]{1,0:T(8,128)(2,1)S(1)}, bf16[88,1152]{1,0:T(8,128)(2,1)S(1)}, u32[]{:S(2)}, u32[]{:S(2)}) collective-permute-start(bf16[88,1152]{1,0:T(8,128)(2,1)S(1)} %collective-permute-done.3.refs_4_), channel_id=1, source_target_pairs={{0,1},{1,0},{2,3},{3,2},{4,5},{5,4},{6,7},{7,6},{8,9},{9,8},{10,11... | collective-permute-start | bytes 608264 | tf_op jit(solution)/shard_map/ppermute | solution.py:19
  13.7 4.1 %collective-permute-start.8 = (bf16[88,1152]{1,0:T(8,128)(2,1)S(1)}, bf16[88,1152]{1,0:T(8,128)(2,1)S(1)}, u32[]{:S(2)}, u32[]{:S(2)}) collective-permute-start(bf16[88,1152]{1,0:T(8,128)(2,1)S(1)} %collective-permute-done.3.refs_4_), channel_id=1, source_target_pairs={{0,16},{16,0},{1,17},{17,1},{2,18},{18,2},{3,19},{19,3},{4,20},{20... | collective-permute-start | bytes 608264 | tf_op jit(solution)/shard_map/ppermute | solution.py:23
  13.7 8.3 %collective-permute-start.6 = (bf16[88,1152]{1,0:T(8,128)(2,1)S(1)}, bf16[88,1152]{1,0:T(8,128)(2,1)S(1)}, u32[]{:S(2)}, u32[]{:S(2)}) collective-permute-start(bf16[88,1152]{1,0:T(8,128)(2,1)S(1)} %collective-permute-done.1.refs_2_), channel_id=1, source_target_pairs={{0,16},{16,0},{1,17},{17,1},{2,18},{18,2},{3,19},{19,3},{4,20},{20... | collective-permute-start | bytes 608264 | tf_op jit(solution)/shard_map/ppermute | solution.py:23
  17.0 5.1 %collective-permute-start.9 = (bf16[88,1152]{1,0:T(8,128)(2,1)S(1)}, bf16[88,1152]{1,0:T(8,128)(2,1)S(1)}, u32[]{:S(2)}, u32[]{:S(2)}) collective-permute-start(bf16[88,1152]{1,0:T(8,128)(2,1)S(1)} %collective-permute-done.4.refs_5_), channel_id=1, source_target_pairs={{0,16},{16,0},{1,17},{17,1},{2,18},{18,2},{3,19},{19,3},{4,20},{20... | collective-permute-start | bytes 608264 | tf_op jit(solution)/shard_map/ppermute | solution.py:23
  17.0 5.1 %collective-permute-start.7 = (bf16[88,1152]{1,0:T(8,128)(2,1)S(1)}, bf16[88,1152]{1,0:T(8,128)(2,1)S(1)}, u32[]{:S(2)}, u32[]{:S(2)}) collective-permute-start(bf16[88,1152]{1,0:T(8,128)(2,1)S(1)} %collective-permute-done.2.refs_3_), channel_id=1, source_target_pairs={{0,16},{16,0},{1,17},{17,1},{2,18},{18,2},{3,19},{19,3},{4,20},{20... | collective-permute-start | bytes 608264 | tf_op jit(solution)/shard_map/ppermute | solution.py:23
  17.8 4.3 %collective-permute-start.11 = (bf16[88,1152]{1,0:T(8,128)(2,1)S(1)}, bf16[88,1152]{1,0:T(8,128)(2,1)S(1)}, u32[]{:S(2)}, u32[]{:S(2)}) collective-permute-start(bf16[88,1152]{1,0:T(8,128)(2,1)S(1)} %collective-permute-done.10.refs_0_), channel_id=1, source_target_pairs={{0,16},{16,0},{1,17},{17,1},{2,18},{18,2},{3,19},{19,3},{4,20},{20... | collective-permute-start | bytes 608264 | tf_op jit(solution)/shard_map/ppermute | solution.py:23
  17.8 8.3 %collective-permute-start.12 = (bf16[88,1152]{1,0:T(8,128)(2,1)S(1)}, bf16[88,1152]{1,0:T(8,128)(2,1)S(1)}, u32[]{:S(2)}, u32[]{:S(2)}) collective-permute-start(bf16[88,1152]{1,0:T(8,128)(2,1)S(1)} %collective-permute-done.4.refs_5_), channel_id=1, source_target_pairs={{0,1},{1,0},{2,3},{3,2},{4,5},{5,4},{6,7},{7,6},{8,9},{9,8},{10,11... | collective-permute-start | bytes 608264 | tf_op jit(solution)/shard_map/ppermute | solution.py:19
  22.1 0.9 %copy-start = (bf16[88,1152]{1,0:T(8,128)(2,1)S(1)}, bf16[88,1152]{1,0:T(8,128)(2,1)}, u32[]{:S(2)}) copy-start(bf16[88,1152]{1,0:T(8,128)(2,1)} %get-tuple-element.29.refs_0_) | copy-start | bytes 608260
  23.0 0.9 %copy-start.2 = (bf16[88,1152]{1,0:T(8,128)(2,1)S(1)}, bf16[88,1152]{1,0:T(8,128)(2,1)}, u32[]{:S(2)}) copy-start(bf16[88,1152]{1,0:T(8,128)(2,1)} %get-tuple-element.33.refs_7_.refs_3_) | copy-start | bytes 608260
  24.0 2.7 %copy-start.3 = (bf16[88,1152]{1,0:T(8,128)(2,1)S(1)}, bf16[88,1152]{1,0:T(8,128)(2,1)}, u32[]{:S(2)}) copy-start(bf16[88,1152]{1,0:T(8,128)(2,1)} %get-tuple-element.33.refs_7_.refs_3_) | copy-start | bytes 608260
  26.1 1.7 %collective-permute-start.13 = (bf16[88,1152]{1,0:T(8,128)(2,1)S(1)}, bf16[88,1152]{1,0:T(8,128)(2,1)S(1)}, u32[]{:S(2)}, u32[]{:S(2)}) collective-permute-start(bf16[88,1152]{1,0:T(8,128)(2,1)S(1)} %collective-permute-done.12.refs_1_), channel_id=1, source_target_pairs={{0,16},{16,0},{1,17},{17,1},{2,18},{18,2},{3,19},{19,3},{4,20},{20... | collective-permute-start | bytes 608264 | tf_op jit(solution)/shard_map/ppermute | solution.py:23
  27.7 3.1 %copy-start.1 = (bf16[88,1152]{1,0:T(8,128)(2,1)S(1)}, bf16[88,1152]{1,0:T(8,128)(2,1)}, u32[]{:S(2)}) copy-start(bf16[88,1152]{1,0:T(8,128)(2,1)} %get-tuple-element.29.refs_0_) | copy-start | bytes 608260
  28.7 5.6 %collective-permute-start.15 = (bf16[80,1152]{1,0:T(8,128)(2,1)S(1)}, bf16[80,1152]{1,0:T(8,128)(2,1)S(1)}, u32[]{:S(2)}, u32[]{:S(2)}) collective-permute-start(bf16[80,1152]{1,0:T(8,128)(2,1)S(1)} %get-tuple-element.50), channel_id=1, source_target_pairs={{0,1},{1,0},{2,3},{3,2},{4,5},{5,4},{6,7},{7,6},{8,9},{9,8},{10,11... | collective-permute-start | bytes 552968 | tf_op jit(solution)/shard_map/ppermute | solution.py:19
  30.2 8.0 %collective-permute-start.17 = (bf16[80,1152]{1,0:T(8,128)(2,1)S(1)}, bf16[80,1152]{1,0:T(8,128)(2,1)S(1)}, u32[]{:S(2)}, u32[]{:S(2)}) collective-permute-start(bf16[80,1152]{1,0:T(8,128)(2,1)S(1)} %get-tuple-element.54), channel_id=1, source_target_pairs={{0,1},{1,0},{2,3},{3,2},{4,5},{5,4},{6,7},{7,6},{8,9},{9,8},{10,11... | collective-permute-start | bytes 552968 | tf_op jit(solution)/shard_map/ppermute | solution.py:19
  32.5 9.2 %collective-permute-start.14 = (f32[80,1152]{1,0:T(8,128)S(1)}, f32[80,1152]{1,0:T(8,128)S(1)}, u32[]{:S(2)}, u32[]{:S(2)}) collective-permute-start(f32[80,1152]{1,0:T(8,128)S(1)} %get-tuple-element.47), channel_id=1, source_target_pairs={{0,16},{16,0},{1,17},{17,1},{2,18},{18,2},{3,19},{19,3},{4,20},{20... | collective-permute-start | bytes 1105928 | tf_op jit(solution)/shard_map/ppermute | solution.py:23
  34.3 8.0 %collective-permute-start.20 = (bf16[80,1152]{1,0:T(8,128)(2,1)S(1)}, bf16[80,1152]{1,0:T(8,128)(2,1)S(1)}, u32[]{:S(2)}, u32[]{:S(2)}) collective-permute-start(bf16[80,1152]{1,0:T(8,128)(2,1)S(1)} %add_convert_fusion.1), channel_id=1, source_target_pairs={{0,24},{1,25},{2,26},{3,27},{4,28},{5,29},{6,30},{7,31},{8,16},{9,... | collective-permute-start | bytes 552968 | tf_op jit(solution)/shard_map/ppermute | solution.py:19
  36.8 5.5 %collective-permute-start.16 = (bf16[80,1152]{1,0:T(8,128)(2,1)S(1)}, bf16[80,1152]{1,0:T(8,128)(2,1)S(1)}, u32[]{:S(2)}, u32[]{:S(2)}) collective-permute-start(bf16[80,1152]{1,0:T(8,128)(2,1)S(1)} %get-tuple-element.51), channel_id=1, source_target_pairs={{0,1},{1,0},{2,3},{3,2},{4,5},{5,4},{6,7},{7,6},{8,9},{9,8},{10,11... | collective-permute-start | bytes 552968 | tf_op jit(solution)/shard_map/ppermute | solution.py:19
  38.3 5.2 %collective-permute-start.18 = (bf16[80,1152]{1,0:T(8,128)(2,1)S(1)}, bf16[80,1152]{1,0:T(8,128)(2,1)S(1)}, u32[]{:S(2)}, u32[]{:S(2)}) collective-permute-start(bf16[80,1152]{1,0:T(8,128)(2,1)S(1)} %get-tuple-element.55), channel_id=1, source_target_pairs={{0,17},{1,16},{2,19},{3,18},{4,21},{5,20},{6,23},{7,22},{8,25},{9,... | collective-permute-start | bytes 552968 | tf_op jit(solution)/shard_map/ppermute | solution.py:19
  38.4 9.0 %collective-permute-start.19 = (bf16[80,1152]{1,0:T(8,128)(2,1)S(1)}, bf16[80,1152]{1,0:T(8,128)(2,1)S(1)}, u32[]{:S(2)}, u32[]{:S(2)}) collective-permute-start(bf16[80,1152]{1,0:T(8,128)(2,1)S(1)} %add_convert_fusion), channel_id=1, source_target_pairs={{0,8},{1,9},{2,10},{3,11},{4,12},{5,13},{6,14},{7,15},{8,0},{9,1},... | collective-permute-start | bytes 552968 | tf_op jit(solution)/shard_map/ppermute | solution.py:19

commit v5 on v4

--- a/solution.py
+++ b/solution.py
@@ -114,15 +114,14 @@
     return at + first + jnp.where(at >= half, jump, 0)
 
 
-def coefficients_of(cols, row_ref, col_ref, scale_ref, bias_ref, grad_ref, sample_ref, mine, others, my_sets, other_sets):
+def coefficients_of(cols, row_ref, col_ref, number_ref, mine, others, my_sets, other_sets):
     row, col = row_ref[0], col_ref[0]
     my_texts, other_texts = row != 0, row == 0
     near, far, other_near, other_far = masks(cols, row)
     my_masks = {"own": 0, "near": near, "far": far, "both": near ^ far}
     other_masks = {"own": 0, "near": other_near, "far": other_far, "both": other_near ^ other_far}
     half = my_sets[0][1][0].shape[0] - SPARE
-    scale, bias = scale_ref[0], bias_ref[0]
-    factor = grad_ref[0] * scale / sample_ref[0].astype(jnp.float32)
+    scale, bias, factor = (number_ref[n : n + 1, :1] for n in range(3))
     my_ids = jnp.concatenate([sample_ids(col ^ my_masks[k], my_texts, half, cols, 0) for k, _ in my_sets], axis=0)
     other_ids = jnp.concatenate(
         [sample_ids(col ^ other_masks[k], other_texts, half, cols, 1) for k, _ in other_sets], axis=1)
@@ -142,7 +141,13 @@
 THREE = ("own", "near", "far")
 
 
-def early_kernel(cols, row_ref, col_ref, scale_ref, bias_ref, grad_ref, sample_ref, *refs):
+def number_kernel(scale_ref, bias_ref, grad_ref, sample_ref, out_ref):
+    factor = grad_ref[0] * scale_ref[0] / sample_ref[0].astype(jnp.float32)
+    line = lax.broadcasted_iota(jnp.int32, out_ref.shape, 0)
+    out_ref[...] = jnp.where(line == 0, scale_ref[0], jnp.where(line == 1, bias_ref[0], factor))
+
+
+def early_kernel(cols, row_ref, col_ref, number_ref, *refs):
     mine_pairs, other_pairs = pairs(refs[:6]), pairs(refs[6:12])
     mine_ref, others_ref, total_ref = refs[12:]
     texts = row_ref[0] != 0
@@ -151,17 +156,17 @@
         unpack(mine_pairs[n], texts, mine_ref, n * size)
         unpack(other_pairs[n], jnp.logical_not(texts), others_ref, n * size)
     others = others_ref[...]
-    coefficient = coefficients_of(cols, row_ref, col_ref, scale_ref, bias_ref, grad_ref, sample_ref, mine_ref[...], others,
+    coefficient = coefficients_of(cols, row_ref, col_ref, number_ref, mine_ref[...], others,
                                   list(zip(THREE, mine_pairs)), list(zip(THREE, other_pairs)))
     total_ref[...] = jnp.dot(coefficient, others, preferred_element_type=jnp.float32)
 
 
-def both_kernel(cols, row_ref, col_ref, scale_ref, bias_ref, grad_ref, sample_ref, *refs):
+def both_kernel(cols, row_ref, col_ref, number_ref, *refs):
     mine_pair, other_pairs = refs[:2], pairs(refs[2:8])
     others_ref, mine_ref, total_ref = refs[8:]
     unpack(mine_pair, row_ref[0] != 0, mine_ref, 0)
     others = others_ref[...]
-    coefficient = coefficients_of(cols, row_ref, col_ref, scale_ref, bias_ref, grad_ref, sample_ref, mine_ref[...], others,
+    coefficient = coefficients_of(cols, row_ref, col_ref, number_ref, mine_ref[...], others,
                                   [("both", mine_pair)], list(zip(THREE, other_pairs)))
     total_ref[...] = jnp.dot(coefficient, others, preferred_element_type=jnp.float32)
 
@@ -182,26 +187,26 @@
         cross_ref[...] = total[half:].astype(cross_ref.dtype)
 
 
-def late_kernel(cols, row_ref, col_ref, scale_ref, bias_ref, grad_ref, sample_ref, *refs):
+def late_kernel(cols, row_ref, col_ref, number_ref, *refs):
     mine_pair, other_pair = refs[:2], refs[2:4]
     mine_ref, total_ref = refs[4:6]
     others_ref, stay_ref, cross_ref = refs[6:]
     texts = row_ref[0] != 0
     unpack(other_pair, jnp.logical_not(texts), others_ref, 0)
     others = others_ref[...]
-    coefficient = coefficients_of(cols, row_ref, col_ref, scale_ref, bias_ref, grad_ref, sample_ref, mine_ref[...], others,
+    coefficient = coefficients_of(cols, row_ref, col_ref, number_ref, mine_ref[...], others,
                                   [("both", mine_pair)], [("both", other_pair)])
     total = total_ref[...] + jnp.dot(coefficient, others, preferred_element_type=jnp.float32)
     pack_sum(total, texts, stay_ref, cross_ref)
 
 
-def rest_kernel(cols, row_ref, col_ref, scale_ref, bias_ref, grad_ref, sample_ref, *refs):
+def rest_kernel(cols, row_ref, col_ref, number_ref, *refs):
     mine_pairs, other_pair = pairs(refs[:6]), refs[6:8]
     mine_ref, others_ref, total_ref = refs[8:11]
     own_stay, own_cross, near_stay, near_cross, far_stay, far_cross = refs[11:]
     texts = row_ref[0] != 0
     others = others_ref[...]
-    coefficient = coefficients_of(cols, row_ref, col_ref, scale_ref, bias_ref, grad_ref, sample_ref, mine_ref[...], others,
+    coefficient = coefficients_of(cols, row_ref, col_ref, number_ref, mine_ref[...], others,
                                   list(zip(THREE, mine_pairs)), [("both", other_pair)])
     total = total_ref[...] + jnp.dot(coefficient, others, preferred_element_type=jnp.float32)
     size = total.shape[0] // 3
@@ -210,15 +215,11 @@
     pack_sum(total[:size], texts, own_stay, own_cross)
 
 
-def last_kernel(spot_ref, stay_ref, crossed_ref, near_stay_ref, near_cross_ref, far_stay_ref, far_cross_ref,
-                image_ref, text_ref):
+def last_kernel(spot_ref, stay_ref, crossed_ref, near_stay_ref, near_cross_ref, image_ref, text_ref):
     half, part = text_ref.shape[0] // 2, text_ref.shape[1]
 
-    def add(own, near, far):
-        return (own[...] + near[...].astype(jnp.float32) + far[...].astype(jnp.float32)).astype(image_ref.dtype)
-
-    stay = add(stay_ref, near_stay_ref, far_stay_ref)
-    crossed = add(crossed_ref, near_cross_ref, far_cross_ref)
+    stay = (stay_ref[...] + near_stay_ref[...].astype(jnp.float32)).astype(image_ref.dtype)
+    crossed = (crossed_ref[...] + near_cross_ref[...].astype(jnp.float32)).astype(image_ref.dtype)
 
     def put(images, texts):
         image_ref[...] = images
@@ -255,7 +256,6 @@
     cols = lax.axis_size("col")
     row, col = lax.axis_index("row")[None], lax.axis_index("col")[None]
     near, far = masks(cols, None)
-    scalars = (row, col, logit_scale, logit_bias, loss_grad, sample_count)
 
     def shape(rows, dtype):
         return jax.ShapeDtypeStruct((rows, width), dtype)
@@ -279,28 +279,31 @@
     both_a = hop(far_a, *near)
     both_b = hop(far_b, *near)
     mine = (own_a, own_b, near_a, near_b, far_a, far_b)
+    number = call(number_kernel, jax.ShapeDtypeStruct((8, 128), f32), 4, logit_scale, logit_bias, loss_grad, sample_count)
+    near_a, number = lax.optimization_barrier((near_a, number))
     others = (swap(own_a), give, swap(near_a), swap(near_b), swap(far_a), swap(far_b))
     others, other_both_a = lax.optimization_barrier((others, swap(both_a)))
 
     pair_flops = 4 * size * size * width
+    scalars = (row, col, number)
     mine_rows, other_rows, early = call(
         functools.partial(early_kernel, cols), (shape(3 * size, bf16), shape(3 * size, bf16), shape(3 * size, f32)),
-        6, *scalars, *mine, *others, flops=9 * pair_flops)
+        2, *scalars, *mine, *others, flops=9 * pair_flops)
     both_b, early = lax.optimization_barrier((both_b, early))
     both = (both_a, both_b)
     other_both = (other_both_a, swap(both_b))
     both_rows, both_early = call(
-        functools.partial(both_kernel, cols), (shape(size, bf16), shape(size, f32)), 6, *scalars, *both, *others,
+        functools.partial(both_kernel, cols), (shape(size, bf16), shape(size, f32)), 2, *scalars, *both, *others,
         other_rows, flops=3 * pair_flops)
     other_late, late_stay, late_cross = call(
-        functools.partial(late_kernel, cols), (shape(size, bf16), shape(half, bf16), shape(half, bf16)), 6, *scalars,
+        functools.partial(late_kernel, cols), (shape(size, bf16), shape(half, bf16), shape(half, bf16)), 2, *scalars,
         *both, *other_both, both_rows, both_early, flops=pair_flops)
     in_cross = hop(late_cross, *near)
     in_stay = hop(late_stay, *near)
     own_stay, own_cross, near_stay, near_cross, far_stay, far_cross = call(
         functools.partial(rest_kernel, cols),
         (shape(half, f32), shape(half, f32), shape(half, bf16), shape(half, bf16), shape(half, f32), shape(half, f32)),
-        6, *scalars, *mine, *other_both, mine_rows, other_late, early, flops=3 * pair_flops)
+        2, *scalars, *mine, *other_both, mine_rows, other_late, early, flops=3 * pair_flops)
     crossed = swap(own_cross)
     far_cross = (far_cross + in_cross.astype(f32)).astype(bf16)
     far_stay = (far_stay + in_stay.astype(f32)).astype(bf16)
@@ -310,8 +313,10 @@
     far_cross = hop(far_cross, *far, across=True)
     far_stay = hop(far_stay, *far)
     near_cross = hop(near_cross, *near, across=True)
+    own_stay = own_stay + far_stay.astype(f32)
+    crossed = crossed + far_cross.astype(f32)
     return call(last_kernel, (shape(half, bf16), jax.ShapeDtypeStruct(text_emb.shape, bf16)), 1, row, own_stay, crossed,
-                near_stay, near_cross, far_stay, far_cross)
+                near_stay, near_cross)
 
 
 def partner(block, axis, distance):

time: 48.6 us -> 45.9 us (0.944)
  waiting for transfers between devices: 11.6 us -> 7.4 us
  starting transfers between devices: 23 us -> 24.4 us
    ppermute x12, waiting for transfers between devices: 11.5 us -> 7.17 us  [hop(): return lax.ppermute(block, ('row', 'col'), route)]
    ppermute x12, starting transfers between devices: 20.6 us -> 22.2 us  [hop(): return lax.ppermute(block, ('row', 'col'), route)]
    pallas_call x5 -> x6, Pallas kernels: 6.68 us -> 6.69 us  [call(): pl.pallas_call(kernel, out_shape=out_shape, in_specs=[pl.BlockSpec(memory...]
  transfers between devices with their start and end apart: 21 -> 21, of which waited for: 8 -> 6; matrix products, arithmetic and copies ran while one was open for 0% -> 0% of each run, Pallas kernels for 10% -> 11%
where the time goes in v5:
time: 45.9 us; the launch traced here: 45.7 us
  starting transfers between devices  24.4 us (53%)
  Pallas kernels  8.53 us (19%)
  waiting for transfers between devices  7.4 us (16%)
  between operations  3.36 us (7%)
  local copies, waits for them, and re-layouts  1.86 us (4%)
    ppermute x12, starting transfers between devices, hop(): return lax.ppermute(block, ('row', 'col'), route)  22.2 us
    ppermute x12, waiting for transfers between devices, hop(): return lax.ppermute(block, ('row', 'col'), route)  7.17 us
    pallas_call x6, Pallas kernels, call(): pl.pallas_call(kernel, out_shape=out_shape, in_specs=[pl.BlockSpec(memory...  6.69 us
    ppermute x9, starting transfers between devices, swap(): return lax.ppermute(block, 'row', [(0, 1), (1, 0)])  2.13 us
    unnamed x8, local copies, waits for them, and re-layouts  1.86 us
    pallas_call x1, Pallas kernels, pair_body(): pl.pallas_call(first_kernel, out_shape=(sent, sent), in_specs=[pl.BlockSp...  1.84 us
  transfers between devices with their start and end apart: 21, of which 6 were waited for; matrix products, arithmetic and copies ran while one was open for 0% of the time, Pallas kernels for 11%

profile of v5, /device:TPU:0, one launch (start us, length us, event | category | flops | bytes accessed | tf_op | source)
XLA Modules:
  0.0 45.7 jit_solution(15824401392705487834)
XLA Ops:
  0.6 1.8 %shard_map.95 = (bf16[88,1152]{1,0:T(8,128)(2,1)}, bf16[88,1152]{1,0:T(8,128)(2,1)}) custom-call(s32[1]{0:T(128)} %bitcast.spot_ref.row_ref, bf16[80,1152]{1,0:T(8,128)(2,1)} %image_ref.1, bf16[160,576]{1,0:T(8,128)(2,1)} %text_ref.1, s32[1,80]{1,0:T(1,128)} %bitcast.5, s32[1,160]{1,0:T(1,128)} %bitcast.4), custom_call_target="tpu_custom_call" | custom-call | tf_op jit(solution)/shard_map/pallas_call | solution.py:266
  2.5 0.5 %collective-permute-start.1 = (bf16[88,1152]{1,0:T(8,128)(2,1)}, bf16[88,1152]{1,0:T(8,128)(2,1)S(1)}, u32[]{:S(2)}, u32[]{:S(2)}) collective-permute-start(bf16[88,1152]{1,0:T(8,128)(2,1)} %get-tuple-element.37.refs_7_.refs_3_), channel_id=1, source_target_pairs={{0,16},{16,0},{1,17},{17,1},{2,18},{18,2},{3,19},{19,3},{4,20},{20... | collective-permute-start | bytes 608264 | tf_op jit(solution)/shard_map/ppermute | solution.py:23
  3.0 3.7 %collective-permute-start.3 = (bf16[88,1152]{1,0:T(8,128)(2,1)}, bf16[88,1152]{1,0:T(8,128)(2,1)S(1)}, u32[]{:S(2)}, u32[]{:S(2)}) collective-permute-start(bf16[88,1152]{1,0:T(8,128)(2,1)} %get-tuple-element.31.refs_0_), channel_id=1, source_target_pairs={{0,8},{1,9},{2,10},{3,11},{4,12},{5,13},{6,14},{7,15},{8,0},{9,1},... | collective-permute-start | bytes 608264 | tf_op jit(solution)/shard_map/ppermute | solution.py:19
  6.7 1.5 %collective-permute-start = (bf16[88,1152]{1,0:T(8,128)(2,1)}, bf16[88,1152]{1,0:T(8,128)(2,1)S(1)}, u32[]{:S(2)}, u32[]{:S(2)}) collective-permute-start(bf16[88,1152]{1,0:T(8,128)(2,1)} %get-tuple-element.31.refs_0_), channel_id=1, source_target_pairs={{0,1},{1,0},{2,3},{3,2},{4,5},{5,4},{6,7},{7,6},{8,9},{9,8},{10,11... | collective-permute-start | bytes 608264 | tf_op jit(solution)/shard_map/ppermute | solution.py:19
  8.2 0.0 collective-permute-start.5
  8.2 0.0 collective-permute-done.1.refs_1_
  8.2 1.5 %collective-permute-start.4 = (bf16[88,1152]{1,0:T(8,128)(2,1)S(1)}, bf16[88,1152]{1,0:T(8,128)(2,1)S(1)}, u32[]{:S(2)}, u32[]{:S(2)}) collective-permute-start(bf16[88,1152]{1,0:T(8,128)(2,1)S(1)} %collective-permute-done.1.refs_1_), channel_id=1, source_target_pairs={{0,8},{1,9},{2,10},{3,11},{4,12},{5,13},{6,14},{7,15},{8,0},{9,1},... | collective-permute-start | bytes 608264 | tf_op jit(solution)/shard_map/ppermute | solution.py:19
  9.6 1.5 %collective-permute-start.2 = (bf16[88,1152]{1,0:T(8,128)(2,1)S(1)}, bf16[88,1152]{1,0:T(8,128)(2,1)S(1)}, u32[]{:S(2)}, u32[]{:S(2)}) collective-permute-start(bf16[88,1152]{1,0:T(8,128)(2,1)S(1)} %collective-permute-done.1.refs_1_), channel_id=1, source_target_pairs={{0,1},{1,0},{2,3},{3,2},{4,5},{5,4},{6,7},{7,6},{8,9},{9,8},{10,11... | collective-permute-start | bytes 608264 | tf_op jit(solution)/shard_map/ppermute | solution.py:19
  11.1 0.5 %collective-permute-done.3.refs_4_ = bf16[88,1152]{1,0:T(8,128)(2,1)S(1)} collective-permute-done((bf16[88,1152]{1,0:T(8,128)(2,1)}, bf16[88,1152]{1,0:T(8,128)(2,1)S(1)}, u32[]{:S(2)}, u32[]{:S(2)}) %collective-permute-start.3) | collective-permute-done | bytes 202784 | tf_op jit(solution)/shard_map/ppermute | solution.py:19
  11.6 2.1 %collective-permute-start.10 = (bf16[88,1152]{1,0:T(8,128)(2,1)S(1)}, bf16[88,1152]{1,0:T(8,128)(2,1)S(1)}, u32[]{:S(2)}, u32[]{:S(2)}) collective-permute-start(bf16[88,1152]{1,0:T(8,128)(2,1)S(1)} %collective-permute-done.3.refs_4_), channel_id=1, source_target_pairs={{0,1},{1,0},{2,3},{3,2},{4,5},{5,4},{6,7},{7,6},{8,9},{9,8},{10,11... | collective-permute-start | bytes 608264 | tf_op jit(solution)/shard_map/ppermute | solution.py:19
  13.7 0.0 collective-permute-done.refs_2_
  13.7 0.0 collective-permute-start.8
  16.4 0.0 collective-permute-done.5.refs_6_.refs_2_
  16.4 0.6 %collective-permute-start.6 = (bf16[88,1152]{1,0:T(8,128)(2,1)S(1)}, bf16[88,1152]{1,0:T(8,128)(2,1)S(1)}, u32[]{:S(2)}, u32[]{:S(2)}) collective-permute-start(bf16[88,1152]{1,0:T(8,128)(2,1)S(1)} %collective-permute-done.refs_2_), channel_id=1, source_target_pairs={{0,16},{16,0},{1,17},{17,1},{2,18},{18,2},{3,19},{19,3},{4,20},{20... | collective-permute-start | bytes 608264 | tf_op jit(solution)/shard_map/ppermute | solution.py:23
  17.0 0.0 collective-permute-done.4.refs_5_
  17.0 0.1 collective-permute-start.9
  17.1 0.0 collective-permute-done.2.refs_3_
  17.1 0.4 collective-permute-start.7
  17.5 0.1 collective-permute-done.10.refs_0_
  17.5 0.0 collective-permute-start.11
  17.6 0.0 collective-permute-done.8.refs_10_.refs_6_
  17.6 1.9 %collective-permute-start.12 = (bf16[88,1152]{1,0:T(8,128)(2,1)S(1)}, bf16[88,1152]{1,0:T(8,128)(2,1)S(1)}, u32[]{:S(2)}, u32[]{:S(2)}) collective-permute-start(bf16[88,1152]{1,0:T(8,128)(2,1)S(1)} %collective-permute-done.4.refs_5_), channel_id=1, source_target_pairs={{0,1},{1,0},{2,3},{3,2},{4,5},{5,4},{6,7},{7,6},{8,9},{9,8},{10,11... | collective-permute-start | bytes 608264 | tf_op jit(solution)/shard_map/ppermute | solution.py:19
  19.5 0.0 collective-permute-done.6.refs_8_.refs_4_
  19.5 0.0 collective-permute-done.9.refs_11_.refs_7_
  19.5 0.0 collective-permute-done.7.refs_9_.refs_5_
  19.5 0.0 copy-start
  19.5 0.9 %copy-done = bf16[88,1152]{1,0:T(8,128)(2,1)S(1)} copy-done((bf16[88,1152]{1,0:T(8,128)(2,1)S(1)}, bf16[88,1152]{1,0:T(8,128)(2,1)}, u32[]{:S(2)}) %copy-start) | copy-done | bytes 202776
  20.4 0.9 %copy-done.2 = bf16[88,1152]{1,0:T(8,128)(2,1)S(1)} copy-done((bf16[88,1152]{1,0:T(8,128)(2,1)S(1)}, bf16[88,1152]{1,0:T(8,128)(2,1)}, u32[]{:S(2)}) %copy-start.2) | copy-done | bytes 202776
  21.4 2.2 %shard_map.97 = (bf16[480,1152]{1,0:T(8,128)(2,1)S(1)}, bf16[480,1152]{1,0:T(8,128)(2,1)S(1)}, f32[480,1152]{1,0:T(8,128)S(1)}) custom-call(s32[1]{0:T(128)} %bitcast.spot_ref.row_ref, s32[1]{0:T(128)} %bitcast.1.col_ref, f32[8,128]{1,0:T(8,128)S(1)} %shard_map.96.number_ref, bf16[88,1152]{1,0:T(8,128)(2,1)S(1)} %copy-done, ...), custom_call_target="tpu_custom_call" | custom-call | flops 1061683200 | bytes 6860808 | tf_op jit(solution)/shard_map/pallas_call | solution.py:240
  23.6 0.3 collective-permute-start.13
  23.9 0.9 %shard_map.98 = (bf16[160,1152]{1,0:T(8,128)(2,1)S(1)}, f32[160,1152]{1,0:T(8,128)S(1)}) custom-call(s32[1]{0:T(128)} %bitcast.spot_ref.row_ref, s32[1]{0:T(128)} %bitcast.1.col_ref, f32[8,128]{1,0:T(8,128)S(1)} %shard_map.96.number_ref, bf16[88,1152]{1,0:T(8,128)(2,1)S(1)} %collective-permute-done.10.refs_0_, ...), custom_call_target="tpu_custom_call" | custom-call | flops 353894400 | bytes 3837960 | tf_op jit(solution)/shard_map/pallas_call | solution.py:240
  24.9 0.0 copy-start.1
  24.9 0.2 collective-permute-done.13.refs_3_.refs_7_
  25.1 0.9 %shard_map.99 = (bf16[160,1152]{1,0:T(8,128)(2,1)S(1)}, bf16[80,1152]{1,0:T(8,128)(2,1)S(1)}, bf16[80,1152]{1,0:T(8,128)(2,1)S(1)}) custom-call(s32[1]{0:T(128)} %bitcast.spot_ref.row_ref, s32[1]{0:T(128)} %bitcast.1.col_ref, f32[8,128]{1,0:T(8,128)S(1)} %shard_map.96.number_ref, bf16[88,1152]{1,0:T(8,128)(2,1)S(1)} %collective-permute-done.10.refs_0_, ...), custom_call_target="tpu_custom_call" | custom-call | flops 117964800 | bytes 2658312 | tf_op jit(solution)/shard_map/pallas_call | solution.py:240
  26.0 1.6 %collective-permute-start.14 = (bf16[80,1152]{1,0:T(8,128)(2,1)S(1)}, bf16[80,1152]{1,0:T(8,128)(2,1)S(1)}, u32[]{:S(2)}, u32[]{:S(2)}) collective-permute-start(bf16[80,1152]{1,0:T(8,128)(2,1)S(1)} %get-tuple-element.52), channel_id=1, source_target_pairs={{0,1},{1,0},{2,3},{3,2},{4,5},{5,4},{6,7},{7,6},{8,9},{9,8},{10,11... | collective-permute-start | bytes 552968 | tf_op jit(solution)/shard_map/ppermute | solution.py:19
  27.6 0.4 collective-permute-start.17
  28.1 1.7 %shard_map.100 = (f32[80,1152]{1,0:T(8,128)S(1)}, f32[80,1152]{1,0:T(8,128)S(1)}, bf16[80,1152]{1,0:T(8,128)(2,1)S(1)}, bf16[80,1152]{1,0:T(8,128)(2,1)S(1)}, f3...) custom-call(s32[1]{0:T(128)} %bitcast.spot_ref.row_ref, s32[1]{0:T(128)} %bitcast.1.col_ref, ...), custom_call_target="tpu_custom_call" | custom-call | flops 353894400 | bytes 7155720 | tf_op jit(solution)/shard_map/pallas_call | solution.py:240
  29.8 0.1 collective-permute-start.16
  29.9 1.7 %collective-permute-done.14 = bf16[80,1152]{1,0:T(8,128)(2,1)S(1)} collective-permute-done((bf16[80,1152]{1,0:T(8,128)(2,1)S(1)}, bf16[80,1152]{1,0:T(8,128)(2,1)S(1)}, u32[]{:S(2)}, u32[]{:S(2)}) %collective-permute-start.14) | collective-permute-done | bytes 184352 | tf_op jit(solution)/shard_map/ppermute | solution.py:19
  31.6 3.2 %collective-permute-start.15 = (bf16[80,1152]{1,0:T(8,128)(2,1)S(1)}, bf16[80,1152]{1,0:T(8,128)(2,1)S(1)}, u32[]{:S(2)}, u32[]{:S(2)}) collective-permute-start(bf16[80,1152]{1,0:T(8,128)(2,1)S(1)} %add_convert_fusion.1), channel_id=1, source_target_pairs={{0,8},{1,9},{2,10},{3,11},{4,12},{5,13},{6,14},{7,15},{8,0},{9,1},... | collective-permute-start | bytes 552968 | tf_op jit(solution)/shard_map/ppermute | solution.py:19
  34.9 1.8 %collective-permute-start.18 = (bf16[80,1152]{1,0:T(8,128)(2,1)S(1)}, bf16[80,1152]{1,0:T(8,128)(2,1)S(1)}, u32[]{:S(2)}, u32[]{:S(2)}) collective-permute-start(bf16[80,1152]{1,0:T(8,128)(2,1)S(1)} %add_convert_fusion), channel_id=1, source_target_pairs={{0,24},{1,25},{2,26},{3,27},{4,28},{5,29},{6,30},{7,31},{8,16},{9,... | collective-permute-start | bytes 552968 | tf_op jit(solution)/shard_map/ppermute | solution.py:19
  36.7 0.6 %collective-permute-start.19 = (bf16[80,1152]{1,0:T(8,128)(2,1)S(1)}, bf16[80,1152]{1,0:T(8,128)(2,1)S(1)}, u32[]{:S(2)}, u32[]{:S(2)}) collective-permute-start(bf16[80,1152]{1,0:T(8,128)(2,1)S(1)} %get-tuple-element.57), channel_id=1, source_target_pairs={{0,1},{1,0},{2,3},{3,2},{4,5},{5,4},{6,7},{7,6},{8,9},{9,8},{10,11... | collective-permute-start | bytes 552968 | tf_op jit(solution)/shard_map/ppermute | solution.py:19
  37.4 2.3 %collective-permute-start.20 = (bf16[80,1152]{1,0:T(8,128)(2,1)S(1)}, bf16[80,1152]{1,0:T(8,128)(2,1)S(1)}, u32[]{:S(2)}, u32[]{:S(2)}) collective-permute-start(bf16[80,1152]{1,0:T(8,128)(2,1)S(1)} %get-tuple-element.59), channel_id=1, source_target_pairs={{0,17},{1,16},{2,19},{3,18},{4,21},{5,20},{6,23},{7,22},{8,25},{9,... | collective-permute-start | bytes 552968 | tf_op jit(solution)/shard_map/ppermute | solution.py:19
  39.7 0.0 collective-permute-done.15
  39.7 2.9 %collective-permute-done.18 = bf16[80,1152]{1,0:T(8,128)(2,1)S(1)} collective-permute-done((bf16[80,1152]{1,0:T(8,128)(2,1)S(1)}, bf16[80,1152]{1,0:T(8,128)(2,1)S(1)}, u32[]{:S(2)}, u32[]{:S(2)}) %collective-permute-start.18) | collective-permute-done | bytes 184352 | tf_op jit(solution)/shard_map/ppermute | solution.py:19
  42.7 0.0 collective-permute-done.19.near_stay_ref
  42.7 2.0 %collective-permute-done.20.near_cross_ref = bf16[80,1152]{1,0:T(8,128)(2,1)S(1)} collective-permute-done((bf16[80,1152]{1,0:T(8,128)(2,1)S(1)}, bf16[80,1152]{1,0:T(8,128)(2,1)S(1)}, u32[]{:S(2)}, u32[]{:S(2)}) %collective-permute-start.20) | collective-permute-done | bytes 184352 | tf_op jit(solution)/shard_map/ppermute | solution.py:19
  44.8 0.9 %shard_map.101 = (bf16[80,1152]{1,0:T(8,128)(2,1)}, bf16[160,576]{1,0:T(8,128)(2,1)}) custom-call(s32[1]{0:T(128)} %bitcast.spot_ref.row_ref, f32[80,1152]{1,0:T(8,128)S(1)} %convert_add_fusion.1.stay_ref, f32[80,1152]{1,0:T(8,128)S(1)} %convert_add_fusion.crossed_ref, bf16[80,1152]{1,0:T(8,128)(2,1)S(1)} %collective-permute-done.19.near_stay_ref, ...), custom_call_target="tpu_custom_call" | custom-call | bytes 1474564 | tf_op jit(solution)/shard_map/pallas_call | solution.py:240
  (13 shorter events, 0.2 us)
Async XLA Ops:
  2.5 5.7 %collective-permute-start.1 = (bf16[88,1152]{1,0:T(8,128)(2,1)}, bf16[88,1152]{1,0:T(8,128)(2,1)S(1)}, u32[]{:S(2)}, u32[]{:S(2)}) collective-permute-start(bf16[88,1152]{1,0:T(8,128)(2,1)} %get-tuple-element.37.refs_7_.refs_3_), channel_id=1, source_target_pairs={{0,16},{16,0},{1,17},{17,1},{2,18},{18,2},{3,19},{19,3},{4,20},{20... | collective-permute-start | bytes 608264 | tf_op jit(solution)/shard_map/ppermute | solution.py:23
  3.0 8.6 %collective-permute-start.3 = (bf16[88,1152]{1,0:T(8,128)(2,1)}, bf16[88,1152]{1,0:T(8,128)(2,1)S(1)}, u32[]{:S(2)}, u32[]{:S(2)}) collective-permute-start(bf16[88,1152]{1,0:T(8,128)(2,1)} %get-tuple-element.31.refs_0_), channel_id=1, source_target_pairs={{0,8},{1,9},{2,10},{3,11},{4,12},{5,13},{6,14},{7,15},{8,0},{9,1},... | collective-permute-start | bytes 608264 | tf_op jit(solution)/shard_map/ppermute | solution.py:19
  6.7 7.1 %collective-permute-start = (bf16[88,1152]{1,0:T(8,128)(2,1)}, bf16[88,1152]{1,0:T(8,128)(2,1)S(1)}, u32[]{:S(2)}, u32[]{:S(2)}) collective-permute-start(bf16[88,1152]{1,0:T(8,128)(2,1)} %get-tuple-element.31.refs_0_), channel_id=1, source_target_pairs={{0,1},{1,0},{2,3},{3,2},{4,5},{5,4},{6,7},{7,6},{8,9},{9,8},{10,11... | collective-permute-start | bytes 608264 | tf_op jit(solution)/shard_map/ppermute | solution.py:19
  8.2 8.2 %collective-permute-start.5 = (bf16[88,1152]{1,0:T(8,128)(2,1)}, bf16[88,1152]{1,0:T(8,128)(2,1)S(1)}, u32[]{:S(2)}, u32[]{:S(2)}) collective-permute-start(bf16[88,1152]{1,0:T(8,128)(2,1)} %get-tuple-element.31.refs_0_), channel_id=1, source_target_pairs={{0,16},{16,0},{1,17},{17,1},{2,18},{18,2},{3,19},{19,3},{4,20},{20... | collective-permute-start | bytes 608264 | tf_op jit(solution)/shard_map/ppermute | solution.py:23
  8.2 8.8 %collective-permute-start.4 = (bf16[88,1152]{1,0:T(8,128)(2,1)S(1)}, bf16[88,1152]{1,0:T(8,128)(2,1)S(1)}, u32[]{:S(2)}, u32[]{:S(2)}) collective-permute-start(bf16[88,1152]{1,0:T(8,128)(2,1)S(1)} %collective-permute-done.1.refs_1_), channel_id=1, source_target_pairs={{0,8},{1,9},{2,10},{3,11},{4,12},{5,13},{6,14},{7,15},{8,0},{9,1},... | collective-permute-start | bytes 608264 | tf_op jit(solution)/shard_map/ppermute | solution.py:19
  9.6 7.4 %collective-permute-start.2 = (bf16[88,1152]{1,0:T(8,128)(2,1)S(1)}, bf16[88,1152]{1,0:T(8,128)(2,1)S(1)}, u32[]{:S(2)}, u32[]{:S(2)}) collective-permute-start(bf16[88,1152]{1,0:T(8,128)(2,1)S(1)} %collective-permute-done.1.refs_1_), channel_id=1, source_target_pairs={{0,1},{1,0},{2,3},{3,2},{4,5},{5,4},{6,7},{7,6},{8,9},{9,8},{10,11... | collective-permute-start | bytes 608264 | tf_op jit(solution)/shard_map/ppermute | solution.py:19
  11.6 6.0 %collective-permute-start.10 = (bf16[88,1152]{1,0:T(8,128)(2,1)S(1)}, bf16[88,1152]{1,0:T(8,128)(2,1)S(1)}, u32[]{:S(2)}, u32[]{:S(2)}) collective-permute-start(bf16[88,1152]{1,0:T(8,128)(2,1)S(1)} %collective-permute-done.3.refs_4_), channel_id=1, source_target_pairs={{0,1},{1,0},{2,3},{3,2},{4,5},{5,4},{6,7},{7,6},{8,9},{9,8},{10,11... | collective-permute-start | bytes 608264 | tf_op jit(solution)/shard_map/ppermute | solution.py:19
  13.7 3.8 %collective-permute-start.8 = (bf16[88,1152]{1,0:T(8,128)(2,1)S(1)}, bf16[88,1152]{1,0:T(8,128)(2,1)S(1)}, u32[]{:S(2)}, u32[]{:S(2)}) collective-permute-start(bf16[88,1152]{1,0:T(8,128)(2,1)S(1)} %collective-permute-done.3.refs_4_), channel_id=1, source_target_pairs={{0,16},{16,0},{1,17},{17,1},{2,18},{18,2},{3,19},{19,3},{4,20},{20... | collective-permute-start | bytes 608264 | tf_op jit(solution)/shard_map/ppermute | solution.py:23
  16.4 3.1 %collective-permute-start.6 = (bf16[88,1152]{1,0:T(8,128)(2,1)S(1)}, bf16[88,1152]{1,0:T(8,128)(2,1)S(1)}, u32[]{:S(2)}, u32[]{:S(2)}) collective-permute-start(bf16[88,1152]{1,0:T(8,128)(2,1)S(1)} %collective-permute-done.refs_2_), channel_id=1, source_target_pairs={{0,16},{16,0},{1,17},{17,1},{2,18},{18,2},{3,19},{19,3},{4,20},{20... | collective-permute-start | bytes 608264 | tf_op jit(solution)/shard_map/ppermute | solution.py:23
  17.0 2.5 %collective-permute-start.9 = (bf16[88,1152]{1,0:T(8,128)(2,1)S(1)}, bf16[88,1152]{1,0:T(8,128)(2,1)S(1)}, u32[]{:S(2)}, u32[]{:S(2)}) collective-permute-start(bf16[88,1152]{1,0:T(8,128)(2,1)S(1)} %collective-permute-done.4.refs_5_), channel_id=1, source_target_pairs={{0,16},{16,0},{1,17},{17,1},{2,18},{18,2},{3,19},{19,3},{4,20},{20... | collective-permute-start | bytes 608264 | tf_op jit(solution)/shard_map/ppermute | solution.py:23
  17.1 2.4 %collective-permute-start.7 = (bf16[88,1152]{1,0:T(8,128)(2,1)S(1)}, bf16[88,1152]{1,0:T(8,128)(2,1)S(1)}, u32[]{:S(2)}, u32[]{:S(2)}) collective-permute-start(bf16[88,1152]{1,0:T(8,128)(2,1)S(1)} %collective-permute-done.2.refs_3_), channel_id=1, source_target_pairs={{0,16},{16,0},{1,17},{17,1},{2,18},{18,2},{3,19},{19,3},{4,20},{20... | collective-permute-start | bytes 608264 | tf_op jit(solution)/shard_map/ppermute | solution.py:23
  17.5 1.9 %collective-permute-start.11 = (bf16[88,1152]{1,0:T(8,128)(2,1)S(1)}, bf16[88,1152]{1,0:T(8,128)(2,1)S(1)}, u32[]{:S(2)}, u32[]{:S(2)}) collective-permute-start(bf16[88,1152]{1,0:T(8,128)(2,1)S(1)} %collective-permute-done.10.refs_0_), channel_id=1, source_target_pairs={{0,16},{16,0},{1,17},{17,1},{2,18},{18,2},{3,19},{19,3},{4,20},{20... | collective-permute-start | bytes 608264 | tf_op jit(solution)/shard_map/ppermute | solution.py:23
  17.6 6.0 %collective-permute-start.12 = (bf16[88,1152]{1,0:T(8,128)(2,1)S(1)}, bf16[88,1152]{1,0:T(8,128)(2,1)S(1)}, u32[]{:S(2)}, u32[]{:S(2)}) collective-permute-start(bf16[88,1152]{1,0:T(8,128)(2,1)S(1)} %collective-permute-done.4.refs_5_), channel_id=1, source_target_pairs={{0,1},{1,0},{2,3},{3,2},{4,5},{5,4},{6,7},{7,6},{8,9},{9,8},{10,11... | collective-permute-start | bytes 608264 | tf_op jit(solution)/shard_map/ppermute | solution.py:19
  19.5 0.9 %copy-start = (bf16[88,1152]{1,0:T(8,128)(2,1)S(1)}, bf16[88,1152]{1,0:T(8,128)(2,1)}, u32[]{:S(2)}) copy-start(bf16[88,1152]{1,0:T(8,128)(2,1)} %get-tuple-element.31.refs_0_) | copy-start | bytes 608260
  20.4 0.9 %copy-start.2 = (bf16[88,1152]{1,0:T(8,128)(2,1)S(1)}, bf16[88,1152]{1,0:T(8,128)(2,1)}, u32[]{:S(2)}) copy-start(bf16[88,1152]{1,0:T(8,128)(2,1)} %get-tuple-element.37.refs_7_.refs_3_) | copy-start | bytes 608260
  21.4 2.6 %copy-start.3 = (bf16[88,1152]{1,0:T(8,128)(2,1)S(1)}, bf16[88,1152]{1,0:T(8,128)(2,1)}, u32[]{:S(2)}) copy-start(bf16[88,1152]{1,0:T(8,128)(2,1)} %get-tuple-element.37.refs_7_.refs_3_) | copy-start | bytes 608260
  23.6 1.5 %collective-permute-start.13 = (bf16[88,1152]{1,0:T(8,128)(2,1)S(1)}, bf16[88,1152]{1,0:T(8,128)(2,1)S(1)}, u32[]{:S(2)}, u32[]{:S(2)}) collective-permute-start(bf16[88,1152]{1,0:T(8,128)(2,1)S(1)} %collective-permute-done.12.refs_1_), channel_id=1, source_target_pairs={{0,16},{16,0},{1,17},{17,1},{2,18},{18,2},{3,19},{19,3},{4,20},{20... | collective-permute-start | bytes 608264 | tf_op jit(solution)/shard_map/ppermute | solution.py:23
  24.9 3.2 %copy-start.1 = (bf16[88,1152]{1,0:T(8,128)(2,1)S(1)}, bf16[88,1152]{1,0:T(8,128)(2,1)}, u32[]{:S(2)}) copy-start(bf16[88,1152]{1,0:T(8,128)(2,1)} %get-tuple-element.31.refs_0_) | copy-start | bytes 608260
  26.0 5.6 %collective-permute-start.14 = (bf16[80,1152]{1,0:T(8,128)(2,1)S(1)}, bf16[80,1152]{1,0:T(8,128)(2,1)S(1)}, u32[]{:S(2)}, u32[]{:S(2)}) collective-permute-start(bf16[80,1152]{1,0:T(8,128)(2,1)S(1)} %get-tuple-element.52), channel_id=1, source_target_pairs={{0,1},{1,0},{2,3},{3,2},{4,5},{5,4},{6,7},{7,6},{8,9},{9,8},{10,11... | collective-permute-start | bytes 552968 | tf_op jit(solution)/shard_map/ppermute | solution.py:19
  27.6 7.2 %collective-permute-start.17 = (bf16[80,1152]{1,0:T(8,128)(2,1)S(1)}, bf16[80,1152]{1,0:T(8,128)(2,1)S(1)}, u32[]{:S(2)}, u32[]{:S(2)}) collective-permute-start(bf16[80,1152]{1,0:T(8,128)(2,1)S(1)} %get-tuple-element.55), channel_id=1, source_target_pairs={{0,1},{1,0},{2,3},{3,2},{4,5},{5,4},{6,7},{7,6},{8,9},{9,8},{10,11... | collective-permute-start | bytes 552968 | tf_op jit(solution)/shard_map/ppermute | solution.py:19
  29.8 9.9 %collective-permute-start.16 = (f32[80,1152]{1,0:T(8,128)S(1)}, f32[80,1152]{1,0:T(8,128)S(1)}, u32[]{:S(2)}, u32[]{:S(2)}) collective-permute-start(f32[80,1152]{1,0:T(8,128)S(1)} %get-tuple-element.53), channel_id=1, source_target_pairs={{0,16},{16,0},{1,17},{17,1},{2,18},{18,2},{3,19},{19,3},{4,20},{20... | collective-permute-start | bytes 1105928 | tf_op jit(solution)/shard_map/ppermute | solution.py:23
  31.6 8.1 %collective-permute-start.15 = (bf16[80,1152]{1,0:T(8,128)(2,1)S(1)}, bf16[80,1152]{1,0:T(8,128)(2,1)S(1)}, u32[]{:S(2)}, u32[]{:S(2)}) collective-permute-start(bf16[80,1152]{1,0:T(8,128)(2,1)S(1)} %add_convert_fusion.1), channel_id=1, source_target_pairs={{0,8},{1,9},{2,10},{3,11},{4,12},{5,13},{6,14},{7,15},{8,0},{9,1},... | collective-permute-start | bytes 552968 | tf_op jit(solution)/shard_map/ppermute | solution.py:19
  34.9 7.7 %collective-permute-start.18 = (bf16[80,1152]{1,0:T(8,128)(2,1)S(1)}, bf16[80,1152]{1,0:T(8,128)(2,1)S(1)}, u32[]{:S(2)}, u32[]{:S(2)}) collective-permute-start(bf16[80,1152]{1,0:T(8,128)(2,1)S(1)} %add_convert_fusion), channel_id=1, source_target_pairs={{0,24},{1,25},{2,26},{3,27},{4,28},{5,29},{6,30},{7,31},{8,16},{9,... | collective-permute-start | bytes 552968 | tf_op jit(solution)/shard_map/ppermute | solution.py:19
  36.7 5.9 %collective-permute-start.19 = (bf16[80,1152]{1,0:T(8,128)(2,1)S(1)}, bf16[80,1152]{1,0:T(8,128)(2,1)S(1)}, u32[]{:S(2)}, u32[]{:S(2)}) collective-permute-start(bf16[80,1152]{1,0:T(8,128)(2,1)S(1)} %get-tuple-element.57), channel_id=1, source_target_pairs={{0,1},{1,0},{2,3},{3,2},{4,5},{5,4},{6,7},{7,6},{8,9},{9,8},{10,11... | collective-permute-start | bytes 552968 | tf_op jit(solution)/shard_map/ppermute | solution.py:19
  37.4 7.4 %collective-permute-start.20 = (bf16[80,1152]{1,0:T(8,128)(2,1)S(1)}, bf16[80,1152]{1,0:T(8,128)(2,1)S(1)}, u32[]{:S(2)}, u32[]{:S(2)}) collective-permute-start(bf16[80,1152]{1,0:T(8,128)(2,1)S(1)} %get-tuple-element.59), channel_id=1, source_target_pairs={{0,17},{1,16},{2,19},{3,18},{4,21},{5,20},{6,23},{7,22},{8,25},{9,... | collective-permute-start | bytes 552968 | tf_op jit(solution)/shard_map/ppermute | solution.py:19

commit v6 on v5

--- a/solution.py
+++ b/solution.py
@@ -307,7 +307,7 @@
     crossed = swap(own_cross)
     far_cross = (far_cross + in_cross.astype(f32)).astype(bf16)
     far_stay = (far_stay + in_stay.astype(f32)).astype(bf16)
-    near_stay, _ = lax.optimization_barrier((near_stay, far_cross))
+    near_stay, _ = lax.optimization_barrier((near_stay, far_stay))
     near_stay = hop(near_stay, *near)
     near_cross, _, _ = lax.optimization_barrier((near_cross, far_cross, far_stay))
     far_cross = hop(far_cross, *far, across=True)

time: 45.9 us -> 44.5 us (0.969)
  waiting for transfers between devices: 7.4 us -> 5.71 us
    ppermute x12, waiting for transfers between devices: 7.17 us -> 5.48 us  [hop(): return lax.ppermute(block, ('row', 'col'), route)]
  transfers between devices with their start and end apart: 21 -> 21, of which waited for: 6 -> 5; matrix products, arithmetic and copies ran while one was open for 0% -> 0% of each run, Pallas kernels for 11% -> 11%
where the time goes in v6:
time: 44.5 us; the launch traced here: 44.2 us
  starting transfers between devices  24.5 us (55%)
  Pallas kernels  8.53 us (19%)
  waiting for transfers between devices  5.71 us (13%)
  between operations  3.37 us (8%)
  local copies, waits for them, and re-layouts  1.86 us (4%)
    ppermute x12, starting transfers between devices, hop(): return lax.ppermute(block, ('row', 'col'), route)  22.4 us
    pallas_call x6, Pallas kernels, call(): pl.pallas_call(kernel, out_shape=out_shape, in_specs=[pl.BlockSpec(memory...  6.7 us
    ppermute x12, waiting for transfers between devices, hop(): return lax.ppermute(block, ('row', 'col'), route)  5.48 us
    ppermute x9, starting transfers between devices, swap(): return lax.ppermute(block, 'row', [(0, 1), (1, 0)])  2.13 us
    unnamed x8, local copies, waits for them, and re-layouts  1.86 us
    pallas_call x1, Pallas kernels, pair_body(): pl.pallas_call(first_kernel, out_shape=(sent, sent), in_specs=[pl.BlockSp...  1.84 us
  transfers between devices with their start and end apart: 21, of which 5 were waited for; matrix products, arithmetic and copies ran while one was open for 0% of the time, Pallas kernels for 11%

profile of v6, /device:TPU:0, one launch (start us, length us, event | category | flops | bytes accessed | tf_op | source)
XLA Modules:
  0.0 44.2 jit_solution(2732543886825694580)
XLA Ops:
  0.6 1.8 %shard_map.95 = (bf16[88,1152]{1,0:T(8,128)(2,1)}, bf16[88,1152]{1,0:T(8,128)(2,1)}) custom-call(s32[1]{0:T(128)} %bitcast.spot_ref.row_ref, bf16[80,1152]{1,0:T(8,128)(2,1)} %image_ref.1, bf16[160,576]{1,0:T(8,128)(2,1)} %text_ref.1, s32[1,80]{1,0:T(1,128)} %bitcast.5, s32[1,160]{1,0:T(1,128)} %bitcast.4), custom_call_target="tpu_custom_call" | custom-call | tf_op jit(solution)/shard_map/pallas_call | solution.py:266
  2.5 0.5 %collective-permute-start.1 = (bf16[88,1152]{1,0:T(8,128)(2,1)}, bf16[88,1152]{1,0:T(8,128)(2,1)S(1)}, u32[]{:S(2)}, u32[]{:S(2)}) collective-permute-start(bf16[88,1152]{1,0:T(8,128)(2,1)} %get-tuple-element.37.refs_7_.refs_3_), channel_id=1, source_target_pairs={{0,16},{16,0},{1,17},{17,1},{2,18},{18,2},{3,19},{19,3},{4,20},{20... | collective-permute-start | bytes 608264 | tf_op jit(solution)/shard_map/ppermute | solution.py:23
  3.0 3.7 %collective-permute-start.3 = (bf16[88,1152]{1,0:T(8,128)(2,1)}, bf16[88,1152]{1,0:T(8,128)(2,1)S(1)}, u32[]{:S(2)}, u32[]{:S(2)}) collective-permute-start(bf16[88,1152]{1,0:T(8,128)(2,1)} %get-tuple-element.31.refs_0_), channel_id=1, source_target_pairs={{0,8},{1,9},{2,10},{3,11},{4,12},{5,13},{6,14},{7,15},{8,0},{9,1},... | collective-permute-start | bytes 608264 | tf_op jit(solution)/shard_map/ppermute | solution.py:19
  6.7 1.5 %collective-permute-start = (bf16[88,1152]{1,0:T(8,128)(2,1)}, bf16[88,1152]{1,0:T(8,128)(2,1)S(1)}, u32[]{:S(2)}, u32[]{:S(2)}) collective-permute-start(bf16[88,1152]{1,0:T(8,128)(2,1)} %get-tuple-element.31.refs_0_), channel_id=1, source_target_pairs={{0,1},{1,0},{2,3},{3,2},{4,5},{5,4},{6,7},{7,6},{8,9},{9,8},{10,11... | collective-permute-start | bytes 608264 | tf_op jit(solution)/shard_map/ppermute | solution.py:19
  8.2 0.0 collective-permute-start.5
  8.2 0.0 collective-permute-done.1.refs_1_
  8.2 1.5 %collective-permute-start.4 = (bf16[88,1152]{1,0:T(8,128)(2,1)S(1)}, bf16[88,1152]{1,0:T(8,128)(2,1)S(1)}, u32[]{:S(2)}, u32[]{:S(2)}) collective-permute-start(bf16[88,1152]{1,0:T(8,128)(2,1)S(1)} %collective-permute-done.1.refs_1_), channel_id=1, source_target_pairs={{0,8},{1,9},{2,10},{3,11},{4,12},{5,13},{6,14},{7,15},{8,0},{9,1},... | collective-permute-start | bytes 608264 | tf_op jit(solution)/shard_map/ppermute | solution.py:19
  9.6 1.5 %collective-permute-start.2 = (bf16[88,1152]{1,0:T(8,128)(2,1)S(1)}, bf16[88,1152]{1,0:T(8,128)(2,1)S(1)}, u32[]{:S(2)}, u32[]{:S(2)}) collective-permute-start(bf16[88,1152]{1,0:T(8,128)(2,1)S(1)} %collective-permute-done.1.refs_1_), channel_id=1, source_target_pairs={{0,1},{1,0},{2,3},{3,2},{4,5},{5,4},{6,7},{7,6},{8,9},{9,8},{10,11... | collective-permute-start | bytes 608264 | tf_op jit(solution)/shard_map/ppermute | solution.py:19
  11.1 0.5 %collective-permute-done.3.refs_4_ = bf16[88,1152]{1,0:T(8,128)(2,1)S(1)} collective-permute-done((bf16[88,1152]{1,0:T(8,128)(2,1)}, bf16[88,1152]{1,0:T(8,128)(2,1)S(1)}, u32[]{:S(2)}, u32[]{:S(2)}) %collective-permute-start.3) | collective-permute-done | bytes 202784 | tf_op jit(solution)/shard_map/ppermute | solution.py:19
  11.6 2.1 %collective-permute-start.10 = (bf16[88,1152]{1,0:T(8,128)(2,1)S(1)}, bf16[88,1152]{1,0:T(8,128)(2,1)S(1)}, u32[]{:S(2)}, u32[]{:S(2)}) collective-permute-start(bf16[88,1152]{1,0:T(8,128)(2,1)S(1)} %collective-permute-done.3.refs_4_), channel_id=1, source_target_pairs={{0,1},{1,0},{2,3},{3,2},{4,5},{5,4},{6,7},{7,6},{8,9},{9,8},{10,11... | collective-permute-start | bytes 608264 | tf_op jit(solution)/shard_map/ppermute | solution.py:19
  13.7 0.0 collective-permute-done.refs_2_
  13.7 0.0 collective-permute-start.8
  16.4 0.0 collective-permute-done.5.refs_6_.refs_2_
  16.4 0.6 %collective-permute-start.6 = (bf16[88,1152]{1,0:T(8,128)(2,1)S(1)}, bf16[88,1152]{1,0:T(8,128)(2,1)S(1)}, u32[]{:S(2)}, u32[]{:S(2)}) collective-permute-start(bf16[88,1152]{1,0:T(8,128)(2,1)S(1)} %collective-permute-done.refs_2_), channel_id=1, source_target_pairs={{0,16},{16,0},{1,17},{17,1},{2,18},{18,2},{3,19},{19,3},{4,20},{20... | collective-permute-start | bytes 608264 | tf_op jit(solution)/shard_map/ppermute | solution.py:23
  17.0 0.0 collective-permute-done.4.refs_5_
  17.0 0.1 collective-permute-start.9
  17.1 0.4 collective-permute-start.7
  17.5 0.1 collective-permute-done.10.refs_0_
  17.5 0.0 collective-permute-start.11
  17.6 1.9 %collective-permute-start.12 = (bf16[88,1152]{1,0:T(8,128)(2,1)S(1)}, bf16[88,1152]{1,0:T(8,128)(2,1)S(1)}, u32[]{:S(2)}, u32[]{:S(2)}) collective-permute-start(bf16[88,1152]{1,0:T(8,128)(2,1)S(1)} %collective-permute-done.4.refs_5_), channel_id=1, source_target_pairs={{0,1},{1,0},{2,3},{3,2},{4,5},{5,4},{6,7},{7,6},{8,9},{9,8},{10,11... | collective-permute-start | bytes 608264 | tf_op jit(solution)/shard_map/ppermute | solution.py:19
  19.5 0.0 collective-permute-done.7.refs_9_.refs_5_
  19.5 0.0 collective-permute-done.11.refs_2_.refs_6_
  19.5 0.0 copy-start
  19.5 0.9 %copy-done = bf16[88,1152]{1,0:T(8,128)(2,1)S(1)} copy-done((bf16[88,1152]{1,0:T(8,128)(2,1)S(1)}, bf16[88,1152]{1,0:T(8,128)(2,1)}, u32[]{:S(2)}) %copy-start) | copy-done | bytes 202776
  20.4 0.9 %copy-done.2 = bf16[88,1152]{1,0:T(8,128)(2,1)S(1)} copy-done((bf16[88,1152]{1,0:T(8,128)(2,1)S(1)}, bf16[88,1152]{1,0:T(8,128)(2,1)}, u32[]{:S(2)}) %copy-start.2) | copy-done | bytes 202776
  21.4 2.2 %shard_map.97 = (bf16[480,1152]{1,0:T(8,128)(2,1)S(1)}, bf16[480,1152]{1,0:T(8,128)(2,1)S(1)}, f32[480,1152]{1,0:T(8,128)S(1)}) custom-call(s32[1]{0:T(128)} %bitcast.spot_ref.row_ref, s32[1]{0:T(128)} %bitcast.1.col_ref, f32[8,128]{1,0:T(8,128)S(1)} %shard_map.96.number_ref, bf16[88,1152]{1,0:T(8,128)(2,1)S(1)} %copy-done, ...), custom_call_target="tpu_custom_call" | custom-call | flops 1061683200 | bytes 6860808 | tf_op jit(solution)/shard_map/pallas_call | solution.py:240
  23.6 0.0 collective-permute-done.12.refs_1_
  23.6 0.3 collective-permute-start.13
  23.9 0.9 %shard_map.98 = (bf16[160,1152]{1,0:T(8,128)(2,1)S(1)}, f32[160,1152]{1,0:T(8,128)S(1)}) custom-call(s32[1]{0:T(128)} %bitcast.spot_ref.row_ref, s32[1]{0:T(128)} %bitcast.1.col_ref, f32[8,128]{1,0:T(8,128)S(1)} %shard_map.96.number_ref, bf16[88,1152]{1,0:T(8,128)(2,1)S(1)} %collective-permute-done.10.refs_0_, ...), custom_call_target="tpu_custom_call" | custom-call | flops 353894400 | bytes 3837960 | tf_op jit(solution)/shard_map/pallas_call | solution.py:240
  24.9 0.0 copy-start.1
  24.9 0.2 collective-permute-done.13.refs_3_.refs_7_
  25.1 0.9 %shard_map.99 = (bf16[160,1152]{1,0:T(8,128)(2,1)S(1)}, bf16[80,1152]{1,0:T(8,128)(2,1)S(1)}, bf16[80,1152]{1,0:T(8,128)(2,1)S(1)}) custom-call(s32[1]{0:T(128)} %bitcast.spot_ref.row_ref, s32[1]{0:T(128)} %bitcast.1.col_ref, f32[8,128]{1,0:T(8,128)S(1)} %shard_map.96.number_ref, bf16[88,1152]{1,0:T(8,128)(2,1)S(1)} %collective-permute-done.10.refs_0_, ...), custom_call_target="tpu_custom_call" | custom-call | flops 117964800 | bytes 2658312 | tf_op jit(solution)/shard_map/pallas_call | solution.py:240
  26.0 1.6 %collective-permute-start.14 = (bf16[80,1152]{1,0:T(8,128)(2,1)S(1)}, bf16[80,1152]{1,0:T(8,128)(2,1)S(1)}, u32[]{:S(2)}, u32[]{:S(2)}) collective-permute-start(bf16[80,1152]{1,0:T(8,128)(2,1)S(1)} %get-tuple-element.52), channel_id=1, source_target_pairs={{0,1},{1,0},{2,3},{3,2},{4,5},{5,4},{6,7},{7,6},{8,9},{9,8},{10,11... | collective-permute-start | bytes 552968 | tf_op jit(solution)/shard_map/ppermute | solution.py:19
  27.6 0.4 %collective-permute-start.17 = (bf16[80,1152]{1,0:T(8,128)(2,1)S(1)}, bf16[80,1152]{1,0:T(8,128)(2,1)S(1)}, u32[]{:S(2)}, u32[]{:S(2)}) collective-permute-start(bf16[80,1152]{1,0:T(8,128)(2,1)S(1)} %get-tuple-element.55), channel_id=1, source_target_pairs={{0,1},{1,0},{2,3},{3,2},{4,5},{5,4},{6,7},{7,6},{8,9},{9,8},{10,11... | collective-permute-start | bytes 552968 | tf_op jit(solution)/shard_map/ppermute | solution.py:19
  28.1 1.7 %shard_map.100 = (f32[80,1152]{1,0:T(8,128)S(1)}, f32[80,1152]{1,0:T(8,128)S(1)}, bf16[80,1152]{1,0:T(8,128)(2,1)S(1)}, bf16[80,1152]{1,0:T(8,128)(2,1)S(1)}, f3...) custom-call(s32[1]{0:T(128)} %bitcast.spot_ref.row_ref, s32[1]{0:T(128)} %bitcast.1.col_ref, ...), custom_call_target="tpu_custom_call" | custom-call | flops 353894400 | bytes 7155720 | tf_op jit(solution)/shard_map/pallas_call | solution.py:240
  29.8 0.1 collective-permute-start.16
  29.9 1.7 %collective-permute-done.14 = bf16[80,1152]{1,0:T(8,128)(2,1)S(1)} collective-permute-done((bf16[80,1152]{1,0:T(8,128)(2,1)S(1)}, bf16[80,1152]{1,0:T(8,128)(2,1)S(1)}, u32[]{:S(2)}, u32[]{:S(2)}) %collective-permute-start.14) | collective-permute-done | bytes 184352 | tf_op jit(solution)/shard_map/ppermute | solution.py:19
  31.6 3.2 %collective-permute-start.15 = (bf16[80,1152]{1,0:T(8,128)(2,1)S(1)}, bf16[80,1152]{1,0:T(8,128)(2,1)S(1)}, u32[]{:S(2)}, u32[]{:S(2)}) collective-permute-start(bf16[80,1152]{1,0:T(8,128)(2,1)S(1)} %add_convert_fusion.1), channel_id=1, source_target_pairs={{0,8},{1,9},{2,10},{3,11},{4,12},{5,13},{6,14},{7,15},{8,0},{9,1},... | collective-permute-start | bytes 552968 | tf_op jit(solution)/shard_map/ppermute | solution.py:19
  34.8 1.6 %collective-permute-start.19 = (bf16[80,1152]{1,0:T(8,128)(2,1)S(1)}, bf16[80,1152]{1,0:T(8,128)(2,1)S(1)}, u32[]{:S(2)}, u32[]{:S(2)}) collective-permute-start(bf16[80,1152]{1,0:T(8,128)(2,1)S(1)} %get-tuple-element.57), channel_id=1, source_target_pairs={{0,1},{1,0},{2,3},{3,2},{4,5},{5,4},{6,7},{7,6},{8,9},{9,8},{10,11... | collective-permute-start | bytes 552968 | tf_op jit(solution)/shard_map/ppermute | solution.py:19
  36.4 0.0 collective-permute-done.17
  36.5 1.4 %collective-permute-start.18 = (bf16[80,1152]{1,0:T(8,128)(2,1)S(1)}, bf16[80,1152]{1,0:T(8,128)(2,1)S(1)}, u32[]{:S(2)}, u32[]{:S(2)}) collective-permute-start(bf16[80,1152]{1,0:T(8,128)(2,1)S(1)} %add_convert_fusion), channel_id=1, source_target_pairs={{0,24},{1,25},{2,26},{3,27},{4,28},{5,29},{6,30},{7,31},{8,16},{9,... | collective-permute-start | bytes 552968 | tf_op jit(solution)/shard_map/ppermute | solution.py:19
  37.9 1.9 %collective-permute-start.20 = (bf16[80,1152]{1,0:T(8,128)(2,1)S(1)}, bf16[80,1152]{1,0:T(8,128)(2,1)S(1)}, u32[]{:S(2)}, u32[]{:S(2)}) collective-permute-start(bf16[80,1152]{1,0:T(8,128)(2,1)S(1)} %get-tuple-element.59), channel_id=1, source_target_pairs={{0,17},{1,16},{2,19},{3,18},{4,21},{5,20},{6,23},{7,22},{8,25},{9,... | collective-permute-start | bytes 552968 | tf_op jit(solution)/shard_map/ppermute | solution.py:19
  39.8 0.0 collective-permute-done.15
  39.9 0.0 collective-permute-done.16
  39.9 3.3 %collective-permute-done.18 = bf16[80,1152]{1,0:T(8,128)(2,1)S(1)} collective-permute-done((bf16[80,1152]{1,0:T(8,128)(2,1)S(1)}, bf16[80,1152]{1,0:T(8,128)(2,1)S(1)}, u32[]{:S(2)}, u32[]{:S(2)}) %collective-permute-start.18) | collective-permute-done | bytes 184352 | tf_op jit(solution)/shard_map/ppermute | solution.py:19
  43.2 0.0 collective-permute-done.19.near_stay_ref
  43.2 0.0 collective-permute-done.20.near_cross_ref
  43.2 0.9 %shard_map.101 = (bf16[80,1152]{1,0:T(8,128)(2,1)}, bf16[160,576]{1,0:T(8,128)(2,1)}) custom-call(s32[1]{0:T(128)} %bitcast.spot_ref.row_ref, f32[80,1152]{1,0:T(8,128)S(1)} %convert_add_fusion.1.stay_ref, f32[80,1152]{1,0:T(8,128)S(1)} %convert_add_fusion.crossed_ref, bf16[80,1152]{1,0:T(8,128)(2,1)S(1)} %collective-permute-done.19.near_stay_ref, ...), custom_call_target="tpu_custom_call" | custom-call | bytes 1474564 | tf_op jit(solution)/shard_map/pallas_call | solution.py:240
  (13 shorter events, 0.2 us)
Async XLA Ops:
  2.5 5.7 %collective-permute-start.1 = (bf16[88,1152]{1,0:T(8,128)(2,1)}, bf16[88,1152]{1,0:T(8,128)(2,1)S(1)}, u32[]{:S(2)}, u32[]{:S(2)}) collective-permute-start(bf16[88,1152]{1,0:T(8,128)(2,1)} %get-tuple-element.37.refs_7_.refs_3_), channel_id=1, source_target_pairs={{0,16},{16,0},{1,17},{17,1},{2,18},{18,2},{3,19},{19,3},{4,20},{20... | collective-permute-start | bytes 608264 | tf_op jit(solution)/shard_map/ppermute | solution.py:23
  3.0 8.6 %collective-permute-start.3 = (bf16[88,1152]{1,0:T(8,128)(2,1)}, bf16[88,1152]{1,0:T(8,128)(2,1)S(1)}, u32[]{:S(2)}, u32[]{:S(2)}) collective-permute-start(bf16[88,1152]{1,0:T(8,128)(2,1)} %get-tuple-element.31.refs_0_), channel_id=1, source_target_pairs={{0,8},{1,9},{2,10},{3,11},{4,12},{5,13},{6,14},{7,15},{8,0},{9,1},... | collective-permute-start | bytes 608264 | tf_op jit(solution)/shard_map/ppermute | solution.py:19
  6.7 7.1 %collective-permute-start = (bf16[88,1152]{1,0:T(8,128)(2,1)}, bf16[88,1152]{1,0:T(8,128)(2,1)S(1)}, u32[]{:S(2)}, u32[]{:S(2)}) collective-permute-start(bf16[88,1152]{1,0:T(8,128)(2,1)} %get-tuple-element.31.refs_0_), channel_id=1, source_target_pairs={{0,1},{1,0},{2,3},{3,2},{4,5},{5,4},{6,7},{7,6},{8,9},{9,8},{10,11... | collective-permute-start | bytes 608264 | tf_op jit(solution)/shard_map/ppermute | solution.py:19
  8.2 8.2 %collective-permute-start.5 = (bf16[88,1152]{1,0:T(8,128)(2,1)}, bf16[88,1152]{1,0:T(8,128)(2,1)S(1)}, u32[]{:S(2)}, u32[]{:S(2)}) collective-permute-start(bf16[88,1152]{1,0:T(8,128)(2,1)} %get-tuple-element.31.refs_0_), channel_id=1, source_target_pairs={{0,16},{16,0},{1,17},{17,1},{2,18},{18,2},{3,19},{19,3},{4,20},{20... | collective-permute-start | bytes 608264 | tf_op jit(solution)/shard_map/ppermute | solution.py:23
  8.2 8.8 %collective-permute-start.4 = (bf16[88,1152]{1,0:T(8,128)(2,1)S(1)}, bf16[88,1152]{1,0:T(8,128)(2,1)S(1)}, u32[]{:S(2)}, u32[]{:S(2)}) collective-permute-start(bf16[88,1152]{1,0:T(8,128)(2,1)S(1)} %collective-permute-done.1.refs_1_), channel_id=1, source_target_pairs={{0,8},{1,9},{2,10},{3,11},{4,12},{5,13},{6,14},{7,15},{8,0},{9,1},... | collective-permute-start | bytes 608264 | tf_op jit(solution)/shard_map/ppermute | solution.py:19
  9.6 7.4 %collective-permute-start.2 = (bf16[88,1152]{1,0:T(8,128)(2,1)S(1)}, bf16[88,1152]{1,0:T(8,128)(2,1)S(1)}, u32[]{:S(2)}, u32[]{:S(2)}) collective-permute-start(bf16[88,1152]{1,0:T(8,128)(2,1)S(1)} %collective-permute-done.1.refs_1_), channel_id=1, source_target_pairs={{0,1},{1,0},{2,3},{3,2},{4,5},{5,4},{6,7},{7,6},{8,9},{9,8},{10,11... | collective-permute-start | bytes 608264 | tf_op jit(solution)/shard_map/ppermute | solution.py:19
  11.6 6.0 %collective-permute-start.10 = (bf16[88,1152]{1,0:T(8,128)(2,1)S(1)}, bf16[88,1152]{1,0:T(8,128)(2,1)S(1)}, u32[]{:S(2)}, u32[]{:S(2)}) collective-permute-start(bf16[88,1152]{1,0:T(8,128)(2,1)S(1)} %collective-permute-done.3.refs_4_), channel_id=1, source_target_pairs={{0,1},{1,0},{2,3},{3,2},{4,5},{5,4},{6,7},{7,6},{8,9},{9,8},{10,11... | collective-permute-start | bytes 608264 | tf_op jit(solution)/shard_map/ppermute | solution.py:19
  13.7 3.8 %collective-permute-start.8 = (bf16[88,1152]{1,0:T(8,128)(2,1)S(1)}, bf16[88,1152]{1,0:T(8,128)(2,1)S(1)}, u32[]{:S(2)}, u32[]{:S(2)}) collective-permute-start(bf16[88,1152]{1,0:T(8,128)(2,1)S(1)} %collective-permute-done.3.refs_4_), channel_id=1, source_target_pairs={{0,16},{16,0},{1,17},{17,1},{2,18},{18,2},{3,19},{19,3},{4,20},{20... | collective-permute-start | bytes 608264 | tf_op jit(solution)/shard_map/ppermute | solution.py:23
  16.4 3.1 %collective-permute-start.6 = (bf16[88,1152]{1,0:T(8,128)(2,1)S(1)}, bf16[88,1152]{1,0:T(8,128)(2,1)S(1)}, u32[]{:S(2)}, u32[]{:S(2)}) collective-permute-start(bf16[88,1152]{1,0:T(8,128)(2,1)S(1)} %collective-permute-done.refs_2_), channel_id=1, source_target_pairs={{0,16},{16,0},{1,17},{17,1},{2,18},{18,2},{3,19},{19,3},{4,20},{20... | collective-permute-start | bytes 608264 | tf_op jit(solution)/shard_map/ppermute | solution.py:23
  17.0 2.5 %collective-permute-start.9 = (bf16[88,1152]{1,0:T(8,128)(2,1)S(1)}, bf16[88,1152]{1,0:T(8,128)(2,1)S(1)}, u32[]{:S(2)}, u32[]{:S(2)}) collective-permute-start(bf16[88,1152]{1,0:T(8,128)(2,1)S(1)} %collective-permute-done.4.refs_5_), channel_id=1, source_target_pairs={{0,16},{16,0},{1,17},{17,1},{2,18},{18,2},{3,19},{19,3},{4,20},{20... | collective-permute-start | bytes 608264 | tf_op jit(solution)/shard_map/ppermute | solution.py:23
  17.1 2.4 %collective-permute-start.7 = (bf16[88,1152]{1,0:T(8,128)(2,1)S(1)}, bf16[88,1152]{1,0:T(8,128)(2,1)S(1)}, u32[]{:S(2)}, u32[]{:S(2)}) collective-permute-start(bf16[88,1152]{1,0:T(8,128)(2,1)S(1)} %collective-permute-done.2.refs_3_), channel_id=1, source_target_pairs={{0,16},{16,0},{1,17},{17,1},{2,18},{18,2},{3,19},{19,3},{4,20},{20... | collective-permute-start | bytes 608264 | tf_op jit(solution)/shard_map/ppermute | solution.py:23
  17.5 1.9 %collective-permute-start.11 = (bf16[88,1152]{1,0:T(8,128)(2,1)S(1)}, bf16[88,1152]{1,0:T(8,128)(2,1)S(1)}, u32[]{:S(2)}, u32[]{:S(2)}) collective-permute-start(bf16[88,1152]{1,0:T(8,128)(2,1)S(1)} %collective-permute-done.10.refs_0_), channel_id=1, source_target_pairs={{0,16},{16,0},{1,17},{17,1},{2,18},{18,2},{3,19},{19,3},{4,20},{20... | collective-permute-start | bytes 608264 | tf_op jit(solution)/shard_map/ppermute | solution.py:23
  17.6 6.0 %collective-permute-start.12 = (bf16[88,1152]{1,0:T(8,128)(2,1)S(1)}, bf16[88,1152]{1,0:T(8,128)(2,1)S(1)}, u32[]{:S(2)}, u32[]{:S(2)}) collective-permute-start(bf16[88,1152]{1,0:T(8,128)(2,1)S(1)} %collective-permute-done.4.refs_5_), channel_id=1, source_target_pairs={{0,1},{1,0},{2,3},{3,2},{4,5},{5,4},{6,7},{7,6},{8,9},{9,8},{10,11... | collective-permute-start | bytes 608264 | tf_op jit(solution)/shard_map/ppermute | solution.py:19
  19.5 0.9 %copy-start = (bf16[88,1152]{1,0:T(8,128)(2,1)S(1)}, bf16[88,1152]{1,0:T(8,128)(2,1)}, u32[]{:S(2)}) copy-start(bf16[88,1152]{1,0:T(8,128)(2,1)} %get-tuple-element.31.refs_0_) | copy-start | bytes 608260
  20.4 0.9 %copy-start.2 = (bf16[88,1152]{1,0:T(8,128)(2,1)S(1)}, bf16[88,1152]{1,0:T(8,128)(2,1)}, u32[]{:S(2)}) copy-start(bf16[88,1152]{1,0:T(8,128)(2,1)} %get-tuple-element.37.refs_7_.refs_3_) | copy-start | bytes 608260
  21.4 2.6 %copy-start.3 = (bf16[88,1152]{1,0:T(8,128)(2,1)S(1)}, bf16[88,1152]{1,0:T(8,128)(2,1)}, u32[]{:S(2)}) copy-start(bf16[88,1152]{1,0:T(8,128)(2,1)} %get-tuple-element.37.refs_7_.refs_3_) | copy-start | bytes 608260
  23.6 1.5 %collective-permute-start.13 = (bf16[88,1152]{1,0:T(8,128)(2,1)S(1)}, bf16[88,1152]{1,0:T(8,128)(2,1)S(1)}, u32[]{:S(2)}, u32[]{:S(2)}) collective-permute-start(bf16[88,1152]{1,0:T(8,128)(2,1)S(1)} %collective-permute-done.12.refs_1_), channel_id=1, source_target_pairs={{0,16},{16,0},{1,17},{17,1},{2,18},{18,2},{3,19},{19,3},{4,20},{20... | collective-permute-start | bytes 608264 | tf_op jit(solution)/shard_map/ppermute | solution.py:23
  24.9 3.2 %copy-start.1 = (bf16[88,1152]{1,0:T(8,128)(2,1)S(1)}, bf16[88,1152]{1,0:T(8,128)(2,1)}, u32[]{:S(2)}) copy-start(bf16[88,1152]{1,0:T(8,128)(2,1)} %get-tuple-element.31.refs_0_) | copy-start | bytes 608260
  26.0 5.6 %collective-permute-start.14 = (bf16[80,1152]{1,0:T(8,128)(2,1)S(1)}, bf16[80,1152]{1,0:T(8,128)(2,1)S(1)}, u32[]{:S(2)}, u32[]{:S(2)}) collective-permute-start(bf16[80,1152]{1,0:T(8,128)(2,1)S(1)} %get-tuple-element.52), channel_id=1, source_target_pairs={{0,1},{1,0},{2,3},{3,2},{4,5},{5,4},{6,7},{7,6},{8,9},{9,8},{10,11... | collective-permute-start | bytes 552968 | tf_op jit(solution)/shard_map/ppermute | solution.py:19
  27.6 8.8 %collective-permute-start.17 = (bf16[80,1152]{1,0:T(8,128)(2,1)S(1)}, bf16[80,1152]{1,0:T(8,128)(2,1)S(1)}, u32[]{:S(2)}, u32[]{:S(2)}) collective-permute-start(bf16[80,1152]{1,0:T(8,128)(2,1)S(1)} %get-tuple-element.55), channel_id=1, source_target_pairs={{0,1},{1,0},{2,3},{3,2},{4,5},{5,4},{6,7},{7,6},{8,9},{9,8},{10,11... | collective-permute-start | bytes 552968 | tf_op jit(solution)/shard_map/ppermute | solution.py:19
  29.8 10.1 %collective-permute-start.16 = (f32[80,1152]{1,0:T(8,128)S(1)}, f32[80,1152]{1,0:T(8,128)S(1)}, u32[]{:S(2)}, u32[]{:S(2)}) collective-permute-start(f32[80,1152]{1,0:T(8,128)S(1)} %get-tuple-element.53), channel_id=1, source_target_pairs={{0,16},{16,0},{1,17},{17,1},{2,18},{18,2},{3,19},{19,3},{4,20},{20... | collective-permute-start | bytes 1105928 | tf_op jit(solution)/shard_map/ppermute | solution.py:23
  31.6 8.2 %collective-permute-start.15 = (bf16[80,1152]{1,0:T(8,128)(2,1)S(1)}, bf16[80,1152]{1,0:T(8,128)(2,1)S(1)}, u32[]{:S(2)}, u32[]{:S(2)}) collective-permute-start(bf16[80,1152]{1,0:T(8,128)(2,1)S(1)} %add_convert_fusion.1), channel_id=1, source_target_pairs={{0,8},{1,9},{2,10},{3,11},{4,12},{5,13},{6,14},{7,15},{8,0},{9,1},... | collective-permute-start | bytes 552968 | tf_op jit(solution)/shard_map/ppermute | solution.py:19
  34.8 8.4 %collective-permute-start.19 = (bf16[80,1152]{1,0:T(8,128)(2,1)S(1)}, bf16[80,1152]{1,0:T(8,128)(2,1)S(1)}, u32[]{:S(2)}, u32[]{:S(2)}) collective-permute-start(bf16[80,1152]{1,0:T(8,128)(2,1)S(1)} %get-tuple-element.57), channel_id=1, source_target_pairs={{0,1},{1,0},{2,3},{3,2},{4,5},{5,4},{6,7},{7,6},{8,9},{9,8},{10,11... | collective-permute-start | bytes 552968 | tf_op jit(solution)/shard_map/ppermute | solution.py:19
  36.5 6.7 %collective-permute-start.18 = (bf16[80,1152]{1,0:T(8,128)(2,1)S(1)}, bf16[80,1152]{1,0:T(8,128)(2,1)S(1)}, u32[]{:S(2)}, u32[]{:S(2)}) collective-permute-start(bf16[80,1152]{1,0:T(8,128)(2,1)S(1)} %add_convert_fusion), channel_id=1, source_target_pairs={{0,24},{1,25},{2,26},{3,27},{4,28},{5,29},{6,30},{7,31},{8,16},{9,... | collective-permute-start | bytes 552968 | tf_op jit(solution)/shard_map/ppermute | solution.py:19
  37.9 5.3 %collective-permute-start.20 = (bf16[80,1152]{1,0:T(8,128)(2,1)S(1)}, bf16[80,1152]{1,0:T(8,128)(2,1)S(1)}, u32[]{:S(2)}, u32[]{:S(2)}) collective-permute-start(bf16[80,1152]{1,0:T(8,128)(2,1)S(1)} %get-tuple-element.59), channel_id=1, source_target_pairs={{0,17},{1,16},{2,19},{3,18},{4,21},{5,20},{6,23},{7,22},{8,25},{9,... | collective-permute-start | bytes 552968 | tf_op jit(solution)/shard_map/ppermute | solution.py:19

commit v7 on v6

--- a/solution.py
+++ b/solution.py
@@ -44,31 +44,38 @@
     ref[:half, part:] = text_ref[half:]
 
 
-def first_kernel(spot_ref, image_ref, text_ref, image_valid_ref, text_valid_ref, mine_ref, give_ref, texts, image_line,
-                 text_line, sems):
+def first_kernel(row_ref, image_ref, text_ref, image_valid_ref, text_valid_ref, mine_ref, give_ref, images, packed, texts,
+                 image_line, text_line, sems):
     half = image_ref.shape[0]
+    copies = [
+        pltpu.make_async_copy(source, target, sems.at[n])
+        for n, (source, target) in enumerate((
+            (image_ref, images.at[pl.ds(0, half)]), (image_valid_ref, image_line), (text_ref, texts),
+            (text_valid_ref, text_line)))
+    ]
+    for copy in copies:
+        copy.start()
 
     def fill(image_to, text_to):
-        copies = [
-            pltpu.make_async_copy(source, target, sems.at[n])
-            for n, (source, target) in enumerate((
-                (text_ref, texts), (image_ref, image_to.at[pl.ds(0, half)]), (image_valid_ref, image_line),
-                (text_valid_ref, text_line)))
-        ]
-        for copy in copies:
-            copy.start()
         copies[0].wait()
-        put_texts(text_to, texts)
-        for copy in copies[1:]:
-            copy.wait()
-        put_line(image_to, image_line[...])
-        put_line(text_to, text_line[...])
-
-    @pl.when(spot_ref[0] == 0)
+        copies[1].wait()
+        put_line(images, image_line[...])
+        image_out = pltpu.make_async_copy(images, image_to, sems.at[4])
+        image_out.start()
+        copies[2].wait()
+        copies[3].wait()
+        put_texts(packed, texts)
+        put_line(packed, text_line[...])
+        text_out = pltpu.make_async_copy(packed, text_to, sems.at[5])
+        text_out.start()
+        image_out.wait()
+        text_out.wait()
+
+    @pl.when(row_ref[0] == 0)
     def _():
         fill(mine_ref, give_ref)
 
-    @pl.when(spot_ref[0] != 0)
+    @pl.when(row_ref[0] != 0)
     def _():
         fill(give_ref, mine_ref)
 
@@ -215,24 +222,28 @@
     pack_sum(total[:size], texts, own_stay, own_cross)
 
 
-def last_kernel(spot_ref, stay_ref, crossed_ref, near_stay_ref, near_cross_ref, image_ref, text_ref):
+def last_kernel(row_ref, stay_ref, crossed_ref, near_stay_ref, near_cross_ref, image_ref, text_ref, images, texts, sems):
     half, part = text_ref.shape[0] // 2, text_ref.shape[1]
 
-    stay = (stay_ref[...] + near_stay_ref[...].astype(jnp.float32)).astype(image_ref.dtype)
-    crossed = (crossed_ref[...] + near_cross_ref[...].astype(jnp.float32)).astype(image_ref.dtype)
-
-    def put(images, texts):
-        image_ref[...] = images
-        text_ref[:half] = texts[:, :part]
-        text_ref[half:] = texts[:, part:]
-
-    @pl.when(spot_ref[0] == 0)
-    def _():
-        put(stay, crossed)
-
-    @pl.when(spot_ref[0] != 0)
-    def _():
-        put(crossed, stay)
+    def put(image_sums, text_sums):
+        images[...] = (image_sums[0][...] + image_sums[1][...].astype(jnp.float32)).astype(images.dtype)
+        image_out = pltpu.make_async_copy(images, image_ref, sems.at[0])
+        image_out.start()
+        rows = (text_sums[0][...] + text_sums[1][...].astype(jnp.float32)).astype(texts.dtype)
+        texts[:half] = rows[:, :part]
+        texts[half:] = rows[:, part:]
+        text_out = pltpu.make_async_copy(texts, text_ref, sems.at[1])
+        text_out.start()
+        image_out.wait()
+        text_out.wait()
+
+    @pl.when(row_ref[0] == 0)
+    def _():
+        put((stay_ref, near_stay_ref), (crossed_ref, near_cross_ref))
+
+    @pl.when(row_ref[0] != 0)
+    def _():
+        put((crossed_ref, near_cross_ref), (stay_ref, near_stay_ref))
 
 
 def call(kernel, out_shape, smem, *arrays, flops=0):
@@ -267,8 +278,9 @@
         first_kernel,
         out_shape=(sent, sent),
         in_specs=[pl.BlockSpec(memory_space=pltpu.SMEM)] + [pl.BlockSpec(memory_space=pltpu.HBM)] * 4,
-        out_specs=(pl.BlockSpec(memory_space=pltpu.VMEM),) * 2,
-        scratch_shapes=[pltpu.VMEM(a.shape, a.dtype) for a in first[1:]] + [pltpu.SemaphoreType.DMA((4,))],
+        out_specs=(pl.BlockSpec(memory_space=pltpu.HBM),) * 2,
+        scratch_shapes=[pltpu.VMEM(sent.shape, bf16)] * 2 + [pltpu.VMEM(a.shape, a.dtype) for a in first[1:]]
+        + [pltpu.SemaphoreType.DMA((6,))],
         compiler_params=pltpu.CompilerParams(vmem_limit_bytes=60 * 1024 * 1024),
     )(row, *first)
     far_a = hop(own_a, *far)
@@ -315,8 +327,15 @@
     near_cross = hop(near_cross, *near, across=True)
     own_stay = own_stay + far_stay.astype(f32)
     crossed = crossed + far_cross.astype(f32)
-    return call(last_kernel, (shape(half, bf16), jax.ShapeDtypeStruct(text_emb.shape, bf16)), 1, row, own_stay, crossed,
-                near_stay, near_cross)
+    outs = (shape(half, bf16), jax.ShapeDtypeStruct(text_emb.shape, bf16))
+    return pl.pallas_call(
+        last_kernel,
+        out_shape=outs,
+        in_specs=[pl.BlockSpec(memory_space=pltpu.SMEM)] + [pl.BlockSpec(memory_space=pltpu.VMEM)] * 4,
+        out_specs=(pl.BlockSpec(memory_space=pltpu.HBM),) * 2,
+        scratch_shapes=[pltpu.VMEM(out.shape, out.dtype) for out in outs] + [pltpu.SemaphoreType.DMA((2,))],
+        compiler_params=pltpu.CompilerParams(vmem_limit_bytes=24 * 1024 * 1024),
+    )(row, own_stay, crossed, near_stay, near_cross)
 
 
 def partner(block, axis, distance):

time: 44.5 us -> 44.4 us (level)
    pallas_call x6 -> x5, Pallas kernels: 6.7 us -> 5.77 us  [call(): pl.pallas_call(kernel, out_shape=out_shape, in_specs=[pl.BlockSpec(memory...]
    pallas_call x0 -> x1, Pallas kernels: none -> 0.85 us  [pair_body(): pl.pallas_call(last_kernel, out_shape=outs, in_specs=[pl.BlockSpec(memory...]
where the time goes in v7:
time: 44.4 us; the launch traced here: 44.1 us
  starting transfers between devices  24.5 us (55%)
  Pallas kernels  8.48 us (19%)
  waiting for transfers between devices  5.71 us (13%)
  between operations  3.37 us (8%)
  local copies, waits for them, and re-layouts  1.86 us (4%)
    ppermute x12, starting transfers between devices, hop(): return lax.ppermute(block, ('row', 'col'), route)  22.4 us
    pallas_call x5, Pallas kernels, call(): pl.pallas_call(kernel, out_shape=out_shape, in_specs=[pl.BlockSpec(memory...  5.77 us
    ppermute x12, waiting for transfers between devices, hop(): return lax.ppermute(block, ('row', 'col'), route)  5.48 us
    ppermute x9, starting transfers between devices, swap(): return lax.ppermute(block, 'row', [(0, 1), (1, 0)])  2.12 us
    pallas_call x1, Pallas kernels, pair_body(): pl.pallas_call(first_kernel, out_shape=(sent, sent), in_specs=[pl.BlockSp...  1.87 us
    unnamed x8, local copies, waits for them, and re-layouts  1.86 us
  transfers between devices with their start and end apart: 21, of which 5 were waited for; matrix products, arithmetic and copies ran while one was open for 0% of the time, Pallas kernels for 11%

profile of v7, /device:TPU:0, one launch (start us, length us, event | category | flops | bytes accessed | tf_op | source)
XLA Modules:
  0.0 44.1 jit_solution(10146874529858855956)
XLA Ops:
  0.6 1.9 %shard_map.95 = (bf16[88,1152]{1,0:T(8,128)(2,1)}, bf16[88,1152]{1,0:T(8,128)(2,1)}) custom-call(s32[1]{0:T(128)} %bitcast.row_ref, bf16[80,1152]{1,0:T(8,128)(2,1)} %image_ref.1, bf16[160,576]{1,0:T(8,128)(2,1)} %text_ref.1, s32[1,80]{1,0:T(1,128)} %bitcast.5, s32[1,160]{1,0:T(1,128)} %bitcast.4), custom_call_target="tpu_custom_call" | custom-call | tf_op jit(solution)/shard_map/pallas_call | solution.py:277
  2.5 0.5 %collective-permute-start.1 = (bf16[88,1152]{1,0:T(8,128)(2,1)}, bf16[88,1152]{1,0:T(8,128)(2,1)S(1)}, u32[]{:S(2)}, u32[]{:S(2)}) collective-permute-start(bf16[88,1152]{1,0:T(8,128)(2,1)} %get-tuple-element.37.refs_7_.refs_3_), channel_id=1, source_target_pairs={{0,16},{16,0},{1,17},{17,1},{2,18},{18,2},{3,19},{19,3},{4,20},{20... | collective-permute-start | bytes 608264 | tf_op jit(solution)/shard_map/ppermute | solution.py:23
  3.0 3.7 %collective-permute-start.3 = (bf16[88,1152]{1,0:T(8,128)(2,1)}, bf16[88,1152]{1,0:T(8,128)(2,1)S(1)}, u32[]{:S(2)}, u32[]{:S(2)}) collective-permute-start(bf16[88,1152]{1,0:T(8,128)(2,1)} %get-tuple-element.31.refs_0_), channel_id=1, source_target_pairs={{0,8},{1,9},{2,10},{3,11},{4,12},{5,13},{6,14},{7,15},{8,0},{9,1},... | collective-permute-start | bytes 608264 | tf_op jit(solution)/shard_map/ppermute | solution.py:19
  6.7 1.5 %collective-permute-start = (bf16[88,1152]{1,0:T(8,128)(2,1)}, bf16[88,1152]{1,0:T(8,128)(2,1)S(1)}, u32[]{:S(2)}, u32[]{:S(2)}) collective-permute-start(bf16[88,1152]{1,0:T(8,128)(2,1)} %get-tuple-element.31.refs_0_), channel_id=1, source_target_pairs={{0,1},{1,0},{2,3},{3,2},{4,5},{5,4},{6,7},{7,6},{8,9},{9,8},{10,11... | collective-permute-start | bytes 608264 | tf_op jit(solution)/shard_map/ppermute | solution.py:19
  8.2 0.0 collective-permute-start.5
  8.2 0.0 collective-permute-done.1.refs_1_
  8.2 1.5 %collective-permute-start.4 = (bf16[88,1152]{1,0:T(8,128)(2,1)S(1)}, bf16[88,1152]{1,0:T(8,128)(2,1)S(1)}, u32[]{:S(2)}, u32[]{:S(2)}) collective-permute-start(bf16[88,1152]{1,0:T(8,128)(2,1)S(1)} %collective-permute-done.1.refs_1_), channel_id=1, source_target_pairs={{0,8},{1,9},{2,10},{3,11},{4,12},{5,13},{6,14},{7,15},{8,0},{9,1},... | collective-permute-start | bytes 608264 | tf_op jit(solution)/shard_map/ppermute | solution.py:19
  9.7 1.5 %collective-permute-start.2 = (bf16[88,1152]{1,0:T(8,128)(2,1)S(1)}, bf16[88,1152]{1,0:T(8,128)(2,1)S(1)}, u32[]{:S(2)}, u32[]{:S(2)}) collective-permute-start(bf16[88,1152]{1,0:T(8,128)(2,1)S(1)} %collective-permute-done.1.refs_1_), channel_id=1, source_target_pairs={{0,1},{1,0},{2,3},{3,2},{4,5},{5,4},{6,7},{7,6},{8,9},{9,8},{10,11... | collective-permute-start | bytes 608264 | tf_op jit(solution)/shard_map/ppermute | solution.py:19
  11.2 0.5 %collective-permute-done.3.refs_4_ = bf16[88,1152]{1,0:T(8,128)(2,1)S(1)} collective-permute-done((bf16[88,1152]{1,0:T(8,128)(2,1)}, bf16[88,1152]{1,0:T(8,128)(2,1)S(1)}, u32[]{:S(2)}, u32[]{:S(2)}) %collective-permute-start.3) | collective-permute-done | bytes 202784 | tf_op jit(solution)/shard_map/ppermute | solution.py:19
  11.6 2.1 %collective-permute-start.10 = (bf16[88,1152]{1,0:T(8,128)(2,1)S(1)}, bf16[88,1152]{1,0:T(8,128)(2,1)S(1)}, u32[]{:S(2)}, u32[]{:S(2)}) collective-permute-start(bf16[88,1152]{1,0:T(8,128)(2,1)S(1)} %collective-permute-done.3.refs_4_), channel_id=1, source_target_pairs={{0,1},{1,0},{2,3},{3,2},{4,5},{5,4},{6,7},{7,6},{8,9},{9,8},{10,11... | collective-permute-start | bytes 608264 | tf_op jit(solution)/shard_map/ppermute | solution.py:19
  13.8 0.0 collective-permute-done.refs_2_
  13.8 0.0 collective-permute-start.8
  16.4 0.6 %collective-permute-start.6 = (bf16[88,1152]{1,0:T(8,128)(2,1)S(1)}, bf16[88,1152]{1,0:T(8,128)(2,1)S(1)}, u32[]{:S(2)}, u32[]{:S(2)}) collective-permute-start(bf16[88,1152]{1,0:T(8,128)(2,1)S(1)} %collective-permute-done.refs_2_), channel_id=1, source_target_pairs={{0,16},{16,0},{1,17},{17,1},{2,18},{18,2},{3,19},{19,3},{4,20},{20... | collective-permute-start | bytes 608264 | tf_op jit(solution)/shard_map/ppermute | solution.py:23
  17.0 0.0 collective-permute-done.4.refs_5_
  17.0 0.1 collective-permute-start.9
  17.1 0.0 collective-permute-done.2.refs_3_
  17.1 0.4 collective-permute-start.7
  17.5 0.1 collective-permute-done.10.refs_0_
  17.6 0.0 collective-permute-start.11
  17.6 0.0 collective-permute-done.8.refs_10_.refs_6_
  17.6 1.9 %collective-permute-start.12 = (bf16[88,1152]{1,0:T(8,128)(2,1)S(1)}, bf16[88,1152]{1,0:T(8,128)(2,1)S(1)}, u32[]{:S(2)}, u32[]{:S(2)}) collective-permute-start(bf16[88,1152]{1,0:T(8,128)(2,1)S(1)} %collective-permute-done.4.refs_5_), channel_id=1, source_target_pairs={{0,1},{1,0},{2,3},{3,2},{4,5},{5,4},{6,7},{7,6},{8,9},{9,8},{10,11... | collective-permute-start | bytes 608264 | tf_op jit(solution)/shard_map/ppermute | solution.py:19
  19.5 0.0 collective-permute-done.6.refs_8_.refs_4_
  19.5 0.0 collective-permute-done.9.refs_11_.refs_7_
  19.5 0.0 collective-permute-done.7.refs_9_.refs_5_
  19.5 0.0 collective-permute-done.11.refs_2_.refs_6_
  19.5 0.0 copy-start
  19.5 0.9 %copy-done = bf16[88,1152]{1,0:T(8,128)(2,1)S(1)} copy-done((bf16[88,1152]{1,0:T(8,128)(2,1)S(1)}, bf16[88,1152]{1,0:T(8,128)(2,1)}, u32[]{:S(2)}) %copy-start) | copy-done | bytes 202776
  20.5 0.9 %copy-done.2 = bf16[88,1152]{1,0:T(8,128)(2,1)S(1)} copy-done((bf16[88,1152]{1,0:T(8,128)(2,1)S(1)}, bf16[88,1152]{1,0:T(8,128)(2,1)}, u32[]{:S(2)}) %copy-start.2) | copy-done | bytes 202776
  21.4 2.2 %shard_map.97 = (bf16[480,1152]{1,0:T(8,128)(2,1)S(1)}, bf16[480,1152]{1,0:T(8,128)(2,1)S(1)}, f32[480,1152]{1,0:T(8,128)S(1)}) custom-call(s32[1]{0:T(128)} %bitcast.row_ref, s32[1]{0:T(128)} %bitcast.1.col_ref, f32[8,128]{1,0:T(8,128)S(1)} %shard_map.96.number_ref, bf16[88,1152]{1,0:T(8,128)(2,1)S(1)} %copy-done, ...), custom_call_target="tpu_custom_call" | custom-call | flops 1061683200 | bytes 6860808 | tf_op jit(solution)/shard_map/pallas_call | solution.py:251
  23.6 0.0 collective-permute-done.12.refs_1_
  23.6 0.3 collective-permute-start.13
  23.9 0.9 %shard_map.98 = (bf16[160,1152]{1,0:T(8,128)(2,1)S(1)}, f32[160,1152]{1,0:T(8,128)S(1)}) custom-call(s32[1]{0:T(128)} %bitcast.row_ref, s32[1]{0:T(128)} %bitcast.1.col_ref, f32[8,128]{1,0:T(8,128)S(1)} %shard_map.96.number_ref, bf16[88,1152]{1,0:T(8,128)(2,1)S(1)} %collective-permute-done.10.refs_0_, bf16[88,1152]{1,0:T(8,128)(2,1)S(1)} %collective-permute-done.12.refs_1_, ...), custom_call_target="tpu_custom_call" | custom-call | flops 353894400 | bytes 3837960 | tf_op jit(solution)/shard_map/pallas_call | solution.py:251
  24.9 0.0 copy-start.1
  24.9 0.2 collective-permute-done.13.refs_3_.refs_7_
  25.1 0.9 %shard_map.99 = (bf16[160,1152]{1,0:T(8,128)(2,1)S(1)}, bf16[80,1152]{1,0:T(8,128)(2,1)S(1)}, bf16[80,1152]{1,0:T(8,128)(2,1)S(1)}) custom-call(s32[1]{0:T(128)} %bitcast.row_ref, s32[1]{0:T(128)} %bitcast.1.col_ref, f32[8,128]{1,0:T(8,128)S(1)} %shard_map.96.number_ref, bf16[88,1152]{1,0:T(8,128)(2,1)S(1)} %collective-permute-done.10.refs_0_, ...), custom_call_target="tpu_custom_call" | custom-call | flops 117964800 | bytes 2658312 | tf_op jit(solution)/shard_map/pallas_call | solution.py:251
  26.0 1.6 %collective-permute-start.14 = (bf16[80,1152]{1,0:T(8,128)(2,1)S(1)}, bf16[80,1152]{1,0:T(8,128)(2,1)S(1)}, u32[]{:S(2)}, u32[]{:S(2)}) collective-permute-start(bf16[80,1152]{1,0:T(8,128)(2,1)S(1)} %get-tuple-element.52), channel_id=1, source_target_pairs={{0,1},{1,0},{2,3},{3,2},{4,5},{5,4},{6,7},{7,6},{8,9},{9,8},{10,11... | collective-permute-start | bytes 552968 | tf_op jit(solution)/shard_map/ppermute | solution.py:19
  27.6 0.4 %collective-permute-start.17 = (bf16[80,1152]{1,0:T(8,128)(2,1)S(1)}, bf16[80,1152]{1,0:T(8,128)(2,1)S(1)}, u32[]{:S(2)}, u32[]{:S(2)}) collective-permute-start(bf16[80,1152]{1,0:T(8,128)(2,1)S(1)} %get-tuple-element.55), channel_id=1, source_target_pairs={{0,1},{1,0},{2,3},{3,2},{4,5},{5,4},{6,7},{7,6},{8,9},{9,8},{10,11... | collective-permute-start | bytes 552968 | tf_op jit(solution)/shard_map/ppermute | solution.py:19
  28.1 1.7 %shard_map.100 = (f32[80,1152]{1,0:T(8,128)S(1)}, f32[80,1152]{1,0:T(8,128)S(1)}, bf16[80,1152]{1,0:T(8,128)(2,1)S(1)}, bf16[80,1152]{1,0:T(8,128)(2,1)S(1)}, f3...) custom-call(s32[1]{0:T(128)} %bitcast.row_ref, s32[1]{0:T(128)} %bitcast.1.col_ref, f32[8,128]{1,0:T(8,128)S(1)} %shard_map.96.number_ref, ...), custom_call_target="tpu_custom_call" | custom-call | flops 353894400 | bytes 7155720 | tf_op jit(solution)/shard_map/pallas_call | solution.py:251
  29.8 0.1 collective-permute-start.16
  30.0 1.7 %collective-permute-done.14 = bf16[80,1152]{1,0:T(8,128)(2,1)S(1)} collective-permute-done((bf16[80,1152]{1,0:T(8,128)(2,1)S(1)}, bf16[80,1152]{1,0:T(8,128)(2,1)S(1)}, u32[]{:S(2)}, u32[]{:S(2)}) %collective-permute-start.14) | collective-permute-done | bytes 184352 | tf_op jit(solution)/shard_map/ppermute | solution.py:19
  31.6 3.2 %collective-permute-start.15 = (bf16[80,1152]{1,0:T(8,128)(2,1)S(1)}, bf16[80,1152]{1,0:T(8,128)(2,1)S(1)}, u32[]{:S(2)}, u32[]{:S(2)}) collective-permute-start(bf16[80,1152]{1,0:T(8,128)(2,1)S(1)} %add_convert_fusion.1), channel_id=1, source_target_pairs={{0,8},{1,9},{2,10},{3,11},{4,12},{5,13},{6,14},{7,15},{8,0},{9,1},... | collective-permute-start | bytes 552968 | tf_op jit(solution)/shard_map/ppermute | solution.py:19
  34.9 1.6 %collective-permute-start.19 = (bf16[80,1152]{1,0:T(8,128)(2,1)S(1)}, bf16[80,1152]{1,0:T(8,128)(2,1)S(1)}, u32[]{:S(2)}, u32[]{:S(2)}) collective-permute-start(bf16[80,1152]{1,0:T(8,128)(2,1)S(1)} %get-tuple-element.57), channel_id=1, source_target_pairs={{0,1},{1,0},{2,3},{3,2},{4,5},{5,4},{6,7},{7,6},{8,9},{9,8},{10,11... | collective-permute-start | bytes 552968 | tf_op jit(solution)/shard_map/ppermute | solution.py:19
  36.5 1.4 %collective-permute-start.18 = (bf16[80,1152]{1,0:T(8,128)(2,1)S(1)}, bf16[80,1152]{1,0:T(8,128)(2,1)S(1)}, u32[]{:S(2)}, u32[]{:S(2)}) collective-permute-start(bf16[80,1152]{1,0:T(8,128)(2,1)S(1)} %add_convert_fusion), channel_id=1, source_target_pairs={{0,24},{1,25},{2,26},{3,27},{4,28},{5,29},{6,30},{7,31},{8,16},{9,... | collective-permute-start | bytes 552968 | tf_op jit(solution)/shard_map/ppermute | solution.py:19
  38.0 1.9 %collective-permute-start.20 = (bf16[80,1152]{1,0:T(8,128)(2,1)S(1)}, bf16[80,1152]{1,0:T(8,128)(2,1)S(1)}, u32[]{:S(2)}, u32[]{:S(2)}) collective-permute-start(bf16[80,1152]{1,0:T(8,128)(2,1)S(1)} %get-tuple-element.59), channel_id=1, source_target_pairs={{0,17},{1,16},{2,19},{3,18},{4,21},{5,20},{6,23},{7,22},{8,25},{9,... | collective-permute-start | bytes 552968 | tf_op jit(solution)/shard_map/ppermute | solution.py:19
  39.9 0.0 collective-permute-done.15
  39.9 3.3 %collective-permute-done.18 = bf16[80,1152]{1,0:T(8,128)(2,1)S(1)} collective-permute-done((bf16[80,1152]{1,0:T(8,128)(2,1)S(1)}, bf16[80,1152]{1,0:T(8,128)(2,1)S(1)}, u32[]{:S(2)}, u32[]{:S(2)}) %collective-permute-start.18) | collective-permute-done | bytes 184352 | tf_op jit(solution)/shard_map/ppermute | solution.py:19
  43.3 0.0 collective-permute-done.20.near_cross_ref
  43.3 0.8 %shard_map.101 = (bf16[80,1152]{1,0:T(8,128)(2,1)}, bf16[160,576]{1,0:T(8,128)(2,1)}) custom-call(s32[1]{0:T(128)} %bitcast.row_ref, f32[80,1152]{1,0:T(8,128)S(1)} %convert_add_fusion.1.stay_ref, f32[80,1152]{1,0:T(8,128)S(1)} %convert_add_fusion.crossed_ref, bf16[80,1152]{1,0:T(8,128)(2,1)S(1)} %collective-permute-done.19.near_stay_ref, ...), custom_call_target="tpu_custom_call" | custom-call | tf_op jit(solution)/shard_map/pallas_call | solution.py:331
  (13 shorter events, 0.2 us)
Async XLA Ops:
  2.5 5.7 %collective-permute-start.1 = (bf16[88,1152]{1,0:T(8,128)(2,1)}, bf16[88,1152]{1,0:T(8,128)(2,1)S(1)}, u32[]{:S(2)}, u32[]{:S(2)}) collective-permute-start(bf16[88,1152]{1,0:T(8,128)(2,1)} %get-tuple-element.37.refs_7_.refs_3_), channel_id=1, source_target_pairs={{0,16},{16,0},{1,17},{17,1},{2,18},{18,2},{3,19},{19,3},{4,20},{20... | collective-permute-start | bytes 608264 | tf_op jit(solution)/shard_map/ppermute | solution.py:23
  3.0 8.6 %collective-permute-start.3 = (bf16[88,1152]{1,0:T(8,128)(2,1)}, bf16[88,1152]{1,0:T(8,128)(2,1)S(1)}, u32[]{:S(2)}, u32[]{:S(2)}) collective-permute-start(bf16[88,1152]{1,0:T(8,128)(2,1)} %get-tuple-element.31.refs_0_), channel_id=1, source_target_pairs={{0,8},{1,9},{2,10},{3,11},{4,12},{5,13},{6,14},{7,15},{8,0},{9,1},... | collective-permute-start | bytes 608264 | tf_op jit(solution)/shard_map/ppermute | solution.py:19
  6.7 7.1 %collective-permute-start = (bf16[88,1152]{1,0:T(8,128)(2,1)}, bf16[88,1152]{1,0:T(8,128)(2,1)S(1)}, u32[]{:S(2)}, u32[]{:S(2)}) collective-permute-start(bf16[88,1152]{1,0:T(8,128)(2,1)} %get-tuple-element.31.refs_0_), channel_id=1, source_target_pairs={{0,1},{1,0},{2,3},{3,2},{4,5},{5,4},{6,7},{7,6},{8,9},{9,8},{10,11... | collective-permute-start | bytes 608264 | tf_op jit(solution)/shard_map/ppermute | solution.py:19
  8.2 8.2 %collective-permute-start.5 = (bf16[88,1152]{1,0:T(8,128)(2,1)}, bf16[88,1152]{1,0:T(8,128)(2,1)S(1)}, u32[]{:S(2)}, u32[]{:S(2)}) collective-permute-start(bf16[88,1152]{1,0:T(8,128)(2,1)} %get-tuple-element.31.refs_0_), channel_id=1, source_target_pairs={{0,16},{16,0},{1,17},{17,1},{2,18},{18,2},{3,19},{19,3},{4,20},{20... | collective-permute-start | bytes 608264 | tf_op jit(solution)/shard_map/ppermute | solution.py:23
  8.2 8.8 %collective-permute-start.4 = (bf16[88,1152]{1,0:T(8,128)(2,1)S(1)}, bf16[88,1152]{1,0:T(8,128)(2,1)S(1)}, u32[]{:S(2)}, u32[]{:S(2)}) collective-permute-start(bf16[88,1152]{1,0:T(8,128)(2,1)S(1)} %collective-permute-done.1.refs_1_), channel_id=1, source_target_pairs={{0,8},{1,9},{2,10},{3,11},{4,12},{5,13},{6,14},{7,15},{8,0},{9,1},... | collective-permute-start | bytes 608264 | tf_op jit(solution)/shard_map/ppermute | solution.py:19
  9.7 7.4 %collective-permute-start.2 = (bf16[88,1152]{1,0:T(8,128)(2,1)S(1)}, bf16[88,1152]{1,0:T(8,128)(2,1)S(1)}, u32[]{:S(2)}, u32[]{:S(2)}) collective-permute-start(bf16[88,1152]{1,0:T(8,128)(2,1)S(1)} %collective-permute-done.1.refs_1_), channel_id=1, source_target_pairs={{0,1},{1,0},{2,3},{3,2},{4,5},{5,4},{6,7},{7,6},{8,9},{9,8},{10,11... | collective-permute-start | bytes 608264 | tf_op jit(solution)/shard_map/ppermute | solution.py:19
  11.6 6.0 %collective-permute-start.10 = (bf16[88,1152]{1,0:T(8,128)(2,1)S(1)}, bf16[88,1152]{1,0:T(8,128)(2,1)S(1)}, u32[]{:S(2)}, u32[]{:S(2)}) collective-permute-start(bf16[88,1152]{1,0:T(8,128)(2,1)S(1)} %collective-permute-done.3.refs_4_), channel_id=1, source_target_pairs={{0,1},{1,0},{2,3},{3,2},{4,5},{5,4},{6,7},{7,6},{8,9},{9,8},{10,11... | collective-permute-start | bytes 608264 | tf_op jit(solution)/shard_map/ppermute | solution.py:19
  13.8 3.8 %collective-permute-start.8 = (bf16[88,1152]{1,0:T(8,128)(2,1)S(1)}, bf16[88,1152]{1,0:T(8,128)(2,1)S(1)}, u32[]{:S(2)}, u32[]{:S(2)}) collective-permute-start(bf16[88,1152]{1,0:T(8,128)(2,1)S(1)} %collective-permute-done.3.refs_4_), channel_id=1, source_target_pairs={{0,16},{16,0},{1,17},{17,1},{2,18},{18,2},{3,19},{19,3},{4,20},{20... | collective-permute-start | bytes 608264 | tf_op jit(solution)/shard_map/ppermute | solution.py:23
  16.4 3.1 %collective-permute-start.6 = (bf16[88,1152]{1,0:T(8,128)(2,1)S(1)}, bf16[88,1152]{1,0:T(8,128)(2,1)S(1)}, u32[]{:S(2)}, u32[]{:S(2)}) collective-permute-start(bf16[88,1152]{1,0:T(8,128)(2,1)S(1)} %collective-permute-done.refs_2_), channel_id=1, source_target_pairs={{0,16},{16,0},{1,17},{17,1},{2,18},{18,2},{3,19},{19,3},{4,20},{20... | collective-permute-start | bytes 608264 | tf_op jit(solution)/shard_map/ppermute | solution.py:23
  17.0 2.5 %collective-permute-start.9 = (bf16[88,1152]{1,0:T(8,128)(2,1)S(1)}, bf16[88,1152]{1,0:T(8,128)(2,1)S(1)}, u32[]{:S(2)}, u32[]{:S(2)}) collective-permute-start(bf16[88,1152]{1,0:T(8,128)(2,1)S(1)} %collective-permute-done.4.refs_5_), channel_id=1, source_target_pairs={{0,16},{16,0},{1,17},{17,1},{2,18},{18,2},{3,19},{19,3},{4,20},{20... | collective-permute-start | bytes 608264 | tf_op jit(solution)/shard_map/ppermute | solution.py:23
  17.1 2.4 %collective-permute-start.7 = (bf16[88,1152]{1,0:T(8,128)(2,1)S(1)}, bf16[88,1152]{1,0:T(8,128)(2,1)S(1)}, u32[]{:S(2)}, u32[]{:S(2)}) collective-permute-start(bf16[88,1152]{1,0:T(8,128)(2,1)S(1)} %collective-permute-done.2.refs_3_), channel_id=1, source_target_pairs={{0,16},{16,0},{1,17},{17,1},{2,18},{18,2},{3,19},{19,3},{4,20},{20... | collective-permute-start | bytes 608264 | tf_op jit(solution)/shard_map/ppermute | solution.py:23
  17.6 1.9 %collective-permute-start.11 = (bf16[88,1152]{1,0:T(8,128)(2,1)S(1)}, bf16[88,1152]{1,0:T(8,128)(2,1)S(1)}, u32[]{:S(2)}, u32[]{:S(2)}) collective-permute-start(bf16[88,1152]{1,0:T(8,128)(2,1)S(1)} %collective-permute-done.10.refs_0_), channel_id=1, source_target_pairs={{0,16},{16,0},{1,17},{17,1},{2,18},{18,2},{3,19},{19,3},{4,20},{20... | collective-permute-start | bytes 608264 | tf_op jit(solution)/shard_map/ppermute | solution.py:23
  17.6 6.0 %collective-permute-start.12 = (bf16[88,1152]{1,0:T(8,128)(2,1)S(1)}, bf16[88,1152]{1,0:T(8,128)(2,1)S(1)}, u32[]{:S(2)}, u32[]{:S(2)}) collective-permute-start(bf16[88,1152]{1,0:T(8,128)(2,1)S(1)} %collective-permute-done.4.refs_5_), channel_id=1, source_target_pairs={{0,1},{1,0},{2,3},{3,2},{4,5},{5,4},{6,7},{7,6},{8,9},{9,8},{10,11... | collective-permute-start | bytes 608264 | tf_op jit(solution)/shard_map/ppermute | solution.py:19
  19.5 0.9 %copy-start = (bf16[88,1152]{1,0:T(8,128)(2,1)S(1)}, bf16[88,1152]{1,0:T(8,128)(2,1)}, u32[]{:S(2)}) copy-start(bf16[88,1152]{1,0:T(8,128)(2,1)} %get-tuple-element.31.refs_0_) | copy-start | bytes 608260
  20.5 0.9 %copy-start.2 = (bf16[88,1152]{1,0:T(8,128)(2,1)S(1)}, bf16[88,1152]{1,0:T(8,128)(2,1)}, u32[]{:S(2)}) copy-start(bf16[88,1152]{1,0:T(8,128)(2,1)} %get-tuple-element.37.refs_7_.refs_3_) | copy-start | bytes 608260
  21.4 2.6 %copy-start.3 = (bf16[88,1152]{1,0:T(8,128)(2,1)S(1)}, bf16[88,1152]{1,0:T(8,128)(2,1)}, u32[]{:S(2)}) copy-start(bf16[88,1152]{1,0:T(8,128)(2,1)} %get-tuple-element.37.refs_7_.refs_3_) | copy-start | bytes 608260
  23.6 1.5 %collective-permute-start.13 = (bf16[88,1152]{1,0:T(8,128)(2,1)S(1)}, bf16[88,1152]{1,0:T(8,128)(2,1)S(1)}, u32[]{:S(2)}, u32[]{:S(2)}) collective-permute-start(bf16[88,1152]{1,0:T(8,128)(2,1)S(1)} %collective-permute-done.12.refs_1_), channel_id=1, source_target_pairs={{0,16},{16,0},{1,17},{17,1},{2,18},{18,2},{3,19},{19,3},{4,20},{20... | collective-permute-start | bytes 608264 | tf_op jit(solution)/shard_map/ppermute | solution.py:23
  24.9 3.2 %copy-start.1 = (bf16[88,1152]{1,0:T(8,128)(2,1)S(1)}, bf16[88,1152]{1,0:T(8,128)(2,1)}, u32[]{:S(2)}) copy-start(bf16[88,1152]{1,0:T(8,128)(2,1)} %get-tuple-element.31.refs_0_) | copy-start | bytes 608260
  26.0 5.6 %collective-permute-start.14 = (bf16[80,1152]{1,0:T(8,128)(2,1)S(1)}, bf16[80,1152]{1,0:T(8,128)(2,1)S(1)}, u32[]{:S(2)}, u32[]{:S(2)}) collective-permute-start(bf16[80,1152]{1,0:T(8,128)(2,1)S(1)} %get-tuple-element.52), channel_id=1, source_target_pairs={{0,1},{1,0},{2,3},{3,2},{4,5},{5,4},{6,7},{7,6},{8,9},{9,8},{10,11... | collective-permute-start | bytes 552968 | tf_op jit(solution)/shard_map/ppermute | solution.py:19
  27.6 8.8 %collective-permute-start.17 = (bf16[80,1152]{1,0:T(8,128)(2,1)S(1)}, bf16[80,1152]{1,0:T(8,128)(2,1)S(1)}, u32[]{:S(2)}, u32[]{:S(2)}) collective-permute-start(bf16[80,1152]{1,0:T(8,128)(2,1)S(1)} %get-tuple-element.55), channel_id=1, source_target_pairs={{0,1},{1,0},{2,3},{3,2},{4,5},{5,4},{6,7},{7,6},{8,9},{9,8},{10,11... | collective-permute-start | bytes 552968 | tf_op jit(solution)/shard_map/ppermute | solution.py:19
  29.8 10.1 %collective-permute-start.16 = (f32[80,1152]{1,0:T(8,128)S(1)}, f32[80,1152]{1,0:T(8,128)S(1)}, u32[]{:S(2)}, u32[]{:S(2)}) collective-permute-start(f32[80,1152]{1,0:T(8,128)S(1)} %get-tuple-element.53), channel_id=1, source_target_pairs={{0,16},{16,0},{1,17},{17,1},{2,18},{18,2},{3,19},{19,3},{4,20},{20... | collective-permute-start | bytes 1105928 | tf_op jit(solution)/shard_map/ppermute | solution.py:23
  31.6 8.2 %collective-permute-start.15 = (bf16[80,1152]{1,0:T(8,128)(2,1)S(1)}, bf16[80,1152]{1,0:T(8,128)(2,1)S(1)}, u32[]{:S(2)}, u32[]{:S(2)}) collective-permute-start(bf16[80,1152]{1,0:T(8,128)(2,1)S(1)} %add_convert_fusion.1), channel_id=1, source_target_pairs={{0,8},{1,9},{2,10},{3,11},{4,12},{5,13},{6,14},{7,15},{8,0},{9,1},... | collective-permute-start | bytes 552968 | tf_op jit(solution)/shard_map/ppermute | solution.py:19
  34.9 8.4 %collective-permute-start.19 = (bf16[80,1152]{1,0:T(8,128)(2,1)S(1)}, bf16[80,1152]{1,0:T(8,128)(2,1)S(1)}, u32[]{:S(2)}, u32[]{:S(2)}) collective-permute-start(bf16[80,1152]{1,0:T(8,128)(2,1)S(1)} %get-tuple-element.57), channel_id=1, source_target_pairs={{0,1},{1,0},{2,3},{3,2},{4,5},{5,4},{6,7},{7,6},{8,9},{9,8},{10,11... | collective-permute-start | bytes 552968 | tf_op jit(solution)/shard_map/ppermute | solution.py:19
  36.5 6.7 %collective-permute-start.18 = (bf16[80,1152]{1,0:T(8,128)(2,1)S(1)}, bf16[80,1152]{1,0:T(8,128)(2,1)S(1)}, u32[]{:S(2)}, u32[]{:S(2)}) collective-permute-start(bf16[80,1152]{1,0:T(8,128)(2,1)S(1)} %add_convert_fusion), channel_id=1, source_target_pairs={{0,24},{1,25},{2,26},{3,27},{4,28},{5,29},{6,30},{7,31},{8,16},{9,... | collective-permute-start | bytes 552968 | tf_op jit(solution)/shard_map/ppermute | solution.py:19
  38.0 5.3 %collective-permute-start.20 = (bf16[80,1152]{1,0:T(8,128)(2,1)S(1)}, bf16[80,1152]{1,0:T(8,128)(2,1)S(1)}, u32[]{:S(2)}, u32[]{:S(2)}) collective-permute-start(bf16[80,1152]{1,0:T(8,128)(2,1)S(1)} %get-tuple-element.59), channel_id=1, source_target_pairs={{0,17},{1,16},{2,19},{3,18},{4,21},{5,20},{6,23},{7,22},{8,25},{9,... | collective-permute-start | bytes 552968 | tf_op jit(solution)/shard_map/ppermute | solution.py:19

commit v8 on v6

--- a/solution.py
+++ b/solution.py
@@ -138,9 +138,6 @@
     return [refs[n : n + 2] for n in range(0, len(refs), 2)]
 
 
-THREE = ("own", "near", "far")
-
-
 def number_kernel(scale_ref, bias_ref, grad_ref, sample_ref, out_ref):
     factor = grad_ref[0] * scale_ref[0] / sample_ref[0].astype(jnp.float32)
     line = lax.broadcasted_iota(jnp.int32, out_ref.shape, 0)
@@ -148,26 +145,30 @@
 
 
 def early_kernel(cols, row_ref, col_ref, number_ref, *refs):
-    mine_pairs, other_pairs = pairs(refs[:6]), pairs(refs[6:12])
-    mine_ref, others_ref, total_ref = refs[12:]
+    near, far, other_far = pairs(refs[:6])
+    mine_ref, far_ref, total_ref = refs[6:]
     texts = row_ref[0] != 0
-    size = 2 * (refs[0].shape[0] - SPARE)
-    for n in range(3):
-        unpack(mine_pairs[n], texts, mine_ref, n * size)
-        unpack(other_pairs[n], jnp.logical_not(texts), others_ref, n * size)
-    others = others_ref[...]
+    size = far_ref.shape[0]
+    unpack(near, texts, mine_ref, 0)
+    unpack(far, texts, mine_ref, size)
+    unpack(other_far, jnp.logical_not(texts), far_ref, 0)
+    others = far_ref[...]
     coefficient = coefficients_of(cols, row_ref, col_ref, number_ref, mine_ref[...], others,
-                                  list(zip(THREE, mine_pairs)), list(zip(THREE, other_pairs)))
+                                  [("near", near), ("far", far)], [("far", other_far)])
     total_ref[...] = jnp.dot(coefficient, others, preferred_element_type=jnp.float32)
 
 
 def both_kernel(cols, row_ref, col_ref, number_ref, *refs):
-    mine_pair, other_pairs = refs[:2], pairs(refs[2:8])
-    others_ref, mine_ref, total_ref = refs[8:]
-    unpack(mine_pair, row_ref[0] != 0, mine_ref, 0)
-    others = others_ref[...]
-    coefficient = coefficients_of(cols, row_ref, col_ref, number_ref, mine_ref[...], others,
-                                  [("both", mine_pair)], list(zip(THREE, other_pairs)))
+    both, own, near, far = pairs(refs[:8])
+    far_ref, others_ref, mine_ref, total_ref = refs[8:]
+    texts = row_ref[0] != 0
+    size = far_ref.shape[0]
+    unpack(both, texts, mine_ref, 0)
+    unpack(own, jnp.logical_not(texts), others_ref, 0)
+    unpack(near, jnp.logical_not(texts), others_ref, size)
+    others = jnp.concatenate([others_ref[...], far_ref[...]], axis=0)
+    coefficient = coefficients_of(cols, row_ref, col_ref, number_ref, mine_ref[...], others, [("both", both)],
+                                  [("own", own), ("near", near), ("far", far)])
     total_ref[...] = jnp.dot(coefficient, others, preferred_element_type=jnp.float32)
 
 
@@ -200,19 +201,33 @@
     pack_sum(total, texts, stay_ref, cross_ref)
 
 
+def far_kernel(cols, row_ref, col_ref, number_ref, *refs):
+    far, own, near, both = pairs(refs[:8])
+    mine_ref, early_ref, late_ref, total_ref, stay_ref, cross_ref = refs[8:]
+    size = late_ref.shape[0]
+    others = jnp.concatenate([early_ref[...], late_ref[...]], axis=0)
+    coefficient = coefficients_of(cols, row_ref, col_ref, number_ref, mine_ref[size:], others, [("far", far)],
+                                  [("own", own), ("near", near), ("both", both)])
+    total = total_ref[size:] + jnp.dot(coefficient, others, preferred_element_type=jnp.float32)
+    pack_sum(total, row_ref[0] != 0, stay_ref, cross_ref)
+
+
 def rest_kernel(cols, row_ref, col_ref, number_ref, *refs):
-    mine_pairs, other_pair = pairs(refs[:6]), refs[6:8]
-    mine_ref, others_ref, total_ref = refs[8:11]
-    own_stay, own_cross, near_stay, near_cross, far_stay, far_cross = refs[11:]
+    mine_near, mine_own, own, near, far, both = pairs(refs[:12])
+    mine_ref, early_ref, far_ref, late_ref, total_ref = refs[12:17]
+    own_stay, own_cross, near_stay, near_cross, own_rows = refs[17:]
     texts = row_ref[0] != 0
-    others = others_ref[...]
-    coefficient = coefficients_of(cols, row_ref, col_ref, number_ref, mine_ref[...], others,
-                                  list(zip(THREE, mine_pairs)), [("both", other_pair)])
-    total = total_ref[...] + jnp.dot(coefficient, others, preferred_element_type=jnp.float32)
-    size = total.shape[0] // 3
-    pack_sum(total[2 * size :], texts, far_stay, far_cross)
-    pack_sum(total[size : 2 * size], texts, near_stay, near_cross)
-    pack_sum(total[:size], texts, own_stay, own_cross)
+    size = late_ref.shape[0]
+    unpack(mine_own, texts, own_rows, 0)
+    others = jnp.concatenate([early_ref[...], late_ref[...]], axis=0)
+    coefficient = coefficients_of(cols, row_ref, col_ref, number_ref, mine_ref[:size], others, [("near", mine_near)],
+                                  [("own", own), ("near", near), ("both", both)])
+    total = total_ref[:size] + jnp.dot(coefficient, others, preferred_element_type=jnp.float32)
+    pack_sum(total, texts, near_stay, near_cross)
+    others = jnp.concatenate([others, far_ref[...]], axis=0)
+    coefficient = coefficients_of(cols, row_ref, col_ref, number_ref, own_rows[...], others, [("own", mine_own)],
+                                  [("own", own), ("near", near), ("both", both), ("far", far)])
+    pack_sum(jnp.dot(coefficient, others, preferred_element_type=jnp.float32), texts, own_stay, own_cross)
 
 
 def last_kernel(spot_ref, stay_ref, crossed_ref, near_stay_ref, near_cross_ref, image_ref, text_ref):
@@ -235,7 +250,7 @@
         put(crossed, stay)
 
 
-def call(kernel, out_shape, smem, *arrays, flops=0):
+def call(kernel, out_shape, smem, *arrays, flops=0, scratch=()):
     size = sum(a.size * a.dtype.itemsize for a in (*arrays, *jax.tree.leaves(out_shape)))
     return pl.pallas_call(
         kernel,
@@ -243,6 +258,7 @@
         in_specs=[pl.BlockSpec(memory_space=pltpu.SMEM)] * smem
         + [pl.BlockSpec(memory_space=pltpu.VMEM)] * (len(arrays) - smem),
         out_specs=jax.tree.map(lambda _: pl.BlockSpec(memory_space=pltpu.VMEM), out_shape),
+        scratch_shapes=scratch,
         compiler_params=pltpu.CompilerParams(vmem_limit_bytes=24 * 1024 * 1024),
         cost_estimate=pl.CostEstimate(flops=flops, bytes_accessed=size, transcendentals=0),
     )(*arrays)
@@ -278,32 +294,36 @@
     near_b = hop(own_b, *near)
     both_a = hop(far_a, *near)
     both_b = hop(far_b, *near)
-    mine = (own_a, own_b, near_a, near_b, far_a, far_b)
     number = call(number_kernel, jax.ShapeDtypeStruct((8, 128), f32), 4, logit_scale, logit_bias, loss_grad, sample_count)
-    near_a, number = lax.optimization_barrier((near_a, number))
-    others = (swap(own_a), give, swap(near_a), swap(near_b), swap(far_a), swap(far_b))
-    others, other_both_a = lax.optimization_barrier((others, swap(both_a)))
+    far_a, number = lax.optimization_barrier((far_a, number))
+    mine_own, mine_near, mine_far = (own_a, own_b), (near_a, near_b), (far_a, far_b)
+    own, near_pair, far_pair = (swap(own_a), give), (swap(near_a), swap(near_b)), (swap(far_a), swap(far_b))
+    other_both_a = swap(both_a)
 
     pair_flops = 4 * size * size * width
     scalars = (row, col, number)
-    mine_rows, other_rows, early = call(
-        functools.partial(early_kernel, cols), (shape(3 * size, bf16), shape(3 * size, bf16), shape(3 * size, f32)),
-        2, *scalars, *mine, *others, flops=9 * pair_flops)
+    mine_rows, far_rows, early = call(
+        functools.partial(early_kernel, cols), (shape(2 * size, bf16), shape(size, bf16), shape(2 * size, f32)), 2,
+        *scalars, *mine_near, *mine_far, *far_pair, flops=2 * pair_flops)
     both_b, early = lax.optimization_barrier((both_b, early))
     both = (both_a, both_b)
     other_both = (other_both_a, swap(both_b))
-    both_rows, both_early = call(
-        functools.partial(both_kernel, cols), (shape(size, bf16), shape(size, f32)), 2, *scalars, *both, *others,
-        other_rows, flops=3 * pair_flops)
-    other_late, late_stay, late_cross = call(
+    early_rows, both_rows, both_early = call(
+        functools.partial(both_kernel, cols), (shape(2 * size, bf16), shape(size, bf16), shape(size, f32)), 2, *scalars,
+        *both, *own, *near_pair, *far_pair, far_rows, flops=3 * pair_flops)
+    late_rows, late_stay, late_cross = call(
         functools.partial(late_kernel, cols), (shape(size, bf16), shape(half, bf16), shape(half, bf16)), 2, *scalars,
         *both, *other_both, both_rows, both_early, flops=pair_flops)
     in_cross = hop(late_cross, *near)
     in_stay = hop(late_stay, *near)
-    own_stay, own_cross, near_stay, near_cross, far_stay, far_cross = call(
+    far_stay, far_cross = call(
+        functools.partial(far_kernel, cols), (shape(half, f32), shape(half, f32)), 2, *scalars, *mine_far, *own,
+        *near_pair, *other_both, mine_rows, early_rows, late_rows, early, flops=3 * pair_flops)
+    own_stay, own_cross, near_stay, near_cross = call(
         functools.partial(rest_kernel, cols),
-        (shape(half, f32), shape(half, f32), shape(half, bf16), shape(half, bf16), shape(half, f32), shape(half, f32)),
-        2, *scalars, *mine, *other_both, mine_rows, other_late, early, flops=3 * pair_flops)
+        (shape(half, f32), shape(half, f32), shape(half, bf16), shape(half, bf16)), 2, *scalars, *mine_near, *mine_own,
+        *own, *near_pair, *far_pair, *other_both, mine_rows, early_rows, far_rows, late_rows, early,
+        flops=7 * pair_flops, scratch=[pltpu.VMEM((size, width), bf16)])
     crossed = swap(own_cross)
     far_cross = (far_cross + in_cross.astype(f32)).astype(bf16)
     far_stay = (far_stay + in_stay.astype(f32)).astype(bf16)

time: 44.5 us -> 44.2 us (level)
  waiting for transfers between devices: 5.71 us -> 8.8 us
  starting transfers between devices: 24.5 us -> 21.5 us
  local copies, waits for them, and re-layouts: 1.86 us -> 0.93 us
  Pallas kernels: 8.53 us -> 9.28 us
    ppermute x12, waiting for transfers between devices: 5.48 us -> 8.78 us  [hop(): return lax.ppermute(block, ('row', 'col'), route)]
    ppermute x12, starting transfers between devices: 22.4 us -> 19.6 us  [hop(): return lax.ppermute(block, ('row', 'col'), route)]
    unnamed x8 -> x6, local copies, waits for them, and re-layouts: 1.86 us -> 0.93 us
    pallas_call x6 -> x7, Pallas kernels: 6.7 us -> 7.44 us  [call(): pl.pallas_call(kernel, out_shape=out_shape, in_specs=[pl.BlockSpec(memory...]
  transfers between devices with their start and end apart: 21 -> 21, of which waited for: 5 -> 7; matrix products, arithmetic and copies ran while one was open for 0% -> 0% of each run, Pallas kernels for 11% -> 13%
where the time goes in v8:
time: 44.2 us; the launch traced here: 44 us
  starting transfers between devices  21.5 us (49%)
  Pallas kernels  9.28 us (21%)
  waiting for transfers between devices  8.8 us (20%)
  between operations  3.38 us (8%)
  local copies, waits for them, and re-layouts  0.93 us (2%)
    ppermute x12, starting transfers between devices, hop(): return lax.ppermute(block, ('row', 'col'), route)  19.6 us
    ppermute x12, waiting for transfers between devices, hop(): return lax.ppermute(block, ('row', 'col'), route)  8.78 us
    pallas_call x7, Pallas kernels, call(): pl.pallas_call(kernel, out_shape=out_shape, in_specs=[pl.BlockSpec(memory...  7.44 us
    pallas_call x1, Pallas kernels, pair_body(): pl.pallas_call(first_kernel, out_shape=(sent, sent), in_specs=[pl.BlockSp...  1.84 us
    ppermute x9, starting transfers between devices, swap(): return lax.ppermute(block, 'row', [(0, 1), (1, 0)])  1.82 us
    unnamed x6, local copies, waits for them, and re-layouts  0.93 us
  transfers between devices with their start and end apart: 21, of which 7 were waited for; matrix products, arithmetic and copies ran while one was open for 0% of the time, Pallas kernels for 13%

profile of v8, /device:TPU:0, one launch (start us, length us, event | category | flops | bytes accessed | tf_op | source)
XLA Modules:
  0.0 44.0 jit_solution(5267413514721311843)
XLA Ops:
  0.6 1.8 %shard_map.95 = (bf16[88,1152]{1,0:T(8,128)(2,1)}, bf16[88,1152]{1,0:T(8,128)(2,1)}) custom-call(s32[1]{0:T(128)} %bitcast.spot_ref.row_ref, bf16[80,1152]{1,0:T(8,128)(2,1)} %image_ref.1, bf16[160,576]{1,0:T(8,128)(2,1)} %text_ref.1, s32[1,80]{1,0:T(1,128)} %bitcast.5, s32[1,160]{1,0:T(1,128)} %bitcast.4), custom_call_target="tpu_custom_call" | custom-call | tf_op jit(solution)/shard_map/pallas_call | solution.py:282
  2.5 0.5 %collective-permute-start.2 = (bf16[88,1152]{1,0:T(8,128)(2,1)}, bf16[88,1152]{1,0:T(8,128)(2,1)S(1)}, u32[]{:S(2)}, u32[]{:S(2)}) collective-permute-start(bf16[88,1152]{1,0:T(8,128)(2,1)} %get-tuple-element.27.refs_3_.refs_5_), channel_id=1, source_target_pairs={{0,16},{16,0},{1,17},{17,1},{2,18},{18,2},{3,19},{19,3},{4,20},{20... | collective-permute-start | bytes 608264 | tf_op jit(solution)/shard_map/ppermute | solution.py:23
  3.0 3.7 %collective-permute-start = (bf16[88,1152]{1,0:T(8,128)(2,1)}, bf16[88,1152]{1,0:T(8,128)(2,1)S(1)}, u32[]{:S(2)}, u32[]{:S(2)}) collective-permute-start(bf16[88,1152]{1,0:T(8,128)(2,1)} %get-tuple-element.25.refs_2_), channel_id=1, source_target_pairs={{0,8},{1,9},{2,10},{3,11},{4,12},{5,13},{6,14},{7,15},{8,0},{9,1},... | collective-permute-start | bytes 608264 | tf_op jit(solution)/shard_map/ppermute | solution.py:19
  6.7 0.0 collective-permute-done.2.refs_3_
  6.7 1.6 %collective-permute-start.8 = (bf16[88,1152]{1,0:T(8,128)(2,1)S(1)}, bf16[88,1152]{1,0:T(8,128)(2,1)S(1)}, u32[]{:S(2)}, u32[]{:S(2)}) collective-permute-start(bf16[88,1152]{1,0:T(8,128)(2,1)S(1)} %collective-permute-done.2.refs_3_), channel_id=1, source_target_pairs={{0,8},{1,9},{2,10},{3,11},{4,12},{5,13},{6,14},{7,15},{8,0},{9,1},... | collective-permute-start | bytes 608264 | tf_op jit(solution)/shard_map/ppermute | solution.py:19
  8.2 1.5 %collective-permute-start.1 = (bf16[88,1152]{1,0:T(8,128)(2,1)}, bf16[88,1152]{1,0:T(8,128)(2,1)S(1)}, u32[]{:S(2)}, u32[]{:S(2)}) collective-permute-start(bf16[88,1152]{1,0:T(8,128)(2,1)} %get-tuple-element.25.refs_2_), channel_id=1, source_target_pairs={{0,1},{1,0},{2,3},{3,2},{4,5},{5,4},{6,7},{7,6},{8,9},{9,8},{10,11... | collective-permute-start | bytes 608264 | tf_op jit(solution)/shard_map/ppermute | solution.py:19
  12.4 0.1 collective-permute-done.refs_2_.refs_0_
  12.5 0.0 collective-permute-start.7
  12.5 1.5 %collective-permute-start.10 = (bf16[88,1152]{1,0:T(8,128)(2,1)S(1)}, bf16[88,1152]{1,0:T(8,128)(2,1)S(1)}, u32[]{:S(2)}, u32[]{:S(2)}) collective-permute-start(bf16[88,1152]{1,0:T(8,128)(2,1)S(1)} %collective-permute-done.refs_2_.refs_0_), channel_id=1, source_target_pairs={{0,1},{1,0},{2,3},{3,2},{4,5},{5,4},{6,7},{7,6},{8,9},{9,8},{10,11... | collective-permute-start | bytes 608264 | tf_op jit(solution)/shard_map/ppermute | solution.py:19
  14.0 0.6 %collective-permute-start.3 = (bf16[88,1152]{1,0:T(8,128)(2,1)S(1)}, bf16[88,1152]{1,0:T(8,128)(2,1)S(1)}, u32[]{:S(2)}, u32[]{:S(2)}) collective-permute-start(bf16[88,1152]{1,0:T(8,128)(2,1)S(1)} %collective-permute-done.2.refs_3_), channel_id=1, source_target_pairs={{0,1},{1,0},{2,3},{3,2},{4,5},{5,4},{6,7},{7,6},{8,9},{9,8},{10,11... | collective-permute-start | bytes 608264 | tf_op jit(solution)/shard_map/ppermute | solution.py:19
  14.6 1.4 %collective-permute-done.8.refs_3_.refs_1_ = bf16[88,1152]{1,0:T(8,128)(2,1)S(1)} collective-permute-done((bf16[88,1152]{1,0:T(8,128)(2,1)S(1)}, bf16[88,1152]{1,0:T(8,128)(2,1)S(1)}, u32[]{:S(2)}, u32[]{:S(2)}) %collective-permute-start.8) | collective-permute-done | bytes 202784 | tf_op jit(solution)/shard_map/ppermute | solution.py:19
  15.9 0.0 collective-permute-start.9
  15.9 0.0 collective-permute-done.1.refs_0_
  15.9 2.1 %collective-permute-start.12 = (bf16[88,1152]{1,0:T(8,128)(2,1)S(1)}, bf16[88,1152]{1,0:T(8,128)(2,1)S(1)}, u32[]{:S(2)}, u32[]{:S(2)}) collective-permute-start(bf16[88,1152]{1,0:T(8,128)(2,1)S(1)} %collective-permute-done.8.refs_3_.refs_1_), channel_id=1, source_target_pairs={{0,1},{1,0},{2,3},{3,2},{4,5},{5,4},{6,7},{7,6},{8,9},{9,8},{10,11... | collective-permute-start | bytes 608264 | tf_op jit(solution)/shard_map/ppermute | solution.py:19
  18.1 0.0 collective-permute-done.7.refs_4_.refs_6_.refs_8_
  18.1 0.3 collective-permute-start.4
  18.3 0.0 collective-permute-done.10.refs_0_
  18.3 0.3 collective-permute-start.5
  18.6 1.8 %collective-permute-done.3.refs_1_ = bf16[88,1152]{1,0:T(8,128)(2,1)S(1)} collective-permute-done((bf16[88,1152]{1,0:T(8,128)(2,1)S(1)}, bf16[88,1152]{1,0:T(8,128)(2,1)S(1)}, u32[]{:S(2)}, u32[]{:S(2)}) %collective-permute-start.3) | collective-permute-done | bytes 202784 | tf_op jit(solution)/shard_map/ppermute | solution.py:19
  20.4 0.0 collective-permute-start.6
  20.4 0.0 collective-permute-done.9.refs_5_.refs_7_.refs_9_
  20.4 0.5 %collective-permute-start.11 = (bf16[88,1152]{1,0:T(8,128)(2,1)S(1)}, bf16[88,1152]{1,0:T(8,128)(2,1)S(1)}, u32[]{:S(2)}, u32[]{:S(2)}) collective-permute-start(bf16[88,1152]{1,0:T(8,128)(2,1)S(1)} %collective-permute-done.10.refs_0_), channel_id=1, source_target_pairs={{0,16},{16,0},{1,17},{17,1},{2,18},{18,2},{3,19},{19,3},{4,20},{20... | collective-permute-start | bytes 608264 | tf_op jit(solution)/shard_map/ppermute | solution.py:23
  21.0 1.3 %shard_map.97 = (bf16[320,1152]{1,0:T(8,128)(2,1)S(1)}, bf16[160,1152]{1,0:T(8,128)(2,1)S(1)}, f32[320,1152]{1,0:T(8,128)S(1)}) custom-call(s32[1]{0:T(128)} %bitcast.spot_ref.row_ref, s32[1]{0:T(128)} %bitcast.1.col_ref, f32[8,128]{1,0:T(8,128)S(1)} %shard_map.96.number_ref, bf16[88,1152]{1,0:T(8,128)(2,1)S(1)} %collective-permute-done.1.refs_0_, ...), custom_call_target="tpu_custom_call" | custom-call | flops 235929600 | bytes 3801096 | tf_op jit(solution)/shard_map/pallas_call | solution.py:255
  22.3 0.4 collective-permute-done.12.refs_1_
  22.6 0.0 collective-permute-start.13
  22.6 0.0 collective-permute-done.4.refs_2_.refs_4_
  22.6 0.0 collective-permute-done.5.refs_4_.refs_6_
  22.6 0.0 collective-permute-done.6.refs_5_.refs_7_
  22.6 0.9 %copy-done = bf16[88,1152]{1,0:T(8,128)(2,1)S(1)} copy-done((bf16[88,1152]{1,0:T(8,128)(2,1)S(1)}, bf16[88,1152]{1,0:T(8,128)(2,1)}, u32[]{:S(2)}) %copy-start) | copy-done | bytes 202776
  23.6 1.2 %shard_map.98 = (bf16[320,1152]{1,0:T(8,128)(2,1)S(1)}, bf16[160,1152]{1,0:T(8,128)(2,1)S(1)}, f32[160,1152]{1,0:T(8,128)S(1)}) custom-call(s32[1]{0:T(128)} %bitcast.spot_ref.row_ref, s32[1]{0:T(128)} %bitcast.1.col_ref, f32[8,128]{1,0:T(8,128)S(1)} %shard_map.96.number_ref, bf16[88,1152]{1,0:T(8,128)(2,1)S(1)} %collective-permute-done.10.refs_0_, ...), custom_call_target="tpu_custom_call" | custom-call | flops 353894400 | bytes 3837960 | tf_op jit(solution)/shard_map/pallas_call | solution.py:255
  24.7 0.0 collective-permute-done.11.refs_2_.refs_10_.refs_6_
  24.7 0.0 collective-permute-done.13.refs_3_.refs_11_.refs_7_
  24.8 0.9 %shard_map.99 = (bf16[160,1152]{1,0:T(8,128)(2,1)S(1)}, bf16[80,1152]{1,0:T(8,128)(2,1)S(1)}, bf16[80,1152]{1,0:T(8,128)(2,1)S(1)}) custom-call(s32[1]{0:T(128)} %bitcast.spot_ref.row_ref, s32[1]{0:T(128)} %bitcast.1.col_ref, f32[8,128]{1,0:T(8,128)S(1)} %shard_map.96.number_ref, bf16[88,1152]{1,0:T(8,128)(2,1)S(1)} %collective-permute-done.10.refs_0_, ...), custom_call_target="tpu_custom_call" | custom-call | flops 117964800 | bytes 2658312 | tf_op jit(solution)/shard_map/pallas_call | solution.py:255
  25.7 1.5 %collective-permute-start.14 = (bf16[80,1152]{1,0:T(8,128)(2,1)S(1)}, bf16[80,1152]{1,0:T(8,128)(2,1)S(1)}, u32[]{:S(2)}, u32[]{:S(2)}) collective-permute-start(bf16[80,1152]{1,0:T(8,128)(2,1)S(1)} %get-tuple-element.40), channel_id=1, source_target_pairs={{0,1},{1,0},{2,3},{3,2},{4,5},{5,4},{6,7},{7,6},{8,9},{9,8},{10,11... | collective-permute-start | bytes 552968 | tf_op jit(solution)/shard_map/ppermute | solution.py:19
  27.2 0.6 %collective-permute-start.17 = (bf16[80,1152]{1,0:T(8,128)(2,1)S(1)}, bf16[80,1152]{1,0:T(8,128)(2,1)S(1)}, u32[]{:S(2)}, u32[]{:S(2)}) collective-permute-start(bf16[80,1152]{1,0:T(8,128)(2,1)S(1)} %get-tuple-element.43), channel_id=1, source_target_pairs={{0,1},{1,0},{2,3},{3,2},{4,5},{5,4},{6,7},{7,6},{8,9},{9,8},{10,11... | collective-permute-start | bytes 552968 | tf_op jit(solution)/shard_map/ppermute | solution.py:19
  27.8 2.2 %shard_map.100 = (f32[80,1152]{1,0:T(8,128)S(1)}, f32[80,1152]{1,0:T(8,128)S(1)}, bf16[80,1152]{1,0:T(8,128)(2,1)S(1)}, bf16[80,1152]{1,0:T(8,128)(2,1)S(1)}) custom-call(s32[1]{0:T(128)} %bitcast.spot_ref.row_ref, s32[1]{0:T(128)} %bitcast.1.col_ref, f32[8,128]{1,0:T(8,128)S(1)} %shard_map.96.number_ref, ...), custom_call_target="tpu_custom_call" | custom-call | flops 825753600 | bytes 7229448 | tf_op jit(solution)/shard_map/pallas_call | solution.py:255
  29.9 0.3 collective-permute-start.16
  30.2 1.0 %shard_map.101 = (f32[80,1152]{1,0:T(8,128)S(1)}, f32[80,1152]{1,0:T(8,128)S(1)}) custom-call(s32[1]{0:T(128)} %bitcast.spot_ref.row_ref, s32[1]{0:T(128)} %bitcast.1.col_ref, f32[8,128]{1,0:T(8,128)S(1)} %shard_map.96.number_ref, bf16[88,1152]{1,0:T(8,128)(2,1)S(1)} %collective-permute-done.refs_2_.refs_0_, ...), custom_call_target="tpu_custom_call" | custom-call | flops 353894400 | bytes 5681160 | tf_op jit(solution)/shard_map/pallas_call | solution.py:255
  31.2 0.1 collective-permute-done.14
  31.3 3.3 %collective-permute-start.15 = (bf16[80,1152]{1,0:T(8,128)(2,1)S(1)}, bf16[80,1152]{1,0:T(8,128)(2,1)S(1)}, u32[]{:S(2)}, u32[]{:S(2)}) collective-permute-start(bf16[80,1152]{1,0:T(8,128)(2,1)S(1)} %add_convert_fusion.1), channel_id=1, source_target_pairs={{0,8},{1,9},{2,10},{3,11},{4,12},{5,13},{6,14},{7,15},{8,0},{9,1},... | collective-permute-start | bytes 552968 | tf_op jit(solution)/shard_map/ppermute | solution.py:19
  34.6 1.5 %collective-permute-start.19 = (bf16[80,1152]{1,0:T(8,128)(2,1)S(1)}, bf16[80,1152]{1,0:T(8,128)(2,1)S(1)}, u32[]{:S(2)}, u32[]{:S(2)}) collective-permute-start(bf16[80,1152]{1,0:T(8,128)(2,1)S(1)} %get-tuple-element.45), channel_id=1, source_target_pairs={{0,1},{1,0},{2,3},{3,2},{4,5},{5,4},{6,7},{7,6},{8,9},{9,8},{10,11... | collective-permute-start | bytes 552968 | tf_op jit(solution)/shard_map/ppermute | solution.py:19
  36.1 0.0 collective-permute-done.17
  36.1 1.0 %collective-permute-start.18 = (bf16[80,1152]{1,0:T(8,128)(2,1)S(1)}, bf16[80,1152]{1,0:T(8,128)(2,1)S(1)}, u32[]{:S(2)}, u32[]{:S(2)}) collective-permute-start(bf16[80,1152]{1,0:T(8,128)(2,1)S(1)} %add_convert_fusion), channel_id=1, source_target_pairs={{0,24},{1,25},{2,26},{3,27},{4,28},{5,29},{6,30},{7,31},{8,16},{9,... | collective-permute-start | bytes 552968 | tf_op jit(solution)/shard_map/ppermute | solution.py:19
  37.2 0.8 %collective-permute-start.20 = (bf16[80,1152]{1,0:T(8,128)(2,1)S(1)}, bf16[80,1152]{1,0:T(8,128)(2,1)S(1)}, u32[]{:S(2)}, u32[]{:S(2)}) collective-permute-start(bf16[80,1152]{1,0:T(8,128)(2,1)S(1)} %get-tuple-element.47), channel_id=1, source_target_pairs={{0,17},{1,16},{2,19},{3,18},{4,21},{5,20},{6,23},{7,22},{8,25},{9,... | collective-permute-start | bytes 552968 | tf_op jit(solution)/shard_map/ppermute | solution.py:19
  37.9 1.0 %collective-permute-done.15 = bf16[80,1152]{1,0:T(8,128)(2,1)S(1)} collective-permute-done((bf16[80,1152]{1,0:T(8,128)(2,1)S(1)}, bf16[80,1152]{1,0:T(8,128)(2,1)S(1)}, u32[]{:S(2)}, u32[]{:S(2)}) %collective-permute-start.15) | collective-permute-done | bytes 184352 | tf_op jit(solution)/shard_map/ppermute | solution.py:19
  39.0 0.0 collective-permute-done.16
  39.0 4.0 %collective-permute-done.18 = bf16[80,1152]{1,0:T(8,128)(2,1)S(1)} collective-permute-done((bf16[80,1152]{1,0:T(8,128)(2,1)S(1)}, bf16[80,1152]{1,0:T(8,128)(2,1)S(1)}, u32[]{:S(2)}, u32[]{:S(2)}) %collective-permute-start.18) | collective-permute-done | bytes 184352 | tf_op jit(solution)/shard_map/ppermute | solution.py:19
  43.1 0.9 %shard_map.102 = (bf16[80,1152]{1,0:T(8,128)(2,1)}, bf16[160,576]{1,0:T(8,128)(2,1)}) custom-call(s32[1]{0:T(128)} %bitcast.spot_ref.row_ref, f32[80,1152]{1,0:T(8,128)S(1)} %convert_add_fusion.1.stay_ref, f32[80,1152]{1,0:T(8,128)S(1)} %convert_add_fusion.crossed_ref, bf16[80,1152]{1,0:T(8,128)(2,1)S(1)} %collective-permute-done.19.near_stay_ref, ...), custom_call_target="tpu_custom_call" | custom-call | bytes 1474564 | tf_op jit(solution)/shard_map/pallas_call | solution.py:255
  (12 shorter events, 0.2 us)
Async XLA Ops:
  2.5 4.2 %collective-permute-start.2 = (bf16[88,1152]{1,0:T(8,128)(2,1)}, bf16[88,1152]{1,0:T(8,128)(2,1)S(1)}, u32[]{:S(2)}, u32[]{:S(2)}) collective-permute-start(bf16[88,1152]{1,0:T(8,128)(2,1)} %get-tuple-element.27.refs_3_.refs_5_), channel_id=1, source_target_pairs={{0,16},{16,0},{1,17},{17,1},{2,18},{18,2},{3,19},{19,3},{4,20},{20... | collective-permute-start | bytes 608264 | tf_op jit(solution)/shard_map/ppermute | solution.py:23
  3.0 9.5 %collective-permute-start = (bf16[88,1152]{1,0:T(8,128)(2,1)}, bf16[88,1152]{1,0:T(8,128)(2,1)S(1)}, u32[]{:S(2)}, u32[]{:S(2)}) collective-permute-start(bf16[88,1152]{1,0:T(8,128)(2,1)} %get-tuple-element.25.refs_2_), channel_id=1, source_target_pairs={{0,8},{1,9},{2,10},{3,11},{4,12},{5,13},{6,14},{7,15},{8,0},{9,1},... | collective-permute-start | bytes 608264 | tf_op jit(solution)/shard_map/ppermute | solution.py:19
  6.7 9.3 %collective-permute-start.8 = (bf16[88,1152]{1,0:T(8,128)(2,1)S(1)}, bf16[88,1152]{1,0:T(8,128)(2,1)S(1)}, u32[]{:S(2)}, u32[]{:S(2)}) collective-permute-start(bf16[88,1152]{1,0:T(8,128)(2,1)S(1)} %collective-permute-done.2.refs_3_), channel_id=1, source_target_pairs={{0,8},{1,9},{2,10},{3,11},{4,12},{5,13},{6,14},{7,15},{8,0},{9,1},... | collective-permute-start | bytes 608264 | tf_op jit(solution)/shard_map/ppermute | solution.py:19
  8.2 7.7 %collective-permute-start.1 = (bf16[88,1152]{1,0:T(8,128)(2,1)}, bf16[88,1152]{1,0:T(8,128)(2,1)S(1)}, u32[]{:S(2)}, u32[]{:S(2)}) collective-permute-start(bf16[88,1152]{1,0:T(8,128)(2,1)} %get-tuple-element.25.refs_2_), channel_id=1, source_target_pairs={{0,1},{1,0},{2,3},{3,2},{4,5},{5,4},{6,7},{7,6},{8,9},{9,8},{10,11... | collective-permute-start | bytes 608264 | tf_op jit(solution)/shard_map/ppermute | solution.py:19
  12.5 5.6 %collective-permute-start.7 = (bf16[88,1152]{1,0:T(8,128)(2,1)S(1)}, bf16[88,1152]{1,0:T(8,128)(2,1)S(1)}, u32[]{:S(2)}, u32[]{:S(2)}) collective-permute-start(bf16[88,1152]{1,0:T(8,128)(2,1)S(1)} %collective-permute-done.refs_2_.refs_0_), channel_id=1, source_target_pairs={{0,16},{16,0},{1,17},{17,1},{2,18},{18,2},{3,19},{19,3},{4,20},{20... | collective-permute-start | bytes 608264 | tf_op jit(solution)/shard_map/ppermute | solution.py:23
  12.5 5.9 %collective-permute-start.10 = (bf16[88,1152]{1,0:T(8,128)(2,1)S(1)}, bf16[88,1152]{1,0:T(8,128)(2,1)S(1)}, u32[]{:S(2)}, u32[]{:S(2)}) collective-permute-start(bf16[88,1152]{1,0:T(8,128)(2,1)S(1)} %collective-permute-done.refs_2_.refs_0_), channel_id=1, source_target_pairs={{0,1},{1,0},{2,3},{3,2},{4,5},{5,4},{6,7},{7,6},{8,9},{9,8},{10,11... | collective-permute-start | bytes 608264 | tf_op jit(solution)/shard_map/ppermute | solution.py:19
  14.0 6.5 %collective-permute-start.3 = (bf16[88,1152]{1,0:T(8,128)(2,1)S(1)}, bf16[88,1152]{1,0:T(8,128)(2,1)S(1)}, u32[]{:S(2)}, u32[]{:S(2)}) collective-permute-start(bf16[88,1152]{1,0:T(8,128)(2,1)S(1)} %collective-permute-done.2.refs_3_), channel_id=1, source_target_pairs={{0,1},{1,0},{2,3},{3,2},{4,5},{5,4},{6,7},{7,6},{8,9},{9,8},{10,11... | collective-permute-start | bytes 608264 | tf_op jit(solution)/shard_map/ppermute | solution.py:19
  15.9 4.5 %collective-permute-start.9 = (bf16[88,1152]{1,0:T(8,128)(2,1)S(1)}, bf16[88,1152]{1,0:T(8,128)(2,1)S(1)}, u32[]{:S(2)}, u32[]{:S(2)}) collective-permute-start(bf16[88,1152]{1,0:T(8,128)(2,1)S(1)} %collective-permute-done.8.refs_3_.refs_1_), channel_id=1, source_target_pairs={{0,16},{16,0},{1,17},{17,1},{2,18},{18,2},{3,19},{19,3},{4,20},{20... | collective-permute-start | bytes 608264 | tf_op jit(solution)/shard_map/ppermute | solution.py:23
  15.9 6.7 %collective-permute-start.12 = (bf16[88,1152]{1,0:T(8,128)(2,1)S(1)}, bf16[88,1152]{1,0:T(8,128)(2,1)S(1)}, u32[]{:S(2)}, u32[]{:S(2)}) collective-permute-start(bf16[88,1152]{1,0:T(8,128)(2,1)S(1)} %collective-permute-done.8.refs_3_.refs_1_), channel_id=1, source_target_pairs={{0,1},{1,0},{2,3},{3,2},{4,5},{5,4},{6,7},{7,6},{8,9},{9,8},{10,11... | collective-permute-start | bytes 608264 | tf_op jit(solution)/shard_map/ppermute | solution.py:19
  18.1 4.5 %collective-permute-start.4 = (bf16[88,1152]{1,0:T(8,128)(2,1)}, bf16[88,1152]{1,0:T(8,128)(2,1)S(1)}, u32[]{:S(2)}, u32[]{:S(2)}) collective-permute-start(bf16[88,1152]{1,0:T(8,128)(2,1)} %get-tuple-element.25.refs_2_), channel_id=1, source_target_pairs={{0,16},{16,0},{1,17},{17,1},{2,18},{18,2},{3,19},{19,3},{4,20},{20... | collective-permute-start | bytes 608264 | tf_op jit(solution)/shard_map/ppermute | solution.py:23
  18.3 4.3 %collective-permute-start.5 = (bf16[88,1152]{1,0:T(8,128)(2,1)S(1)}, bf16[88,1152]{1,0:T(8,128)(2,1)S(1)}, u32[]{:S(2)}, u32[]{:S(2)}) collective-permute-start(bf16[88,1152]{1,0:T(8,128)(2,1)S(1)} %collective-permute-done.1.refs_0_), channel_id=1, source_target_pairs={{0,16},{16,0},{1,17},{17,1},{2,18},{18,2},{3,19},{19,3},{4,20},{20... | collective-permute-start | bytes 608264 | tf_op jit(solution)/shard_map/ppermute | solution.py:23
  20.4 2.2 %collective-permute-start.6 = (bf16[88,1152]{1,0:T(8,128)(2,1)S(1)}, bf16[88,1152]{1,0:T(8,128)(2,1)S(1)}, u32[]{:S(2)}, u32[]{:S(2)}) collective-permute-start(bf16[88,1152]{1,0:T(8,128)(2,1)S(1)} %collective-permute-done.3.refs_1_), channel_id=1, source_target_pairs={{0,16},{16,0},{1,17},{17,1},{2,18},{18,2},{3,19},{19,3},{4,20},{20... | collective-permute-start | bytes 608264 | tf_op jit(solution)/shard_map/ppermute | solution.py:23
  20.4 4.3 %collective-permute-start.11 = (bf16[88,1152]{1,0:T(8,128)(2,1)S(1)}, bf16[88,1152]{1,0:T(8,128)(2,1)S(1)}, u32[]{:S(2)}, u32[]{:S(2)}) collective-permute-start(bf16[88,1152]{1,0:T(8,128)(2,1)S(1)} %collective-permute-done.10.refs_0_), channel_id=1, source_target_pairs={{0,16},{16,0},{1,17},{17,1},{2,18},{18,2},{3,19},{19,3},{4,20},{20... | collective-permute-start | bytes 608264 | tf_op jit(solution)/shard_map/ppermute | solution.py:23
  22.6 2.1 %collective-permute-start.13 = (bf16[88,1152]{1,0:T(8,128)(2,1)S(1)}, bf16[88,1152]{1,0:T(8,128)(2,1)S(1)}, u32[]{:S(2)}, u32[]{:S(2)}) collective-permute-start(bf16[88,1152]{1,0:T(8,128)(2,1)S(1)} %collective-permute-done.12.refs_1_), channel_id=1, source_target_pairs={{0,16},{16,0},{1,17},{17,1},{2,18},{18,2},{3,19},{19,3},{4,20},{20... | collective-permute-start | bytes 608264 | tf_op jit(solution)/shard_map/ppermute | solution.py:23
  22.6 0.9 %copy-start = (bf16[88,1152]{1,0:T(8,128)(2,1)S(1)}, bf16[88,1152]{1,0:T(8,128)(2,1)}, u32[]{:S(2)}) copy-start(bf16[88,1152]{1,0:T(8,128)(2,1)} %get-tuple-element.27.refs_3_.refs_5_) | copy-start | bytes 608260
  23.6 4.2 %copy-start.1 = (bf16[88,1152]{1,0:T(8,128)(2,1)S(1)}, bf16[88,1152]{1,0:T(8,128)(2,1)}, u32[]{:S(2)}) copy-start(bf16[88,1152]{1,0:T(8,128)(2,1)} %get-tuple-element.27.refs_3_.refs_5_) | copy-start | bytes 608260
  23.6 4.2 %copy-start.2 = (bf16[88,1152]{1,0:T(8,128)(2,1)S(1)}, bf16[88,1152]{1,0:T(8,128)(2,1)}, u32[]{:S(2)}) copy-start(bf16[88,1152]{1,0:T(8,128)(2,1)} %get-tuple-element.25.refs_2_) | copy-start | bytes 608260
  25.7 5.6 %collective-permute-start.14 = (bf16[80,1152]{1,0:T(8,128)(2,1)S(1)}, bf16[80,1152]{1,0:T(8,128)(2,1)S(1)}, u32[]{:S(2)}, u32[]{:S(2)}) collective-permute-start(bf16[80,1152]{1,0:T(8,128)(2,1)S(1)} %get-tuple-element.40), channel_id=1, source_target_pairs={{0,1},{1,0},{2,3},{3,2},{4,5},{5,4},{6,7},{7,6},{8,9},{9,8},{10,11... | collective-permute-start | bytes 552968 | tf_op jit(solution)/shard_map/ppermute | solution.py:19
  27.2 8.9 %collective-permute-start.17 = (bf16[80,1152]{1,0:T(8,128)(2,1)S(1)}, bf16[80,1152]{1,0:T(8,128)(2,1)S(1)}, u32[]{:S(2)}, u32[]{:S(2)}) collective-permute-start(bf16[80,1152]{1,0:T(8,128)(2,1)S(1)} %get-tuple-element.43), channel_id=1, source_target_pairs={{0,1},{1,0},{2,3},{3,2},{4,5},{5,4},{6,7},{7,6},{8,9},{9,8},{10,11... | collective-permute-start | bytes 552968 | tf_op jit(solution)/shard_map/ppermute | solution.py:19
  29.9 9.1 %collective-permute-start.16 = (f32[80,1152]{1,0:T(8,128)S(1)}, f32[80,1152]{1,0:T(8,128)S(1)}, u32[]{:S(2)}, u32[]{:S(2)}) collective-permute-start(f32[80,1152]{1,0:T(8,128)S(1)} %get-tuple-element.41), channel_id=1, source_target_pairs={{0,16},{16,0},{1,17},{17,1},{2,18},{18,2},{3,19},{19,3},{4,20},{20... | collective-permute-start | bytes 1105928 | tf_op jit(solution)/shard_map/ppermute | solution.py:23
  31.3 7.7 %collective-permute-start.15 = (bf16[80,1152]{1,0:T(8,128)(2,1)S(1)}, bf16[80,1152]{1,0:T(8,128)(2,1)S(1)}, u32[]{:S(2)}, u32[]{:S(2)}) collective-permute-start(bf16[80,1152]{1,0:T(8,128)(2,1)S(1)} %add_convert_fusion.1), channel_id=1, source_target_pairs={{0,8},{1,9},{2,10},{3,11},{4,12},{5,13},{6,14},{7,15},{8,0},{9,1},... | collective-permute-start | bytes 552968 | tf_op jit(solution)/shard_map/ppermute | solution.py:19
  34.6 8.5 %collective-permute-start.19 = (bf16[80,1152]{1,0:T(8,128)(2,1)S(1)}, bf16[80,1152]{1,0:T(8,128)(2,1)S(1)}, u32[]{:S(2)}, u32[]{:S(2)}) collective-permute-start(bf16[80,1152]{1,0:T(8,128)(2,1)S(1)} %get-tuple-element.45), channel_id=1, source_target_pairs={{0,1},{1,0},{2,3},{3,2},{4,5},{5,4},{6,7},{7,6},{8,9},{9,8},{10,11... | collective-permute-start | bytes 552968 | tf_op jit(solution)/shard_map/ppermute | solution.py:19
  36.1 6.9 %collective-permute-start.18 = (bf16[80,1152]{1,0:T(8,128)(2,1)S(1)}, bf16[80,1152]{1,0:T(8,128)(2,1)S(1)}, u32[]{:S(2)}, u32[]{:S(2)}) collective-permute-start(bf16[80,1152]{1,0:T(8,128)(2,1)S(1)} %add_convert_fusion), channel_id=1, source_target_pairs={{0,24},{1,25},{2,26},{3,27},{4,28},{5,29},{6,30},{7,31},{8,16},{9,... | collective-permute-start | bytes 552968 | tf_op jit(solution)/shard_map/ppermute | solution.py:19
  37.2 5.9 %collective-permute-start.20 = (bf16[80,1152]{1,0:T(8,128)(2,1)S(1)}, bf16[80,1152]{1,0:T(8,128)(2,1)S(1)}, u32[]{:S(2)}, u32[]{:S(2)}) collective-permute-start(bf16[80,1152]{1,0:T(8,128)(2,1)S(1)} %get-tuple-element.47), channel_id=1, source_target_pairs={{0,17},{1,16},{2,19},{3,18},{4,21},{5,20},{6,23},{7,22},{8,25},{9,... | collective-permute-start | bytes 552968 | tf_op jit(solution)/shard_map/ppermute | solution.py:19

commit v9 on v8

--- a/solution.py
+++ b/solution.py
@@ -297,7 +297,7 @@
     number = call(number_kernel, jax.ShapeDtypeStruct((8, 128), f32), 4, logit_scale, logit_bias, loss_grad, sample_count)
     far_a, number = lax.optimization_barrier((far_a, number))
     mine_own, mine_near, mine_far = (own_a, own_b), (near_a, near_b), (far_a, far_b)
-    own, near_pair, far_pair = (swap(own_a), give), (swap(near_a), swap(near_b)), (swap(far_a), swap(far_b))
+    own, near_pair, far_pair = (swap(own_a), swap(own_b)), (swap(near_a), swap(near_b)), (swap(far_a), swap(far_b))
     other_both_a = swap(both_a)
 
     pair_flops = 4 * size * size * width

time: 44.2 us -> 43 us (0.973)
  waiting for transfers between devices: 8.8 us -> 6.98 us
  starting transfers between devices: 21.5 us -> 22.9 us
  local copies, waits for them, and re-layouts: 0.93 us -> 0.01 us
    ppermute x12, waiting for transfers between devices: 8.78 us -> 6.95 us  [hop(): return lax.ppermute(block, ('row', 'col'), route)]
    unnamed x6 -> x2, local copies, waits for them, and re-layouts: 0.93 us -> 0.01 us
    ppermute x12, starting transfers between devices: 19.6 us -> 20.4 us  [hop(): return lax.ppermute(block, ('row', 'col'), route)]
    ppermute x9 -> x10, starting transfers between devices: 1.82 us -> 2.48 us  [swap(): return lax.ppermute(block, 'row', [(0, 1), (1, 0)])]
  transfers between devices with their start and end apart: 21 -> 22, of which waited for: 7 -> 4; matrix products, arithmetic and copies ran while one was open for 0% -> 0% of each run, Pallas kernels for 13% -> 13%
where the time goes in v9:
time: 43 us; the launch traced here: 42.7 us
  starting transfers between devices  22.9 us (53%)
  Pallas kernels  9.31 us (22%)
  waiting for transfers between devices  6.98 us (16%)
  between operations  3.39 us (8%)
    ppermute x12, starting transfers between devices, hop(): return lax.ppermute(block, ('row', 'col'), route)  20.4 us
    pallas_call x7, Pallas kernels, call(): pl.pallas_call(kernel, out_shape=out_shape, in_specs=[pl.BlockSpec(memory...  7.46 us
    ppermute x12, waiting for transfers between devices, hop(): return lax.ppermute(block, ('row', 'col'), route)  6.95 us
    ppermute x10, starting transfers between devices, swap(): return lax.ppermute(block, 'row', [(0, 1), (1, 0)])  2.48 us
    pallas_call x1, Pallas kernels, pair_body(): pl.pallas_call(first_kernel, out_shape=(sent, sent), in_specs=[pl.BlockSp...  1.85 us
  transfers between devices with their start and end apart: 22, of which 4 were waited for; matrix products, arithmetic and copies ran while one was open for 0% of the time, Pallas kernels for 13%

profile of v9, /device:TPU:0, one launch (start us, length us, event | category | flops | bytes accessed | tf_op | source)
XLA Modules:
  0.0 42.7 jit_solution(11105326122264440131)
XLA Ops:
  0.6 1.8 %shard_map.95 = (bf16[88,1152]{1,0:T(8,128)(2,1)}, bf16[88,1152]{1,0:T(8,128)(2,1)}) custom-call(s32[1]{0:T(128)} %bitcast.spot_ref.row_ref, bf16[80,1152]{1,0:T(8,128)(2,1)} %image_ref.1, bf16[160,576]{1,0:T(8,128)(2,1)} %text_ref.1, s32[1,80]{1,0:T(1,128)} %bitcast.5, s32[1,160]{1,0:T(1,128)} %bitcast.4), custom_call_target="tpu_custom_call" | custom-call | tf_op jit(solution)/shard_map/pallas_call | solution.py:282
  2.5 0.5 %collective-permute-start.2 = (bf16[88,1152]{1,0:T(8,128)(2,1)}, bf16[88,1152]{1,0:T(8,128)(2,1)S(1)}, u32[]{:S(2)}, u32[]{:S(2)}) collective-permute-start(bf16[88,1152]{1,0:T(8,128)(2,1)} %get-tuple-element.27), channel_id=1, source_target_pairs={{0,16},{16,0},{1,17},{17,1},{2,18},{18,2},{3,19},{19,3},{4,20},{20... | collective-permute-start | bytes 608264 | tf_op jit(solution)/shard_map/ppermute | solution.py:23
  3.0 3.7 %collective-permute-start = (bf16[88,1152]{1,0:T(8,128)(2,1)}, bf16[88,1152]{1,0:T(8,128)(2,1)S(1)}, u32[]{:S(2)}, u32[]{:S(2)}) collective-permute-start(bf16[88,1152]{1,0:T(8,128)(2,1)} %get-tuple-element.25.refs_2_), channel_id=1, source_target_pairs={{0,8},{1,9},{2,10},{3,11},{4,12},{5,13},{6,14},{7,15},{8,0},{9,1},... | collective-permute-start | bytes 608264 | tf_op jit(solution)/shard_map/ppermute | solution.py:19
  6.7 0.0 collective-permute-done.2.refs_3_
  6.7 1.6 %collective-permute-start.9 = (bf16[88,1152]{1,0:T(8,128)(2,1)S(1)}, bf16[88,1152]{1,0:T(8,128)(2,1)S(1)}, u32[]{:S(2)}, u32[]{:S(2)}) collective-permute-start(bf16[88,1152]{1,0:T(8,128)(2,1)S(1)} %collective-permute-done.2.refs_3_), channel_id=1, source_target_pairs={{0,8},{1,9},{2,10},{3,11},{4,12},{5,13},{6,14},{7,15},{8,0},{9,1},... | collective-permute-start | bytes 608264 | tf_op jit(solution)/shard_map/ppermute | solution.py:19
  8.3 1.5 %collective-permute-start.1 = (bf16[88,1152]{1,0:T(8,128)(2,1)}, bf16[88,1152]{1,0:T(8,128)(2,1)S(1)}, u32[]{:S(2)}, u32[]{:S(2)}) collective-permute-start(bf16[88,1152]{1,0:T(8,128)(2,1)} %get-tuple-element.25.refs_2_), channel_id=1, source_target_pairs={{0,1},{1,0},{2,3},{3,2},{4,5},{5,4},{6,7},{7,6},{8,9},{9,8},{10,11... | collective-permute-start | bytes 608264 | tf_op jit(solution)/shard_map/ppermute | solution.py:19
  9.7 0.5 %collective-permute-start.3 = (bf16[88,1152]{1,0:T(8,128)(2,1)S(1)}, bf16[88,1152]{1,0:T(8,128)(2,1)S(1)}, u32[]{:S(2)}, u32[]{:S(2)}) collective-permute-start(bf16[88,1152]{1,0:T(8,128)(2,1)S(1)} %collective-permute-done.2.refs_3_), channel_id=1, source_target_pairs={{0,1},{1,0},{2,3},{3,2},{4,5},{5,4},{6,7},{7,6},{8,9},{9,8},{10,11... | collective-permute-start | bytes 608264 | tf_op jit(solution)/shard_map/ppermute | solution.py:19
  12.9 0.0 collective-permute-done.refs_2_.refs_0_
  12.9 0.1 collective-permute-start.8
  13.0 1.6 %collective-permute-start.11 = (bf16[88,1152]{1,0:T(8,128)(2,1)S(1)}, bf16[88,1152]{1,0:T(8,128)(2,1)S(1)}, u32[]{:S(2)}, u32[]{:S(2)}) collective-permute-start(bf16[88,1152]{1,0:T(8,128)(2,1)S(1)} %collective-permute-done.refs_2_.refs_0_), channel_id=1, source_target_pairs={{0,1},{1,0},{2,3},{3,2},{4,5},{5,4},{6,7},{7,6},{8,9},{9,8},{10,11... | collective-permute-start | bytes 608264 | tf_op jit(solution)/shard_map/ppermute | solution.py:19
  14.6 1.4 %collective-permute-done.9.refs_3_.refs_1_ = bf16[88,1152]{1,0:T(8,128)(2,1)S(1)} collective-permute-done((bf16[88,1152]{1,0:T(8,128)(2,1)S(1)}, bf16[88,1152]{1,0:T(8,128)(2,1)S(1)}, u32[]{:S(2)}, u32[]{:S(2)}) %collective-permute-start.9) | collective-permute-done | bytes 202784 | tf_op jit(solution)/shard_map/ppermute | solution.py:19
  15.9 0.0 collective-permute-start.10
  15.9 0.0 collective-permute-done.1.refs_0_
  16.0 2.1 %collective-permute-start.13 = (bf16[88,1152]{1,0:T(8,128)(2,1)S(1)}, bf16[88,1152]{1,0:T(8,128)(2,1)S(1)}, u32[]{:S(2)}, u32[]{:S(2)}) collective-permute-start(bf16[88,1152]{1,0:T(8,128)(2,1)S(1)} %collective-permute-done.9.refs_3_.refs_1_), channel_id=1, source_target_pairs={{0,1},{1,0},{2,3},{3,2},{4,5},{5,4},{6,7},{7,6},{8,9},{9,8},{10,11... | collective-permute-start | bytes 608264 | tf_op jit(solution)/shard_map/ppermute | solution.py:19
  18.1 0.0 collective-permute-done.3.refs_1_
  18.1 0.3 collective-permute-start.4
  18.4 0.0 collective-permute-done.8.refs_4_.refs_6_.refs_8_
  18.4 0.3 collective-permute-start.5
  18.6 0.2 collective-permute-done.11.refs_0_
  18.8 0.1 collective-permute-start.6
  18.9 0.0 collective-permute-done.10.refs_5_.refs_7_.refs_9_
  18.9 0.5 %collective-permute-start.7 = (bf16[88,1152]{1,0:T(8,128)(2,1)S(1)}, bf16[88,1152]{1,0:T(8,128)(2,1)S(1)}, u32[]{:S(2)}, u32[]{:S(2)}) collective-permute-start(bf16[88,1152]{1,0:T(8,128)(2,1)S(1)} %collective-permute-done.3.refs_1_), channel_id=1, source_target_pairs={{0,16},{16,0},{1,17},{17,1},{2,18},{18,2},{3,19},{19,3},{4,20},{20... | collective-permute-start | bytes 608264 | tf_op jit(solution)/shard_map/ppermute | solution.py:23
  19.3 1.3 %shard_map.97 = (bf16[320,1152]{1,0:T(8,128)(2,1)S(1)}, bf16[160,1152]{1,0:T(8,128)(2,1)S(1)}, f32[320,1152]{1,0:T(8,128)S(1)}) custom-call(s32[1]{0:T(128)} %bitcast.spot_ref.row_ref, s32[1]{0:T(128)} %bitcast.1.col_ref, f32[8,128]{1,0:T(8,128)S(1)} %shard_map.96.number_ref, bf16[88,1152]{1,0:T(8,128)(2,1)S(1)} %collective-permute-done.1.refs_0_, ...), custom_call_target="tpu_custom_call" | custom-call | flops 235929600 | bytes 3801096 | tf_op jit(solution)/shard_map/pallas_call | solution.py:255
  20.6 1.2 %collective-permute-done.13.refs_1_ = bf16[88,1152]{1,0:T(8,128)(2,1)S(1)} collective-permute-done((bf16[88,1152]{1,0:T(8,128)(2,1)S(1)}, bf16[88,1152]{1,0:T(8,128)(2,1)S(1)}, u32[]{:S(2)}, u32[]{:S(2)}) %collective-permute-start.13) | collective-permute-done | bytes 202784 | tf_op jit(solution)/shard_map/ppermute | solution.py:19
  21.8 0.0 collective-permute-start.12
  21.8 0.0 collective-permute-done.4.refs_2_.refs_4_
  21.8 0.5 %collective-permute-start.14 = (bf16[88,1152]{1,0:T(8,128)(2,1)S(1)}, bf16[88,1152]{1,0:T(8,128)(2,1)S(1)}, u32[]{:S(2)}, u32[]{:S(2)}) collective-permute-start(bf16[88,1152]{1,0:T(8,128)(2,1)S(1)} %collective-permute-done.13.refs_1_), channel_id=1, source_target_pairs={{0,16},{16,0},{1,17},{17,1},{2,18},{18,2},{3,19},{19,3},{4,20},{20... | collective-permute-start | bytes 608264 | tf_op jit(solution)/shard_map/ppermute | solution.py:23
  22.3 0.0 collective-permute-done.5.refs_3_.refs_5_
  22.3 0.0 collective-permute-done.6.refs_4_.refs_6_
  22.3 0.0 collective-permute-done.7.refs_5_.refs_7_
  22.3 0.0 copy-start
  22.3 1.2 %shard_map.98 = (bf16[320,1152]{1,0:T(8,128)(2,1)S(1)}, bf16[160,1152]{1,0:T(8,128)(2,1)S(1)}, f32[160,1152]{1,0:T(8,128)S(1)}) custom-call(s32[1]{0:T(128)} %bitcast.spot_ref.row_ref, s32[1]{0:T(128)} %bitcast.1.col_ref, f32[8,128]{1,0:T(8,128)S(1)} %shard_map.96.number_ref, bf16[88,1152]{1,0:T(8,128)(2,1)S(1)} %collective-permute-done.11.refs_0_, ...), custom_call_target="tpu_custom_call" | custom-call | flops 353894400 | bytes 3837960 | tf_op jit(solution)/shard_map/pallas_call | solution.py:255
  23.5 0.0 collective-permute-done.12.refs_2_.refs_10_.refs_6_
  23.5 0.0 collective-permute-done.14.refs_3_.refs_11_.refs_7_
  23.6 0.9 %shard_map.99 = (bf16[160,1152]{1,0:T(8,128)(2,1)S(1)}, bf16[80,1152]{1,0:T(8,128)(2,1)S(1)}, bf16[80,1152]{1,0:T(8,128)(2,1)S(1)}) custom-call(s32[1]{0:T(128)} %bitcast.spot_ref.row_ref, s32[1]{0:T(128)} %bitcast.1.col_ref, f32[8,128]{1,0:T(8,128)S(1)} %shard_map.96.number_ref, bf16[88,1152]{1,0:T(8,128)(2,1)S(1)} %collective-permute-done.11.refs_0_, ...), custom_call_target="tpu_custom_call" | custom-call | flops 117964800 | bytes 2658312 | tf_op jit(solution)/shard_map/pallas_call | solution.py:255
  24.4 2.1 %collective-permute-start.15 = (bf16[80,1152]{1,0:T(8,128)(2,1)S(1)}, bf16[80,1152]{1,0:T(8,128)(2,1)S(1)}, u32[]{:S(2)}, u32[]{:S(2)}) collective-permute-start(bf16[80,1152]{1,0:T(8,128)(2,1)S(1)} %get-tuple-element.40), channel_id=1, source_target_pairs={{0,1},{1,0},{2,3},{3,2},{4,5},{5,4},{6,7},{7,6},{8,9},{9,8},{10,11... | collective-permute-start | bytes 552968 | tf_op jit(solution)/shard_map/ppermute | solution.py:19
  26.5 0.1 collective-permute-start.18
  26.6 2.2 %shard_map.100 = (f32[80,1152]{1,0:T(8,128)S(1)}, f32[80,1152]{1,0:T(8,128)S(1)}, bf16[80,1152]{1,0:T(8,128)(2,1)S(1)}, bf16[80,1152]{1,0:T(8,128)(2,1)S(1)}) custom-call(s32[1]{0:T(128)} %bitcast.spot_ref.row_ref, s32[1]{0:T(128)} %bitcast.1.col_ref, f32[8,128]{1,0:T(8,128)S(1)} %shard_map.96.number_ref, ...), custom_call_target="tpu_custom_call" | custom-call | flops 825753600 | bytes 7229448 | tf_op jit(solution)/shard_map/pallas_call | solution.py:255
  28.8 0.4 collective-permute-start.17
  29.1 1.0 %shard_map.101 = (f32[80,1152]{1,0:T(8,128)S(1)}, f32[80,1152]{1,0:T(8,128)S(1)}) custom-call(s32[1]{0:T(128)} %bitcast.spot_ref.row_ref, s32[1]{0:T(128)} %bitcast.1.col_ref, f32[8,128]{1,0:T(8,128)S(1)} %shard_map.96.number_ref, bf16[88,1152]{1,0:T(8,128)(2,1)S(1)} %collective-permute-done.refs_2_.refs_0_, ...), custom_call_target="tpu_custom_call" | custom-call | flops 353894400 | bytes 5681160 | tf_op jit(solution)/shard_map/pallas_call | solution.py:255
  30.2 2.5 %collective-permute-start.16 = (bf16[80,1152]{1,0:T(8,128)(2,1)S(1)}, bf16[80,1152]{1,0:T(8,128)(2,1)S(1)}, u32[]{:S(2)}, u32[]{:S(2)}) collective-permute-start(bf16[80,1152]{1,0:T(8,128)(2,1)S(1)} %add_convert_fusion.1), channel_id=1, source_target_pairs={{0,8},{1,9},{2,10},{3,11},{4,12},{5,13},{6,14},{7,15},{8,0},{9,1},... | collective-permute-start | bytes 552968 | tf_op jit(solution)/shard_map/ppermute | solution.py:19
  32.7 1.5 %collective-permute-start.20 = (bf16[80,1152]{1,0:T(8,128)(2,1)S(1)}, bf16[80,1152]{1,0:T(8,128)(2,1)S(1)}, u32[]{:S(2)}, u32[]{:S(2)}) collective-permute-start(bf16[80,1152]{1,0:T(8,128)(2,1)S(1)} %get-tuple-element.45), channel_id=1, source_target_pairs={{0,1},{1,0},{2,3},{3,2},{4,5},{5,4},{6,7},{7,6},{8,9},{9,8},{10,11... | collective-permute-start | bytes 552968 | tf_op jit(solution)/shard_map/ppermute | solution.py:19
  34.2 0.0 collective-permute-done.18
  34.2 2.5 %collective-permute-start.19 = (bf16[80,1152]{1,0:T(8,128)(2,1)S(1)}, bf16[80,1152]{1,0:T(8,128)(2,1)S(1)}, u32[]{:S(2)}, u32[]{:S(2)}) collective-permute-start(bf16[80,1152]{1,0:T(8,128)(2,1)S(1)} %add_convert_fusion), channel_id=1, source_target_pairs={{0,24},{1,25},{2,26},{3,27},{4,28},{5,29},{6,30},{7,31},{8,16},{9,... | collective-permute-start | bytes 552968 | tf_op jit(solution)/shard_map/ppermute | solution.py:19
  36.7 0.8 %collective-permute-start.21 = (bf16[80,1152]{1,0:T(8,128)(2,1)S(1)}, bf16[80,1152]{1,0:T(8,128)(2,1)S(1)}, u32[]{:S(2)}, u32[]{:S(2)}) collective-permute-start(bf16[80,1152]{1,0:T(8,128)(2,1)S(1)} %get-tuple-element.47), channel_id=1, source_target_pairs={{0,17},{1,16},{2,19},{3,18},{4,21},{5,20},{6,23},{7,22},{8,25},{9,... | collective-permute-start | bytes 552968 | tf_op jit(solution)/shard_map/ppermute | solution.py:19
  37.6 0.0 collective-permute-done.17
  37.6 4.2 %collective-permute-done.19 = bf16[80,1152]{1,0:T(8,128)(2,1)S(1)} collective-permute-done((bf16[80,1152]{1,0:T(8,128)(2,1)S(1)}, bf16[80,1152]{1,0:T(8,128)(2,1)S(1)}, u32[]{:S(2)}, u32[]{:S(2)}) %collective-permute-start.19) | collective-permute-done | bytes 184352 | tf_op jit(solution)/shard_map/ppermute | solution.py:19
  41.8 0.9 %shard_map.102 = (bf16[80,1152]{1,0:T(8,128)(2,1)}, bf16[160,576]{1,0:T(8,128)(2,1)}) custom-call(s32[1]{0:T(128)} %bitcast.spot_ref.row_ref, f32[80,1152]{1,0:T(8,128)S(1)} %convert_add_fusion.1.stay_ref, f32[80,1152]{1,0:T(8,128)S(1)} %convert_add_fusion.crossed_ref, bf16[80,1152]{1,0:T(8,128)(2,1)S(1)} %collective-permute-done.20.near_stay_ref, ...), custom_call_target="tpu_custom_call" | custom-call | bytes 1474564 | tf_op jit(solution)/shard_map/pallas_call | solution.py:255
  (10 shorter events, 0.2 us)
Async XLA Ops:
  2.5 4.2 %collective-permute-start.2 = (bf16[88,1152]{1,0:T(8,128)(2,1)}, bf16[88,1152]{1,0:T(8,128)(2,1)S(1)}, u32[]{:S(2)}, u32[]{:S(2)}) collective-permute-start(bf16[88,1152]{1,0:T(8,128)(2,1)} %get-tuple-element.27), channel_id=1, source_target_pairs={{0,16},{16,0},{1,17},{17,1},{2,18},{18,2},{3,19},{19,3},{4,20},{20... | collective-permute-start | bytes 608264 | tf_op jit(solution)/shard_map/ppermute | solution.py:23
  3.0 9.9 %collective-permute-start = (bf16[88,1152]{1,0:T(8,128)(2,1)}, bf16[88,1152]{1,0:T(8,128)(2,1)S(1)}, u32[]{:S(2)}, u32[]{:S(2)}) collective-permute-start(bf16[88,1152]{1,0:T(8,128)(2,1)} %get-tuple-element.25.refs_2_), channel_id=1, source_target_pairs={{0,8},{1,9},{2,10},{3,11},{4,12},{5,13},{6,14},{7,15},{8,0},{9,1},... | collective-permute-start | bytes 608264 | tf_op jit(solution)/shard_map/ppermute | solution.py:19
  6.7 9.3 %collective-permute-start.9 = (bf16[88,1152]{1,0:T(8,128)(2,1)S(1)}, bf16[88,1152]{1,0:T(8,128)(2,1)S(1)}, u32[]{:S(2)}, u32[]{:S(2)}) collective-permute-start(bf16[88,1152]{1,0:T(8,128)(2,1)S(1)} %collective-permute-done.2.refs_3_), channel_id=1, source_target_pairs={{0,8},{1,9},{2,10},{3,11},{4,12},{5,13},{6,14},{7,15},{8,0},{9,1},... | collective-permute-start | bytes 608264 | tf_op jit(solution)/shard_map/ppermute | solution.py:19
  8.3 7.7 %collective-permute-start.1 = (bf16[88,1152]{1,0:T(8,128)(2,1)}, bf16[88,1152]{1,0:T(8,128)(2,1)S(1)}, u32[]{:S(2)}, u32[]{:S(2)}) collective-permute-start(bf16[88,1152]{1,0:T(8,128)(2,1)} %get-tuple-element.25.refs_2_), channel_id=1, source_target_pairs={{0,1},{1,0},{2,3},{3,2},{4,5},{5,4},{6,7},{7,6},{8,9},{9,8},{10,11... | collective-permute-start | bytes 608264 | tf_op jit(solution)/shard_map/ppermute | solution.py:19
  9.7 8.4 %collective-permute-start.3 = (bf16[88,1152]{1,0:T(8,128)(2,1)S(1)}, bf16[88,1152]{1,0:T(8,128)(2,1)S(1)}, u32[]{:S(2)}, u32[]{:S(2)}) collective-permute-start(bf16[88,1152]{1,0:T(8,128)(2,1)S(1)} %collective-permute-done.2.refs_3_), channel_id=1, source_target_pairs={{0,1},{1,0},{2,3},{3,2},{4,5},{5,4},{6,7},{7,6},{8,9},{9,8},{10,11... | collective-permute-start | bytes 608264 | tf_op jit(solution)/shard_map/ppermute | solution.py:19
  12.9 5.4 %collective-permute-start.8 = (bf16[88,1152]{1,0:T(8,128)(2,1)S(1)}, bf16[88,1152]{1,0:T(8,128)(2,1)S(1)}, u32[]{:S(2)}, u32[]{:S(2)}) collective-permute-start(bf16[88,1152]{1,0:T(8,128)(2,1)S(1)} %collective-permute-done.refs_2_.refs_0_), channel_id=1, source_target_pairs={{0,16},{16,0},{1,17},{17,1},{2,18},{18,2},{3,19},{19,3},{4,20},{20... | collective-permute-start | bytes 608264 | tf_op jit(solution)/shard_map/ppermute | solution.py:23
  13.0 5.8 %collective-permute-start.11 = (bf16[88,1152]{1,0:T(8,128)(2,1)S(1)}, bf16[88,1152]{1,0:T(8,128)(2,1)S(1)}, u32[]{:S(2)}, u32[]{:S(2)}) collective-permute-start(bf16[88,1152]{1,0:T(8,128)(2,1)S(1)} %collective-permute-done.refs_2_.refs_0_), channel_id=1, source_target_pairs={{0,1},{1,0},{2,3},{3,2},{4,5},{5,4},{6,7},{7,6},{8,9},{9,8},{10,11... | collective-permute-start | bytes 608264 | tf_op jit(solution)/shard_map/ppermute | solution.py:19
  15.9 2.9 %collective-permute-start.10 = (bf16[88,1152]{1,0:T(8,128)(2,1)S(1)}, bf16[88,1152]{1,0:T(8,128)(2,1)S(1)}, u32[]{:S(2)}, u32[]{:S(2)}) collective-permute-start(bf16[88,1152]{1,0:T(8,128)(2,1)S(1)} %collective-permute-done.9.refs_3_.refs_1_), channel_id=1, source_target_pairs={{0,16},{16,0},{1,17},{17,1},{2,18},{18,2},{3,19},{19,3},{4,20},{20... | collective-permute-start | bytes 608264 | tf_op jit(solution)/shard_map/ppermute | solution.py:23
  16.0 5.9 %collective-permute-start.13 = (bf16[88,1152]{1,0:T(8,128)(2,1)S(1)}, bf16[88,1152]{1,0:T(8,128)(2,1)S(1)}, u32[]{:S(2)}, u32[]{:S(2)}) collective-permute-start(bf16[88,1152]{1,0:T(8,128)(2,1)S(1)} %collective-permute-done.9.refs_3_.refs_1_), channel_id=1, source_target_pairs={{0,1},{1,0},{2,3},{3,2},{4,5},{5,4},{6,7},{7,6},{8,9},{9,8},{10,11... | collective-permute-start | bytes 608264 | tf_op jit(solution)/shard_map/ppermute | solution.py:19
  18.1 3.7 %collective-permute-start.4 = (bf16[88,1152]{1,0:T(8,128)(2,1)}, bf16[88,1152]{1,0:T(8,128)(2,1)S(1)}, u32[]{:S(2)}, u32[]{:S(2)}) collective-permute-start(bf16[88,1152]{1,0:T(8,128)(2,1)} %get-tuple-element.25.refs_2_), channel_id=1, source_target_pairs={{0,16},{16,0},{1,17},{17,1},{2,18},{18,2},{3,19},{19,3},{4,20},{20... | collective-permute-start | bytes 608264 | tf_op jit(solution)/shard_map/ppermute | solution.py:23
  18.4 4.0 %collective-permute-start.5 = (bf16[88,1152]{1,0:T(8,128)(2,1)S(1)}, bf16[88,1152]{1,0:T(8,128)(2,1)S(1)}, u32[]{:S(2)}, u32[]{:S(2)}) collective-permute-start(bf16[88,1152]{1,0:T(8,128)(2,1)S(1)} %collective-permute-done.2.refs_3_), channel_id=1, source_target_pairs={{0,16},{16,0},{1,17},{17,1},{2,18},{18,2},{3,19},{19,3},{4,20},{20... | collective-permute-start | bytes 608264 | tf_op jit(solution)/shard_map/ppermute | solution.py:23
  18.8 3.5 %collective-permute-start.6 = (bf16[88,1152]{1,0:T(8,128)(2,1)S(1)}, bf16[88,1152]{1,0:T(8,128)(2,1)S(1)}, u32[]{:S(2)}, u32[]{:S(2)}) collective-permute-start(bf16[88,1152]{1,0:T(8,128)(2,1)S(1)} %collective-permute-done.1.refs_0_), channel_id=1, source_target_pairs={{0,16},{16,0},{1,17},{17,1},{2,18},{18,2},{3,19},{19,3},{4,20},{20... | collective-permute-start | bytes 608264 | tf_op jit(solution)/shard_map/ppermute | solution.py:23
  18.9 3.5 %collective-permute-start.7 = (bf16[88,1152]{1,0:T(8,128)(2,1)S(1)}, bf16[88,1152]{1,0:T(8,128)(2,1)S(1)}, u32[]{:S(2)}, u32[]{:S(2)}) collective-permute-start(bf16[88,1152]{1,0:T(8,128)(2,1)S(1)} %collective-permute-done.3.refs_1_), channel_id=1, source_target_pairs={{0,16},{16,0},{1,17},{17,1},{2,18},{18,2},{3,19},{19,3},{4,20},{20... | collective-permute-start | bytes 608264 | tf_op jit(solution)/shard_map/ppermute | solution.py:23
  21.8 1.7 %collective-permute-start.12 = (bf16[88,1152]{1,0:T(8,128)(2,1)S(1)}, bf16[88,1152]{1,0:T(8,128)(2,1)S(1)}, u32[]{:S(2)}, u32[]{:S(2)}) collective-permute-start(bf16[88,1152]{1,0:T(8,128)(2,1)S(1)} %collective-permute-done.11.refs_0_), channel_id=1, source_target_pairs={{0,16},{16,0},{1,17},{17,1},{2,18},{18,2},{3,19},{19,3},{4,20},{20... | collective-permute-start | bytes 608264 | tf_op jit(solution)/shard_map/ppermute | solution.py:23
  21.8 1.7 %collective-permute-start.14 = (bf16[88,1152]{1,0:T(8,128)(2,1)S(1)}, bf16[88,1152]{1,0:T(8,128)(2,1)S(1)}, u32[]{:S(2)}, u32[]{:S(2)}) collective-permute-start(bf16[88,1152]{1,0:T(8,128)(2,1)S(1)} %collective-permute-done.13.refs_1_), channel_id=1, source_target_pairs={{0,16},{16,0},{1,17},{17,1},{2,18},{18,2},{3,19},{19,3},{4,20},{20... | collective-permute-start | bytes 608264 | tf_op jit(solution)/shard_map/ppermute | solution.py:23
  22.3 4.3 %copy-start = (bf16[88,1152]{1,0:T(8,128)(2,1)S(1)}, bf16[88,1152]{1,0:T(8,128)(2,1)}, u32[]{:S(2)}) copy-start(bf16[88,1152]{1,0:T(8,128)(2,1)} %get-tuple-element.25.refs_2_) | copy-start | bytes 608260
  24.4 5.7 %collective-permute-start.15 = (bf16[80,1152]{1,0:T(8,128)(2,1)S(1)}, bf16[80,1152]{1,0:T(8,128)(2,1)S(1)}, u32[]{:S(2)}, u32[]{:S(2)}) collective-permute-start(bf16[80,1152]{1,0:T(8,128)(2,1)S(1)} %get-tuple-element.40), channel_id=1, source_target_pairs={{0,1},{1,0},{2,3},{3,2},{4,5},{5,4},{6,7},{7,6},{8,9},{9,8},{10,11... | collective-permute-start | bytes 552968 | tf_op jit(solution)/shard_map/ppermute | solution.py:19
  26.5 7.7 %collective-permute-start.18 = (bf16[80,1152]{1,0:T(8,128)(2,1)S(1)}, bf16[80,1152]{1,0:T(8,128)(2,1)S(1)}, u32[]{:S(2)}, u32[]{:S(2)}) collective-permute-start(bf16[80,1152]{1,0:T(8,128)(2,1)S(1)} %get-tuple-element.43), channel_id=1, source_target_pairs={{0,1},{1,0},{2,3},{3,2},{4,5},{5,4},{6,7},{7,6},{8,9},{9,8},{10,11... | collective-permute-start | bytes 552968 | tf_op jit(solution)/shard_map/ppermute | solution.py:19
  28.8 8.8 %collective-permute-start.17 = (f32[80,1152]{1,0:T(8,128)S(1)}, f32[80,1152]{1,0:T(8,128)S(1)}, u32[]{:S(2)}, u32[]{:S(2)}) collective-permute-start(f32[80,1152]{1,0:T(8,128)S(1)} %get-tuple-element.41), channel_id=1, source_target_pairs={{0,16},{16,0},{1,17},{17,1},{2,18},{18,2},{3,19},{19,3},{4,20},{20... | collective-permute-start | bytes 1105928 | tf_op jit(solution)/shard_map/ppermute | solution.py:23
  30.2 7.3 %collective-permute-start.16 = (bf16[80,1152]{1,0:T(8,128)(2,1)S(1)}, bf16[80,1152]{1,0:T(8,128)(2,1)S(1)}, u32[]{:S(2)}, u32[]{:S(2)}) collective-permute-start(bf16[80,1152]{1,0:T(8,128)(2,1)S(1)} %add_convert_fusion.1), channel_id=1, source_target_pairs={{0,8},{1,9},{2,10},{3,11},{4,12},{5,13},{6,14},{7,15},{8,0},{9,1},... | collective-permute-start | bytes 552968 | tf_op jit(solution)/shard_map/ppermute | solution.py:19
  32.7 9.1 %collective-permute-start.20 = (bf16[80,1152]{1,0:T(8,128)(2,1)S(1)}, bf16[80,1152]{1,0:T(8,128)(2,1)S(1)}, u32[]{:S(2)}, u32[]{:S(2)}) collective-permute-start(bf16[80,1152]{1,0:T(8,128)(2,1)S(1)} %get-tuple-element.45), channel_id=1, source_target_pairs={{0,1},{1,0},{2,3},{3,2},{4,5},{5,4},{6,7},{7,6},{8,9},{9,8},{10,11... | collective-permute-start | bytes 552968 | tf_op jit(solution)/shard_map/ppermute | solution.py:19
  34.2 7.5 %collective-permute-start.19 = (bf16[80,1152]{1,0:T(8,128)(2,1)S(1)}, bf16[80,1152]{1,0:T(8,128)(2,1)S(1)}, u32[]{:S(2)}, u32[]{:S(2)}) collective-permute-start(bf16[80,1152]{1,0:T(8,128)(2,1)S(1)} %add_convert_fusion), channel_id=1, source_target_pairs={{0,24},{1,25},{2,26},{3,27},{4,28},{5,29},{6,30},{7,31},{8,16},{9,... | collective-permute-start | bytes 552968 | tf_op jit(solution)/shard_map/ppermute | solution.py:19
  36.7 5.1 %collective-permute-start.21 = (bf16[80,1152]{1,0:T(8,128)(2,1)S(1)}, bf16[80,1152]{1,0:T(8,128)(2,1)S(1)}, u32[]{:S(2)}, u32[]{:S(2)}) collective-permute-start(bf16[80,1152]{1,0:T(8,128)(2,1)S(1)} %get-tuple-element.47), channel_id=1, source_target_pairs={{0,17},{1,16},{2,19},{3,18},{4,21},{5,20},{6,23},{7,22},{8,25},{9,... | collective-permute-start | bytes 552968 | tf_op jit(solution)/shard_map/ppermute | solution.py:19

commit v10 on v9

--- a/solution.py
+++ b/solution.py
@@ -230,24 +230,28 @@
     pack_sum(jnp.dot(coefficient, others, preferred_element_type=jnp.float32), texts, own_stay, own_cross)
 
 
-def last_kernel(spot_ref, stay_ref, crossed_ref, near_stay_ref, near_cross_ref, image_ref, text_ref):
+def last_kernel(row_ref, stay_ref, crossed_ref, near_stay_ref, near_cross_ref, image_ref, text_ref, images, texts, sems):
     half, part = text_ref.shape[0] // 2, text_ref.shape[1]
 
-    stay = (stay_ref[...] + near_stay_ref[...].astype(jnp.float32)).astype(image_ref.dtype)
-    crossed = (crossed_ref[...] + near_cross_ref[...].astype(jnp.float32)).astype(image_ref.dtype)
-
-    def put(images, texts):
-        image_ref[...] = images
-        text_ref[:half] = texts[:, :part]
-        text_ref[half:] = texts[:, part:]
-
-    @pl.when(spot_ref[0] == 0)
-    def _():
-        put(stay, crossed)
-
-    @pl.when(spot_ref[0] != 0)
-    def _():
-        put(crossed, stay)
+    def put(image_sums, text_sums):
+        images[...] = (image_sums[0][...] + image_sums[1][...].astype(jnp.float32)).astype(images.dtype)
+        image_out = pltpu.make_async_copy(images, image_ref, sems.at[0])
+        image_out.start()
+        rows = (text_sums[0][...] + text_sums[1][...].astype(jnp.float32)).astype(texts.dtype)
+        texts[:half] = rows[:, :part]
+        texts[half:] = rows[:, part:]
+        text_out = pltpu.make_async_copy(texts, text_ref, sems.at[1])
+        text_out.start()
+        image_out.wait()
+        text_out.wait()
+
+    @pl.when(row_ref[0] == 0)
+    def _():
+        put((stay_ref, near_stay_ref), (crossed_ref, near_cross_ref))
+
+    @pl.when(row_ref[0] != 0)
+    def _():
+        put((crossed_ref, near_cross_ref), (stay_ref, near_stay_ref))
 
 
 def call(kernel, out_shape, smem, *arrays, flops=0, scratch=()):
@@ -335,8 +339,15 @@
     near_cross = hop(near_cross, *near, across=True)
     own_stay = own_stay + far_stay.astype(f32)
     crossed = crossed + far_cross.astype(f32)
-    return call(last_kernel, (shape(half, bf16), jax.ShapeDtypeStruct(text_emb.shape, bf16)), 1, row, own_stay, crossed,
-                near_stay, near_cross)
+    outs = (shape(half, bf16), jax.ShapeDtypeStruct(text_emb.shape, bf16))
+    return pl.pallas_call(
+        last_kernel,
+        out_shape=outs,
+        in_specs=[pl.BlockSpec(memory_space=pltpu.SMEM)] + [pl.BlockSpec(memory_space=pltpu.VMEM)] * 4,
+        out_specs=(pl.BlockSpec(memory_space=pltpu.HBM),) * 2,
+        scratch_shapes=[pltpu.VMEM(out.shape, out.dtype) for out in outs] + [pltpu.SemaphoreType.DMA((2,))],
+        compiler_params=pltpu.CompilerParams(vmem_limit_bytes=24 * 1024 * 1024),
+    )(row, own_stay, crossed, near_stay, near_cross)
 
 
 def partner(block, axis, distance):

time: 43 us -> 42.9 us (level)
    pallas_call x7 -> x6, Pallas kernels: 7.46 us -> 6.53 us  [call(): pl.pallas_call(kernel, out_shape=out_shape, in_specs=[pl.BlockSpec(memory...]
    pallas_call x0 -> x1, Pallas kernels: none -> 0.85 us  [pair_body(): pl.pallas_call(last_kernel, out_shape=outs, in_specs=[pl.BlockSpec(memory...]
where the time goes in v10:
time: 42.9 us; the launch traced here: 42.7 us
  starting transfers between devices  22.9 us (53%)
  Pallas kernels  9.23 us (22%)
  waiting for transfers between devices  6.98 us (16%)
  between operations  3.39 us (8%)
    ppermute x12, starting transfers between devices, hop(): return lax.ppermute(block, ('row', 'col'), route)  20.4 us
    ppermute x12, waiting for transfers between devices, hop(): return lax.ppermute(block, ('row', 'col'), route)  6.95 us
    pallas_call x6, Pallas kernels, call(): pl.pallas_call(kernel, out_shape=out_shape, in_specs=[pl.BlockSpec(memory...  6.53 us
    ppermute x10, starting transfers between devices, swap(): return lax.ppermute(block, 'row', [(0, 1), (1, 0)])  2.48 us
    pallas_call x1, Pallas kernels, pair_body(): pl.pallas_call(first_kernel, out_shape=(sent, sent), in_specs=[pl.BlockSp...  1.85 us
  transfers between devices with their start and end apart: 22, of which 4 were waited for; matrix products, arithmetic and copies ran while one was open for 0% of the time, Pallas kernels for 13%

profile of v10, /device:TPU:0, one launch (start us, length us, event | category | flops | bytes accessed | tf_op | source)
XLA Modules:
  0.0 42.7 jit_solution(12039013621600811247)
XLA Ops:
  0.6 1.8 %shard_map.95 = (bf16[88,1152]{1,0:T(8,128)(2,1)}, bf16[88,1152]{1,0:T(8,128)(2,1)}) custom-call(s32[1]{0:T(128)} %bitcast.spot_ref.row_ref, bf16[80,1152]{1,0:T(8,128)(2,1)} %image_ref.1, bf16[160,576]{1,0:T(8,128)(2,1)} %text_ref.1, s32[1,80]{1,0:T(1,128)} %bitcast.5, s32[1,160]{1,0:T(1,128)} %bitcast.4), custom_call_target="tpu_custom_call" | custom-call | tf_op jit(solution)/shard_map/pallas_call | solution.py:286
  2.5 0.5 %collective-permute-start.2 = (bf16[88,1152]{1,0:T(8,128)(2,1)}, bf16[88,1152]{1,0:T(8,128)(2,1)S(1)}, u32[]{:S(2)}, u32[]{:S(2)}) collective-permute-start(bf16[88,1152]{1,0:T(8,128)(2,1)} %get-tuple-element.27), channel_id=1, source_target_pairs={{0,16},{16,0},{1,17},{17,1},{2,18},{18,2},{3,19},{19,3},{4,20},{20... | collective-permute-start | bytes 608264 | tf_op jit(solution)/shard_map/ppermute | solution.py:23
  3.0 3.7 %collective-permute-start = (bf16[88,1152]{1,0:T(8,128)(2,1)}, bf16[88,1152]{1,0:T(8,128)(2,1)S(1)}, u32[]{:S(2)}, u32[]{:S(2)}) collective-permute-start(bf16[88,1152]{1,0:T(8,128)(2,1)} %get-tuple-element.25.refs_2_), channel_id=1, source_target_pairs={{0,8},{1,9},{2,10},{3,11},{4,12},{5,13},{6,14},{7,15},{8,0},{9,1},... | collective-permute-start | bytes 608264 | tf_op jit(solution)/shard_map/ppermute | solution.py:19
  6.7 0.0 collective-permute-done.2.refs_3_
  6.7 1.6 %collective-permute-start.9 = (bf16[88,1152]{1,0:T(8,128)(2,1)S(1)}, bf16[88,1152]{1,0:T(8,128)(2,1)S(1)}, u32[]{:S(2)}, u32[]{:S(2)}) collective-permute-start(bf16[88,1152]{1,0:T(8,128)(2,1)S(1)} %collective-permute-done.2.refs_3_), channel_id=1, source_target_pairs={{0,8},{1,9},{2,10},{3,11},{4,12},{5,13},{6,14},{7,15},{8,0},{9,1},... | collective-permute-start | bytes 608264 | tf_op jit(solution)/shard_map/ppermute | solution.py:19
  8.3 1.5 %collective-permute-start.1 = (bf16[88,1152]{1,0:T(8,128)(2,1)}, bf16[88,1152]{1,0:T(8,128)(2,1)S(1)}, u32[]{:S(2)}, u32[]{:S(2)}) collective-permute-start(bf16[88,1152]{1,0:T(8,128)(2,1)} %get-tuple-element.25.refs_2_), channel_id=1, source_target_pairs={{0,1},{1,0},{2,3},{3,2},{4,5},{5,4},{6,7},{7,6},{8,9},{9,8},{10,11... | collective-permute-start | bytes 608264 | tf_op jit(solution)/shard_map/ppermute | solution.py:19
  9.7 0.5 %collective-permute-start.3 = (bf16[88,1152]{1,0:T(8,128)(2,1)S(1)}, bf16[88,1152]{1,0:T(8,128)(2,1)S(1)}, u32[]{:S(2)}, u32[]{:S(2)}) collective-permute-start(bf16[88,1152]{1,0:T(8,128)(2,1)S(1)} %collective-permute-done.2.refs_3_), channel_id=1, source_target_pairs={{0,1},{1,0},{2,3},{3,2},{4,5},{5,4},{6,7},{7,6},{8,9},{9,8},{10,11... | collective-permute-start | bytes 608264 | tf_op jit(solution)/shard_map/ppermute | solution.py:19
  12.9 0.0 collective-permute-done.refs_2_.refs_0_
  12.9 0.1 collective-permute-start.8
  13.0 1.6 %collective-permute-start.11 = (bf16[88,1152]{1,0:T(8,128)(2,1)S(1)}, bf16[88,1152]{1,0:T(8,128)(2,1)S(1)}, u32[]{:S(2)}, u32[]{:S(2)}) collective-permute-start(bf16[88,1152]{1,0:T(8,128)(2,1)S(1)} %collective-permute-done.refs_2_.refs_0_), channel_id=1, source_target_pairs={{0,1},{1,0},{2,3},{3,2},{4,5},{5,4},{6,7},{7,6},{8,9},{9,8},{10,11... | collective-permute-start | bytes 608264 | tf_op jit(solution)/shard_map/ppermute | solution.py:19
  14.6 1.4 %collective-permute-done.9.refs_3_.refs_1_ = bf16[88,1152]{1,0:T(8,128)(2,1)S(1)} collective-permute-done((bf16[88,1152]{1,0:T(8,128)(2,1)S(1)}, bf16[88,1152]{1,0:T(8,128)(2,1)S(1)}, u32[]{:S(2)}, u32[]{:S(2)}) %collective-permute-start.9) | collective-permute-done | bytes 202784 | tf_op jit(solution)/shard_map/ppermute | solution.py:19
  15.9 0.0 collective-permute-start.10
  15.9 0.0 collective-permute-done.1.refs_0_
  16.0 2.1 %collective-permute-start.13 = (bf16[88,1152]{1,0:T(8,128)(2,1)S(1)}, bf16[88,1152]{1,0:T(8,128)(2,1)S(1)}, u32[]{:S(2)}, u32[]{:S(2)}) collective-permute-start(bf16[88,1152]{1,0:T(8,128)(2,1)S(1)} %collective-permute-done.9.refs_3_.refs_1_), channel_id=1, source_target_pairs={{0,1},{1,0},{2,3},{3,2},{4,5},{5,4},{6,7},{7,6},{8,9},{9,8},{10,11... | collective-permute-start | bytes 608264 | tf_op jit(solution)/shard_map/ppermute | solution.py:19
  18.1 0.0 collective-permute-done.3.refs_1_
  18.1 0.3 collective-permute-start.4
  18.4 0.0 collective-permute-done.8.refs_4_.refs_6_.refs_8_
  18.4 0.3 collective-permute-start.5
  18.6 0.2 collective-permute-done.11.refs_0_
  18.8 0.1 collective-permute-start.6
  18.9 0.0 collective-permute-done.10.refs_5_.refs_7_.refs_9_
  18.9 0.5 %collective-permute-start.7 = (bf16[88,1152]{1,0:T(8,128)(2,1)S(1)}, bf16[88,1152]{1,0:T(8,128)(2,1)S(1)}, u32[]{:S(2)}, u32[]{:S(2)}) collective-permute-start(bf16[88,1152]{1,0:T(8,128)(2,1)S(1)} %collective-permute-done.3.refs_1_), channel_id=1, source_target_pairs={{0,16},{16,0},{1,17},{17,1},{2,18},{18,2},{3,19},{19,3},{4,20},{20... | collective-permute-start | bytes 608264 | tf_op jit(solution)/shard_map/ppermute | solution.py:23
  19.3 1.3 %shard_map.97 = (bf16[320,1152]{1,0:T(8,128)(2,1)S(1)}, bf16[160,1152]{1,0:T(8,128)(2,1)S(1)}, f32[320,1152]{1,0:T(8,128)S(1)}) custom-call(s32[1]{0:T(128)} %bitcast.spot_ref.row_ref, s32[1]{0:T(128)} %bitcast.1.col_ref, f32[8,128]{1,0:T(8,128)S(1)} %shard_map.96.number_ref, bf16[88,1152]{1,0:T(8,128)(2,1)S(1)} %collective-permute-done.1.refs_0_, ...), custom_call_target="tpu_custom_call" | custom-call | flops 235929600 | bytes 3801096 | tf_op jit(solution)/shard_map/pallas_call | solution.py:259
  20.6 1.2 %collective-permute-done.13.refs_1_ = bf16[88,1152]{1,0:T(8,128)(2,1)S(1)} collective-permute-done((bf16[88,1152]{1,0:T(8,128)(2,1)S(1)}, bf16[88,1152]{1,0:T(8,128)(2,1)S(1)}, u32[]{:S(2)}, u32[]{:S(2)}) %collective-permute-start.13) | collective-permute-done | bytes 202784 | tf_op jit(solution)/shard_map/ppermute | solution.py:19
  21.8 0.0 collective-permute-start.12
  21.8 0.0 collective-permute-done.4.refs_2_.refs_4_
  21.8 0.5 %collective-permute-start.14 = (bf16[88,1152]{1,0:T(8,128)(2,1)S(1)}, bf16[88,1152]{1,0:T(8,128)(2,1)S(1)}, u32[]{:S(2)}, u32[]{:S(2)}) collective-permute-start(bf16[88,1152]{1,0:T(8,128)(2,1)S(1)} %collective-permute-done.13.refs_1_), channel_id=1, source_target_pairs={{0,16},{16,0},{1,17},{17,1},{2,18},{18,2},{3,19},{19,3},{4,20},{20... | collective-permute-start | bytes 608264 | tf_op jit(solution)/shard_map/ppermute | solution.py:23
  22.3 0.0 collective-permute-done.5.refs_3_.refs_5_
  22.3 0.0 collective-permute-done.6.refs_4_.refs_6_
  22.3 0.0 copy-start
  22.3 1.2 %shard_map.98 = (bf16[320,1152]{1,0:T(8,128)(2,1)S(1)}, bf16[160,1152]{1,0:T(8,128)(2,1)S(1)}, f32[160,1152]{1,0:T(8,128)S(1)}) custom-call(s32[1]{0:T(128)} %bitcast.spot_ref.row_ref, s32[1]{0:T(128)} %bitcast.1.col_ref, f32[8,128]{1,0:T(8,128)S(1)} %shard_map.96.number_ref, bf16[88,1152]{1,0:T(8,128)(2,1)S(1)} %collective-permute-done.11.refs_0_, ...), custom_call_target="tpu_custom_call" | custom-call | flops 353894400 | bytes 3837960 | tf_op jit(solution)/shard_map/pallas_call | solution.py:259
  23.5 0.0 collective-permute-done.12.refs_2_.refs_10_.refs_6_
  23.5 0.0 collective-permute-done.14.refs_3_.refs_11_.refs_7_
  23.6 0.9 %shard_map.99 = (bf16[160,1152]{1,0:T(8,128)(2,1)S(1)}, bf16[80,1152]{1,0:T(8,128)(2,1)S(1)}, bf16[80,1152]{1,0:T(8,128)(2,1)S(1)}) custom-call(s32[1]{0:T(128)} %bitcast.spot_ref.row_ref, s32[1]{0:T(128)} %bitcast.1.col_ref, f32[8,128]{1,0:T(8,128)S(1)} %shard_map.96.number_ref, bf16[88,1152]{1,0:T(8,128)(2,1)S(1)} %collective-permute-done.11.refs_0_, ...), custom_call_target="tpu_custom_call" | custom-call | flops 117964800 | bytes 2658312 | tf_op jit(solution)/shard_map/pallas_call | solution.py:259
  24.4 2.1 %collective-permute-start.15 = (bf16[80,1152]{1,0:T(8,128)(2,1)S(1)}, bf16[80,1152]{1,0:T(8,128)(2,1)S(1)}, u32[]{:S(2)}, u32[]{:S(2)}) collective-permute-start(bf16[80,1152]{1,0:T(8,128)(2,1)S(1)} %get-tuple-element.40), channel_id=1, source_target_pairs={{0,1},{1,0},{2,3},{3,2},{4,5},{5,4},{6,7},{7,6},{8,9},{9,8},{10,11... | collective-permute-start | bytes 552968 | tf_op jit(solution)/shard_map/ppermute | solution.py:19
  26.5 0.1 collective-permute-start.18
  26.6 2.2 %shard_map.100 = (f32[80,1152]{1,0:T(8,128)S(1)}, f32[80,1152]{1,0:T(8,128)S(1)}, bf16[80,1152]{1,0:T(8,128)(2,1)S(1)}, bf16[80,1152]{1,0:T(8,128)(2,1)S(1)}) custom-call(s32[1]{0:T(128)} %bitcast.spot_ref.row_ref, s32[1]{0:T(128)} %bitcast.1.col_ref, f32[8,128]{1,0:T(8,128)S(1)} %shard_map.96.number_ref, ...), custom_call_target="tpu_custom_call" | custom-call | flops 825753600 | bytes 7229448 | tf_op jit(solution)/shard_map/pallas_call | solution.py:259
  28.8 0.4 collective-permute-start.17
  29.1 1.0 %shard_map.101 = (f32[80,1152]{1,0:T(8,128)S(1)}, f32[80,1152]{1,0:T(8,128)S(1)}) custom-call(s32[1]{0:T(128)} %bitcast.spot_ref.row_ref, s32[1]{0:T(128)} %bitcast.1.col_ref, f32[8,128]{1,0:T(8,128)S(1)} %shard_map.96.number_ref, bf16[88,1152]{1,0:T(8,128)(2,1)S(1)} %collective-permute-done.refs_2_.refs_0_, ...), custom_call_target="tpu_custom_call" | custom-call | flops 353894400 | bytes 5681160 | tf_op jit(solution)/shard_map/pallas_call | solution.py:259
  30.1 0.0 collective-permute-done.15
  30.2 2.5 %collective-permute-start.16 = (bf16[80,1152]{1,0:T(8,128)(2,1)S(1)}, bf16[80,1152]{1,0:T(8,128)(2,1)S(1)}, u32[]{:S(2)}, u32[]{:S(2)}) collective-permute-start(bf16[80,1152]{1,0:T(8,128)(2,1)S(1)} %add_convert_fusion.1), channel_id=1, source_target_pairs={{0,8},{1,9},{2,10},{3,11},{4,12},{5,13},{6,14},{7,15},{8,0},{9,1},... | collective-permute-start | bytes 552968 | tf_op jit(solution)/shard_map/ppermute | solution.py:19
  32.7 1.5 %collective-permute-start.20 = (bf16[80,1152]{1,0:T(8,128)(2,1)S(1)}, bf16[80,1152]{1,0:T(8,128)(2,1)S(1)}, u32[]{:S(2)}, u32[]{:S(2)}) collective-permute-start(bf16[80,1152]{1,0:T(8,128)(2,1)S(1)} %get-tuple-element.45), channel_id=1, source_target_pairs={{0,1},{1,0},{2,3},{3,2},{4,5},{5,4},{6,7},{7,6},{8,9},{9,8},{10,11... | collective-permute-start | bytes 552968 | tf_op jit(solution)/shard_map/ppermute | solution.py:19
  34.2 2.5 %collective-permute-start.19 = (bf16[80,1152]{1,0:T(8,128)(2,1)S(1)}, bf16[80,1152]{1,0:T(8,128)(2,1)S(1)}, u32[]{:S(2)}, u32[]{:S(2)}) collective-permute-start(bf16[80,1152]{1,0:T(8,128)(2,1)S(1)} %add_convert_fusion), channel_id=1, source_target_pairs={{0,24},{1,25},{2,26},{3,27},{4,28},{5,29},{6,30},{7,31},{8,16},{9,... | collective-permute-start | bytes 552968 | tf_op jit(solution)/shard_map/ppermute | solution.py:19
  36.7 0.8 %collective-permute-start.21 = (bf16[80,1152]{1,0:T(8,128)(2,1)S(1)}, bf16[80,1152]{1,0:T(8,128)(2,1)S(1)}, u32[]{:S(2)}, u32[]{:S(2)}) collective-permute-start(bf16[80,1152]{1,0:T(8,128)(2,1)S(1)} %get-tuple-element.47), channel_id=1, source_target_pairs={{0,17},{1,16},{2,19},{3,18},{4,21},{5,20},{6,23},{7,22},{8,25},{9,... | collective-permute-start | bytes 552968 | tf_op jit(solution)/shard_map/ppermute | solution.py:19
  37.5 0.0 collective-permute-done.16
  37.6 4.2 %collective-permute-done.19 = bf16[80,1152]{1,0:T(8,128)(2,1)S(1)} collective-permute-done((bf16[80,1152]{1,0:T(8,128)(2,1)S(1)}, bf16[80,1152]{1,0:T(8,128)(2,1)S(1)}, u32[]{:S(2)}, u32[]{:S(2)}) %collective-permute-start.19) | collective-permute-done | bytes 184352 | tf_op jit(solution)/shard_map/ppermute | solution.py:19
  41.8 0.0 collective-permute-done.20.near_stay_ref
  41.8 0.8 %shard_map.102 = (bf16[80,1152]{1,0:T(8,128)(2,1)}, bf16[160,576]{1,0:T(8,128)(2,1)}) custom-call(s32[1]{0:T(128)} %bitcast.spot_ref.row_ref, f32[80,1152]{1,0:T(8,128)S(1)} %convert_add_fusion.1.stay_ref, f32[80,1152]{1,0:T(8,128)S(1)} %convert_add_fusion.crossed_ref, bf16[80,1152]{1,0:T(8,128)(2,1)S(1)} %collective-permute-done.20.near_stay_ref, ...), custom_call_target="tpu_custom_call" | custom-call | tf_op jit(solution)/shard_map/pallas_call | solution.py:343
  (10 shorter events, 0.2 us)
Async XLA Ops:
  2.5 4.2 %collective-permute-start.2 = (bf16[88,1152]{1,0:T(8,128)(2,1)}, bf16[88,1152]{1,0:T(8,128)(2,1)S(1)}, u32[]{:S(2)}, u32[]{:S(2)}) collective-permute-start(bf16[88,1152]{1,0:T(8,128)(2,1)} %get-tuple-element.27), channel_id=1, source_target_pairs={{0,16},{16,0},{1,17},{17,1},{2,18},{18,2},{3,19},{19,3},{4,20},{20... | collective-permute-start | bytes 608264 | tf_op jit(solution)/shard_map/ppermute | solution.py:23
  3.0 9.9 %collective-permute-start = (bf16[88,1152]{1,0:T(8,128)(2,1)}, bf16[88,1152]{1,0:T(8,128)(2,1)S(1)}, u32[]{:S(2)}, u32[]{:S(2)}) collective-permute-start(bf16[88,1152]{1,0:T(8,128)(2,1)} %get-tuple-element.25.refs_2_), channel_id=1, source_target_pairs={{0,8},{1,9},{2,10},{3,11},{4,12},{5,13},{6,14},{7,15},{8,0},{9,1},... | collective-permute-start | bytes 608264 | tf_op jit(solution)/shard_map/ppermute | solution.py:19
  6.7 9.3 %collective-permute-start.9 = (bf16[88,1152]{1,0:T(8,128)(2,1)S(1)}, bf16[88,1152]{1,0:T(8,128)(2,1)S(1)}, u32[]{:S(2)}, u32[]{:S(2)}) collective-permute-start(bf16[88,1152]{1,0:T(8,128)(2,1)S(1)} %collective-permute-done.2.refs_3_), channel_id=1, source_target_pairs={{0,8},{1,9},{2,10},{3,11},{4,12},{5,13},{6,14},{7,15},{8,0},{9,1},... | collective-permute-start | bytes 608264 | tf_op jit(solution)/shard_map/ppermute | solution.py:19
  8.3 7.7 %collective-permute-start.1 = (bf16[88,1152]{1,0:T(8,128)(2,1)}, bf16[88,1152]{1,0:T(8,128)(2,1)S(1)}, u32[]{:S(2)}, u32[]{:S(2)}) collective-permute-start(bf16[88,1152]{1,0:T(8,128)(2,1)} %get-tuple-element.25.refs_2_), channel_id=1, source_target_pairs={{0,1},{1,0},{2,3},{3,2},{4,5},{5,4},{6,7},{7,6},{8,9},{9,8},{10,11... | collective-permute-start | bytes 608264 | tf_op jit(solution)/shard_map/ppermute | solution.py:19
  9.7 8.4 %collective-permute-start.3 = (bf16[88,1152]{1,0:T(8,128)(2,1)S(1)}, bf16[88,1152]{1,0:T(8,128)(2,1)S(1)}, u32[]{:S(2)}, u32[]{:S(2)}) collective-permute-start(bf16[88,1152]{1,0:T(8,128)(2,1)S(1)} %collective-permute-done.2.refs_3_), channel_id=1, source_target_pairs={{0,1},{1,0},{2,3},{3,2},{4,5},{5,4},{6,7},{7,6},{8,9},{9,8},{10,11... | collective-permute-start | bytes 608264 | tf_op jit(solution)/shard_map/ppermute | solution.py:19
  12.9 5.4 %collective-permute-start.8 = (bf16[88,1152]{1,0:T(8,128)(2,1)S(1)}, bf16[88,1152]{1,0:T(8,128)(2,1)S(1)}, u32[]{:S(2)}, u32[]{:S(2)}) collective-permute-start(bf16[88,1152]{1,0:T(8,128)(2,1)S(1)} %collective-permute-done.refs_2_.refs_0_), channel_id=1, source_target_pairs={{0,16},{16,0},{1,17},{17,1},{2,18},{18,2},{3,19},{19,3},{4,20},{20... | collective-permute-start | bytes 608264 | tf_op jit(solution)/shard_map/ppermute | solution.py:23
  13.0 5.8 %collective-permute-start.11 = (bf16[88,1152]{1,0:T(8,128)(2,1)S(1)}, bf16[88,1152]{1,0:T(8,128)(2,1)S(1)}, u32[]{:S(2)}, u32[]{:S(2)}) collective-permute-start(bf16[88,1152]{1,0:T(8,128)(2,1)S(1)} %collective-permute-done.refs_2_.refs_0_), channel_id=1, source_target_pairs={{0,1},{1,0},{2,3},{3,2},{4,5},{5,4},{6,7},{7,6},{8,9},{9,8},{10,11... | collective-permute-start | bytes 608264 | tf_op jit(solution)/shard_map/ppermute | solution.py:19
  15.9 2.9 %collective-permute-start.10 = (bf16[88,1152]{1,0:T(8,128)(2,1)S(1)}, bf16[88,1152]{1,0:T(8,128)(2,1)S(1)}, u32[]{:S(2)}, u32[]{:S(2)}) collective-permute-start(bf16[88,1152]{1,0:T(8,128)(2,1)S(1)} %collective-permute-done.9.refs_3_.refs_1_), channel_id=1, source_target_pairs={{0,16},{16,0},{1,17},{17,1},{2,18},{18,2},{3,19},{19,3},{4,20},{20... | collective-permute-start | bytes 608264 | tf_op jit(solution)/shard_map/ppermute | solution.py:23
  16.0 5.9 %collective-permute-start.13 = (bf16[88,1152]{1,0:T(8,128)(2,1)S(1)}, bf16[88,1152]{1,0:T(8,128)(2,1)S(1)}, u32[]{:S(2)}, u32[]{:S(2)}) collective-permute-start(bf16[88,1152]{1,0:T(8,128)(2,1)S(1)} %collective-permute-done.9.refs_3_.refs_1_), channel_id=1, source_target_pairs={{0,1},{1,0},{2,3},{3,2},{4,5},{5,4},{6,7},{7,6},{8,9},{9,8},{10,11... | collective-permute-start | bytes 608264 | tf_op jit(solution)/shard_map/ppermute | solution.py:19
  18.1 3.7 %collective-permute-start.4 = (bf16[88,1152]{1,0:T(8,128)(2,1)}, bf16[88,1152]{1,0:T(8,128)(2,1)S(1)}, u32[]{:S(2)}, u32[]{:S(2)}) collective-permute-start(bf16[88,1152]{1,0:T(8,128)(2,1)} %get-tuple-element.25.refs_2_), channel_id=1, source_target_pairs={{0,16},{16,0},{1,17},{17,1},{2,18},{18,2},{3,19},{19,3},{4,20},{20... | collective-permute-start | bytes 608264 | tf_op jit(solution)/shard_map/ppermute | solution.py:23
  18.4 4.0 %collective-permute-start.5 = (bf16[88,1152]{1,0:T(8,128)(2,1)S(1)}, bf16[88,1152]{1,0:T(8,128)(2,1)S(1)}, u32[]{:S(2)}, u32[]{:S(2)}) collective-permute-start(bf16[88,1152]{1,0:T(8,128)(2,1)S(1)} %collective-permute-done.2.refs_3_), channel_id=1, source_target_pairs={{0,16},{16,0},{1,17},{17,1},{2,18},{18,2},{3,19},{19,3},{4,20},{20... | collective-permute-start | bytes 608264 | tf_op jit(solution)/shard_map/ppermute | solution.py:23
  18.8 3.5 %collective-permute-start.6 = (bf16[88,1152]{1,0:T(8,128)(2,1)S(1)}, bf16[88,1152]{1,0:T(8,128)(2,1)S(1)}, u32[]{:S(2)}, u32[]{:S(2)}) collective-permute-start(bf16[88,1152]{1,0:T(8,128)(2,1)S(1)} %collective-permute-done.1.refs_0_), channel_id=1, source_target_pairs={{0,16},{16,0},{1,17},{17,1},{2,18},{18,2},{3,19},{19,3},{4,20},{20... | collective-permute-start | bytes 608264 | tf_op jit(solution)/shard_map/ppermute | solution.py:23
  18.9 3.5 %collective-permute-start.7 = (bf16[88,1152]{1,0:T(8,128)(2,1)S(1)}, bf16[88,1152]{1,0:T(8,128)(2,1)S(1)}, u32[]{:S(2)}, u32[]{:S(2)}) collective-permute-start(bf16[88,1152]{1,0:T(8,128)(2,1)S(1)} %collective-permute-done.3.refs_1_), channel_id=1, source_target_pairs={{0,16},{16,0},{1,17},{17,1},{2,18},{18,2},{3,19},{19,3},{4,20},{20... | collective-permute-start | bytes 608264 | tf_op jit(solution)/shard_map/ppermute | solution.py:23
  21.8 1.7 %collective-permute-start.12 = (bf16[88,1152]{1,0:T(8,128)(2,1)S(1)}, bf16[88,1152]{1,0:T(8,128)(2,1)S(1)}, u32[]{:S(2)}, u32[]{:S(2)}) collective-permute-start(bf16[88,1152]{1,0:T(8,128)(2,1)S(1)} %collective-permute-done.11.refs_0_), channel_id=1, source_target_pairs={{0,16},{16,0},{1,17},{17,1},{2,18},{18,2},{3,19},{19,3},{4,20},{20... | collective-permute-start | bytes 608264 | tf_op jit(solution)/shard_map/ppermute | solution.py:23
  21.8 1.7 %collective-permute-start.14 = (bf16[88,1152]{1,0:T(8,128)(2,1)S(1)}, bf16[88,1152]{1,0:T(8,128)(2,1)S(1)}, u32[]{:S(2)}, u32[]{:S(2)}) collective-permute-start(bf16[88,1152]{1,0:T(8,128)(2,1)S(1)} %collective-permute-done.13.refs_1_), channel_id=1, source_target_pairs={{0,16},{16,0},{1,17},{17,1},{2,18},{18,2},{3,19},{19,3},{4,20},{20... | collective-permute-start | bytes 608264 | tf_op jit(solution)/shard_map/ppermute | solution.py:23
  22.3 4.3 %copy-start = (bf16[88,1152]{1,0:T(8,128)(2,1)S(1)}, bf16[88,1152]{1,0:T(8,128)(2,1)}, u32[]{:S(2)}) copy-start(bf16[88,1152]{1,0:T(8,128)(2,1)} %get-tuple-element.25.refs_2_) | copy-start | bytes 608260
  24.4 5.7 %collective-permute-start.15 = (bf16[80,1152]{1,0:T(8,128)(2,1)S(1)}, bf16[80,1152]{1,0:T(8,128)(2,1)S(1)}, u32[]{:S(2)}, u32[]{:S(2)}) collective-permute-start(bf16[80,1152]{1,0:T(8,128)(2,1)S(1)} %get-tuple-element.40), channel_id=1, source_target_pairs={{0,1},{1,0},{2,3},{3,2},{4,5},{5,4},{6,7},{7,6},{8,9},{9,8},{10,11... | collective-permute-start | bytes 552968 | tf_op jit(solution)/shard_map/ppermute | solution.py:19
  26.5 7.7 %collective-permute-start.18 = (bf16[80,1152]{1,0:T(8,128)(2,1)S(1)}, bf16[80,1152]{1,0:T(8,128)(2,1)S(1)}, u32[]{:S(2)}, u32[]{:S(2)}) collective-permute-start(bf16[80,1152]{1,0:T(8,128)(2,1)S(1)} %get-tuple-element.43), channel_id=1, source_target_pairs={{0,1},{1,0},{2,3},{3,2},{4,5},{5,4},{6,7},{7,6},{8,9},{9,8},{10,11... | collective-permute-start | bytes 552968 | tf_op jit(solution)/shard_map/ppermute | solution.py:19
  28.8 8.8 %collective-permute-start.17 = (f32[80,1152]{1,0:T(8,128)S(1)}, f32[80,1152]{1,0:T(8,128)S(1)}, u32[]{:S(2)}, u32[]{:S(2)}) collective-permute-start(f32[80,1152]{1,0:T(8,128)S(1)} %get-tuple-element.41), channel_id=1, source_target_pairs={{0,16},{16,0},{1,17},{17,1},{2,18},{18,2},{3,19},{19,3},{4,20},{20... | collective-permute-start | bytes 1105928 | tf_op jit(solution)/shard_map/ppermute | solution.py:23
  30.2 7.3 %collective-permute-start.16 = (bf16[80,1152]{1,0:T(8,128)(2,1)S(1)}, bf16[80,1152]{1,0:T(8,128)(2,1)S(1)}, u32[]{:S(2)}, u32[]{:S(2)}) collective-permute-start(bf16[80,1152]{1,0:T(8,128)(2,1)S(1)} %add_convert_fusion.1), channel_id=1, source_target_pairs={{0,8},{1,9},{2,10},{3,11},{4,12},{5,13},{6,14},{7,15},{8,0},{9,1},... | collective-permute-start | bytes 552968 | tf_op jit(solution)/shard_map/ppermute | solution.py:19
  32.7 9.1 %collective-permute-start.20 = (bf16[80,1152]{1,0:T(8,128)(2,1)S(1)}, bf16[80,1152]{1,0:T(8,128)(2,1)S(1)}, u32[]{:S(2)}, u32[]{:S(2)}) collective-permute-start(bf16[80,1152]{1,0:T(8,128)(2,1)S(1)} %get-tuple-element.45), channel_id=1, source_target_pairs={{0,1},{1,0},{2,3},{3,2},{4,5},{5,4},{6,7},{7,6},{8,9},{9,8},{10,11... | collective-permute-start | bytes 552968 | tf_op jit(solution)/shard_map/ppermute | solution.py:19
  34.2 7.5 %collective-permute-start.19 = (bf16[80,1152]{1,0:T(8,128)(2,1)S(1)}, bf16[80,1152]{1,0:T(8,128)(2,1)S(1)}, u32[]{:S(2)}, u32[]{:S(2)}) collective-permute-start(bf16[80,1152]{1,0:T(8,128)(2,1)S(1)} %add_convert_fusion), channel_id=1, source_target_pairs={{0,24},{1,25},{2,26},{3,27},{4,28},{5,29},{6,30},{7,31},{8,16},{9,... | collective-permute-start | bytes 552968 | tf_op jit(solution)/shard_map/ppermute | solution.py:19
  36.7 5.1 %collective-permute-start.21 = (bf16[80,1152]{1,0:T(8,128)(2,1)S(1)}, bf16[80,1152]{1,0:T(8,128)(2,1)S(1)}, u32[]{:S(2)}, u32[]{:S(2)}) collective-permute-start(bf16[80,1152]{1,0:T(8,128)(2,1)S(1)} %get-tuple-element.47), channel_id=1, source_target_pairs={{0,17},{1,16},{2,19},{3,18},{4,21},{5,20},{6,23},{7,22},{8,25},{9,... | collective-permute-start | bytes 552968 | tf_op jit(solution)/shard_map/ppermute | solution.py:19

commit v11 on v10

--- a/solution.py
+++ b/solution.py
@@ -100,10 +100,7 @@
 
 
 def upright(line):
-    size = line.shape[1]
-    at = lax.broadcasted_iota(jnp.int32, (size, size), 0)
-    to = lax.broadcasted_iota(jnp.int32, (size, size), 1)
-    return jnp.sum(jnp.where(at == to, line, 0.0), axis=1, keepdims=True)
+    return jnp.transpose(jnp.broadcast_to(line, (8, line.shape[1])))[:, :1]
 
 
 def sample_ids(col, texts, half, cols, axis):

time: 42.9 us -> 43 us (level)
  no operation moved by 1% of the time
where the time goes in v11:
time: 43 us; the launch traced here: 42.7 us
  starting transfers between devices  22.9 us (53%)
  Pallas kernels  9.33 us (22%)
  waiting for transfers between devices  6.97 us (16%)
  between operations  3.39 us (8%)
    ppermute x12, starting transfers between devices, hop(): return lax.ppermute(block, ('row', 'col'), route)  20.4 us
    ppermute x12, waiting for transfers between devices, hop(): return lax.ppermute(block, ('row', 'col'), route)  6.94 us
    pallas_call x6, Pallas kernels, call(): pl.pallas_call(kernel, out_shape=out_shape, in_specs=[pl.BlockSpec(memory...  6.64 us
    ppermute x10, starting transfers between devices, swap(): return lax.ppermute(block, 'row', [(0, 1), (1, 0)])  2.44 us
    pallas_call x1, Pallas kernels, pair_body(): pl.pallas_call(first_kernel, out_shape=(sent, sent), in_specs=[pl.BlockSp...  1.85 us
  transfers between devices with their start and end apart: 22, of which 4 were waited for; matrix products, arithmetic and copies ran while one was open for 0% of the time, Pallas kernels for 13%

profile of v11, /device:TPU:0, one launch (start us, length us, event | category | flops | bytes accessed | tf_op | source)
XLA Modules:
  0.0 42.7 jit_solution(5141616276341374780)
XLA Ops:
  0.6 1.8 %shard_map.95 = (bf16[88,1152]{1,0:T(8,128)(2,1)}, bf16[88,1152]{1,0:T(8,128)(2,1)}) custom-call(s32[1]{0:T(128)} %bitcast.spot_ref.row_ref, bf16[80,1152]{1,0:T(8,128)(2,1)} %image_ref.1, bf16[160,576]{1,0:T(8,128)(2,1)} %text_ref.1, s32[1,80]{1,0:T(1,128)} %bitcast.5, s32[1,160]{1,0:T(1,128)} %bitcast.4), custom_call_target="tpu_custom_call" | custom-call | tf_op jit(solution)/shard_map/pallas_call | solution.py:283
  2.5 0.5 %collective-permute-start.2 = (bf16[88,1152]{1,0:T(8,128)(2,1)}, bf16[88,1152]{1,0:T(8,128)(2,1)S(1)}, u32[]{:S(2)}, u32[]{:S(2)}) collective-permute-start(bf16[88,1152]{1,0:T(8,128)(2,1)} %get-tuple-element.27), channel_id=1, source_target_pairs={{0,16},{16,0},{1,17},{17,1},{2,18},{18,2},{3,19},{19,3},{4,20},{20... | collective-permute-start | bytes 608264 | tf_op jit(solution)/shard_map/ppermute | solution.py:23
  3.0 3.7 %collective-permute-start = (bf16[88,1152]{1,0:T(8,128)(2,1)}, bf16[88,1152]{1,0:T(8,128)(2,1)S(1)}, u32[]{:S(2)}, u32[]{:S(2)}) collective-permute-start(bf16[88,1152]{1,0:T(8,128)(2,1)} %get-tuple-element.25.refs_2_), channel_id=1, source_target_pairs={{0,8},{1,9},{2,10},{3,11},{4,12},{5,13},{6,14},{7,15},{8,0},{9,1},... | collective-permute-start | bytes 608264 | tf_op jit(solution)/shard_map/ppermute | solution.py:19
  6.7 0.0 collective-permute-done.2.refs_3_
  6.7 1.6 %collective-permute-start.9 = (bf16[88,1152]{1,0:T(8,128)(2,1)S(1)}, bf16[88,1152]{1,0:T(8,128)(2,1)S(1)}, u32[]{:S(2)}, u32[]{:S(2)}) collective-permute-start(bf16[88,1152]{1,0:T(8,128)(2,1)S(1)} %collective-permute-done.2.refs_3_), channel_id=1, source_target_pairs={{0,8},{1,9},{2,10},{3,11},{4,12},{5,13},{6,14},{7,15},{8,0},{9,1},... | collective-permute-start | bytes 608264 | tf_op jit(solution)/shard_map/ppermute | solution.py:19
  8.3 1.5 %collective-permute-start.1 = (bf16[88,1152]{1,0:T(8,128)(2,1)}, bf16[88,1152]{1,0:T(8,128)(2,1)S(1)}, u32[]{:S(2)}, u32[]{:S(2)}) collective-permute-start(bf16[88,1152]{1,0:T(8,128)(2,1)} %get-tuple-element.25.refs_2_), channel_id=1, source_target_pairs={{0,1},{1,0},{2,3},{3,2},{4,5},{5,4},{6,7},{7,6},{8,9},{9,8},{10,11... | collective-permute-start | bytes 608264 | tf_op jit(solution)/shard_map/ppermute | solution.py:19
  9.7 0.5 %collective-permute-start.3 = (bf16[88,1152]{1,0:T(8,128)(2,1)S(1)}, bf16[88,1152]{1,0:T(8,128)(2,1)S(1)}, u32[]{:S(2)}, u32[]{:S(2)}) collective-permute-start(bf16[88,1152]{1,0:T(8,128)(2,1)S(1)} %collective-permute-done.2.refs_3_), channel_id=1, source_target_pairs={{0,1},{1,0},{2,3},{3,2},{4,5},{5,4},{6,7},{7,6},{8,9},{9,8},{10,11... | collective-permute-start | bytes 608264 | tf_op jit(solution)/shard_map/ppermute | solution.py:19
  12.9 0.0 collective-permute-done.refs_2_.refs_0_
  12.9 0.1 collective-permute-start.8
  13.0 1.6 %collective-permute-start.11 = (bf16[88,1152]{1,0:T(8,128)(2,1)S(1)}, bf16[88,1152]{1,0:T(8,128)(2,1)S(1)}, u32[]{:S(2)}, u32[]{:S(2)}) collective-permute-start(bf16[88,1152]{1,0:T(8,128)(2,1)S(1)} %collective-permute-done.refs_2_.refs_0_), channel_id=1, source_target_pairs={{0,1},{1,0},{2,3},{3,2},{4,5},{5,4},{6,7},{7,6},{8,9},{9,8},{10,11... | collective-permute-start | bytes 608264 | tf_op jit(solution)/shard_map/ppermute | solution.py:19
  14.6 1.4 %collective-permute-done.9.refs_3_.refs_1_ = bf16[88,1152]{1,0:T(8,128)(2,1)S(1)} collective-permute-done((bf16[88,1152]{1,0:T(8,128)(2,1)S(1)}, bf16[88,1152]{1,0:T(8,128)(2,1)S(1)}, u32[]{:S(2)}, u32[]{:S(2)}) %collective-permute-start.9) | collective-permute-done | bytes 202784 | tf_op jit(solution)/shard_map/ppermute | solution.py:19
  15.9 0.0 collective-permute-start.10
  15.9 0.0 collective-permute-done.1.refs_0_
  16.0 2.1 %collective-permute-start.13 = (bf16[88,1152]{1,0:T(8,128)(2,1)S(1)}, bf16[88,1152]{1,0:T(8,128)(2,1)S(1)}, u32[]{:S(2)}, u32[]{:S(2)}) collective-permute-start(bf16[88,1152]{1,0:T(8,128)(2,1)S(1)} %collective-permute-done.9.refs_3_.refs_1_), channel_id=1, source_target_pairs={{0,1},{1,0},{2,3},{3,2},{4,5},{5,4},{6,7},{7,6},{8,9},{9,8},{10,11... | collective-permute-start | bytes 608264 | tf_op jit(solution)/shard_map/ppermute | solution.py:19
  18.1 0.0 collective-permute-done.3.refs_1_
  18.1 0.3 collective-permute-start.4
  18.4 0.0 collective-permute-done.8.refs_4_.refs_6_.refs_8_
  18.4 0.3 collective-permute-start.5
  18.6 0.2 collective-permute-done.11.refs_0_
  18.8 0.1 collective-permute-start.6
  18.9 0.0 collective-permute-done.10.refs_5_.refs_7_.refs_9_
  18.9 0.5 %collective-permute-start.7 = (bf16[88,1152]{1,0:T(8,128)(2,1)S(1)}, bf16[88,1152]{1,0:T(8,128)(2,1)S(1)}, u32[]{:S(2)}, u32[]{:S(2)}) collective-permute-start(bf16[88,1152]{1,0:T(8,128)(2,1)S(1)} %collective-permute-done.3.refs_1_), channel_id=1, source_target_pairs={{0,16},{16,0},{1,17},{17,1},{2,18},{18,2},{3,19},{19,3},{4,20},{20... | collective-permute-start | bytes 608264 | tf_op jit(solution)/shard_map/ppermute | solution.py:23
  19.3 1.3 %shard_map.97 = (bf16[320,1152]{1,0:T(8,128)(2,1)S(1)}, bf16[160,1152]{1,0:T(8,128)(2,1)S(1)}, f32[320,1152]{1,0:T(8,128)S(1)}) custom-call(s32[1]{0:T(128)} %bitcast.spot_ref.row_ref, s32[1]{0:T(128)} %bitcast.1.col_ref, f32[8,128]{1,0:T(8,128)S(1)} %shard_map.96.number_ref, bf16[88,1152]{1,0:T(8,128)(2,1)S(1)} %collective-permute-done.1.refs_0_, ...), custom_call_target="tpu_custom_call" | custom-call | flops 235929600 | bytes 3801096 | tf_op jit(solution)/shard_map/pallas_call | solution.py:256
  20.6 1.2 %collective-permute-done.13.refs_1_ = bf16[88,1152]{1,0:T(8,128)(2,1)S(1)} collective-permute-done((bf16[88,1152]{1,0:T(8,128)(2,1)S(1)}, bf16[88,1152]{1,0:T(8,128)(2,1)S(1)}, u32[]{:S(2)}, u32[]{:S(2)}) %collective-permute-start.13) | collective-permute-done | bytes 202784 | tf_op jit(solution)/shard_map/ppermute | solution.py:19
  21.8 0.0 collective-permute-start.12
  21.8 0.0 collective-permute-done.4.refs_2_.refs_4_
  21.8 0.5 %collective-permute-start.14 = (bf16[88,1152]{1,0:T(8,128)(2,1)S(1)}, bf16[88,1152]{1,0:T(8,128)(2,1)S(1)}, u32[]{:S(2)}, u32[]{:S(2)}) collective-permute-start(bf16[88,1152]{1,0:T(8,128)(2,1)S(1)} %collective-permute-done.13.refs_1_), channel_id=1, source_target_pairs={{0,16},{16,0},{1,17},{17,1},{2,18},{18,2},{3,19},{19,3},{4,20},{20... | collective-permute-start | bytes 608264 | tf_op jit(solution)/shard_map/ppermute | solution.py:23
  22.3 0.0 collective-permute-done.5.refs_3_.refs_5_
  22.3 0.0 collective-permute-done.6.refs_4_.refs_6_
  22.3 0.0 collective-permute-done.7.refs_5_.refs_7_
  22.3 0.0 copy-start
  22.3 1.2 %shard_map.98 = (bf16[320,1152]{1,0:T(8,128)(2,1)S(1)}, bf16[160,1152]{1,0:T(8,128)(2,1)S(1)}, f32[160,1152]{1,0:T(8,128)S(1)}) custom-call(s32[1]{0:T(128)} %bitcast.spot_ref.row_ref, s32[1]{0:T(128)} %bitcast.1.col_ref, f32[8,128]{1,0:T(8,128)S(1)} %shard_map.96.number_ref, bf16[88,1152]{1,0:T(8,128)(2,1)S(1)} %collective-permute-done.11.refs_0_, ...), custom_call_target="tpu_custom_call" | custom-call | flops 353894400 | bytes 3837960 | tf_op jit(solution)/shard_map/pallas_call | solution.py:256
  23.6 0.0 collective-permute-done.12.refs_2_.refs_10_.refs_6_
  23.6 0.0 collective-permute-done.14.refs_3_.refs_11_.refs_7_
  23.6 0.9 %shard_map.99 = (bf16[160,1152]{1,0:T(8,128)(2,1)S(1)}, bf16[80,1152]{1,0:T(8,128)(2,1)S(1)}, bf16[80,1152]{1,0:T(8,128)(2,1)S(1)}) custom-call(s32[1]{0:T(128)} %bitcast.spot_ref.row_ref, s32[1]{0:T(128)} %bitcast.1.col_ref, f32[8,128]{1,0:T(8,128)S(1)} %shard_map.96.number_ref, bf16[88,1152]{1,0:T(8,128)(2,1)S(1)} %collective-permute-done.11.refs_0_, ...), custom_call_target="tpu_custom_call" | custom-call | flops 117964800 | bytes 2658312 | tf_op jit(solution)/shard_map/pallas_call | solution.py:256
  24.5 2.1 %collective-permute-start.15 = (bf16[80,1152]{1,0:T(8,128)(2,1)S(1)}, bf16[80,1152]{1,0:T(8,128)(2,1)S(1)}, u32[]{:S(2)}, u32[]{:S(2)}) collective-permute-start(bf16[80,1152]{1,0:T(8,128)(2,1)S(1)} %get-tuple-element.40), channel_id=1, source_target_pairs={{0,1},{1,0},{2,3},{3,2},{4,5},{5,4},{6,7},{7,6},{8,9},{9,8},{10,11... | collective-permute-start | bytes 552968 | tf_op jit(solution)/shard_map/ppermute | solution.py:19
  26.6 0.1 collective-permute-start.18
  26.7 2.2 %shard_map.100 = (f32[80,1152]{1,0:T(8,128)S(1)}, f32[80,1152]{1,0:T(8,128)S(1)}, bf16[80,1152]{1,0:T(8,128)(2,1)S(1)}, bf16[80,1152]{1,0:T(8,128)(2,1)S(1)}) custom-call(s32[1]{0:T(128)} %bitcast.spot_ref.row_ref, s32[1]{0:T(128)} %bitcast.1.col_ref, f32[8,128]{1,0:T(8,128)S(1)} %shard_map.96.number_ref, ...), custom_call_target="tpu_custom_call" | custom-call | flops 825753600 | bytes 7229448 | tf_op jit(solution)/shard_map/pallas_call | solution.py:256
  28.9 0.3 collective-permute-start.17
  29.2 1.0 %shard_map.101 = (f32[80,1152]{1,0:T(8,128)S(1)}, f32[80,1152]{1,0:T(8,128)S(1)}) custom-call(s32[1]{0:T(128)} %bitcast.spot_ref.row_ref, s32[1]{0:T(128)} %bitcast.1.col_ref, f32[8,128]{1,0:T(8,128)S(1)} %shard_map.96.number_ref, bf16[88,1152]{1,0:T(8,128)(2,1)S(1)} %collective-permute-done.refs_2_.refs_0_, ...), custom_call_target="tpu_custom_call" | custom-call | flops 353894400 | bytes 5681160 | tf_op jit(solution)/shard_map/pallas_call | solution.py:256
  30.2 0.0 collective-permute-done.15
  30.3 2.5 %collective-permute-start.16 = (bf16[80,1152]{1,0:T(8,128)(2,1)S(1)}, bf16[80,1152]{1,0:T(8,128)(2,1)S(1)}, u32[]{:S(2)}, u32[]{:S(2)}) collective-permute-start(bf16[80,1152]{1,0:T(8,128)(2,1)S(1)} %add_convert_fusion.1), channel_id=1, source_target_pairs={{0,8},{1,9},{2,10},{3,11},{4,12},{5,13},{6,14},{7,15},{8,0},{9,1},... | collective-permute-start | bytes 552968 | tf_op jit(solution)/shard_map/ppermute | solution.py:19
  32.7 1.5 %collective-permute-start.20 = (bf16[80,1152]{1,0:T(8,128)(2,1)S(1)}, bf16[80,1152]{1,0:T(8,128)(2,1)S(1)}, u32[]{:S(2)}, u32[]{:S(2)}) collective-permute-start(bf16[80,1152]{1,0:T(8,128)(2,1)S(1)} %get-tuple-element.45), channel_id=1, source_target_pairs={{0,1},{1,0},{2,3},{3,2},{4,5},{5,4},{6,7},{7,6},{8,9},{9,8},{10,11... | collective-permute-start | bytes 552968 | tf_op jit(solution)/shard_map/ppermute | solution.py:19
  34.3 2.6 %collective-permute-start.19 = (bf16[80,1152]{1,0:T(8,128)(2,1)S(1)}, bf16[80,1152]{1,0:T(8,128)(2,1)S(1)}, u32[]{:S(2)}, u32[]{:S(2)}) collective-permute-start(bf16[80,1152]{1,0:T(8,128)(2,1)S(1)} %add_convert_fusion), channel_id=1, source_target_pairs={{0,24},{1,25},{2,26},{3,27},{4,28},{5,29},{6,30},{7,31},{8,16},{9,... | collective-permute-start | bytes 552968 | tf_op jit(solution)/shard_map/ppermute | solution.py:19
  36.8 0.8 %collective-permute-start.21 = (bf16[80,1152]{1,0:T(8,128)(2,1)S(1)}, bf16[80,1152]{1,0:T(8,128)(2,1)S(1)}, u32[]{:S(2)}, u32[]{:S(2)}) collective-permute-start(bf16[80,1152]{1,0:T(8,128)(2,1)S(1)} %get-tuple-element.47), channel_id=1, source_target_pairs={{0,17},{1,16},{2,19},{3,18},{4,21},{5,20},{6,23},{7,22},{8,25},{9,... | collective-permute-start | bytes 552968 | tf_op jit(solution)/shard_map/ppermute | solution.py:19
  37.6 0.0 collective-permute-done.16
  37.7 4.1 %collective-permute-done.19 = bf16[80,1152]{1,0:T(8,128)(2,1)S(1)} collective-permute-done((bf16[80,1152]{1,0:T(8,128)(2,1)S(1)}, bf16[80,1152]{1,0:T(8,128)(2,1)S(1)}, u32[]{:S(2)}, u32[]{:S(2)}) %collective-permute-start.19) | collective-permute-done | bytes 184352 | tf_op jit(solution)/shard_map/ppermute | solution.py:19
  41.9 0.8 %shard_map.102 = (bf16[80,1152]{1,0:T(8,128)(2,1)}, bf16[160,576]{1,0:T(8,128)(2,1)}) custom-call(s32[1]{0:T(128)} %bitcast.spot_ref.row_ref, f32[80,1152]{1,0:T(8,128)S(1)} %convert_add_fusion.1.stay_ref, f32[80,1152]{1,0:T(8,128)S(1)} %convert_add_fusion.crossed_ref, bf16[80,1152]{1,0:T(8,128)(2,1)S(1)} %collective-permute-done.20.near_stay_ref, ...), custom_call_target="tpu_custom_call" | custom-call | tf_op jit(solution)/shard_map/pallas_call | solution.py:340
  (10 shorter events, 0.2 us)
Async XLA Ops:
  2.5 4.2 %collective-permute-start.2 = (bf16[88,1152]{1,0:T(8,128)(2,1)}, bf16[88,1152]{1,0:T(8,128)(2,1)S(1)}, u32[]{:S(2)}, u32[]{:S(2)}) collective-permute-start(bf16[88,1152]{1,0:T(8,128)(2,1)} %get-tuple-element.27), channel_id=1, source_target_pairs={{0,16},{16,0},{1,17},{17,1},{2,18},{18,2},{3,19},{19,3},{4,20},{20... | collective-permute-start | bytes 608264 | tf_op jit(solution)/shard_map/ppermute | solution.py:23
  3.0 9.9 %collective-permute-start = (bf16[88,1152]{1,0:T(8,128)(2,1)}, bf16[88,1152]{1,0:T(8,128)(2,1)S(1)}, u32[]{:S(2)}, u32[]{:S(2)}) collective-permute-start(bf16[88,1152]{1,0:T(8,128)(2,1)} %get-tuple-element.25.refs_2_), channel_id=1, source_target_pairs={{0,8},{1,9},{2,10},{3,11},{4,12},{5,13},{6,14},{7,15},{8,0},{9,1},... | collective-permute-start | bytes 608264 | tf_op jit(solution)/shard_map/ppermute | solution.py:19
  6.7 9.3 %collective-permute-start.9 = (bf16[88,1152]{1,0:T(8,128)(2,1)S(1)}, bf16[88,1152]{1,0:T(8,128)(2,1)S(1)}, u32[]{:S(2)}, u32[]{:S(2)}) collective-permute-start(bf16[88,1152]{1,0:T(8,128)(2,1)S(1)} %collective-permute-done.2.refs_3_), channel_id=1, source_target_pairs={{0,8},{1,9},{2,10},{3,11},{4,12},{5,13},{6,14},{7,15},{8,0},{9,1},... | collective-permute-start | bytes 608264 | tf_op jit(solution)/shard_map/ppermute | solution.py:19
  8.3 7.7 %collective-permute-start.1 = (bf16[88,1152]{1,0:T(8,128)(2,1)}, bf16[88,1152]{1,0:T(8,128)(2,1)S(1)}, u32[]{:S(2)}, u32[]{:S(2)}) collective-permute-start(bf16[88,1152]{1,0:T(8,128)(2,1)} %get-tuple-element.25.refs_2_), channel_id=1, source_target_pairs={{0,1},{1,0},{2,3},{3,2},{4,5},{5,4},{6,7},{7,6},{8,9},{9,8},{10,11... | collective-permute-start | bytes 608264 | tf_op jit(solution)/shard_map/ppermute | solution.py:19
  9.7 8.4 %collective-permute-start.3 = (bf16[88,1152]{1,0:T(8,128)(2,1)S(1)}, bf16[88,1152]{1,0:T(8,128)(2,1)S(1)}, u32[]{:S(2)}, u32[]{:S(2)}) collective-permute-start(bf16[88,1152]{1,0:T(8,128)(2,1)S(1)} %collective-permute-done.2.refs_3_), channel_id=1, source_target_pairs={{0,1},{1,0},{2,3},{3,2},{4,5},{5,4},{6,7},{7,6},{8,9},{9,8},{10,11... | collective-permute-start | bytes 608264 | tf_op jit(solution)/shard_map/ppermute | solution.py:19
  12.9 5.4 %collective-permute-start.8 = (bf16[88,1152]{1,0:T(8,128)(2,1)S(1)}, bf16[88,1152]{1,0:T(8,128)(2,1)S(1)}, u32[]{:S(2)}, u32[]{:S(2)}) collective-permute-start(bf16[88,1152]{1,0:T(8,128)(2,1)S(1)} %collective-permute-done.refs_2_.refs_0_), channel_id=1, source_target_pairs={{0,16},{16,0},{1,17},{17,1},{2,18},{18,2},{3,19},{19,3},{4,20},{20... | collective-permute-start | bytes 608264 | tf_op jit(solution)/shard_map/ppermute | solution.py:23
  13.0 5.8 %collective-permute-start.11 = (bf16[88,1152]{1,0:T(8,128)(2,1)S(1)}, bf16[88,1152]{1,0:T(8,128)(2,1)S(1)}, u32[]{:S(2)}, u32[]{:S(2)}) collective-permute-start(bf16[88,1152]{1,0:T(8,128)(2,1)S(1)} %collective-permute-done.refs_2_.refs_0_), channel_id=1, source_target_pairs={{0,1},{1,0},{2,3},{3,2},{4,5},{5,4},{6,7},{7,6},{8,9},{9,8},{10,11... | collective-permute-start | bytes 608264 | tf_op jit(solution)/shard_map/ppermute | solution.py:19
  15.9 2.9 %collective-permute-start.10 = (bf16[88,1152]{1,0:T(8,128)(2,1)S(1)}, bf16[88,1152]{1,0:T(8,128)(2,1)S(1)}, u32[]{:S(2)}, u32[]{:S(2)}) collective-permute-start(bf16[88,1152]{1,0:T(8,128)(2,1)S(1)} %collective-permute-done.9.refs_3_.refs_1_), channel_id=1, source_target_pairs={{0,16},{16,0},{1,17},{17,1},{2,18},{18,2},{3,19},{19,3},{4,20},{20... | collective-permute-start | bytes 608264 | tf_op jit(solution)/shard_map/ppermute | solution.py:23
  16.0 5.9 %collective-permute-start.13 = (bf16[88,1152]{1,0:T(8,128)(2,1)S(1)}, bf16[88,1152]{1,0:T(8,128)(2,1)S(1)}, u32[]{:S(2)}, u32[]{:S(2)}) collective-permute-start(bf16[88,1152]{1,0:T(8,128)(2,1)S(1)} %collective-permute-done.9.refs_3_.refs_1_), channel_id=1, source_target_pairs={{0,1},{1,0},{2,3},{3,2},{4,5},{5,4},{6,7},{7,6},{8,9},{9,8},{10,11... | collective-permute-start | bytes 608264 | tf_op jit(solution)/shard_map/ppermute | solution.py:19
  18.1 3.7 %collective-permute-start.4 = (bf16[88,1152]{1,0:T(8,128)(2,1)}, bf16[88,1152]{1,0:T(8,128)(2,1)S(1)}, u32[]{:S(2)}, u32[]{:S(2)}) collective-permute-start(bf16[88,1152]{1,0:T(8,128)(2,1)} %get-tuple-element.25.refs_2_), channel_id=1, source_target_pairs={{0,16},{16,0},{1,17},{17,1},{2,18},{18,2},{3,19},{19,3},{4,20},{20... | collective-permute-start | bytes 608264 | tf_op jit(solution)/shard_map/ppermute | solution.py:23
  18.4 4.0 %collective-permute-start.5 = (bf16[88,1152]{1,0:T(8,128)(2,1)S(1)}, bf16[88,1152]{1,0:T(8,128)(2,1)S(1)}, u32[]{:S(2)}, u32[]{:S(2)}) collective-permute-start(bf16[88,1152]{1,0:T(8,128)(2,1)S(1)} %collective-permute-done.2.refs_3_), channel_id=1, source_target_pairs={{0,16},{16,0},{1,17},{17,1},{2,18},{18,2},{3,19},{19,3},{4,20},{20... | collective-permute-start | bytes 608264 | tf_op jit(solution)/shard_map/ppermute | solution.py:23
  18.8 3.5 %collective-permute-start.6 = (bf16[88,1152]{1,0:T(8,128)(2,1)S(1)}, bf16[88,1152]{1,0:T(8,128)(2,1)S(1)}, u32[]{:S(2)}, u32[]{:S(2)}) collective-permute-start(bf16[88,1152]{1,0:T(8,128)(2,1)S(1)} %collective-permute-done.1.refs_0_), channel_id=1, source_target_pairs={{0,16},{16,0},{1,17},{17,1},{2,18},{18,2},{3,19},{19,3},{4,20},{20... | collective-permute-start | bytes 608264 | tf_op jit(solution)/shard_map/ppermute | solution.py:23
  18.9 3.5 %collective-permute-start.7 = (bf16[88,1152]{1,0:T(8,128)(2,1)S(1)}, bf16[88,1152]{1,0:T(8,128)(2,1)S(1)}, u32[]{:S(2)}, u32[]{:S(2)}) collective-permute-start(bf16[88,1152]{1,0:T(8,128)(2,1)S(1)} %collective-permute-done.3.refs_1_), channel_id=1, source_target_pairs={{0,16},{16,0},{1,17},{17,1},{2,18},{18,2},{3,19},{19,3},{4,20},{20... | collective-permute-start | bytes 608264 | tf_op jit(solution)/shard_map/ppermute | solution.py:23
  21.8 1.8 %collective-permute-start.12 = (bf16[88,1152]{1,0:T(8,128)(2,1)S(1)}, bf16[88,1152]{1,0:T(8,128)(2,1)S(1)}, u32[]{:S(2)}, u32[]{:S(2)}) collective-permute-start(bf16[88,1152]{1,0:T(8,128)(2,1)S(1)} %collective-permute-done.11.refs_0_), channel_id=1, source_target_pairs={{0,16},{16,0},{1,17},{17,1},{2,18},{18,2},{3,19},{19,3},{4,20},{20... | collective-permute-start | bytes 608264 | tf_op jit(solution)/shard_map/ppermute | solution.py:23
  21.8 1.8 %collective-permute-start.14 = (bf16[88,1152]{1,0:T(8,128)(2,1)S(1)}, bf16[88,1152]{1,0:T(8,128)(2,1)S(1)}, u32[]{:S(2)}, u32[]{:S(2)}) collective-permute-start(bf16[88,1152]{1,0:T(8,128)(2,1)S(1)} %collective-permute-done.13.refs_1_), channel_id=1, source_target_pairs={{0,16},{16,0},{1,17},{17,1},{2,18},{18,2},{3,19},{19,3},{4,20},{20... | collective-permute-start | bytes 608264 | tf_op jit(solution)/shard_map/ppermute | solution.py:23
  22.3 4.4 %copy-start = (bf16[88,1152]{1,0:T(8,128)(2,1)S(1)}, bf16[88,1152]{1,0:T(8,128)(2,1)}, u32[]{:S(2)}) copy-start(bf16[88,1152]{1,0:T(8,128)(2,1)} %get-tuple-element.25.refs_2_) | copy-start | bytes 608260
  24.5 5.7 %collective-permute-start.15 = (bf16[80,1152]{1,0:T(8,128)(2,1)S(1)}, bf16[80,1152]{1,0:T(8,128)(2,1)S(1)}, u32[]{:S(2)}, u32[]{:S(2)}) collective-permute-start(bf16[80,1152]{1,0:T(8,128)(2,1)S(1)} %get-tuple-element.40), channel_id=1, source_target_pairs={{0,1},{1,0},{2,3},{3,2},{4,5},{5,4},{6,7},{7,6},{8,9},{9,8},{10,11... | collective-permute-start | bytes 552968 | tf_op jit(solution)/shard_map/ppermute | solution.py:19
  26.6 7.6 %collective-permute-start.18 = (bf16[80,1152]{1,0:T(8,128)(2,1)S(1)}, bf16[80,1152]{1,0:T(8,128)(2,1)S(1)}, u32[]{:S(2)}, u32[]{:S(2)}) collective-permute-start(bf16[80,1152]{1,0:T(8,128)(2,1)S(1)} %get-tuple-element.43), channel_id=1, source_target_pairs={{0,1},{1,0},{2,3},{3,2},{4,5},{5,4},{6,7},{7,6},{8,9},{9,8},{10,11... | collective-permute-start | bytes 552968 | tf_op jit(solution)/shard_map/ppermute | solution.py:19
  28.9 8.8 %collective-permute-start.17 = (f32[80,1152]{1,0:T(8,128)S(1)}, f32[80,1152]{1,0:T(8,128)S(1)}, u32[]{:S(2)}, u32[]{:S(2)}) collective-permute-start(f32[80,1152]{1,0:T(8,128)S(1)} %get-tuple-element.41), channel_id=1, source_target_pairs={{0,16},{16,0},{1,17},{17,1},{2,18},{18,2},{3,19},{19,3},{4,20},{20... | collective-permute-start | bytes 1105928 | tf_op jit(solution)/shard_map/ppermute | solution.py:23
  30.3 7.3 %collective-permute-start.16 = (bf16[80,1152]{1,0:T(8,128)(2,1)S(1)}, bf16[80,1152]{1,0:T(8,128)(2,1)S(1)}, u32[]{:S(2)}, u32[]{:S(2)}) collective-permute-start(bf16[80,1152]{1,0:T(8,128)(2,1)S(1)} %add_convert_fusion.1), channel_id=1, source_target_pairs={{0,8},{1,9},{2,10},{3,11},{4,12},{5,13},{6,14},{7,15},{8,0},{9,1},... | collective-permute-start | bytes 552968 | tf_op jit(solution)/shard_map/ppermute | solution.py:19
  32.7 9.1 %collective-permute-start.20 = (bf16[80,1152]{1,0:T(8,128)(2,1)S(1)}, bf16[80,1152]{1,0:T(8,128)(2,1)S(1)}, u32[]{:S(2)}, u32[]{:S(2)}) collective-permute-start(bf16[80,1152]{1,0:T(8,128)(2,1)S(1)} %get-tuple-element.45), channel_id=1, source_target_pairs={{0,1},{1,0},{2,3},{3,2},{4,5},{5,4},{6,7},{7,6},{8,9},{9,8},{10,11... | collective-permute-start | bytes 552968 | tf_op jit(solution)/shard_map/ppermute | solution.py:19
  34.3 7.5 %collective-permute-start.19 = (bf16[80,1152]{1,0:T(8,128)(2,1)S(1)}, bf16[80,1152]{1,0:T(8,128)(2,1)S(1)}, u32[]{:S(2)}, u32[]{:S(2)}) collective-permute-start(bf16[80,1152]{1,0:T(8,128)(2,1)S(1)} %add_convert_fusion), channel_id=1, source_target_pairs={{0,24},{1,25},{2,26},{3,27},{4,28},{5,29},{6,30},{7,31},{8,16},{9,... | collective-permute-start | bytes 552968 | tf_op jit(solution)/shard_map/ppermute | solution.py:19
  36.8 5.0 %collective-permute-start.21 = (bf16[80,1152]{1,0:T(8,128)(2,1)S(1)}, bf16[80,1152]{1,0:T(8,128)(2,1)S(1)}, u32[]{:S(2)}, u32[]{:S(2)}) collective-permute-start(bf16[80,1152]{1,0:T(8,128)(2,1)S(1)} %get-tuple-element.47), channel_id=1, source_target_pairs={{0,17},{1,16},{2,19},{3,18},{4,21},{5,20},{6,23},{7,22},{8,25},{9,... | collective-permute-start | bytes 552968 | tf_op jit(solution)/shard_map/ppermute | solution.py:19
